TPU v7x, 32 devices: a whole 2x2x4 slice. The times are simulated.
32 devices in a mesh: leaf: 4 (over z), trunk: 8 (over y, x, core).
Axes of the slice: x: 2, y: 2, z: 4, core: 2. Of those that a mesh axis runs over, the one named last changes fastest.
Arguments:
- trunk_tokens: bfloat16 [8, 2048, 1024], P('leaf', 'trunk'), may hold values from -6 to 6
- branch_tokens: bfloat16 [128, 128, 1024], P(('leaf', 'trunk')), may hold values from -6 to 6
- fork_offset: int32 [4, 8, 4], P('leaf', 'trunk'), may hold values from 0 to 255
- fork_tree: int32 [4, 8, 4], P('leaf', 'trunk'), may hold values from 0 to 1
- branch_len: int32 [128], P(('leaf', 'trunk')), may hold values from 0 to 128, as said below
- w_query: bfloat16 [1024, 1024], P('trunk'), may hold values from -0.1875 to 0.1875
- w_key: bfloat16 [1024, 1024], P('trunk'), may hold values from -0.1875 to 0.1875
- w_value: bfloat16 [1024, 1024], P('trunk'), may hold values from -0.1875 to 0.1875
- w_out: bfloat16 [1024, 1024], P('trunk'), may hold values from -0.1875 to 0.1875
Outputs:
- mixed: bfloat16 [128, 128, 1024], P(('leaf', 'trunk'))
Inputs may be any that keep to these rules, and one draw needn't show every extreme that they name: `branch_len`: each length is a multiple of 128; some slot has the full 128 in every draw.
All inputs are finite; a program needn't handle non-finite values.
Results may differ from a plain program's by a relative error of at most 0.0065.
Values may be sent and summed in bfloat16 or wider, within the bound.
No kernel may reach another device: no remote copies, remote signals or barrier semaphores. Data moves between devices by JAX's collectives and lax.ppermute only.
A program may use at most 128 MiB of HBM per device.

v0:
```python
import jax
import jax.numpy as jnp
from jax import lax
from jax.sharding import PartitionSpec as P

H = 8
DH = 128


def carried_in(value, axis, join, neutral):
    count, mine = (lax.axis_size(axis), lax.axis_index(axis))
    pieces = lax.all_gather(value, axis)
    subtotal = jnp.full_like(value, 0) + jnp.asarray(neutral, value.dtype)

    def step(position, subtotal):
        longer = join(subtotal, pieces[position])
        return jnp.where(position < mine, longer, subtotal)

    return lax.fori_loop(0, count - 1, step, subtotal)


def matmul(left, right):
    return jnp.dot(left, right, preferred_element_type=jnp.float32)


def add_states(earlier, later):
    return earlier + later


def shards(
    trunk_tokens, branch_tokens, fork_offset, fork_tree, branch_len, w_query, w_key, w_value, w_out
):
    trees, trunk_tok, width = trunk_tokens.shape
    slots, blen, _ = branch_tokens.shape
    heads_dim = w_key.shape[1]
    trunk_rows = trunk_tokens.reshape(trees * trunk_tok, width)
    branch_rows = branch_tokens.reshape(slots * blen, width)
    pieces = (
        lax.all_gather(w_query, "trunk", axis=0, tiled=True),
        lax.all_gather(w_key, "trunk", axis=0, tiled=True),
        lax.all_gather(w_value, "trunk", axis=0, tiled=True),
    )
    trunk_key = matmul(trunk_rows, pieces[1])
    trunk_value = matmul(trunk_rows, pieces[2])
    branch_query = matmul(branch_rows, pieces[0])
    branch_key = matmul(branch_rows, pieces[1])
    branch_value = matmul(branch_rows, pieces[2])
    trunk_key = trunk_key.astype(jnp.bfloat16)
    trunk_value = trunk_value.astype(jnp.bfloat16)
    key_four = trunk_key.reshape(trees, trunk_tok, H, DH)
    value_four = trunk_value.reshape(trees, trunk_tok, H, DH)
    totals = jnp.einsum("rthd,rthf->rhdf", key_four, value_four, preferred_element_type=jnp.float32)
    carried = carried_in(totals, "trunk", add_states, jnp.zeros_like(totals))
    entries = fork_offset.shape[2]
    offsets = fork_offset.reshape(entries)
    which_tree = fork_tree.reshape(entries)
    positions = jnp.arange(trees * trunk_tok, dtype=jnp.int32)
    tree_of = positions // trunk_tok
    place_in = positions % trunk_tok
    selected_rows = (tree_of[None, :] == which_tree[:, None]) & (
        place_in[None, :] < offsets[:, None]
    )
    masked_key = selected_rows.astype(jnp.bfloat16)[:, :, None] * trunk_key[None]
    masked_key = masked_key.reshape(entries, trees * trunk_tok, H, DH)
    partial_value = jnp.einsum(
        "erhd,rhf->ehdf",
        masked_key,
        trunk_value.reshape(trees * trunk_tok, H, DH),
        preferred_element_type=jnp.float32,
    )
    tree_pick = (jnp.arange(trees, dtype=jnp.int32)[None, :] == which_tree[:, None]).astype(
        jnp.float32
    )
    chosen = jnp.sum(tree_pick[:, :, None, None, None] * carried[None], axis=1)
    fork_state = chosen + partial_value
    query = branch_query.astype(jnp.bfloat16).reshape(slots, blen, H, DH)
    key = branch_key.astype(jnp.bfloat16).reshape(slots, blen, H, DH)
    value = branch_value.astype(jnp.bfloat16).reshape(slots, blen, H, DH)
    received = lax.all_to_all(fork_state, "leaf", split_axis=0, concat_axis=0, tiled=True)
    inter = jnp.einsum(
        "sbhd,shdf->sbhf", query.astype(jnp.float32), received, precision=lax.Precision.HIGHEST
    )
    scores = jnp.einsum("sbhd,schd->shbc", query, key, preferred_element_type=jnp.float32)
    rows = jnp.arange(blen, dtype=jnp.int32)
    causal = rows[None, :] <= rows[:, None]
    weights = jnp.where(causal[None, None], scores, 0.0).astype(jnp.bfloat16)
    numerator = inter + jnp.einsum(
        "shbc,schf->sbhf", weights, value, preferred_element_type=jnp.float32
    )
    meansq = jnp.mean(numerator * numerator, axis=-1, keepdims=True)
    normed = (
        (numerator * lax.rsqrt(meansq + 1e-06))
        .astype(jnp.bfloat16)
        .reshape(slots * blen, heads_dim)
    )
    projected = matmul(normed, lax.all_gather(w_out, "trunk", axis=0, tiled=True))
    live = rows[None, :] < branch_len[:, None]
    projected = projected.reshape(slots, blen, width)
    return jnp.where(live[:, :, None], projected, 0.0).astype(jnp.bfloat16)


def solution(mesh):
    in_specs = (
        P("leaf", "trunk", None),
        P(("leaf", "trunk"), None, None),
        P("leaf", "trunk", None),
        P("leaf", "trunk", None),
        P(("leaf", "trunk")),
        P("trunk", None),
        P("trunk", None),
        P("trunk", None),
        P("trunk", None),
    )
    out_specs = P(("leaf", "trunk"), None, None)
    return jax.shard_map(shards, mesh=mesh, in_specs=in_specs, out_specs=out_specs, check_vma=False)
```

profile of v0, /device:TPU:0, one launch (start us, length us, event | category | flops | bytes accessed | tf_op | source)
XLA Modules:
  0.0 225.0 jit_solution(13106616534962809881)
XLA Ops:
  6.5 0.7 all-gather.7.cloned.1.call-update
  7.3 0.0 all-gather.9.cloned.1.call-start
  7.3 0.7 all-gather.9.cloned.1.call-update
  8.0 0.0 all-gather.15.cloned.1.call-start
  8.1 31.8 %all-gather.7.cloned.1.call-done = bf16[1024,1024]{1,0:T(8,128)(2,1)} async-done(((bf16[128,1024]{1,0:T(8,128)(2,1)}), bf16[1024,1024]{1,0:T(8,128)(2,1)}) %all-gather.7.cloned.1.call-update) | async-done | bytes 2097168 | tf_op jit(solution)/shard_map/all_gather | solution.py:40
  39.9 3.2 %convolution_convert_fusion.4 = bf16[512,1024]{1,0:T(8,128)(2,1)S(1)} fusion(bf16[512,1024]{1,0:T(8,128)(2,1)} %bitcast.80, bf16[1024,1024]{1,0:T(8,128)(2,1)} %all-gather.7.cloned.1.call-done), kind=kOutput, calls=%fused_computation.20 | convolution fusion | flops 1074266112 | bytes 4194304 | tf_op jit(solution)/shard_map/dot_general | solution.py:23
  43.1 0.3 copy.33
  43.3 26.4 %all-gather.9.cloned.1.call-done = bf16[1024,1024]{1,0:T(8,128)(2,1)} async-done(((bf16[128,1024]{1,0:T(8,128)(2,1)}), bf16[1024,1024]{1,0:T(8,128)(2,1)}) %all-gather.9.cloned.1.call-update) | async-done | bytes 2097168 | tf_op jit(solution)/shard_map/all_gather | solution.py:41
  69.7 3.2 %convolution_convert_fusion.3 = bf16[512,1024]{1,0:T(8,128)(2,1)S(1)} fusion(bf16[512,1024]{1,0:T(8,128)(2,1)} %bitcast.81, bf16[1024,1024]{1,0:T(8,128)(2,1)} %all-gather.9.cloned.1.call-done), kind=kOutput, calls=%fused_computation.19 | convolution fusion | flops 1074266112 | bytes 4194304 | tf_op jit(solution)/shard_map/dot_general | solution.py:23
  72.9 1.0 copy-done.1
  73.8 0.3 copy.34
  74.1 1.5 fusion.18
  75.6 0.0 all-gather.11.cloned.1.call-start
  75.7 0.5 all-gather.11.cloned.1.call-update
  76.3 0.1 and_convert_fusion
  76.3 0.1 fusion.34
  76.4 2.3 %copy.31 = bf16[512,1024]{0,1:T(8,128)(2,1)} copy(bf16[512,1024]{1,0:T(8,128)(2,1)} %copy-done.1) | data formatting | bytes 2097152 | tf_op jit(solution)/shard_map/reshape | solution.py:68
  78.7 1.2 copy_bitcast_fusion
  79.9 50.3 %all-gather.15.cloned.1.call-done = f32[16,8,128,128]{3,2,1,0:T(8,128)} async-done(((f32[2,8,128,128]{3,2,1,0:T(8,128)}), f32[16,8,128,128]{3,2,1,0:T(8,128)}) %all-gather.15.cloned.1.call-update) | async-done | bytes 8388624 | tf_op jit(solution)/shard_map/all_gather | solution.py:12
  130.2 11.3 %while.14 = (s32[]{:T(128)}, f32[2,8,128,128]{3,2,1,0:T(8,128)S(1)}, s32[]{:T(128)}, f32[8,2,8,128,128]{4,3,2,1,0:T(8,128)}, s32[]{:T(128)}, /*index=5*/s32[]{:T(128)}) while((s32[]{:T(128)}, f32[2,8,128,128]{3,2,1,0:T(8,128)S(1)}, s32[]{:T(128)}, f32[8,2,8,128,128]{4,3,2,1,0:T(8,128)}, s32[]{:T(128)}, /*index=5*/s32[]{:T(128)}) %tuple.47), condition=%wide.region_1.2_spmd.clone, body=%wide.region_0.1_spmd.clone.sunk | while | flops 786436 | bytes 3145821 | solution.py:19
  130.2 1.6 add_select_fusion.3
  131.8 1.6 add_select_fusion.3
  133.4 1.6 add_select_fusion.3
  135.0 1.6 add_select_fusion.3
  136.6 1.6 add_select_fusion.3
  138.3 1.6 add_select_fusion.3
  139.9 1.6 add_select_fusion.3
  141.5 1.8 multiply_reduce_fusion
  143.3 1.9 copy.24
  145.2 4.0 %bitcast_add_fusion = f32[4,8,128,128]{2,3,1,0:T(8,128)} fusion(f32[4,8,128,128]{2,3,1,0:T(8,128)S(1)} %copy.24, bf16[512,8,128,1]{0,2,1,3:T(8,128)(2,1)} %bitcast.74, bf16[512,8,128]{2,0,1:T(8,128)(2,1)} %copy_bitcast_fusion, bf16[4,512]{1,0:T(4,128)(2,1)S(1)} %and_convert_fusion), kind=kOutput, calls=%fused_computation.10 | convolution fusion | flops 545783808 | bytes 6295552 | tf_op jit(solution)/shard_map/erhd,rhf->ehdf/dot_general | solution.py:65
  149.2 4.8 %all-to-all-start = ((f32[4,8,128,128]{2,3,1,0:T(8,128)}), f32[4,8,128,128]{2,3,1,0:T(8,128)}, u32[]{:S(2)}, u32[]{:S(2)}) async-start(f32[4,8,128,128]{2,3,1,0:T(8,128)} %bitcast_add_fusion), calls=%async_computation | async-start | bytes 4194304 | tf_op jit(solution)/shard_map/all_to_all | solution.py:79
  154.0 0.0 all-gather.13.cloned.1.call-start
  154.0 0.5 all-gather.13.cloned.1.call-update
  154.6 0.1 iota_compare_fusion.2
  154.6 5.2 %all-gather.11.cloned.1.call-done = bf16[1024,1024]{1,0:T(8,128)(2,1)} async-done(((bf16[128,1024]{1,0:T(8,128)(2,1)}), bf16[1024,1024]{1,0:T(8,128)(2,1)}) %all-gather.11.cloned.1.call-update) | async-done | bytes 2097168 | tf_op jit(solution)/shard_map/all_gather | solution.py:39
  159.9 2.8 %fusion.12 = bf16[64,8,8,128]{3,1,2,0:T(8,128)(2,1)S(1)} fusion(bf16[512,1024]{1,0:T(8,128)(2,1)S(1)} %bitcast.63, bf16[1024,1024]{1,0:T(8,128)(2,1)} %all-gather.11.cloned.1.call-done), kind=kOutput, calls=%fused_computation.21 | convolution fusion | flops 1074266112 | bytes 4194304 | tf_op jit(solution)/shard_map/dot_general | solution.py:23
  162.7 0.3 copy.35
  163.0 1.3 copy-done.5
  164.3 1.3 fusion.13
  165.6 0.3 copy.36
  165.9 1.3 copy-done.4
  167.2 1.3 fusion.14
  168.5 1.3 copy.37
  169.7 33.0 %all-to-all-done = f32[4,8,128,128]{2,3,1,0:T(8,128)} async-done(((f32[4,8,128,128]{2,3,1,0:T(8,128)}), f32[4,8,128,128]{2,3,1,0:T(8,128)}, u32[]{:S(2)}, u32[]{:S(2)}) %all-to-all-start) | async-done | bytes 2097184 | tf_op jit(solution)/shard_map/all_to_all | solution.py:79
  202.7 5.2 %fusion.25 = f32[4,8,128,128]{3,2,1,0:T(8,128)} fusion(f32[4,8,128,128]{2,3,1,0:T(8,128)} %all-to-all-done, bf16[4,128,8,128]{3,2,1,0:T(8,128)(2,1)S(1)} %bitcast.66), kind=kOutput, calls=%fused_computation.33 | convolution fusion | flops 805306368 | bytes 5242880 | tf_op jit(solution)/shard_map/sbhd,shdf->sbhf/dot_general | solution.py:80
  207.9 4.8 %fusion.4 = (f32[4,128,8]{1,2,0:T(8,128)S(1)}, f32[4,8,128,128]{3,2,1,0:T(8,128)}) fusion(f32[4,8,128,128]{3,2,1,0:T(8,128)} %fusion.25, bf16[4,128,8,128]{3,2,1,0:T(8,128)(2,1)} %bitcast.69, pred[128,128]{1,0:T(8,128)(4,1)S(1)} %iota_compare_fusion, bf16[4,128,8,128]{3,2,1,0:T(8,128)(2,1)S(1)} %bitcast.67, bf16[4,128,8,128]{3,2,1,0:T(8,128)(2,1)S(1)} %bitcast.68), kind=kOutput, calls=%fused_computation.8 | convolution fusion | flops 271052800 | bytes 7372800 | tf_op jit(solution)/shard_map/shbc,schf->sbhf/dot_general | solution.py:87
  212.7 1.8 fusion.5
  214.6 3.8 %select_convert_fusion = bf16[4,128,1024]{2,1,0:T(8,128)(2,1)} fusion(bf16[4,128,1024]{1,2,0:T(8,128)(2,1)S(1)} %bitcast.76, bf16[1024,1024]{1,0:T(8,128)(2,1)} %all-gather.13.cloned.1.call-done, pred[4,128]{1,0:T(4,128)(4,1)S(1)} %iota_compare_fusion.2), kind=kOutput, calls=%fused_computation.11 | convolution fusion | flops 1074790400 | bytes 4194816 | tf_op jit(solution)/shard_map/dot_general | solution.py:23
  (18 shorter events, 0.1 us)
Async XLA Ops:
  6.5 153.3 %copy-start = (bf16[4,128,1024]{2,1,0:T(8,128)(2,1)S(1)}, bf16[4,128,1024]{2,1,0:T(8,128)(2,1)}, u32[]{:S(2)}) copy-start(bf16[4,128,1024]{2,1,0:T(8,128)(2,1)} %param.12) | copy-start | bytes 3145732
  6.5 33.3 %all-gather.7.cloned.1.call-start = ((), (), s32[]{:S(2)}) async-start(), calls=%async_computation.1 | async-start | bytes 2359296 | tf_op jit(solution)/shard_map/all_gather | solution.py:40
  7.3 62.4 %all-gather.9.cloned.1.call-start = ((), (), s32[]{:S(2)}) async-start(), calls=%async_computation.2 | async-start | bytes 2359296 | tf_op jit(solution)/shard_map/all_gather | solution.py:41
  8.0 122.2 %all-gather.15.cloned.1.call-start = ((), (), s32[]{:S(2)}) async-start(), calls=%async_computation.5 | async-start | bytes 9437184 | tf_op jit(solution)/shard_map/all_gather | solution.py:12
  72.9 1.0 copy-start.1
  74.1 2.1 copy-start.2
  74.1 2.1 copy-start.3
  75.6 84.2 %all-gather.11.cloned.1.call-start = ((), (), s32[]{:S(2)}) async-start(), calls=%async_computation.3 | async-start | bytes 2359296 | tf_op jit(solution)/shard_map/all_gather | solution.py:39
  149.2 5.4 %copy-start.6 = (s32[4]{0:T(128)S(1)}, s32[4]{0:T(128)}, u32[]{:S(2)}) copy-start(s32[4]{0:T(128)} %param.15) | copy-start | bytes 52
  149.2 53.5 %all-to-all-start = ((f32[4,8,128,128]{2,3,1,0:T(8,128)}), f32[4,8,128,128]{2,3,1,0:T(8,128)}, u32[]{:S(2)}, u32[]{:S(2)}) async-start(f32[4,8,128,128]{2,3,1,0:T(8,128)} %bitcast_add_fusion), calls=%async_computation | async-start | bytes 4194304 | tf_op jit(solution)/shard_map/all_to_all | solution.py:79
  154.0 60.7 %all-gather.13.cloned.1.call-start = ((), (), s32[]{:S(2)}) async-start(), calls=%async_computation.4 | async-start | bytes 2359296 | tf_op jit(solution)/shard_map/all_gather | solution.py:96
  162.7 1.6 copy-start.5
  165.6 1.6 copy-start.4
Sparse Core Ops, SparseCore 0:
  9.2 30.5 all-gather.6
  41.8 27.8 all-gather.8
  75.8 54.3 all-gather.14
  131.9 27.8 all-gather.10
  161.6 27.8 all-gather.12
where the time goes:
time: 226 us; the launch traced here: 225 us
  waiting for transfers between devices  149 us (66%)
  matrix products  31 us (14%)
  other arithmetic  15.1 us (7%)
  between operations  13.3 us (6%)
  local copies, waits for them, and re-layouts  11.3 us (5%)
  starting transfers between devices  4.93 us (2%)
    all_gather x1, waiting for transfers between devices, carried_in(): pieces = lax.all_gather(value, axis)  50.3 us
    all_to_all x1, waiting for transfers between devices, shards(): lax.all_to_all(fork_state, 'leaf', split_axis=0, concat_axis=0, tiled=True)  33 us
    all_gather x1, waiting for transfers between devices, shards(): lax.all_gather(w_key, 'trunk', axis=0, tiled=True)  31.8 us
    all_gather x1, waiting for transfers between devices, shards(): lax.all_gather(w_value, 'trunk', axis=0, tiled=True)  26.4 us
    dot_general x6, matrix products, matmul(): return jnp.dot(left, right, preferred_element_type=jnp.float32)  15.6 us
    select_n x7, other arithmetic, step(): return jnp.where(position < mine, longer, subtotal)  11.2 us
    unnamed x19, local copies, waits for them, and re-layouts  5.93 us
    all_gather x1, waiting for transfers between devices, shards(): lax.all_gather(w_query, 'trunk', axis=0, tiled=True)  5.23 us
  transfers between devices with their start and end apart: 6, of which 5 were waited for; matrix products, arithmetic and copies ran while one was open for 20% of the time, Pallas kernels for 0%

commit v1 on v0

v1 whole, which is shorter than its diff:
```python
import functools

import jax
import jax.numpy as jnp
from jax import lax
from jax.experimental import pallas as pl
from jax.experimental.pallas import tpu as pltpu
from jax.sharding import PartitionSpec as P

H = 8
DH = 128
F32 = jnp.float32
BF16 = jnp.bfloat16
VMEM_BYTES = 48 * 1024 * 1024


def swap(value, axis, bit):
    return lax.ppermute(value, axis, [(i, i ^ bit) for i in range(lax.axis_size(axis))])


def dot(left, right):
    return jnp.dot(left, right, preferred_element_type=F32)


def vmem(count):
    return [pl.BlockSpec(memory_space=pltpu.VMEM)] * count


def smem(count):
    return [pl.BlockSpec(memory_space=pltpu.SMEM)] * count


def params():
    return pltpu.CompilerParams(vmem_limit_bytes=VMEM_BYTES)


def halves_kernel(count, *refs):
    core = lax.axis_index("trunk") % 2
    mine, other, outs = refs[:count], refs[count : 2 * count], refs[2 * count :]
    for a, b, out in zip(mine, other, outs):
        rows, width = a.shape
        half = width // 2
        columns = pl.ds(pl.multiple_of(core * half, half), half)
        first, second = a[:, columns], b[:, columns]
        out[pl.ds(pl.multiple_of(core * rows, rows), rows), :] = first
        out[pl.ds(pl.multiple_of((1 - core) * rows, rows), rows), :] = second


def chip_halves(mine, other):
    rows, width = mine[0].shape
    shape = jax.ShapeDtypeStruct((2 * rows, width // 2), mine[0].dtype)
    return pl.pallas_call(
        functools.partial(halves_kernel, len(mine)),
        out_shape=[shape] * len(mine),
        in_specs=vmem(2 * len(mine)),
        out_specs=vmem(len(mine)),
        compiler_params=params(),
    )(*mine, *other)


def gather_chips(value, bits):
    held, offsets = value[None], [0]
    for bit in bits:
        other = swap(held, "trunk", bit)
        other_offsets = [o ^ bit for o in offsets]
        if bit == bits[-1]:
            return [(held, offsets), (other, other_offsets)]
        held = jnp.concatenate([held, other])
        offsets = offsets + other_offsets
    return [(held, offsets)]


def in_order(pieces):
    held = jnp.concatenate([p for p, _ in pieces])
    offsets = [o // 2 for _, part in pieces for o in part]
    place = [offsets.index(i) for i in range(len(offsets))]
    chip = lax.axis_index("trunk") // 2
    order = jnp.asarray(place, jnp.int32)[chip ^ jnp.arange(len(place), dtype=jnp.int32)]
    held = jnp.take(held, order, axis=0)
    return [(held.reshape(1, -1, held.shape[-1]), [0])]


def project(x_ref, pieces, refs, columns):
    chip = lax.axis_index("trunk") // 2
    total = None
    for offsets, ref in zip(pieces, refs):
        depth = ref.shape[1]
        for slot, offset in enumerate(offsets):
            if len(pieces) == 1 and len(offsets) == 1:
                left = x_ref[...]
            else:
                start = (chip ^ (offset // 2)) * depth
                left = x_ref[:, pl.ds(pl.multiple_of(start, depth), depth)]
            term = dot(left, ref[slot, :, columns])
            total = term if total is None else total + term
    return total


def trunk_kernel(key_offsets, value_offsets, heads, entries, *refs):
    nk, nv = len(key_offsets), len(value_offsets)
    off_ref, tree_ref, xm_ref, xo_ref = refs[:4]
    k_refs = refs[4 : 4 + nk]
    v_refs = refs[4 + nk : 4 + nk + nv]
    total_ref, fork_ref, x_ref, state_ref = refs[4 + nk + nv :]
    side, tree = pl.program_id(0), pl.program_id(1)
    trees = pl.num_programs(1)
    core = lax.axis_index("trunk") % 2

    @pl.when(side == 0)
    def _():
        x_ref[...] = xm_ref[0]

    @pl.when(side == 1)
    def _():
        x_ref[...] = xo_ref[0]

    tok = x_ref.shape[0]
    keys = project(x_ref, key_offsets, k_refs, slice(None))
    values = project(x_ref, value_offsets, v_refs, slice(None)).astype(BF16)
    keys_t = keys.T.astype(BF16)
    place = lax.broadcasted_iota(jnp.int32, (DH, tok), 1)
    limits = [
        jnp.where(tree_ref[side, e] == tree, off_ref[side, e], 0) for e in range(entries)
    ]
    for h in range(heads):
        key_h = keys_t[h * DH : (h + 1) * DH]
        rows = [key_h] + [jnp.where(place < limit, key_h, jnp.zeros_like(key_h)) for limit in limits]
        product = dot(jnp.concatenate(rows), values[:, h * DH : (h + 1) * DH])
        state_ref[side, tree, h] = product[:DH]
        for e in range(entries):
            part = product[(e + 1) * DH : (e + 2) * DH]

            @pl.when(tree == 0)
            def _():
                fork_ref[side, e, h] = part

            @pl.when(tree != 0)
            def _():
                fork_ref[side, e, h] += part

    @pl.when((side == 1) & (tree == trees - 1))
    def _():
        total_ref[...] = (state_ref[0] + state_ref[1]).astype(BF16)
        for e in range(entries):
            fork_ref[1 - core, e] += state_ref[core, tree_ref[1 - core, e]]


def trunk_states(offsets, trees_of, mine, other, keys, values):
    trees, tok, width = mine.shape
    entries = offsets.shape[1]
    cols = keys[0][0].shape[-1]
    heads = cols // DH
    whole = lambda a: pl.BlockSpec(a.shape, lambda i, g: (0,) * a.ndim)
    pieces = [p for p, _ in keys] + [p for p, _ in values]
    kernel = functools.partial(
        trunk_kernel, [o for _, o in keys], [o for _, o in values], heads, entries
    )
    return pl.pallas_call(
        kernel,
        grid=(2, trees),
        out_shape=[
            jax.ShapeDtypeStruct((trees, heads, DH, DH), BF16),
            jax.ShapeDtypeStruct((2, entries, heads, DH, DH), F32),
        ],
        in_specs=smem(2)
        + [
            pl.BlockSpec((1, tok, width), lambda i, g: (jnp.where(i == 0, g, trees - 1), 0, 0)),
            pl.BlockSpec((1, tok, width), lambda i, g: (jnp.where(i == 0, 0, g), 0, 0)),
        ]
        + [whole(p) for p in pieces],
        out_specs=[
            pl.BlockSpec((trees, heads, DH, DH), lambda i, g: (0, 0, 0, 0)),
            pl.BlockSpec((2, entries, heads, DH, DH), lambda i, g: (0, 0, 0, 0, 0)),
        ],
        scratch_shapes=[
            pltpu.VMEM((tok, width), BF16),
            pltpu.VMEM((2, trees, heads, DH, DH), F32),
        ],
        compiler_params=params(),
        name="trunk_states",
    )(offsets, trees_of, mine, other, *pieces)


def scan_up(total, bits):
    index = lax.axis_index("trunk")
    terms, held = [], total
    for bit in bits:
        other = swap(held, "trunk", bit)
        terms.append((other, (index & bit) != 0))
        if bit != bits[-1]:
            held = (held.astype(F32) + other.astype(F32)).astype(BF16)
    return terms


def scan_down(total, bits):
    index = lax.axis_index("trunk")
    terms, lower = [], None
    for bit in bits[::-1]:
        message = jnp.where((index & bit) == 0, total.astype(F32), 0.0)
        if lower is not None:
            message = message + lower
        other = swap(message.astype(BF16), "trunk", bit)
        terms.append((other, None))
        lower = other.astype(F32) if lower is None else lower + other.astype(F32)
    return terms


def fork_kernel(masks, lanes, cap, *refs):
    n = len(masks)
    tree_ref, fork_ref = refs[:2]
    terms, outs, carried_ref = refs[2 : 2 + n], refs[2 + n : -1], refs[-1]
    index, lane = lax.axis_index("trunk"), lax.axis_index("leaf")
    carried = None
    for mask, ref in zip(masks, terms):
        term = ref[...].astype(F32)
        if mask:
            term = jnp.where((index & mask) != 0, term, 0.0)
        carried = term if carried is None else carried + term
    carried_ref[...] = carried
    for apart in range(lanes):
        for side in range(2):
            for c in range(cap):
                entry = (lane ^ apart) * cap + c
                state = fork_ref[side, entry] + carried_ref[tree_ref[side, entry]]
                outs[apart][side, c] = state.astype(BF16)


def fork_states(trees_of, forks, terms, masks, lanes):
    _, entries, heads = forks.shape[:3]
    cap = entries // lanes
    shape = jax.ShapeDtypeStruct((2, cap, heads, DH, DH), BF16)
    return pl.pallas_call(
        functools.partial(fork_kernel, masks, lanes, cap),
        out_shape=[shape] * lanes,
        in_specs=smem(1) + vmem(1 + len(terms)),
        out_specs=vmem(lanes),
        scratch_shapes=[pltpu.VMEM(terms[0].shape, F32)],
        compiler_params=params(),
        name="fork_states",
    )(trees_of, forks, *terms)


def branch_kernel(query_offsets, groups, blen, *refs):
    nq = len(query_offsets)
    flat = [offsets for pair in groups for offsets in pair]
    xm_ref, xo_ref = refs[:2]
    q_refs = refs[2 : 2 + nq]
    rest = list(refs[2 + nq : -3])
    kv = []
    for offsets in flat:
        kv.append(rest[: len(offsets)])
        rest = rest[len(offsets) :]
    q_out, intra_out, x_ref = refs[-3:]
    side = pl.program_id(0)

    @pl.when(side == 0)
    def _():
        x_ref[...] = xm_ref[...]

    @pl.when(side == 1)
    def _():
        x_ref[...] = xo_ref[...]

    queries = project(x_ref, query_offsets, q_refs, slice(None)).astype(BF16)
    q_out[0] = queries
    causal = lax.broadcasted_iota(jnp.int32, (blen, blen), 1) <= lax.broadcasted_iota(
        jnp.int32, (blen, blen), 0
    )
    column = 0
    for group in range(len(groups)):
        keys = project(x_ref, flat[2 * group], kv[2 * group], slice(None)).astype(BF16)
        values = project(x_ref, flat[2 * group + 1], kv[2 * group + 1], slice(None)).astype(BF16)
        for h in range(keys.shape[1] // DH):
            at = slice(h * DH, (h + 1) * DH)
            out_at = slice(column, column + DH)
            for start in range(0, x_ref.shape[0], blen):
                rows = slice(start, start + blen)
                scores = lax.dot_general(
                    queries[rows, out_at],
                    keys[rows, at],
                    (((1,), (1,)), ((), ())),
                    preferred_element_type=F32,
                )
                weights = jnp.where(causal, scores, 0.0).astype(BF16)
                intra_out[0, rows, out_at] = dot(weights, values[rows, at])
            column += DH


def branch_parts(mine, other, queries, groups, blen):
    rows, width = mine.shape
    block = 2 * blen if rows % (2 * blen) == 0 else blen
    steps = rows // block
    cols = queries[0][0].shape[-1]
    pieces = [p for p, _ in queries] + [p for pair in groups for part in pair for p, _ in part]
    whole = lambda a: pl.BlockSpec(a.shape, lambda i, g: (0,) * a.ndim)
    kernel = functools.partial(
        branch_kernel,
        [o for _, o in queries],
        [[[o for _, o in part] for part in pair] for pair in groups],
        blen,
    )
    return pl.pallas_call(
        kernel,
        grid=(2, steps),
        out_shape=[
            jax.ShapeDtypeStruct((2, rows, cols), BF16),
            jax.ShapeDtypeStruct((2, rows, cols), F32),
        ],
        in_specs=[
            pl.BlockSpec((block, width), lambda i, g: (jnp.where(i == 0, g, steps - 1), 0)),
            pl.BlockSpec((block, width), lambda i, g: (jnp.where(i == 0, 0, g), 0)),
        ]
        + [whole(p) for p in pieces],
        out_specs=[pl.BlockSpec((1, block, cols), lambda i, g: (i, g, 0))] * 2,
        scratch_shapes=[pltpu.VMEM((block, width), BF16)],
        compiler_params=params(),
        name="branch_parts",
    )(mine, other, *pieces)


def norm_kernel(lanes, cap, groups, *refs):
    q_ref, intra_ref = refs[:2]
    state_refs = refs[2:-2]
    outs = refs[-2:]
    lane = lax.axis_index("leaf")
    blen = q_ref.shape[2]
    for apart in range(lanes):
        for side in range(2):
            for c in range(cap):
                slot = (lane ^ apart) * cap + c
                column = 0
                for group in range(groups):
                    ref = state_refs[group * lanes + apart]
                    for h in range(ref.shape[2]):
                        at = slice(column, column + DH)
                        total = intra_ref[side, slot, :, at] + dot(
                            q_ref[side, slot, :, at], ref[side, c, h]
                        )
                        meansq = jnp.mean(total * total, axis=-1, keepdims=True)
                        outs[side][slot, :, at] = (total * lax.rsqrt(meansq + 1e-06)).astype(BF16)
                        column += DH


def norm_parts(queries, intra, states, lanes):
    _, slots, blen, cols = queries.shape
    shape = jax.ShapeDtypeStruct((slots, blen, cols), BF16)
    flat = [s for group in states for s in group]
    return pl.pallas_call(
        functools.partial(norm_kernel, lanes, slots // lanes, len(states)),
        out_shape=[shape] * 2,
        in_specs=vmem(2 + len(flat)),
        out_specs=vmem(2),
        compiler_params=params(),
        name="norm_parts",
    )(queries, intra, *flat)


def out_kernel(len_ref, mine_ref, other_ref, w_ref, out_ref):
    core = lax.axis_index("trunk") % 2
    slots, blen, half = mine_ref.shape
    first = w_ref[pl.ds(pl.multiple_of(core * half, half), half), :]
    second = w_ref[pl.ds(pl.multiple_of((1 - core) * half, half), half), :]
    row = lax.broadcasted_iota(jnp.int32, (blen, w_ref.shape[1]), 0)
    for slot in range(slots):
        total = dot(mine_ref[slot], first) + dot(other_ref[slot], second)
        out_ref[slot] = jnp.where(row < len_ref[slot], total, 0.0).astype(BF16)


def out_project(lengths, mine, other, weights):
    slots, blen, _ = mine.shape
    return pl.pallas_call(
        out_kernel,
        out_shape=jax.ShapeDtypeStruct((slots, blen, weights.shape[1]), BF16),
        in_specs=smem(1) + vmem(3),
        out_specs=pl.BlockSpec(memory_space=pltpu.VMEM),
        compiler_params=params(),
        name="out_project",
    )(lengths, mine, other, weights)


def shards(
    trunk_tokens, branch_tokens, fork_offset, fork_tree, branch_len, w_query, w_key, w_value, w_out
):
    trees, trunk_tok, width = trunk_tokens.shape
    slots, blen, _ = branch_tokens.shape
    lanes, count = lax.axis_size("leaf"), lax.axis_size("trunk")
    entries = fork_offset.shape[2]
    bits = [1 << i for i in range(1, count.bit_length() - 1)]
    index = lax.axis_index("trunk")
    natural = (2 * w_key.shape[0]) % DH != 0

    def arranged(pieces):
        return in_order(pieces) if natural else pieces

    key_other, value_other = swap(w_key, "trunk", 1), swap(w_value, "trunk", 1)
    key_half, value_half = chip_halves([w_key, w_value], [key_other, value_other])
    keys = arranged(gather_chips(key_half, bits))
    values = arranged(gather_chips(value_half, bits[::-1]))

    forks = jnp.stack([fork_offset.reshape(entries), fork_tree.reshape(entries)])
    forks_other = swap(forks, "trunk", 1)
    offsets = jnp.stack([forks[0], forks_other[0]])
    trees_of = jnp.stack([forks[1], forks_other[1]])
    trunk_other = swap(trunk_tokens, "trunk", 1)
    branch_other = swap(branch_tokens, "trunk", 1)

    totals, fork_parts = trunk_states(offsets, trees_of, trunk_tokens, trunk_other, keys, values)
    terms = scan_up(totals, bits)
    sends = fork_states(
        trees_of, fork_parts, [t for t, _ in terms], bits, lanes
    )
    received = [sends[0]] + [swap(sends[a], "leaf", a) for a in range(1, lanes)]

    query_other = swap(w_query, "trunk", 1)
    (query_half,) = chip_halves([w_query], [query_other])
    queries = arranged(gather_chips(query_half, bits[::-1]))
    out_pieces = gather_chips(w_out, bits)
    out_mine = jnp.concatenate([p for p, _ in out_pieces])
    out_offsets = [o for _, part in out_pieces for o in part]
    out_other = swap(out_mine, "trunk", 1)
    held = jnp.concatenate([out_mine, out_other])
    out_offsets = out_offsets + [o ^ 1 for o in out_offsets]
    place = jnp.asarray([out_offsets.index(i) for i in range(count)], jnp.int32)
    out_full = jnp.take(held, place[index ^ jnp.arange(count, dtype=jnp.int32)], axis=0)
    out_full = out_full.reshape(-1, w_out.shape[1])

    q, intra = branch_parts(
        branch_tokens.reshape(slots * blen, width),
        branch_other.reshape(slots * blen, width),
        queries,
        [(keys, values)],
        blen,
    )
    q = q.reshape(2, slots, blen, -1)
    intra = intra.reshape(2, slots, blen, -1)
    normed_mine, normed_other = norm_parts(q, intra, [received], lanes)
    normed_swapped = swap(normed_other, "trunk", 1)
    return out_project(branch_len, normed_mine, normed_swapped, out_full)


def solution(mesh):
    in_specs = (
        P("leaf", "trunk", None),
        P(("leaf", "trunk"), None, None),
        P("leaf", "trunk", None),
        P("leaf", "trunk", None),
        P(("leaf", "trunk")),
        P("trunk", None),
        P("trunk", None),
        P("trunk", None),
        P("trunk", None),
    )
    out_specs = P(("leaf", "trunk"), None, None)
    return jax.shard_map(shards, mesh=mesh, in_specs=in_specs, out_specs=out_specs, check_vma=False)
```

time: 226 us -> 97.7 us (0.43)
  waiting for transfers between devices: 149 us -> 27.2 us
  matrix products: 31 us -> 0 us
  Pallas kernels: 0 us -> 27.6 us
  starting transfers between devices: 4.93 us -> 21.2 us
  between operations: 13.3 us -> 0.18 us
  other arithmetic: 15.1 us -> 10.5 us
    all_gather x5 -> x0, waiting for transfers between devices: 114 us -> none  [the longest x1 50.3 us: carried_in(): pieces = lax.all_gather(value, axis)]
    all_to_all x1 -> x0, waiting for transfers between devices: 33 us -> none  [shards(): lax.all_to_all(fork_state, 'leaf', split_axis=0, concat_axis=0, tiled=True)]
    dot_general x10 -> x0, matrix products: 31 us -> none  [the longest x6 15.6 us: matmul(): return jnp.dot(left, right, preferred_element_type=jnp.float32)]
    pallas_call x0 -> x7, Pallas kernels: none -> 27.6 us  [the longest x1 11.1 us: trunk_states(): pl.pallas_call(kernel, grid=(2, trees), out_shape=[jax.ShapeDtypeStruct((...]
    ppermute x0 -> x21, waiting for transfers between devices: none -> 27.2 us  [swap(): lax.ppermute(value, axis, [(i, i ^ bit) for i in range(lax.axis_size(axis...]
    ppermute x0 -> x21, starting transfers between devices: none -> 21.2 us  [swap(): lax.ppermute(value, axis, [(i, i ^ bit) for i in range(lax.axis_size(axis...]
    select_n x8 -> x3, other arithmetic: 11.2 us -> 1.88 us  [the longest x2 1.87 us: shards(): jnp.take(held, place[index ^ jnp.arange(count, dtype=jnp.int32)], axis=0)]
    concatenate x0 -> x6, other arithmetic: none -> 7.11 us  [the longest x1 2.82 us: shards(): held = jnp.concatenate([out_mine, out_other])]
  transfers between devices with their start and end apart: 6 -> 21, of which waited for: 5 -> 11; matrix products, arithmetic and copies ran while one was open for 20% -> 15% of each run, Pallas kernels for 0% -> 26%
where the time goes in v1:
time: 97.7 us; the launch traced here: 96.3 us
  Pallas kernels  27.6 us (28%)
  waiting for transfers between devices  27.2 us (28%)
  starting transfers between devices  21.2 us (22%)
  other arithmetic  10.5 us (11%)
  local copies, waits for them, and re-layouts  9.67 us (10%)
    ppermute x21, waiting for transfers between devices, swap(): lax.ppermute(value, axis, [(i, i ^ bit) for i in range(lax.axis_size(axis...  27.2 us
    ppermute x21, starting transfers between devices, swap(): lax.ppermute(value, axis, [(i, i ^ bit) for i in range(lax.axis_size(axis...  21.2 us
    pallas_call x1, Pallas kernels, trunk_states(): pl.pallas_call(kernel, grid=(2, trees), out_shape=[jax.ShapeDtypeStruct((...  11.1 us
    pallas_call x1, Pallas kernels, branch_parts(): pl.pallas_call(kernel, grid=(2, steps), out_shape=[jax.ShapeDtypeStruct((...  10.6 us
    unnamed x28, local copies, waits for them, and re-layouts  5.35 us
    gather x1, local copies, waits for them, and re-layouts, shards(): jnp.take(held, place[index ^ jnp.arange(count, dtype=jnp.int32)], axis=0)  3.6 us
    concatenate x1, other arithmetic, shards(): held = jnp.concatenate([out_mine, out_other])  2.82 us
    pallas_call x1, Pallas kernels, out_project(): pl.pallas_call(out_kernel, out_shape=jax.ShapeDtypeStruct((slots, blen, w...  2.8 us
  transfers between devices with their start and end apart: 21, of which 11 were waited for; matrix products, arithmetic and copies ran while one was open for 15% of the time, Pallas kernels for 26%

profile of v1, /device:TPU:0, one launch (start us, length us, event | category | flops | bytes accessed | tf_op | source)
XLA Modules:
  0.0 96.3 jit_solution(8060269848085093449)
XLA Ops:
  0.0 0.5 collective-permute-start.4
  0.5 1.3 %collective-permute-done.4.refs_2_ = bf16[128,1024]{1,0:T(8,128)(2,1)S(1)} collective-permute-done((bf16[128,1024]{1,0:T(8,128)(2,1)}, bf16[128,1024]{1,0:T(8,128)(2,1)S(1)}, u32[]{:S(2)}, u32[]{:S(2)}) %collective-permute-start.4) | collective-permute-done | bytes 262176 | tf_op jit(solution)/shard_map/ppermute | solution.py:18
  1.8 0.4 collective-permute-done.5.refs_3_
  2.2 0.9 copy-done.4
  3.2 0.9 copy-done.5
  4.2 2.9 %collective-permute-start.6 = (bf16[1,256,512]{2,1,0:T(8,128)(2,1)S(1)}, bf16[1,256,512]{2,1,0:T(8,128)(2,1)S(1)}, u32[]{:S(2)}, u32[]{:S(2)}) collective-permute-start(bf16[1,256,512]{2,1,0:T(8,128)(2,1)S(1)} %bitcast.26), channel_id=1, source_target_pairs={{0,2},{1,3},{2,0},{3,1},{4,6},{5,7},{6,4},{7,5},{8,10},{9,11},{10,... | collective-permute-start | bytes 786440 | tf_op jit(solution)/shard_map/ppermute | solution.py:18
  7.1 1.5 %collective-permute-start.8 = (bf16[1,256,512]{2,1,0:T(8,128)(2,1)S(1)}, bf16[1,256,512]{2,1,0:T(8,128)(2,1)}, u32[]{:S(2)}, u32[]{:S(2)}) collective-permute-start(bf16[1,256,512]{2,1,0:T(8,128)(2,1)S(1)} %bitcast.24), channel_id=1, source_target_pairs={{0,4},{1,5},{2,6},{3,7},{4,0},{5,1},{6,2},{7,3},{8,12},{9,13},{10,... | collective-permute-start | bytes 786440 | tf_op jit(solution)/shard_map/ppermute | solution.py:18
  8.6 0.2 collective-permute-start.1
  8.9 0.5 collective-permute-start.18
  9.4 0.7 pad_add_fusion.1
  10.1 4.1 %collective-permute-done.6 = bf16[1,256,512]{2,1,0:T(8,128)(2,1)S(1)} collective-permute-done((bf16[1,256,512]{2,1,0:T(8,128)(2,1)S(1)}, bf16[1,256,512]{2,1,0:T(8,128)(2,1)S(1)}, u32[]{:S(2)}, u32[]{:S(2)}) %collective-permute-start.6) | collective-permute-done | bytes 262176 | tf_op jit(solution)/shard_map/ppermute | solution.py:18
  14.2 2.2 %collective-permute-start.7 = (bf16[2,256,512]{2,1,0:T(8,128)(2,1)S(1)}, bf16[2,256,512]{2,1,0:T(8,128)(2,1)S(1)}, u32[]{:S(2)}, u32[]{:S(2)}) collective-permute-start(bf16[2,256,512]{2,1,0:T(8,128)(2,1)S(1)} %pad_maximum_fusion.3.refs_4_), channel_id=1, source_target_pairs={{0,4},{1,5},{2,6},{3,7},{4,0},{5,1},{6,2},{7,3},{8,12},{9,13},{10,... | collective-permute-start | bytes 1572872 | tf_op jit(solution)/shard_map/ppermute | solution.py:18
  16.4 1.0 %pad_maximum_fusion.4.refs_6_ = bf16[2,256,512]{2,1,0:T(8,128)(2,1)S(1)} fusion(bf16[1,256,512]{2,1,0:T(8,128)(2,1)} %collective-permute-done.8, bf16[1,256,512]{2,1,0:T(8,128)(2,1)S(1)} %bitcast.25), kind=kLoop, calls=%fused_computation.7 | loop fusion | flops 262144 | bytes 1048576 | tf_op jit(solution)/shard_map/concatenate | solution.py:68
  17.4 1.6 %collective-permute-start.9 = (bf16[2,256,512]{2,1,0:T(8,128)(2,1)S(1)}, bf16[2,256,512]{2,1,0:T(8,128)(2,1)S(1)}, u32[]{:S(2)}, u32[]{:S(2)}) collective-permute-start(bf16[2,256,512]{2,1,0:T(8,128)(2,1)S(1)} %pad_maximum_fusion.4.refs_6_), channel_id=1, source_target_pairs={{0,2},{1,3},{2,0},{3,1},{4,6},{5,7},{6,4},{7,5},{8,10},{9,11},{10,... | collective-permute-start | bytes 1572872 | tf_op jit(solution)/shard_map/ppermute | solution.py:18
  19.0 0.5 collective-permute-done.18
  19.5 1.0 %pad_maximum_fusion.5 = bf16[2,128,1024]{2,1,0:T(8,128)(2,1)S(1)} fusion(bf16[1,128,1024]{2,1,0:T(8,128)(2,1)} %collective-permute-done.18, bf16[1,128,1024]{2,1,0:T(8,128)(2,1)S(1)} %bitcast.29), kind=kLoop, calls=%fused_computation.8 | loop fusion | flops 262144 | bytes 1048576 | tf_op jit(solution)/shard_map/concatenate | solution.py:68
  20.5 2.0 %collective-permute-start.19 = (bf16[2,128,1024]{2,1,0:T(8,128)(2,1)S(1)}, bf16[2,128,1024]{2,1,0:T(8,128)(2,1)S(1)}, u32[]{:S(2)}, u32[]{:S(2)}) collective-permute-start(bf16[2,128,1024]{2,1,0:T(8,128)(2,1)S(1)} %pad_maximum_fusion.5), channel_id=1, source_target_pairs={{0,4},{1,5},{2,6},{3,7},{4,0},{5,1},{6,2},{7,3},{8,12},{9,13},{10,... | collective-permute-start | bytes 1572872 | tf_op jit(solution)/shard_map/ppermute | solution.py:18
  22.5 0.1 collective-permute-start.10
  22.6 1.0 %shard_map.100 = bf16[256,512]{1,0:T(8,128)(2,1)S(1)} custom-call(bf16[128,1024]{1,0:T(8,128)(2,1)S(1)} %copy-done.3, bf16[128,1024]{1,0:T(8,128)(2,1)} %collective-permute-done.1.refs_1_), custom_call_target="tpu_custom_call" | custom-call | tf_op jit(solution)/shard_map/pallas_call | solution.py:52
  23.5 0.1 collective-permute-done.10
  23.7 0.1 collective-permute-start.2
  23.8 5.4 %collective-permute-done.7.refs_5_ = bf16[2,256,512]{2,1,0:T(8,128)(2,1)S(1)} collective-permute-done((bf16[2,256,512]{2,1,0:T(8,128)(2,1)S(1)}, bf16[2,256,512]{2,1,0:T(8,128)(2,1)S(1)}, u32[]{:S(2)}, u32[]{:S(2)}) %collective-permute-start.7) | collective-permute-done | bytes 524320 | tf_op jit(solution)/shard_map/ppermute | solution.py:18
  29.2 1.3 %collective-permute-done.9.refs_7_ = bf16[2,256,512]{2,1,0:T(8,128)(2,1)S(1)} collective-permute-done((bf16[2,256,512]{2,1,0:T(8,128)(2,1)S(1)}, bf16[2,256,512]{2,1,0:T(8,128)(2,1)S(1)}, u32[]{:S(2)}, u32[]{:S(2)}) %collective-permute-start.9) | collective-permute-done | bytes 524320 | tf_op jit(solution)/shard_map/ppermute | solution.py:18
  30.6 11.1 %trunk_states.1 = (bf16[2,4,128,128]{3,2,1,0:T(8,128)(2,1)S(1)}, f32[2,4,4,128,128]{4,3,2,1,0:T(8,128)}) custom-call(s32[2,4]{1,0:T(2,128)S(1)} %get-tuple-element.31.refs_0_, s32[2,4]{1,0:T(2,128)S(1)} %get-tuple-element.32.refs_1_.refs_0_, bf16[2,256,1024]{2,1,0:T(8,128)(2,1)S(1)} %copy-done.2, bf16[2,256,1024]{2,1,0:T(8,128)(2,1)} %collective-permute-done.11.refs_3_, ...), custom_call_target="tpu_custom_call" | custom-call | tf_op jit(solution)/shard_map/trunk_states/pallas_call | solution.py:158
  41.7 1.8 %collective-permute-start.12 = (bf16[2,4,128,128]{3,2,1,0:T(8,128)(2,1)S(1)}, bf16[2,4,128,128]{3,2,1,0:T(8,128)(2,1)S(1)}, u32[]{:S(2)}, u32[]{:S(2)}) collective-permute-start(bf16[2,4,128,128]{3,2,1,0:T(8,128)(2,1)S(1)} %get-tuple-element.22), channel_id=1, source_target_pairs={{0,2},{1,3},{2,0},{3,1},{4,6},{5,7},{6,4},{7,5},{8,10},{9,11},{10,... | collective-permute-start | bytes 786440 | tf_op jit(solution)/shard_map/ppermute | solution.py:18
  43.4 0.8 collective-permute-done.2
  44.3 1.5 %collective-permute-start.3 = (bf16[2,256,512]{2,1,0:T(8,128)(2,1)S(1)}, bf16[2,256,512]{2,1,0:T(8,128)(2,1)S(1)}, u32[]{:S(2)}, u32[]{:S(2)}) collective-permute-start(bf16[2,256,512]{2,1,0:T(8,128)(2,1)S(1)} %pad_maximum_fusion.2.refs_2_), channel_id=1, source_target_pairs={{0,2},{1,3},{2,0},{3,1},{4,6},{5,7},{6,4},{7,5},{8,10},{9,11},{10,... | collective-permute-start | bytes 1572872 | tf_op jit(solution)/shard_map/ppermute | solution.py:18
  45.8 2.2 %pad_maximum_fusion.1 = bf16[4,128,1024]{2,1,0:T(8,128)(2,1)} fusion(bf16[2,128,1024]{2,1,0:T(8,128)(2,1)S(1)} %collective-permute-done.19, bf16[1,128,1024]{2,1,0:T(8,128)(2,1)} %collective-permute-done.18, bf16[1,128,1024]{2,1,0:T(8,128)(2,1)S(1)} %bitcast.30), kind=kLoop, calls=%fused_computation.4 | loop fusion | flops 1048576 | bytes 2097152 | tf_op jit(solution)/shard_map/concatenate | solution.py:418
  48.0 2.9 %collective-permute-done.12.refs_2_ = bf16[2,4,128,128]{3,2,1,0:T(8,128)(2,1)S(1)} collective-permute-done((bf16[2,4,128,128]{3,2,1,0:T(8,128)(2,1)S(1)}, bf16[2,4,128,128]{3,2,1,0:T(8,128)(2,1)S(1)}, u32[]{:S(2)}, u32[]{:S(2)}) %collective-permute-start.12) | collective-permute-done | bytes 262176 | tf_op jit(solution)/shard_map/ppermute | solution.py:18
  50.9 0.8 add_convert_fusion
  51.7 1.8 %collective-permute-start.13 = (bf16[2,4,128,128]{3,2,1,0:T(8,128)(2,1)}, bf16[2,4,128,128]{3,2,1,0:T(8,128)(2,1)}, u32[]{:S(2)}, u32[]{:S(2)}) collective-permute-start(bf16[2,4,128,128]{3,2,1,0:T(8,128)(2,1)} %add_convert_fusion), channel_id=1, source_target_pairs={{0,4},{1,5},{2,6},{3,7},{4,0},{5,1},{6,2},{7,3},{8,12},{9,13},{10,... | collective-permute-start | bytes 786440 | tf_op jit(solution)/shard_map/ppermute | solution.py:18
  53.5 0.6 gather_fusion
  54.2 4.2 %collective-permute-done.13.refs_3_ = bf16[2,4,128,128]{3,2,1,0:T(8,128)(2,1)} collective-permute-done((bf16[2,4,128,128]{3,2,1,0:T(8,128)(2,1)}, bf16[2,4,128,128]{3,2,1,0:T(8,128)(2,1)}, u32[]{:S(2)}, u32[]{:S(2)}) %collective-permute-start.13) | collective-permute-done | bytes 262176 | tf_op jit(solution)/shard_map/ppermute | solution.py:18
  58.4 1.6 %copy-done = f32[2,4,4,128,128]{4,3,2,1,0:T(8,128)S(1)} copy-done((f32[2,4,4,128,128]{4,3,2,1,0:T(8,128)S(1)}, f32[2,4,4,128,128]{4,3,2,1,0:T(8,128)}, u32[]{:S(2)}) %copy-start) | copy-done | bytes 2097176
  60.0 1.3 %fork_states.1 = (bf16[2,1,4,128,128]{4,3,2,1,0:T(8,128)(2,1)S(1)}, bf16[2,1,4,128,128]{4,3,2,1,0:T(8,128)(2,1)S(1)}, bf16[2,1,4,128,128]{4,3,2,1,0:T(8,128)(2,1)S(1)}, bf16[2,1,4,128,128]{4,3,2,1,0:T(8,128)(2,1)S(1)}) custom-call(s32[2,4]{1,0:T(2,128)S(1)} %get-tuple-element.32.refs_1_.refs_0_, f32[2,4,4,128,128]{4,3,2,1,0:T(8,128)S(1)} %copy-done, ...), custom_call_target="tpu_custom_call" | custom-call | tf_op jit(solution)/shard_map/fork_states/pallas_call | solution.py:232
  61.3 1.9 %collective-permute-start.14 = (bf16[2,1,4,128,128]{4,3,2,1,0:T(8,128)(2,1)S(1)}, bf16[2,1,4,128,128]{4,3,2,1,0:T(8,128)(2,1)S(1)}, u32[]{:S(2)}, u32[]{:S(2)}) collective-permute-start(bf16[2,1,4,128,128]{4,3,2,1,0:T(8,128)(2,1)S(1)} %get-tuple-element.24), channel_id=1, source_target_pairs={{0,8},{8,0},{16,24},{24,16},{1,9},{9,1},{17,25},{25,17},{2,10},{10... | collective-permute-start | bytes 786440 | tf_op jit(solution)/shard_map/ppermute | solution.py:18
  63.2 2.6 %collective-permute-start.15 = (bf16[2,1,4,128,128]{4,3,2,1,0:T(8,128)(2,1)S(1)}, bf16[2,1,4,128,128]{4,3,2,1,0:T(8,128)(2,1)S(1)}, u32[]{:S(2)}, u32[]{:S(2)}) collective-permute-start(bf16[2,1,4,128,128]{4,3,2,1,0:T(8,128)(2,1)S(1)} %get-tuple-element.25), channel_id=1, source_target_pairs={{0,16},{8,24},{16,0},{24,8},{1,17},{9,25},{17,1},{25,9},{2,18},{10... | collective-permute-start | bytes 786440 | tf_op jit(solution)/shard_map/ppermute | solution.py:18
  65.8 0.1 broadcast_bitcast_fusion
  65.9 10.6 %branch_parts.1 = (bf16[2,512,512]{2,1,0:T(8,128)(2,1)S(1)}, f32[2,512,512]{2,1,0:T(8,128)}) custom-call(bf16[512,1024]{1,0:T(8,128)(2,1)} %bitcast.refs_0_, bf16[512,1024]{1,0:T(8,128)(2,1)} %bitcast.1.refs_1_, bf16[2,256,512]{2,1,0:T(8,128)(2,1)S(1)} %pad_maximum_fusion.2.refs_2_, bf16[2,256,512]{2,1,0:T(8,128)(2,1)S(1)} %collective-permute-done.3.refs_3_, ...), custom_call_target="tpu_custom_call" | custom-call | tf_op jit(solution)/shard_map/branch_parts/pallas_call | solution.py:302
  76.4 6.0 %collective-permute-done.15.refs_4_ = bf16[2,1,4,128,128]{4,3,2,1,0:T(8,128)(2,1)S(1)} collective-permute-done((bf16[2,1,4,128,128]{4,3,2,1,0:T(8,128)(2,1)S(1)}, bf16[2,1,4,128,128]{4,3,2,1,0:T(8,128)(2,1)S(1)}, u32[]{:S(2)}, u32[]{:S(2)}) %collective-permute-start.15) | collective-permute-done | bytes 262176 | tf_op jit(solution)/shard_map/ppermute | solution.py:18
  82.5 1.6 %copy-done.1 = f32[2,512,512]{2,1,0:T(8,128)S(1)} copy-done((f32[2,512,512]{2,1,0:T(8,128)S(1)}, f32[2,512,512]{2,1,0:T(8,128)}, u32[]{:S(2)}) %copy-start.1) | copy-done | bytes 2097176
  84.1 0.8 norm_parts.1
  84.9 0.1 collective-permute-start.17
  85.0 0.2 copy-done.11
  85.2 2.8 %pad_maximum_fusion = bf16[8,128,1024]{2,1,0:T(8,128)(2,1)} fusion(bf16[4,128,1024]{2,1,0:T(8,128)(2,1)} %collective-permute-done.20, bf16[2,128,1024]{2,1,0:T(8,128)(2,1)S(1)} %copy-done.11, bf16[1,128,1024]{2,1,0:T(8,128)(2,1)} %collective-permute-done.18, bf16[1,128,1024]{2,1,0:T(8,128)(2,1)S(1)} %bitcast.31), kind=kLoop, calls=%fused_computation.2 | loop fusion | flops 3145728 | bytes 4194304 | tf_op jit(solution)/shard_map/concatenate | solution.py:421
  88.0 3.6 %gather_fusion.1 = bf16[8,128,1024]{2,1,0:T(8,128)(2,1)} fusion(bf16[8,128,1024]{2,1,0:T(8,128)(2,1)} %pad_maximum_fusion, s32[1024]{0:T(1024)S(1)} %pad_clamp_fusion), kind=kCustom, calls=%fused_computation.1 | custom fusion | bytes 4194336 | tf_op jit(solution)/shard_map/jit(_take)/gather | solution.py:424
  91.6 1.9 %bitcast_select_fusion.w_ref = bf16[1024,1024]{1,0:T(8,128)(2,1)S(1)} fusion(bf16[8,128,1024]{2,1,0:T(8,128)(2,1)} %gather_fusion.1, pred[1024]{0:T(1024)(128)(4,1)S(1)} %broadcast_bitcast_fusion), kind=kLoop, calls=%fused_computation.3 | loop fusion | flops 1048576 | bytes 4195328 | tf_op jit(solution)/shard_map/jit(_take)/select_n | solution.py:424
  93.5 2.8 %out_project.1 = bf16[4,128,1024]{2,1,0:T(8,128)(2,1)} custom-call(s32[4]{0:T(128)S(1)} %copy-done.6, bf16[4,128,512]{2,1,0:T(8,128)(2,1)S(1)} %get-tuple-element.27.mine_ref, bf16[4,128,512]{2,1,0:T(8,128)(2,1)S(1)} %collective-permute-done.17.other_ref, bf16[1024,1024]{1,0:T(8,128)(2,1)S(1)} %bitcast_select_fusion.w_ref), custom_call_target="tpu_custom_call" | custom-call | tf_op jit(solution)/shard_map/out_project/pallas_call | solution.py:371
  (48 shorter events, 0.4 us)
Async XLA Ops:
  0.0 22.6 %copy-start.3 = (bf16[128,1024]{1,0:T(8,128)(2,1)S(1)}, bf16[128,1024]{1,0:T(8,128)(2,1)}, u32[]{:S(2)}) copy-start(bf16[128,1024]{1,0:T(8,128)(2,1)} %refs_0_.2) | copy-start | bytes 786436
  0.0 1.8 %collective-permute-start.4 = (bf16[128,1024]{1,0:T(8,128)(2,1)}, bf16[128,1024]{1,0:T(8,128)(2,1)S(1)}, u32[]{:S(2)}, u32[]{:S(2)}) collective-permute-start(bf16[128,1024]{1,0:T(8,128)(2,1)} %refs_0_.3), channel_id=1, source_target_pairs={{0,1},{1,0},{2,3},{3,2},{4,5},{5,4},{6,7},{7,6},{8,9},{9,8},{10,11... | collective-permute-start | bytes 786440 | tf_op jit(solution)/shard_map/ppermute | solution.py:18
  0.5 1.7 %collective-permute-start.5 = (bf16[128,1024]{1,0:T(8,128)(2,1)}, bf16[128,1024]{1,0:T(8,128)(2,1)S(1)}, u32[]{:S(2)}, u32[]{:S(2)}) collective-permute-start(bf16[128,1024]{1,0:T(8,128)(2,1)} %refs_1_.1), channel_id=1, source_target_pairs={{0,1},{1,0},{2,3},{3,2},{4,5},{5,4},{6,7},{7,6},{8,9},{9,8},{10,11... | collective-permute-start | bytes 786440 | tf_op jit(solution)/shard_map/ppermute | solution.py:18
  2.2 0.9 copy-start.4
  3.2 0.9 copy-start.5
  4.1 19.7 %copy-start.12 = (s32[1,1,4]{2,1,0:T(1,128)S(1)}, s32[1,1,4]{2,1,0:T(1,128)}, u32[]{:S(2)}) copy-start(s32[1,1,4]{2,1,0:T(1,128)} %param.12) | copy-start | bytes 52
  4.2 19.7 %copy-start.13 = (s32[1,1,4]{2,1,0:T(1,128)S(1)}, s32[1,1,4]{2,1,0:T(1,128)}, u32[]{:S(2)}) copy-start(s32[1,1,4]{2,1,0:T(1,128)} %param.13) | copy-start | bytes 52
  4.2 26.4 %copy-start.2 = (bf16[2,256,1024]{2,1,0:T(8,128)(2,1)S(1)}, bf16[2,256,1024]{2,1,0:T(8,128)(2,1)}, u32[]{:S(2)}) copy-start(bf16[2,256,1024]{2,1,0:T(8,128)(2,1)} %refs_2_.1) | copy-start | bytes 3145732
  4.2 10.0 %collective-permute-start.6 = (bf16[1,256,512]{2,1,0:T(8,128)(2,1)S(1)}, bf16[1,256,512]{2,1,0:T(8,128)(2,1)S(1)}, u32[]{:S(2)}, u32[]{:S(2)}) collective-permute-start(bf16[1,256,512]{2,1,0:T(8,128)(2,1)S(1)} %bitcast.26), channel_id=1, source_target_pairs={{0,2},{1,3},{2,0},{3,1},{4,6},{5,7},{6,4},{7,5},{8,10},{9,11},{10,... | collective-permute-start | bytes 786440 | tf_op jit(solution)/shard_map/ppermute | solution.py:18
  7.1 23.5 %collective-permute-start.11 = (bf16[2,256,1024]{2,1,0:T(8,128)(2,1)}, bf16[2,256,1024]{2,1,0:T(8,128)(2,1)}, u32[]{:S(2)}, u32[]{:S(2)}) collective-permute-start(bf16[2,256,1024]{2,1,0:T(8,128)(2,1)} %refs_2_.1), channel_id=1, source_target_pairs={{0,1},{1,0},{2,3},{3,2},{4,5},{5,4},{6,7},{7,6},{8,9},{9,8},{10,11... | collective-permute-start | bytes 3145736 | tf_op jit(solution)/shard_map/ppermute | solution.py:18
  7.1 9.3 %collective-permute-start.8 = (bf16[1,256,512]{2,1,0:T(8,128)(2,1)S(1)}, bf16[1,256,512]{2,1,0:T(8,128)(2,1)}, u32[]{:S(2)}, u32[]{:S(2)}) collective-permute-start(bf16[1,256,512]{2,1,0:T(8,128)(2,1)S(1)} %bitcast.24), channel_id=1, source_target_pairs={{0,4},{1,5},{2,6},{3,7},{4,0},{5,1},{6,2},{7,3},{8,12},{9,13},{10,... | collective-permute-start | bytes 786440 | tf_op jit(solution)/shard_map/ppermute | solution.py:18
  8.6 13.8 %collective-permute-start.1 = (bf16[128,1024]{1,0:T(8,128)(2,1)}, bf16[128,1024]{1,0:T(8,128)(2,1)}, u32[]{:S(2)}, u32[]{:S(2)}) collective-permute-start(bf16[128,1024]{1,0:T(8,128)(2,1)} %refs_0_.2), channel_id=1, source_target_pairs={{0,1},{1,0},{2,3},{3,2},{4,5},{5,4},{6,7},{7,6},{8,9},{9,8},{10,11... | collective-permute-start | bytes 786440 | tf_op jit(solution)/shard_map/ppermute | solution.py:18
  8.9 10.6 %collective-permute-start.18 = (bf16[1,128,1024]{2,1,0:T(8,128)(2,1)}, bf16[1,128,1024]{2,1,0:T(8,128)(2,1)}, u32[]{:S(2)}, u32[]{:S(2)}) collective-permute-start(bf16[1,128,1024]{2,1,0:T(8,128)(2,1)} %bitcast.28), channel_id=1, source_target_pairs={{0,2},{1,3},{2,0},{3,1},{4,6},{5,7},{6,4},{7,5},{8,10},{9,11},{10,... | collective-permute-start | bytes 786440 | tf_op jit(solution)/shard_map/ppermute | solution.py:18
  10.1 9.4 %copy-start.8 = (bf16[128,1024]{1,0:T(8,128)(2,1)S(1)}, bf16[128,1024]{1,0:T(8,128)(2,1)}, u32[]{:S(2)}) copy-start(bf16[128,1024]{1,0:T(8,128)(2,1)} %param.18) | copy-start | bytes 786436
  14.2 15.0 %collective-permute-start.7 = (bf16[2,256,512]{2,1,0:T(8,128)(2,1)S(1)}, bf16[2,256,512]{2,1,0:T(8,128)(2,1)S(1)}, u32[]{:S(2)}, u32[]{:S(2)}) collective-permute-start(bf16[2,256,512]{2,1,0:T(8,128)(2,1)S(1)} %pad_maximum_fusion.3.refs_4_), channel_id=1, source_target_pairs={{0,4},{1,5},{2,6},{3,7},{4,0},{5,1},{6,2},{7,3},{8,12},{9,13},{10,... | collective-permute-start | bytes 1572872 | tf_op jit(solution)/shard_map/ppermute | solution.py:18
  17.4 13.2 %collective-permute-start.9 = (bf16[2,256,512]{2,1,0:T(8,128)(2,1)S(1)}, bf16[2,256,512]{2,1,0:T(8,128)(2,1)S(1)}, u32[]{:S(2)}, u32[]{:S(2)}) collective-permute-start(bf16[2,256,512]{2,1,0:T(8,128)(2,1)S(1)} %pad_maximum_fusion.4.refs_6_), channel_id=1, source_target_pairs={{0,2},{1,3},{2,0},{3,1},{4,6},{5,7},{6,4},{7,5},{8,10},{9,11},{10,... | collective-permute-start | bytes 1572872 | tf_op jit(solution)/shard_map/ppermute | solution.py:18
  20.5 25.3 %collective-permute-start.19 = (bf16[2,128,1024]{2,1,0:T(8,128)(2,1)S(1)}, bf16[2,128,1024]{2,1,0:T(8,128)(2,1)S(1)}, u32[]{:S(2)}, u32[]{:S(2)}) collective-permute-start(bf16[2,128,1024]{2,1,0:T(8,128)(2,1)S(1)} %pad_maximum_fusion.5), channel_id=1, source_target_pairs={{0,4},{1,5},{2,6},{3,7},{4,0},{5,1},{6,2},{7,3},{8,12},{9,13},{10,... | collective-permute-start | bytes 1572872 | tf_op jit(solution)/shard_map/ppermute | solution.py:18
  22.5 1.2 %collective-permute-start.10 = (s32[2,4]{1,0:T(2,128)S(1)}, s32[2,4]{1,0:T(2,128)S(1)}, u32[]{:S(2)}, u32[]{:S(2)}) collective-permute-start(s32[2,4]{1,0:T(2,128)S(1)} %pad_add_fusion.1), channel_id=1, source_target_pairs={{0,1},{1,0},{2,3},{3,2},{4,5},{5,4},{6,7},{7,6},{8,9},{9,8},{10,11... | collective-permute-start | bytes 104 | tf_op jit(solution)/shard_map/ppermute | solution.py:18
  23.7 20.6 %collective-permute-start.2 = (bf16[1,256,512]{2,1,0:T(8,128)(2,1)S(1)}, bf16[1,256,512]{2,1,0:T(8,128)(2,1)S(1)}, u32[]{:S(2)}, u32[]{:S(2)}) collective-permute-start(bf16[1,256,512]{2,1,0:T(8,128)(2,1)S(1)} %bitcast.21), channel_id=1, source_target_pairs={{0,4},{1,5},{2,6},{3,7},{4,0},{5,1},{6,2},{7,3},{8,12},{9,13},{10,... | collective-permute-start | bytes 786440 | tf_op jit(solution)/shard_map/ppermute | solution.py:18
  29.2 36.6 %collective-permute-start = (bf16[4,128,1024]{2,1,0:T(8,128)(2,1)}, bf16[4,128,1024]{2,1,0:T(8,128)(2,1)}, u32[]{:S(2)}, u32[]{:S(2)}) collective-permute-start(bf16[4,128,1024]{2,1,0:T(8,128)(2,1)} %param.11), channel_id=1, source_target_pairs={{0,1},{1,0},{2,3},{3,2},{4,5},{5,4},{6,7},{7,6},{8,9},{9,8},{10,11... | collective-permute-start | bytes 3145736 | tf_op jit(solution)/shard_map/ppermute | solution.py:18
  41.7 11.8 %copy-start.7 = (s32[8]{0:T(128)S(1)}, s32[8]{0:T(128)}, u32[]{:S(2)}) copy-start(s32[8]{0:T(128)} %constant.24.clone) | copy-start | bytes 100
  41.7 9.2 %collective-permute-start.12 = (bf16[2,4,128,128]{3,2,1,0:T(8,128)(2,1)S(1)}, bf16[2,4,128,128]{3,2,1,0:T(8,128)(2,1)S(1)}, u32[]{:S(2)}, u32[]{:S(2)}) collective-permute-start(bf16[2,4,128,128]{3,2,1,0:T(8,128)(2,1)S(1)} %get-tuple-element.22), channel_id=1, source_target_pairs={{0,2},{1,3},{2,0},{3,1},{4,6},{5,7},{6,4},{7,5},{8,10},{9,11},{10,... | collective-permute-start | bytes 786440 | tf_op jit(solution)/shard_map/ppermute | solution.py:18
  44.3 21.5 %collective-permute-start.3 = (bf16[2,256,512]{2,1,0:T(8,128)(2,1)S(1)}, bf16[2,256,512]{2,1,0:T(8,128)(2,1)S(1)}, u32[]{:S(2)}, u32[]{:S(2)}) collective-permute-start(bf16[2,256,512]{2,1,0:T(8,128)(2,1)S(1)} %pad_maximum_fusion.2.refs_2_), channel_id=1, source_target_pairs={{0,2},{1,3},{2,0},{3,1},{4,6},{5,7},{6,4},{7,5},{8,10},{9,11},{10,... | collective-permute-start | bytes 1572872 | tf_op jit(solution)/shard_map/ppermute | solution.py:18
  45.8 5.9 %copy-start.10 = (bf16[2,128,1024]{2,1,0:T(8,128)(2,1)}, bf16[2,128,1024]{2,1,0:T(8,128)(2,1)S(1)}, u32[]{:S(2)}) copy-start(bf16[2,128,1024]{2,1,0:T(8,128)(2,1)S(1)} %collective-permute-done.19) | copy-start | bytes 1572868
  48.0 37.0 %collective-permute-start.20 = (bf16[4,128,1024]{2,1,0:T(8,128)(2,1)}, bf16[4,128,1024]{2,1,0:T(8,128)(2,1)}, u32[]{:S(2)}, u32[]{:S(2)}) collective-permute-start(bf16[4,128,1024]{2,1,0:T(8,128)(2,1)} %pad_maximum_fusion.1), channel_id=1, source_target_pairs={{0,1},{1,0},{2,3},{3,2},{4,5},{5,4},{6,7},{7,6},{8,9},{9,8},{10,11... | collective-permute-start | bytes 3145736 | tf_op jit(solution)/shard_map/ppermute | solution.py:18
  51.7 6.7 %collective-permute-start.13 = (bf16[2,4,128,128]{3,2,1,0:T(8,128)(2,1)}, bf16[2,4,128,128]{3,2,1,0:T(8,128)(2,1)}, u32[]{:S(2)}, u32[]{:S(2)}) collective-permute-start(bf16[2,4,128,128]{3,2,1,0:T(8,128)(2,1)} %add_convert_fusion), channel_id=1, source_target_pairs={{0,4},{1,5},{2,6},{3,7},{4,0},{5,1},{6,2},{7,3},{8,12},{9,13},{10,... | collective-permute-start | bytes 786440 | tf_op jit(solution)/shard_map/ppermute | solution.py:18
  58.4 1.6 %copy-start = (f32[2,4,4,128,128]{4,3,2,1,0:T(8,128)S(1)}, f32[2,4,4,128,128]{4,3,2,1,0:T(8,128)}, u32[]{:S(2)}) copy-start(f32[2,4,4,128,128]{4,3,2,1,0:T(8,128)} %get-tuple-element.21.refs_1_) | copy-start | bytes 6291460
  61.3 15.1 %collective-permute-start.14 = (bf16[2,1,4,128,128]{4,3,2,1,0:T(8,128)(2,1)S(1)}, bf16[2,1,4,128,128]{4,3,2,1,0:T(8,128)(2,1)S(1)}, u32[]{:S(2)}, u32[]{:S(2)}) collective-permute-start(bf16[2,1,4,128,128]{4,3,2,1,0:T(8,128)(2,1)S(1)} %get-tuple-element.24), channel_id=1, source_target_pairs={{0,8},{8,0},{16,24},{24,16},{1,9},{9,1},{17,25},{25,17},{2,10},{10... | collective-permute-start | bytes 786440 | tf_op jit(solution)/shard_map/ppermute | solution.py:18
  63.2 19.3 %collective-permute-start.15 = (bf16[2,1,4,128,128]{4,3,2,1,0:T(8,128)(2,1)S(1)}, bf16[2,1,4,128,128]{4,3,2,1,0:T(8,128)(2,1)S(1)}, u32[]{:S(2)}, u32[]{:S(2)}) collective-permute-start(bf16[2,1,4,128,128]{4,3,2,1,0:T(8,128)(2,1)S(1)} %get-tuple-element.25), channel_id=1, source_target_pairs={{0,16},{8,24},{16,0},{24,8},{1,17},{9,25},{17,1},{25,9},{2,18},{10... | collective-permute-start | bytes 786440 | tf_op jit(solution)/shard_map/ppermute | solution.py:18
  65.8 16.7 %collective-permute-start.16 = (bf16[2,1,4,128,128]{4,3,2,1,0:T(8,128)(2,1)S(1)}, bf16[2,1,4,128,128]{4,3,2,1,0:T(8,128)(2,1)S(1)}, u32[]{:S(2)}, u32[]{:S(2)}) collective-permute-start(bf16[2,1,4,128,128]{4,3,2,1,0:T(8,128)(2,1)S(1)} %get-tuple-element.26), channel_id=1, source_target_pairs={{0,24},{8,16},{16,8},{24,0},{1,25},{9,17},{17,9},{25,1},{2,26},{10... | collective-permute-start | bytes 786440 | tf_op jit(solution)/shard_map/ppermute | solution.py:18
  82.5 1.6 %copy-start.1 = (f32[2,512,512]{2,1,0:T(8,128)S(1)}, f32[2,512,512]{2,1,0:T(8,128)}, u32[]{:S(2)}) copy-start(f32[2,512,512]{2,1,0:T(8,128)} %get-tuple-element.20) | copy-start | bytes 6291460
  84.1 0.9 copy-start.9
  84.1 1.1 %copy-start.11 = (bf16[2,128,1024]{2,1,0:T(8,128)(2,1)S(1)}, bf16[2,128,1024]{2,1,0:T(8,128)(2,1)}, u32[]{:S(2)}) copy-start(bf16[2,128,1024]{2,1,0:T(8,128)(2,1)} %copy-done.10) | copy-start | bytes 1572868
  84.9 8.6 %collective-permute-start.17 = (bf16[4,128,512]{2,1,0:T(8,128)(2,1)S(1)}, bf16[4,128,512]{2,1,0:T(8,128)(2,1)S(1)}, u32[]{:S(2)}, u32[]{:S(2)}) collective-permute-start(bf16[4,128,512]{2,1,0:T(8,128)(2,1)S(1)} %get-tuple-element.28), channel_id=1, source_target_pairs={{0,1},{1,0},{2,3},{3,2},{4,5},{5,4},{6,7},{7,6},{8,9},{9,8},{10,11... | collective-permute-start | bytes 1572872 | tf_op jit(solution)/shard_map/ppermute | solution.py:18
  91.6 1.9 %copy-start.6 = (s32[4]{0:T(128)S(1)}, s32[4]{0:T(128)}, u32[]{:S(2)}) copy-start(s32[4]{0:T(128)} %len_ref.1) | copy-start | bytes 52

commit v2 on v0

v2 whole, which is shorter than its diff:
```python
import functools

import jax
import jax.numpy as jnp
from jax import lax
from jax.experimental import pallas as pl
from jax.experimental.pallas import tpu as pltpu
from jax.sharding import PartitionSpec as P

H = 8
DH = 128
F32 = jnp.float32
BF16 = jnp.bfloat16
VMEM_BYTES = 16 * 1024 * 1024
ANY = pl.BlockSpec(memory_space=pl.ANY)
VMEM = pl.BlockSpec(memory_space=pltpu.VMEM)
SMEM = pl.BlockSpec(memory_space=pltpu.SMEM)


def swap(value, axis, bit, name="rows"):
    with jax.named_scope("to_" + name):
        return lax.ppermute(value, axis, [(i, i ^ bit) for i in range(lax.axis_size(axis))])


def dot(left, right):
    return jnp.dot(left, right, preferred_element_type=F32)


def shape_of(shape, dtype=BF16):
    return jax.ShapeDtypeStruct(tuple(shape), dtype)


def call(kernel, name, outs, inputs, specs, out_specs=None, scratch=(), order=None, through=(), landed=(), weight=0.0):
    after = (*(order or ()), *landed)
    n, t, w, m = len(inputs), len(through), len(after), len(outs)

    def body(*refs):
        kernel(*refs[:n], *refs[n + t + w : n + t + w + m], *refs[n + 2 * t + w + m :])

    results = pl.pallas_call(
        body,
        out_shape=[*outs, *(shape_of(a.shape, a.dtype) for a in through)],
        in_specs=[*specs, *[ANY] * (t + w)],
        out_specs=[*(out_specs or [VMEM] * m), *[ANY] * t],
        scratch_shapes=list(scratch),
        input_output_aliases={n + i: m + i for i in range(t)},
        compiler_params=pltpu.CompilerParams(vmem_limit_bytes=VMEM_BYTES),
        cost_estimate=pl.CostEstimate(
            flops=int(weight * 1e9), bytes_accessed=0, transcendentals=0
        ),
        name=name,
    )(*inputs, *through, *after)
    if order is not None:
        order[:] = [results[0]]
    return results


def core_index():
    return lax.axis_index("trunk") % 2


def chip_index():
    return lax.axis_index("trunk") // 2


def touch_kernel(*refs):
    refs[-1][...] = jnp.zeros_like(refs[-1])


def touch(arrays, **rest):
    return call(touch_kernel, "touch", [shape_of((8, DH), F32)], arrays, [ANY] * len(arrays), **rest)


def halves_kernel(count, chosen, *refs):
    core = core_index()
    mine, other, outs, sem = refs[:count], refs[count : 2 * count], refs[2 * count : -1], refs[-1]
    copies = []
    for out, (parts, picks) in zip(outs, chosen):
        for slot, (i, p, own) in enumerate(picks):
            rows, width = mine[i].shape
            part = width // 2 // parts
            first = (core if own else 1 - core) * (width // 2) + p * part
            columns = pl.ds(pl.multiple_of(first, part), part)
            for source, place in ((mine[i], core), (other[i], 1 - core)):
                target = out.at[slot, pl.ds(pl.multiple_of(place * rows, rows), rows)]
                copies.append(
                    pltpu.make_async_copy(source.at[:, columns], target, sem.at[len(copies)])
                )
    for copy in copies:
        copy.start()
    for copy in copies:
        copy.wait()


def chip_halves(mine, other, chosen, **rest):
    rows, width = mine[0].shape
    return call(
        functools.partial(halves_kernel, len(mine), chosen),
        "chip_halves",
        [shape_of((len(picks), 2 * rows, width // 2 // parts)) for parts, picks in chosen],
        [*mine, *other],
        [ANY] * (2 * len(mine)),
        scratch=[pltpu.SemaphoreType.DMA((sum(2 * len(picks) for _, picks in chosen),))],
        **rest,
    )


def ahead_kernel(first_ref, second_ref, first_out, second_out, sem):
    copies = [
        pltpu.make_async_copy(first_ref.at[0], first_out, sem.at[0]),
        pltpu.make_async_copy(second_ref.at[1], second_out, sem.at[1]),
    ]
    for copy in copies:
        copy.start()
    for copy in copies:
        copy.wait()


def send_pair(pair, bits, name):
    return [pair, *(swap(pair, "trunk", bit, name) for bit in bits)]


def send_direct(pair, bits, name):
    steps = [0, bits[0], bits[1], bits[0] ^ bits[1]]
    arrays = [pair, *(swap(pair, "trunk", step, name) for step in steps[1:])]
    return arrays, [[(i, (slot,), steps[i] // 2) for i in range(4)] for slot in range(2)]


def send_ahead(held, bits, name, through=(), **rest):
    first, second = bits
    _, rows, cols = held[0].shape
    out = call(
        ahead_kernel,
        "send_ahead",
        [shape_of((rows, cols))] * 2,
        held[1:],
        [ANY] * 2,
        scratch=[pltpu.SemaphoreType.DMA((2,))],
        through=through,
        **rest,
    )
    far = [
        swap(out[0], "trunk", second, name + "_ahead"),
        swap(out[1], "trunk", first, name + "_ahead"),
    ]
    steps = (0, first // 2, second // 2, (first ^ second) // 2)
    picks = [
        [(i, (slot,), steps[i]) for i in range(3)] + [(3 + slot, (), steps[3])] for slot in range(2)
    ]
    return ([*held, *far], picks), out[2:]


def whole_pair(weights, parts, chosen):
    arrays = []
    for i, p in chosen:
        full = lax.all_gather(weights[i], "trunk", axis=0, tiled=True)
        part = full.shape[1] // 2 // parts
        start = core_index() * (full.shape[1] // 2) + p * part
        arrays.append(lax.dynamic_slice_in_dim(full, start, part, axis=1))
    return arrays, [[(i, (), None)] for i in range(len(arrays))]


def project(x_ref, lead, picks, refs):
    chip = chip_index()
    total = None
    for number, index, offset in picks:
        weight = refs[number][index] if index else refs[number][...]
        depth = weight.shape[0]
        if offset is None:
            left = x_ref[lead]
        else:
            left = x_ref[lead, :, pl.ds(pl.multiple_of((chip ^ offset) * depth, depth), depth)]
        term = dot(left, weight)
        total = term if total is None else total + term
    return total


def pack_kernel(offset_ref, tree_ref, out_ref):
    out_ref[0:1] = offset_ref[0]
    out_ref[1:2] = tree_ref[0]


def pack_forks(offset, tree, **rest):
    return call(
        pack_kernel,
        "pack_forks",
        [shape_of((2, offset.shape[2]), jnp.int32)],
        [offset, tree],
        [VMEM] * 2,
        **rest,
    )[0]


def trunk_kernel(picks, mask, *refs):
    xs, weights = refs[:2], refs[2:-6]
    low_ref, high_ref, first_ref, keys_ref, values_ref, state_ref = refs[-6:]
    top = (lax.axis_index("trunk") & mask) == 0
    trees, heads = state_ref.shape[1:3]
    low = low_ref.shape[1]
    for side in range(2):
        for tree in range(trees):
            keys = project(xs[side], tree, picks[0], weights).astype(BF16)
            values = project(xs[side], tree, picks[1], weights).astype(BF16)
            keys_ref[side, tree] = keys
            values_ref[side, tree] = values
            for h in range(heads):
                at = slice(h * DH, (h + 1) * DH)
                state = lax.dot_general(
                    keys[:, at], values[:, at], (((0,), (0,)), ((), ())), preferred_element_type=F32
                )
                state_ref[side, tree, h] = state
                if side:
                    total = (state_ref[0, tree, h] + state).astype(BF16)
                    if h < low:
                        low_ref[tree, h] = total
                    else:
                        high_ref[tree, h - low] = total
                        first_ref[tree, h - low] = jnp.where(top, total, jnp.zeros_like(total))


def trunk_states(mine, other, weights, mask, **rest):
    trees, tok, width = mine.shape
    arrays, picks = weights
    cols = arrays[0].shape[-1]
    heads = cols // DH
    low = heads // 2
    return call(
        functools.partial(trunk_kernel, picks, mask),
        "trunk_states",
        [
            shape_of((trees, low, DH, DH)),
            shape_of((trees, heads - low, DH, DH)),
            shape_of((trees, heads - low, DH, DH)),
            shape_of((2, trees, tok, cols)),
            shape_of((2, trees, tok, cols)),
            shape_of((2, trees, heads, DH, DH), F32),
        ],
        [mine, other, *arrays],
        [VMEM] * (2 + len(arrays)),
        **rest,
    )


def part_kernel(mine_ref, other_ref, keys_ref, values_ref, state_ref, fork_ref):
    core = core_index()
    tok = keys_ref.shape[2]
    entries, heads = fork_ref.shape[1:3]
    place = lax.broadcasted_iota(jnp.int32, (tok, DH), 0)
    for side in range(2):
        ints = other_ref if side else mine_ref
        for e in range(entries):
            tree = ints[1, e]
            inside = place < ints[0, e]
            odd = core != side
            for h in range(heads):
                at = slice(h * DH, (h + 1) * DH)
                keys = keys_ref[side, tree, :, at]
                part = lax.dot_general(
                    jnp.where(inside, keys, jnp.zeros_like(keys)),
                    values_ref[side, tree, :, at],
                    (((0,), (0,)), ((), ())),
                    preferred_element_type=F32,
                )
                lower = state_ref[1 - side, tree, h]
                fork_ref[side, e, h] = part + jnp.where(odd, lower, jnp.zeros_like(lower))


def fork_parts(forks, keys, values, states, **rest):
    _, _, tok, cols = keys.shape
    entries, heads = forks[0].shape[1], cols // DH
    return call(
        part_kernel,
        "fork_parts",
        [shape_of((2, entries, heads, DH, DH), F32)],
        [*forks, keys, values, states],
        [SMEM] * 2 + [VMEM] * 3,
        **rest,
    )


def scan_kernel(mask, low_ref, low_in_ref, high_ref, *refs):
    high_in, (low_out, high_out) = refs[:-2], refs[-2:]
    low_out[...] = (low_ref[...].astype(F32) + low_in_ref[...].astype(F32)).astype(BF16)
    total = jnp.where((lax.axis_index("trunk") & mask) == 0, high_ref[...].astype(F32), 0.0)
    for ref in high_in:
        total = total + ref[...].astype(F32)
    high_out[...] = total.astype(BF16)


def scan_step(low, low_in, high, high_in, mask, **rest):
    return call(
        functools.partial(scan_kernel, mask),
        "scan_step",
        [shape_of(low.shape), shape_of(high.shape)],
        [low, low_in, high, *high_in],
        [VMEM] * (3 + len(high_in)),
        **rest,
    )


def fork_kernel(low_masks, high_masks, lanes, *refs):
    ints, fork_ref, terms = refs[:2], refs[2], refs[3:]
    low_refs = terms[: len(low_masks)]
    high_refs = terms[len(low_masks) : len(low_masks) + len(high_masks)]
    outs, carried_ref = refs[-1 - lanes : -1], refs[-1]
    index, lane = lax.axis_index("trunk"), lax.axis_index("leaf")
    cap = outs[0].shape[1]
    first = 0
    for masks, terms in ((low_masks, low_refs), (high_masks, high_refs)):
        carried = None
        for mask, ref in zip(masks, terms):
            term = ref[...].astype(F32)
            if mask:
                term = jnp.where((index & mask) != 0, term, jnp.zeros_like(term))
            carried = term if carried is None else carried + term
        if terms:
            heads = terms[0].shape[1]
            carried_ref[:, first : first + heads] = carried
            first += heads
    for apart in range(lanes):
        for side in range(2):
            for c in range(cap):
                entry = (lane ^ apart) * cap + c
                state = fork_ref[side, entry] + carried_ref[ints[side][1, entry]]
                outs[apart][side, c] = state.astype(BF16)


def fork_states(forks, parts, low, high, lanes, **rest):
    _, entries, heads = parts.shape[:3]
    terms = [t for t, _ in low] + high
    trees = terms[0].shape[0]
    return call(
        functools.partial(fork_kernel, [m for _, m in low], [0] * len(high), lanes),
        "fork_states",
        [shape_of((2, entries // lanes, heads, DH, DH))] * lanes,
        [*forks, parts, *terms],
        [SMEM] * 2 + [VMEM] * (1 + len(terms)),
        scratch=[pltpu.VMEM((trees, heads, DH, DH), F32)],
        **rest,
    )


def branch_kernel(query_picks, picks, count, blen, *refs):
    xs, query_refs, weights = refs[:2], refs[2 : 2 + count], refs[2 + count : -2]
    q_out, intra_out = refs[-2:]
    rows = xs[0].shape[1]
    row = lax.broadcasted_iota(jnp.int32, (rows, rows), 0)
    column = lax.broadcasted_iota(jnp.int32, (rows, rows), 1)
    seen = (column <= row) & (column >= row - lax.rem(row, blen))
    for side in range(2):
        for slot in range(xs[0].shape[0]):
            first = 0
            for part in query_picks:
                q = project(xs[side], slot, part, query_refs).astype(BF16)
                q_out[side, slot, :, first : first + q.shape[1]] = q
                first += q.shape[1]
            k = project(xs[side], slot, picks[0], weights).astype(BF16)
            v = project(xs[side], slot, picks[1], weights).astype(BF16)
            for h in range(k.shape[1] // DH):
                at = slice(h * DH, (h + 1) * DH)
                scores = lax.dot_general(
                    q_out[side, slot, :, at],
                    k[:, at],
                    (((1,), (1,)), ((), ())),
                    preferred_element_type=F32,
                )
                scores = jnp.where(seen, scores, 0.0).astype(BF16)
                intra_out[side, slot, :, at] = dot(scores, v[:, at])


def branch_parts(mine, other, queries, weights, **rest):
    slots, blen, width = mine.shape
    join = 2 if slots % 2 == 0 else 1
    mine, other = (a.reshape(slots // join, join * blen, width) for a in (mine, other))
    arrays = [*queries[0], *weights[0]]
    cols = weights[0][0].shape[-1]
    lead = (2, slots // join, join * blen, cols)
    outs = call(
        functools.partial(branch_kernel, queries[1], weights[1], len(queries[0]), blen),
        "branch_parts",
        [shape_of(lead), shape_of(lead, F32)],
        [mine, other, *arrays],
        [VMEM] * (2 + len(arrays)),
        **rest,
    )
    return [o.reshape(2, slots, blen, cols) for o in outs]


def norm_kernel(lanes, q_ref, intra_ref, *refs):
    states, outs = refs[:lanes], refs[lanes:]
    lane = lax.axis_index("leaf")
    cap, heads = states[0].shape[1:3]
    for apart in range(lanes):
        for side in range(2):
            for c in range(cap):
                slot = (lane ^ apart) * cap + c
                for h in range(heads):
                    at = slice(h * DH, (h + 1) * DH)
                    total = intra_ref[side, slot, :, at] + dot(
                        q_ref[side, slot, :, at], states[apart][side, c, h]
                    )
                    meansq = jnp.mean(total * total, axis=-1, keepdims=True)
                    normed = (total * lax.rsqrt(meansq + 1e-06)).astype(BF16)
                    if side == 0:
                        outs[0][slot, :, at] = normed
                    elif h < heads // 2:
                        outs[1][slot, :, at] = normed
                    else:
                        outs[2][slot, :, (h - heads // 2) * DH : (h - heads // 2 + 1) * DH] = normed


def norm_parts(queries, intra, states, **rest):
    _, slots, blen, cols = queries.shape
    return call(
        functools.partial(norm_kernel, len(states)),
        "norm_parts",
        [shape_of((slots, blen, w)) for w in (cols, cols // 2, cols // 2)],
        [queries, intra, *states],
        [VMEM] * (2 + len(states)),
        **rest,
    )


def place_kernel(picks, *refs):
    core, chip = core_index(), chip_index()
    sources, out_ref, sem = refs[:-2], refs[-2], refs[-1]
    copies = []
    for slot, number, index, offset in picks:
        source = sources[number].at[index] if index else sources[number]
        rows, half = source.shape
        first = (core if slot == 0 else 1 - core) * half
        target = out_ref.at[
            pl.ds(pl.multiple_of((chip ^ offset) * rows, rows), rows),
            pl.ds(pl.multiple_of(first, half), half),
        ]
        copies.append(pltpu.make_async_copy(source, target, sem.at[len(copies)]))
    for copy in copies:
        copy.start()
    for copy in copies:
        copy.wait()


def place_rows(weights, shape, **rest):
    arrays, picks = weights
    chosen = [(slot, *pick) for slot, part in enumerate(picks) for pick in part]
    return call(
        functools.partial(place_kernel, chosen),
        "place_rows",
        [shape_of(shape)],
        arrays,
        [ANY] * len(arrays),
        scratch=[pltpu.SemaphoreType.DMA((len(chosen),))],
        **rest,
    )[0]


def rows_of(w_ref, first, core, count):
    half = w_ref.shape[0] // 2
    return w_ref[pl.ds(pl.multiple_of(core * half + first, count), count), :]


def out_sum_kernel(first, terms, *refs):
    inputs, w_ref, out_ref = refs[: len(terms)], refs[len(terms)], refs[-1]
    core = core_index()
    slots, _, cols = inputs[0].shape
    weights = [rows_of(w_ref, f, core if own else 1 - core, cols) for f, own in terms]
    for slot in range(slots):
        total = refs[len(terms) + 1][slot] if first else None
        for ref, weight in zip(inputs, weights):
            term = dot(ref[slot], weight)
            total = term if total is None else total + term
        out_ref[slot] = total


def out_sum(inputs, terms, weights, total=None, **rest):
    slots, blen, cols = inputs[0].shape
    extra = [] if total is None else [total]
    return call(
        functools.partial(out_sum_kernel, total is not None, terms),
        "out_sum",
        [shape_of((slots, blen, weights.shape[1]), F32)],
        [*inputs, weights, *extra],
        [VMEM] * (len(inputs) + 1 + len(extra)),
        **rest,
    )[0]


def out_last_kernel(count, len_ref, *refs):
    inputs, (w_ref, total_ref, out_ref, held_ref, sem) = refs[:count], refs[count:]
    core = core_index()
    slots, blen, cols = inputs[0].shape
    weights = [rows_of(w_ref, i * cols, 1 - core, cols) for i in range(count)]
    row = lax.broadcasted_iota(jnp.int32, (blen, w_ref.shape[1]), 0)
    copies = []
    for slot in range(slots):
        total = total_ref[slot]
        for ref, weight in zip(inputs, weights):
            total = total + dot(ref[slot], weight)
        held_ref[slot] = jnp.where(row < len_ref[slot], total, 0.0).astype(BF16)
        copies.append(pltpu.make_async_copy(held_ref.at[slot], out_ref.at[slot], sem.at[slot]))
        copies[-1].start()
    for copy in copies:
        copy.wait()


def out_last(lengths, inputs, weights, total, **rest):
    slots, blen, _ = inputs[0].shape
    shape = (slots, blen, weights.shape[1])
    return call(
        functools.partial(out_last_kernel, len(inputs)),
        "out_last",
        [shape_of(shape)],
        [lengths, *inputs, weights, total],
        [SMEM] + [VMEM] * (2 + len(inputs)),
        [ANY],
        scratch=[pltpu.VMEM(shape, BF16), pltpu.SemaphoreType.DMA((slots,))],
        **rest,
    )[0]


def shards(
    trunk_tokens, branch_tokens, fork_offset, fork_tree, branch_len, w_query, w_key, w_value, w_out
):
    lanes, count = lax.axis_size("leaf"), lax.axis_size("trunk")
    bits = [1 << i for i in range(1, count.bit_length() - 1)]
    paired = len(bits) == 2 and (2 * w_key.shape[0]) % DH == 0
    order = []

    if paired:
        kv, qo = [w_key, w_value], [w_query, w_out]
        kv_other = [swap(w, "trunk", 1, "core") for w in kv]
        touch(kv, order=order)
        (pair,) = chip_halves(kv, kv_other, [(1, [(0, 0, True), (1, 0, True)])], order=order)
        held = send_pair(pair, bits, "kv")
        qo_other = [swap(w, "trunk", 1, "core") for w in qo]
    own_forks = pack_forks(fork_offset, fork_tree, order=order)
    forks = (own_forks, swap(own_forks, "trunk", 1, "forks"))
    trunk_other = swap(trunk_tokens, "trunk", 1, "tokens")
    branch_other = swap(branch_tokens, "trunk", 1, "tokens")
    if paired:
        chosen = [(2, [(0, 0, True), (0, 1, True)]), (1, [(1, 0, True), (1, 0, False)])]
        query_pair, out_pair = chip_halves(qo, qo_other, chosen, order=order)
        pair, _ = send_ahead(held, bits, "kv", order=order)
        ready = [*pair[0][3:], branch_other, forks[1]]
        _, query_pair = touch(ready, order=order, through=[query_pair])
        queries = send_direct(query_pair, bits, "query")
    else:
        pair = whole_pair([w_key, w_value], 1, [(0, 0), (1, 0)])
        queries = whole_pair([w_query], 2, [(0, 0), (0, 1)])
        out_full = lax.all_gather(w_out, "trunk", axis=0, tiled=True)

    low, high, message, *kept = trunk_states(trunk_tokens, trunk_other, pair, bits[-1], order=order)
    low_terms, high_terms = [], []
    for step, (up, down) in enumerate(zip(bits, bits[::-1])):
        if step:
            low, message = scan_step(low, low_terms[-1][0], high, high_terms, down, order=order)
        low_terms.append((swap(low, "trunk", up, "scan"), up))
        high_terms.append(swap(message, "trunk", down, "scan"))
        if not step:
            (parts,) = fork_parts(forks, *kept, order=order)
    passed = []
    if paired:
        touch(queries[0][1:], order=order, weight=10.0)
        passed = [out_pair]
    sends = fork_states(
        forks, parts, low_terms, high_terms, lanes, order=order, through=passed
    )
    far = sorted(range(1, lanes), key=lambda a: a == 1)
    moved = {a: swap(sends[a], "leaf", a, "lane") for a in far}
    received = [sends[0]] + [moved[a] for a in range(1, lanes)]
    if paired:
        held = send_pair(sends[lanes], bits, "out")
    q, intra = branch_parts(branch_tokens, branch_other, queries, pair, order=order)
    if paired:
        outs, _ = send_ahead(held, bits, "out", order=order)
    mine, *other = norm_parts(q, intra, received, order=order)
    other = [swap(o, "trunk", 1, "normed") for o in other]
    if paired:
        out_full = place_rows(outs, (w_out.shape[0] * count, w_out.shape[1]), order=order)
    total = out_sum([mine], [(0, True)], out_full, order=order, weight=4.0)
    return out_last(branch_len, other, out_full, total, order=order)


def solution(mesh):
    in_specs = (
        P("leaf", "trunk", None),
        P(("leaf", "trunk"), None, None),
        P("leaf", "trunk", None),
        P("leaf", "trunk", None),
        P(("leaf", "trunk")),
        P("trunk", None),
        P("trunk", None),
        P("trunk", None),
        P("trunk", None),
    )
    out_specs = P(("leaf", "trunk"), None, None)
    return jax.shard_map(shards, mesh=mesh, in_specs=in_specs, out_specs=out_specs, check_vma=False)
```

time: 226 us -> 80.8 us (0.36)
  waiting for transfers between devices: 149 us -> 38.6 us
  matrix products: 31 us -> 0 us
  starting transfers between devices: 4.93 us -> 24.6 us
  other arithmetic: 15.1 us -> 0 us
  Pallas kernels: 0 us -> 14.6 us
  between operations: 13.3 us -> 0.22 us
  local copies, waits for them, and re-layouts: 11.3 us -> 1.93 us
    all_gather x5 -> x0, waiting for transfers between devices: 114 us -> none  [the longest x1 50.3 us: carried_in(): pieces = lax.all_gather(value, axis)]
    ppermute x0 -> x27, waiting for transfers between devices: none -> 38.6 us  [swap(): lax.ppermute(value, axis, [(i, i ^ bit) for i in range(lax.axis_size(axis...]
    all_to_all x1 -> x0, waiting for transfers between devices: 33 us -> none  [shards(): lax.all_to_all(fork_state, 'leaf', split_axis=0, concat_axis=0, tiled=True)]
    dot_general x10 -> x0, matrix products: 31 us -> none  [the longest x6 15.6 us: matmul(): return jnp.dot(left, right, preferred_element_type=jnp.float32)]
    ppermute x0 -> x27, starting transfers between devices: none -> 24.6 us  [swap(): lax.ppermute(value, axis, [(i, i ^ bit) for i in range(lax.axis_size(axis...]
    pallas_call x0 -> x17, Pallas kernels: none -> 14.6 us  [call(): pl.pallas_call(body, out_shape=[*outs, *(shape_of(a.shape, a.dtype) for a...]
    select_n x8 -> x0, other arithmetic: 11.2 us -> none  [the longest x7 11.2 us: step(): return jnp.where(position < mine, longer, subtotal)]
    all_to_all x1 -> x0, starting transfers between devices: 4.77 us -> none  [shards(): lax.all_to_all(fork_state, 'leaf', split_axis=0, concat_axis=0, tiled=True)]
  transfers between devices with their start and end apart: 6 -> 27, of which waited for: 5 -> 14; matrix products, arithmetic and copies ran while one was open for 20% -> 0% of each run, Pallas kernels for 0% -> 15%
where the time goes in v2:
time: 80.8 us; the launch traced here: 80 us
  waiting for transfers between devices  38.6 us (48%)
  starting transfers between devices  24.6 us (30%)
  Pallas kernels  14.6 us (18%)
  local copies, waits for them, and re-layouts  1.93 us (2%)
    ppermute x27, waiting for transfers between devices, swap(): lax.ppermute(value, axis, [(i, i ^ bit) for i in range(lax.axis_size(axis...  38.6 us
    ppermute x27, starting transfers between devices, swap(): lax.ppermute(value, axis, [(i, i ^ bit) for i in range(lax.axis_size(axis...  24.6 us
    pallas_call x17, Pallas kernels, call(): pl.pallas_call(body, out_shape=[*outs, *(shape_of(a.shape, a.dtype) for a...  14.6 us
    unnamed x18, local copies, waits for them, and re-layouts  1.93 us
  transfers between devices with their start and end apart: 27, of which 14 were waited for; matrix products, arithmetic and copies ran while one was open for 0% of the time, Pallas kernels for 15%

profile of v2, /device:TPU:0, one launch (start us, length us, event | category | flops | bytes accessed | tf_op | source)
XLA Modules:
  0.0 80.0 jit_solution(1090704249328108774)
XLA Ops:
  0.0 0.5 collective-permute-start.1
  0.5 0.5 collective-permute-start
  1.0 0.5 collective-permute-start.5
  1.5 0.9 %copy-done.1 = bf16[128,1024]{1,0:T(8,128)(2,1)S(1)} copy-done((bf16[128,1024]{1,0:T(8,128)(2,1)S(1)}, bf16[128,1024]{1,0:T(8,128)(2,1)}, u32[]{:S(2)}) %copy-start.1) | copy-done | bytes 262168
  2.4 0.9 %copy-done.2 = bf16[128,1024]{1,0:T(8,128)(2,1)S(1)} copy-done((bf16[128,1024]{1,0:T(8,128)(2,1)S(1)}, bf16[128,1024]{1,0:T(8,128)(2,1)}, u32[]{:S(2)}) %copy-start.2) | copy-done | bytes 262168
  3.4 0.1 chip_halves.2.refs_2_.refs_6_
  3.6 2.6 %collective-permute-start.3 = (bf16[2,256,512]{2,1,0:T(8,128)(2,1)S(1)}, bf16[2,256,512]{2,1,0:T(8,128)(2,1)S(1)}, u32[]{:S(2)}, u32[]{:S(2)}) collective-permute-start(bf16[2,256,512]{2,1,0:T(8,128)(2,1)S(1)} %chip_halves.2.refs_2_.refs_6_), channel_id=1, source_target_pairs={{0,2},{1,3},{2,0},{3,1},{4,6},{5,7},{6,4},{7,5},{8,10},{9,11},{10,... | collective-permute-start | bytes 1572872 | tf_op jit(solution)/shard_map/to_kv/ppermute | solution.py:22
  6.1 1.5 %collective-permute-start.4 = (bf16[2,256,512]{2,1,0:T(8,128)(2,1)S(1)}, bf16[2,256,512]{2,1,0:T(8,128)(2,1)S(1)}, u32[]{:S(2)}, u32[]{:S(2)}) collective-permute-start(bf16[2,256,512]{2,1,0:T(8,128)(2,1)S(1)} %chip_halves.2.refs_2_.refs_6_), channel_id=1, source_target_pairs={{0,4},{1,5},{2,6},{3,7},{4,0},{5,1},{6,2},{7,3},{8,12},{9,13},{10,... | collective-permute-start | bytes 1572872 | tf_op jit(solution)/shard_map/to_kv/ppermute | solution.py:22
  7.7 1.5 %collective-permute-done.6.refs_3_ = bf16[128,1024]{1,0:T(8,128)(2,1)S(1)} collective-permute-done((bf16[128,1024]{1,0:T(8,128)(2,1)S(1)}, bf16[128,1024]{1,0:T(8,128)(2,1)S(1)}, u32[]{:S(2)}, u32[]{:S(2)}) %collective-permute-start.6) | collective-permute-done | bytes 262176 | tf_op jit(solution)/shard_map/to_core/ppermute | solution.py:22
  9.2 0.2 chip_halves.3
  9.4 9.3 %collective-permute-done.3.refs_0_.refs_3_.refs_7_ = bf16[2,256,512]{2,1,0:T(8,128)(2,1)S(1)} collective-permute-done((bf16[2,256,512]{2,1,0:T(8,128)(2,1)S(1)}, bf16[2,256,512]{2,1,0:T(8,128)(2,1)S(1)}, u32[]{:S(2)}, u32[]{:S(2)}) %collective-permute-start.3) | collective-permute-done | bytes 524320 | tf_op jit(solution)/shard_map/to_kv/ppermute | solution.py:22
  18.7 1.5 %collective-permute-done.4.refs_1_.refs_4_.refs_8_ = bf16[2,256,512]{2,1,0:T(8,128)(2,1)S(1)} collective-permute-done((bf16[2,256,512]{2,1,0:T(8,128)(2,1)S(1)}, bf16[2,256,512]{2,1,0:T(8,128)(2,1)S(1)}, u32[]{:S(2)}, u32[]{:S(2)}) %collective-permute-start.4) | collective-permute-done | bytes 524320 | tf_op jit(solution)/shard_map/to_kv/ppermute | solution.py:22
  20.2 1.6 %collective-permute-start.7 = (bf16[256,512]{1,0:T(8,128)(2,1)S(1)}, bf16[256,512]{1,0:T(8,128)(2,1)S(1)}, u32[]{:S(2)}, u32[]{:S(2)}) collective-permute-start(bf16[256,512]{1,0:T(8,128)(2,1)S(1)} %get-tuple-element.32.refs_5_), channel_id=1, source_target_pairs={{0,4},{1,5},{2,6},{3,7},{4,0},{5,1},{6,2},{7,3},{8,12},{9,13},{10,... | collective-permute-start | bytes 786440 | tf_op jit(solution)/shard_map/to_kv_ahead/ppermute | solution.py:22
  21.8 0.5 collective-permute-start.8
  22.4 1.1 %collective-permute-done.9.refs_3_.refs_1_ = s32[2,4]{1,0:T(2,128)S(1)} collective-permute-done((s32[2,4]{1,0:T(2,128)S(1)}, s32[2,4]{1,0:T(2,128)S(1)}, u32[]{:S(2)}, u32[]{:S(2)}) %collective-permute-start.9) | collective-permute-done | bytes 64 | tf_op jit(solution)/shard_map/to_forks/ppermute | solution.py:22
  23.5 4.4 %collective-permute-done.7.refs_0_.refs_5_.refs_9_ = bf16[256,512]{1,0:T(8,128)(2,1)S(1)} collective-permute-done((bf16[256,512]{1,0:T(8,128)(2,1)S(1)}, bf16[256,512]{1,0:T(8,128)(2,1)S(1)}, u32[]{:S(2)}, u32[]{:S(2)}) %collective-permute-start.7) | collective-permute-done | bytes 262176 | tf_op jit(solution)/shard_map/to_kv_ahead/ppermute | solution.py:22
  27.9 1.2 %collective-permute-done.8.refs_1_.refs_6_.refs_10_ = bf16[256,512]{1,0:T(8,128)(2,1)S(1)} collective-permute-done((bf16[256,512]{1,0:T(8,128)(2,1)S(1)}, bf16[256,512]{1,0:T(8,128)(2,1)S(1)}, u32[]{:S(2)}, u32[]{:S(2)}) %collective-permute-start.8) | collective-permute-done | bytes 262176 | tf_op jit(solution)/shard_map/to_kv_ahead/ppermute | solution.py:22
  29.2 0.6 collective-permute-start.10
  29.8 0.6 collective-permute-start.11
  30.4 2.3 %collective-permute-start.12 = (bf16[2,256,256]{2,1,0:T(8,128)(2,1)S(1)}, bf16[2,256,256]{2,1,0:T(8,128)(2,1)S(1)}, u32[]{:S(2)}, u32[]{:S(2)}) collective-permute-start(bf16[2,256,256]{2,1,0:T(8,128)(2,1)S(1)} %get-tuple-element.34.refs_2_), channel_id=1, source_target_pairs={{0,6},{1,7},{2,4},{3,5},{4,2},{5,3},{6,0},{7,1},{8,14},{9,15},{10,... | collective-permute-start | bytes 786440 | tf_op jit(solution)/shard_map/to_query/ppermute | solution.py:22
  32.7 3.2 %trunk_states.1 = (bf16[2,2,128,128]{3,2,1,0:T(8,128)(2,1)S(1)}, bf16[2,2,128,128]{3,2,1,0:T(8,128)(2,1)S(1)}, bf16[2,2,128,128]{3,2,1,0:T(8,128)(2,1)S(1)}, bf1...) custom-call(bf16[2,256,1024]{2,1,0:T(8,128)(2,1)S(1)} %copy-done, ...), custom_call_target="tpu_custom_call" | custom-call | tf_op jit(solution)/shard_map/trunk_states/pallas_call | solution.py:40
  35.9 0.7 collective-permute-start.14
  36.5 0.6 collective-permute-start.15
  37.1 1.5 %fork_parts.1.refs_4_.refs_2_ = f32[2,4,4,128,128]{4,3,2,1,0:T(8,128)S(1)} custom-call(s32[2,4]{1,0:T(2,128)S(1)} %pack_forks.1.refs_4_.refs_0_, s32[2,4]{1,0:T(2,128)S(1)} %collective-permute-done.9.refs_3_.refs_1_, bf16[2,2,256,512]{3,2,1,0:T(8,128)(2,1)S(1)} %get-tuple-element.36.refs_2_, bf16[2,2,256,512]{3,2,1,0:T(8,128)(2,1)S(1)} %get-tuple-element.37.refs_3_, ...), custom_call_target="tpu_custom_call" | custom-call | tf_op jit(solution)/shard_map/fork_parts/pallas_call | solution.py:40
  38.6 5.4 %collective-permute-done.14.refs_1_.refs_3_ = bf16[2,2,128,128]{3,2,1,0:T(8,128)(2,1)S(1)} collective-permute-done((bf16[2,2,128,128]{3,2,1,0:T(8,128)(2,1)S(1)}, bf16[2,2,128,128]{3,2,1,0:T(8,128)(2,1)S(1)}, u32[]{:S(2)}, u32[]{:S(2)}) %collective-permute-start.14) | collective-permute-done | bytes 131104 | tf_op jit(solution)/shard_map/to_scan/ppermute | solution.py:22
  44.0 0.4 collective-permute-done.15.refs_3_.refs_5_
  44.5 0.9 %collective-permute-start.16 = (bf16[2,2,128,128]{3,2,1,0:T(8,128)(2,1)S(1)}, bf16[2,2,128,128]{3,2,1,0:T(8,128)(2,1)S(1)}, u32[]{:S(2)}, u32[]{:S(2)}) collective-permute-start(bf16[2,2,128,128]{3,2,1,0:T(8,128)(2,1)S(1)} %get-tuple-element.42.refs_3_), channel_id=1, source_target_pairs={{0,4},{1,5},{2,6},{3,7},{4,0},{5,1},{6,2},{7,3},{8,12},{9,13},{10,... | collective-permute-start | bytes 393224 | tf_op jit(solution)/shard_map/to_scan/ppermute | solution.py:22
  45.4 1.2 %collective-permute-start.17 = (bf16[2,2,128,128]{3,2,1,0:T(8,128)(2,1)S(1)}, bf16[2,2,128,128]{3,2,1,0:T(8,128)(2,1)S(1)}, u32[]{:S(2)}, u32[]{:S(2)}) collective-permute-start(bf16[2,2,128,128]{3,2,1,0:T(8,128)(2,1)S(1)} %get-tuple-element.43), channel_id=1, source_target_pairs={{0,2},{1,3},{2,0},{3,1},{4,6},{5,7},{6,4},{7,5},{8,10},{9,11},{10,... | collective-permute-start | bytes 393224 | tf_op jit(solution)/shard_map/to_scan/ppermute | solution.py:22
  46.6 2.9 %collective-permute-done.16.refs_4_ = bf16[2,2,128,128]{3,2,1,0:T(8,128)(2,1)S(1)} collective-permute-done((bf16[2,2,128,128]{3,2,1,0:T(8,128)(2,1)S(1)}, bf16[2,2,128,128]{3,2,1,0:T(8,128)(2,1)S(1)}, u32[]{:S(2)}, u32[]{:S(2)}) %collective-permute-start.16) | collective-permute-done | bytes 131104 | tf_op jit(solution)/shard_map/to_scan/ppermute | solution.py:22
  49.5 0.8 %collective-permute-done.17.refs_6_ = bf16[2,2,128,128]{3,2,1,0:T(8,128)(2,1)S(1)} collective-permute-done((bf16[2,2,128,128]{3,2,1,0:T(8,128)(2,1)S(1)}, bf16[2,2,128,128]{3,2,1,0:T(8,128)(2,1)S(1)}, u32[]{:S(2)}, u32[]{:S(2)}) %collective-permute-start.17) | collective-permute-done | bytes 131104 | tf_op jit(solution)/shard_map/to_scan/ppermute | solution.py:22
  50.4 0.9 %fork_states.1 = (bf16[2,1,4,128,128]{4,3,2,1,0:T(8,128)(2,1)S(1)}, bf16[2,1,4,128,128]{4,3,2,1,0:T(8,128)(2,1)S(1)}, bf16[2,1,4,128,128]{4,3,2,1,0:T(8,128)(2,1...) custom-call(s32[2,4]{1,0:T(2,128)S(1)} %pack_forks.1.refs_4_.refs_0_, ...), custom_call_target="tpu_custom_call", output_to_operand_aliasing={{4}: (7, {})} | custom-call | tf_op jit(solution)/shard_map/fork_states/pallas_call | solution.py:40
  51.3 1.2 %collective-permute-start.21 = (bf16[2,256,512]{2,1,0:T(8,128)(2,1)S(1)}, bf16[2,256,512]{2,1,0:T(8,128)(2,1)S(1)}, u32[]{:S(2)}, u32[]{:S(2)}) collective-permute-start(bf16[2,256,512]{2,1,0:T(8,128)(2,1)S(1)} %get-tuple-element.51.refs_0_), channel_id=1, source_target_pairs={{0,2},{1,3},{2,0},{3,1},{4,6},{5,7},{6,4},{7,5},{8,10},{9,11},{10,... | collective-permute-start | bytes 1572872 | tf_op jit(solution)/shard_map/to_out/ppermute | solution.py:22
  52.5 1.4 %collective-permute-start.22 = (bf16[2,256,512]{2,1,0:T(8,128)(2,1)S(1)}, bf16[2,256,512]{2,1,0:T(8,128)(2,1)S(1)}, u32[]{:S(2)}, u32[]{:S(2)}) collective-permute-start(bf16[2,256,512]{2,1,0:T(8,128)(2,1)S(1)} %get-tuple-element.51.refs_0_), channel_id=1, source_target_pairs={{0,4},{1,5},{2,6},{3,7},{4,0},{5,1},{6,2},{7,3},{8,12},{9,13},{10,... | collective-permute-start | bytes 1572872 | tf_op jit(solution)/shard_map/to_out/ppermute | solution.py:22
  53.9 1.6 %collective-permute-start.18 = (bf16[2,1,4,128,128]{4,3,2,1,0:T(8,128)(2,1)S(1)}, bf16[2,1,4,128,128]{4,3,2,1,0:T(8,128)(2,1)S(1)}, u32[]{:S(2)}, u32[]{:S(2)}) collective-permute-start(bf16[2,1,4,128,128]{4,3,2,1,0:T(8,128)(2,1)S(1)} %get-tuple-element.48), channel_id=1, source_target_pairs={{0,8},{8,0},{16,24},{24,16},{1,9},{9,1},{17,25},{25,17},{2,10},{10... | collective-permute-start | bytes 786440 | tf_op jit(solution)/shard_map/to_lane/ppermute | solution.py:22
  55.5 2.6 %collective-permute-start.19 = (bf16[2,1,4,128,128]{4,3,2,1,0:T(8,128)(2,1)S(1)}, bf16[2,1,4,128,128]{4,3,2,1,0:T(8,128)(2,1)S(1)}, u32[]{:S(2)}, u32[]{:S(2)}) collective-permute-start(bf16[2,1,4,128,128]{4,3,2,1,0:T(8,128)(2,1)S(1)} %get-tuple-element.49), channel_id=1, source_target_pairs={{0,16},{8,24},{16,0},{24,8},{1,17},{9,25},{17,1},{25,9},{2,18},{10... | collective-permute-start | bytes 786440 | tf_op jit(solution)/shard_map/to_lane/ppermute | solution.py:22
  58.1 0.2 collective-permute-start.20
  58.3 4.7 %branch_parts.1 = (bf16[2,2,256,512]{3,2,1,0:T(8,128)(2,1)S(1)}, f32[2,2,256,512]{3,2,1,0:T(8,128)S(1)}) custom-call(bf16[2,256,1024]{2,1,0:T(8,128)(2,1)S(1)} %bitcast.7, bf16[2,256,1024]{2,1,0:T(8,128)(2,1)S(1)} %bitcast.5, bf16[2,256,256]{2,1,0:T(8,128)(2,1)S(1)} %get-tuple-element.34.refs_2_, ...), custom_call_target="tpu_custom_call" | custom-call | tf_op jit(solution)/shard_map/branch_parts/pallas_call | solution.py:40
  63.0 0.1 collective-permute-done.21.refs_0_.refs_1_
  63.1 0.9 %collective-permute-done.22.refs_1_.refs_2_ = bf16[2,256,512]{2,1,0:T(8,128)(2,1)S(1)} collective-permute-done((bf16[2,256,512]{2,1,0:T(8,128)(2,1)S(1)}, bf16[2,256,512]{2,1,0:T(8,128)(2,1)S(1)}, u32[]{:S(2)}, u32[]{:S(2)}) %collective-permute-start.22) | collective-permute-done | bytes 524320 | tf_op jit(solution)/shard_map/to_out/ppermute | solution.py:22
  64.1 1.9 %collective-permute-start.25 = (bf16[256,512]{1,0:T(8,128)(2,1)S(1)}, bf16[256,512]{1,0:T(8,128)(2,1)S(1)}, u32[]{:S(2)}, u32[]{:S(2)}) collective-permute-start(bf16[256,512]{1,0:T(8,128)(2,1)S(1)} %get-tuple-element.52.refs_6_), channel_id=1, source_target_pairs={{0,4},{1,5},{2,6},{3,7},{4,0},{5,1},{6,2},{7,3},{8,12},{9,13},{10,... | collective-permute-start | bytes 786440 | tf_op jit(solution)/shard_map/to_out_ahead/ppermute | solution.py:22
  66.0 0.7 collective-permute-start.26
  66.7 8.5 %collective-permute-done.19.refs_4_ = bf16[2,1,4,128,128]{4,3,2,1,0:T(8,128)(2,1)S(1)} collective-permute-done((bf16[2,1,4,128,128]{4,3,2,1,0:T(8,128)(2,1)S(1)}, bf16[2,1,4,128,128]{4,3,2,1,0:T(8,128)(2,1)S(1)}, u32[]{:S(2)}, u32[]{:S(2)}) %collective-permute-start.19) | collective-permute-done | bytes 262176 | tf_op jit(solution)/shard_map/to_lane/ppermute | solution.py:22
  75.2 0.8 norm_parts.1
  76.1 0.5 collective-permute-start.24
  76.6 0.3 place_rows.1.refs_1_.refs_2_.refs_3_
  76.9 0.7 out_sum.1.refs_4_.refs_5_
  77.6 0.3 collective-permute-done.24.refs_2_
  78.0 2.0 %out_last.1 = bf16[4,128,1024]{2,1,0:T(8,128)(2,1)} custom-call(s32[4]{0:T(128)S(1)} %copy-done.6, bf16[4,128,256]{2,1,0:T(8,128)(2,1)S(1)} %collective-permute-done.23.refs_1_, bf16[4,128,256]{2,1,0:T(8,128)(2,1)S(1)} %collective-permute-done.24.refs_2_, bf16[1024,1024]{1,0:T(8,128)(2,1)S(1)} %place_rows.1.refs_1_.refs_2_.refs_3_, ...), custom_call_target="tpu_custom_call" | custom-call | tf_op jit(solution)/shard_map/out_last/pallas_call | solution.py:40
  (41 shorter events, 0.5 us)
Async XLA Ops:
  0.0 3.4 %collective-permute-start.1 = (bf16[128,1024]{1,0:T(8,128)(2,1)}, bf16[128,1024]{1,0:T(8,128)(2,1)S(1)}, u32[]{:S(2)}, u32[]{:S(2)}) collective-permute-start(bf16[128,1024]{1,0:T(8,128)(2,1)} %refs_0_.7), channel_id=1, source_target_pairs={{0,1},{1,0},{2,3},{3,2},{4,5},{5,4},{6,7},{7,6},{8,9},{9,8},{10,11... | collective-permute-start | bytes 786440 | tf_op jit(solution)/shard_map/to_core/ppermute | solution.py:22
  0.5 3.0 %collective-permute-start.2 = (bf16[128,1024]{1,0:T(8,128)(2,1)}, bf16[128,1024]{1,0:T(8,128)(2,1)S(1)}, u32[]{:S(2)}, u32[]{:S(2)}) collective-permute-start(bf16[128,1024]{1,0:T(8,128)(2,1)} %refs_1_.5), channel_id=1, source_target_pairs={{0,1},{1,0},{2,3},{3,2},{4,5},{5,4},{6,7},{7,6},{8,9},{9,8},{10,11... | collective-permute-start | bytes 786440 | tf_op jit(solution)/shard_map/to_core/ppermute | solution.py:22
  0.5 28.7 %collective-permute-start = (bf16[4,128,1024]{2,1,0:T(8,128)(2,1)}, bf16[4,128,1024]{2,1,0:T(8,128)(2,1)S(1)}, u32[]{:S(2)}, u32[]{:S(2)}) collective-permute-start(bf16[4,128,1024]{2,1,0:T(8,128)(2,1)} %param.10), channel_id=1, source_target_pairs={{0,1},{1,0},{2,3},{3,2},{4,5},{5,4},{6,7},{7,6},{8,9},{9,8},{10,11... | collective-permute-start | bytes 3145736 | tf_op jit(solution)/shard_map/to_tokens/ppermute | solution.py:22
  1.0 31.7 %collective-permute-start.13 = (bf16[2,256,1024]{2,1,0:T(8,128)(2,1)}, bf16[2,256,1024]{2,1,0:T(8,128)(2,1)S(1)}, u32[]{:S(2)}, u32[]{:S(2)}) collective-permute-start(bf16[2,256,1024]{2,1,0:T(8,128)(2,1)} %refs_0_.10), channel_id=1, source_target_pairs={{0,1},{1,0},{2,3},{3,2},{4,5},{5,4},{6,7},{7,6},{8,9},{9,8},{10,11... | collective-permute-start | bytes 3145736 | tf_op jit(solution)/shard_map/to_tokens/ppermute | solution.py:22
  1.0 6.6 %collective-permute-start.5 = (bf16[128,1024]{1,0:T(8,128)(2,1)}, bf16[128,1024]{1,0:T(8,128)(2,1)S(1)}, u32[]{:S(2)}, u32[]{:S(2)}) collective-permute-start(bf16[128,1024]{1,0:T(8,128)(2,1)} %refs_0_.9), channel_id=1, source_target_pairs={{0,1},{1,0},{2,3},{3,2},{4,5},{5,4},{6,7},{7,6},{8,9},{9,8},{10,11... | collective-permute-start | bytes 786440 | tf_op jit(solution)/shard_map/to_core/ppermute | solution.py:22
  1.5 0.9 %copy-start.1 = (bf16[128,1024]{1,0:T(8,128)(2,1)S(1)}, bf16[128,1024]{1,0:T(8,128)(2,1)}, u32[]{:S(2)}) copy-start(bf16[128,1024]{1,0:T(8,128)(2,1)} %refs_0_.7) | copy-start | bytes 786436
  2.4 0.9 %copy-start.2 = (bf16[128,1024]{1,0:T(8,128)(2,1)S(1)}, bf16[128,1024]{1,0:T(8,128)(2,1)}, u32[]{:S(2)}) copy-start(bf16[128,1024]{1,0:T(8,128)(2,1)} %refs_1_.5) | copy-start | bytes 786436
  3.4 4.3 %copy-start.5 = (bf16[128,1024]{1,0:T(8,128)(2,1)S(1)}, bf16[128,1024]{1,0:T(8,128)(2,1)}, u32[]{:S(2)}) copy-start(bf16[128,1024]{1,0:T(8,128)(2,1)} %refs_1_.7) | copy-start | bytes 786436
  3.4 4.3 %copy-start.7 = (s32[1,1,4]{2,1,0:T(1,128)S(1)}, s32[1,1,4]{2,1,0:T(1,128)}, u32[]{:S(2)}) copy-start(s32[1,1,4]{2,1,0:T(1,128)} %refs_0_.8) | copy-start | bytes 52
  3.4 4.3 %copy-start.8 = (s32[1,1,4]{2,1,0:T(1,128)S(1)}, s32[1,1,4]{2,1,0:T(1,128)}, u32[]{:S(2)}) copy-start(s32[1,1,4]{2,1,0:T(1,128)} %refs_1_.6) | copy-start | bytes 52
  3.4 5.8 %copy-start.4 = (bf16[128,1024]{1,0:T(8,128)(2,1)S(1)}, bf16[128,1024]{1,0:T(8,128)(2,1)}, u32[]{:S(2)}) copy-start(bf16[128,1024]{1,0:T(8,128)(2,1)} %refs_0_.9) | copy-start | bytes 786436
  3.6 15.2 %collective-permute-start.3 = (bf16[2,256,512]{2,1,0:T(8,128)(2,1)S(1)}, bf16[2,256,512]{2,1,0:T(8,128)(2,1)S(1)}, u32[]{:S(2)}, u32[]{:S(2)}) collective-permute-start(bf16[2,256,512]{2,1,0:T(8,128)(2,1)S(1)} %chip_halves.2.refs_2_.refs_6_), channel_id=1, source_target_pairs={{0,2},{1,3},{2,0},{3,1},{4,6},{5,7},{6,4},{7,5},{8,10},{9,11},{10,... | collective-permute-start | bytes 1572872 | tf_op jit(solution)/shard_map/to_kv/ppermute | solution.py:22
  6.1 14.1 %collective-permute-start.4 = (bf16[2,256,512]{2,1,0:T(8,128)(2,1)S(1)}, bf16[2,256,512]{2,1,0:T(8,128)(2,1)S(1)}, u32[]{:S(2)}, u32[]{:S(2)}) collective-permute-start(bf16[2,256,512]{2,1,0:T(8,128)(2,1)S(1)} %chip_halves.2.refs_2_.refs_6_), channel_id=1, source_target_pairs={{0,4},{1,5},{2,6},{3,7},{4,0},{5,1},{6,2},{7,3},{8,12},{9,13},{10,... | collective-permute-start | bytes 1572872 | tf_op jit(solution)/shard_map/to_kv/ppermute | solution.py:22
  7.6 1.5 %collective-permute-start.6 = (bf16[128,1024]{1,0:T(8,128)(2,1)S(1)}, bf16[128,1024]{1,0:T(8,128)(2,1)S(1)}, u32[]{:S(2)}, u32[]{:S(2)}) collective-permute-start(bf16[128,1024]{1,0:T(8,128)(2,1)S(1)} %copy-done.5), channel_id=1, source_target_pairs={{0,1},{1,0},{2,3},{3,2},{4,5},{5,4},{6,7},{7,6},{8,9},{9,8},{10,11... | collective-permute-start | bytes 786440 | tf_op jit(solution)/shard_map/to_core/ppermute | solution.py:22
  7.7 25.0 %copy-start = (bf16[2,256,1024]{2,1,0:T(8,128)(2,1)S(1)}, bf16[2,256,1024]{2,1,0:T(8,128)(2,1)}, u32[]{:S(2)}) copy-start(bf16[2,256,1024]{2,1,0:T(8,128)(2,1)} %refs_0_.10) | copy-start | bytes 3145732
  20.2 7.7 %collective-permute-start.7 = (bf16[256,512]{1,0:T(8,128)(2,1)S(1)}, bf16[256,512]{1,0:T(8,128)(2,1)S(1)}, u32[]{:S(2)}, u32[]{:S(2)}) collective-permute-start(bf16[256,512]{1,0:T(8,128)(2,1)S(1)} %get-tuple-element.32.refs_5_), channel_id=1, source_target_pairs={{0,4},{1,5},{2,6},{3,7},{4,0},{5,1},{6,2},{7,3},{8,12},{9,13},{10,... | collective-permute-start | bytes 786440 | tf_op jit(solution)/shard_map/to_kv_ahead/ppermute | solution.py:22
  21.8 7.3 %collective-permute-start.8 = (bf16[256,512]{1,0:T(8,128)(2,1)S(1)}, bf16[256,512]{1,0:T(8,128)(2,1)S(1)}, u32[]{:S(2)}, u32[]{:S(2)}) collective-permute-start(bf16[256,512]{1,0:T(8,128)(2,1)S(1)} %get-tuple-element.33), channel_id=1, source_target_pairs={{0,2},{1,3},{2,0},{3,1},{4,6},{5,7},{6,4},{7,5},{8,10},{9,11},{10,... | collective-permute-start | bytes 786440 | tf_op jit(solution)/shard_map/to_kv_ahead/ppermute | solution.py:22
  22.4 1.1 %collective-permute-start.9 = (s32[2,4]{1,0:T(2,128)S(1)}, s32[2,4]{1,0:T(2,128)S(1)}, u32[]{:S(2)}, u32[]{:S(2)}) collective-permute-start(s32[2,4]{1,0:T(2,128)S(1)} %pack_forks.1.refs_4_.refs_0_), channel_id=1, source_target_pairs={{0,1},{1,0},{2,3},{3,2},{4,5},{5,4},{6,7},{7,6},{8,9},{9,8},{10,11... | collective-permute-start | bytes 104 | tf_op jit(solution)/shard_map/to_forks/ppermute | solution.py:22
  29.2 17.4 %collective-permute-start.10 = (bf16[2,256,256]{2,1,0:T(8,128)(2,1)S(1)}, bf16[2,256,256]{2,1,0:T(8,128)(2,1)S(1)}, u32[]{:S(2)}, u32[]{:S(2)}) collective-permute-start(bf16[2,256,256]{2,1,0:T(8,128)(2,1)S(1)} %get-tuple-element.34.refs_2_), channel_id=1, source_target_pairs={{0,2},{1,3},{2,0},{3,1},{4,6},{5,7},{6,4},{7,5},{8,10},{9,11},{10,... | collective-permute-start | bytes 786440 | tf_op jit(solution)/shard_map/to_query/ppermute | solution.py:22
  29.8 16.8 %collective-permute-start.11 = (bf16[2,256,256]{2,1,0:T(8,128)(2,1)S(1)}, bf16[2,256,256]{2,1,0:T(8,128)(2,1)S(1)}, u32[]{:S(2)}, u32[]{:S(2)}) collective-permute-start(bf16[2,256,256]{2,1,0:T(8,128)(2,1)S(1)} %get-tuple-element.34.refs_2_), channel_id=1, source_target_pairs={{0,4},{1,5},{2,6},{3,7},{4,0},{5,1},{6,2},{7,3},{8,12},{9,13},{10,... | collective-permute-start | bytes 786440 | tf_op jit(solution)/shard_map/to_query/ppermute | solution.py:22
  30.4 16.2 %collective-permute-start.12 = (bf16[2,256,256]{2,1,0:T(8,128)(2,1)S(1)}, bf16[2,256,256]{2,1,0:T(8,128)(2,1)S(1)}, u32[]{:S(2)}, u32[]{:S(2)}) collective-permute-start(bf16[2,256,256]{2,1,0:T(8,128)(2,1)S(1)} %get-tuple-element.34.refs_2_), channel_id=1, source_target_pairs={{0,6},{1,7},{2,4},{3,5},{4,2},{5,3},{6,0},{7,1},{8,14},{9,15},{10,... | collective-permute-start | bytes 786440 | tf_op jit(solution)/shard_map/to_query/ppermute | solution.py:22
  35.9 8.2 %collective-permute-start.14 = (bf16[2,2,128,128]{3,2,1,0:T(8,128)(2,1)S(1)}, bf16[2,2,128,128]{3,2,1,0:T(8,128)(2,1)S(1)}, u32[]{:S(2)}, u32[]{:S(2)}) collective-permute-start(bf16[2,2,128,128]{3,2,1,0:T(8,128)(2,1)S(1)} %get-tuple-element.39.refs_5_.refs_0_), channel_id=1, source_target_pairs={{0,2},{1,3},{2,0},{3,1},{4,6},{5,7},{6,4},{7,5},{8,10},{9,11},{10,... | collective-permute-start | bytes 393224 | tf_op jit(solution)/shard_map/to_scan/ppermute | solution.py:22
  36.5 7.9 %collective-permute-start.15 = (bf16[2,2,128,128]{3,2,1,0:T(8,128)(2,1)S(1)}, bf16[2,2,128,128]{3,2,1,0:T(8,128)(2,1)S(1)}, u32[]{:S(2)}, u32[]{:S(2)}) collective-permute-start(bf16[2,2,128,128]{3,2,1,0:T(8,128)(2,1)S(1)} %get-tuple-element.41), channel_id=1, source_target_pairs={{0,4},{1,5},{2,6},{3,7},{4,0},{5,1},{6,2},{7,3},{8,12},{9,13},{10,... | collective-permute-start | bytes 393224 | tf_op jit(solution)/shard_map/to_scan/ppermute | solution.py:22
  44.5 5.0 %collective-permute-start.16 = (bf16[2,2,128,128]{3,2,1,0:T(8,128)(2,1)S(1)}, bf16[2,2,128,128]{3,2,1,0:T(8,128)(2,1)S(1)}, u32[]{:S(2)}, u32[]{:S(2)}) collective-permute-start(bf16[2,2,128,128]{3,2,1,0:T(8,128)(2,1)S(1)} %get-tuple-element.42.refs_3_), channel_id=1, source_target_pairs={{0,4},{1,5},{2,6},{3,7},{4,0},{5,1},{6,2},{7,3},{8,12},{9,13},{10,... | collective-permute-start | bytes 393224 | tf_op jit(solution)/shard_map/to_scan/ppermute | solution.py:22
  45.4 5.0 %collective-permute-start.17 = (bf16[2,2,128,128]{3,2,1,0:T(8,128)(2,1)S(1)}, bf16[2,2,128,128]{3,2,1,0:T(8,128)(2,1)S(1)}, u32[]{:S(2)}, u32[]{:S(2)}) collective-permute-start(bf16[2,2,128,128]{3,2,1,0:T(8,128)(2,1)S(1)} %get-tuple-element.43), channel_id=1, source_target_pairs={{0,2},{1,3},{2,0},{3,1},{4,6},{5,7},{6,4},{7,5},{8,10},{9,11},{10,... | collective-permute-start | bytes 393224 | tf_op jit(solution)/shard_map/to_scan/ppermute | solution.py:22
  46.6 11.7 %copy-start.3 = (bf16[4,128,1024]{2,1,0:T(8,128)(2,1)S(1)}, bf16[4,128,1024]{2,1,0:T(8,128)(2,1)}, u32[]{:S(2)}) copy-start(bf16[4,128,1024]{2,1,0:T(8,128)(2,1)} %param.10) | copy-start | bytes 3145732
  51.3 11.8 %collective-permute-start.21 = (bf16[2,256,512]{2,1,0:T(8,128)(2,1)S(1)}, bf16[2,256,512]{2,1,0:T(8,128)(2,1)S(1)}, u32[]{:S(2)}, u32[]{:S(2)}) collective-permute-start(bf16[2,256,512]{2,1,0:T(8,128)(2,1)S(1)} %get-tuple-element.51.refs_0_), channel_id=1, source_target_pairs={{0,2},{1,3},{2,0},{3,1},{4,6},{5,7},{6,4},{7,5},{8,10},{9,11},{10,... | collective-permute-start | bytes 1572872 | tf_op jit(solution)/shard_map/to_out/ppermute | solution.py:22
  52.5 11.5 %collective-permute-start.22 = (bf16[2,256,512]{2,1,0:T(8,128)(2,1)S(1)}, bf16[2,256,512]{2,1,0:T(8,128)(2,1)S(1)}, u32[]{:S(2)}, u32[]{:S(2)}) collective-permute-start(bf16[2,256,512]{2,1,0:T(8,128)(2,1)S(1)} %get-tuple-element.51.refs_0_), channel_id=1, source_target_pairs={{0,4},{1,5},{2,6},{3,7},{4,0},{5,1},{6,2},{7,3},{8,12},{9,13},{10,... | collective-permute-start | bytes 1572872 | tf_op jit(solution)/shard_map/to_out/ppermute | solution.py:22
  53.9 12.8 %collective-permute-start.18 = (bf16[2,1,4,128,128]{4,3,2,1,0:T(8,128)(2,1)S(1)}, bf16[2,1,4,128,128]{4,3,2,1,0:T(8,128)(2,1)S(1)}, u32[]{:S(2)}, u32[]{:S(2)}) collective-permute-start(bf16[2,1,4,128,128]{4,3,2,1,0:T(8,128)(2,1)S(1)} %get-tuple-element.48), channel_id=1, source_target_pairs={{0,8},{8,0},{16,24},{24,16},{1,9},{9,1},{17,25},{25,17},{2,10},{10... | collective-permute-start | bytes 786440 | tf_op jit(solution)/shard_map/to_lane/ppermute | solution.py:22
  55.5 19.7 %collective-permute-start.19 = (bf16[2,1,4,128,128]{4,3,2,1,0:T(8,128)(2,1)S(1)}, bf16[2,1,4,128,128]{4,3,2,1,0:T(8,128)(2,1)S(1)}, u32[]{:S(2)}, u32[]{:S(2)}) collective-permute-start(bf16[2,1,4,128,128]{4,3,2,1,0:T(8,128)(2,1)S(1)} %get-tuple-element.49), channel_id=1, source_target_pairs={{0,16},{8,24},{16,0},{24,8},{1,17},{9,25},{17,1},{25,9},{2,18},{10... | collective-permute-start | bytes 786440 | tf_op jit(solution)/shard_map/to_lane/ppermute | solution.py:22
  58.1 17.1 %collective-permute-start.20 = (bf16[2,1,4,128,128]{4,3,2,1,0:T(8,128)(2,1)S(1)}, bf16[2,1,4,128,128]{4,3,2,1,0:T(8,128)(2,1)S(1)}, u32[]{:S(2)}, u32[]{:S(2)}) collective-permute-start(bf16[2,1,4,128,128]{4,3,2,1,0:T(8,128)(2,1)S(1)} %get-tuple-element.50), channel_id=1, source_target_pairs={{0,24},{8,16},{16,8},{24,0},{1,25},{9,17},{17,9},{25,1},{2,26},{10... | collective-permute-start | bytes 786440 | tf_op jit(solution)/shard_map/to_lane/ppermute | solution.py:22
  64.1 12.5 %collective-permute-start.25 = (bf16[256,512]{1,0:T(8,128)(2,1)S(1)}, bf16[256,512]{1,0:T(8,128)(2,1)S(1)}, u32[]{:S(2)}, u32[]{:S(2)}) collective-permute-start(bf16[256,512]{1,0:T(8,128)(2,1)S(1)} %get-tuple-element.52.refs_6_), channel_id=1, source_target_pairs={{0,4},{1,5},{2,6},{3,7},{4,0},{5,1},{6,2},{7,3},{8,12},{9,13},{10,... | collective-permute-start | bytes 786440 | tf_op jit(solution)/shard_map/to_out_ahead/ppermute | solution.py:22
  66.0 10.6 %collective-permute-start.26 = (bf16[256,512]{1,0:T(8,128)(2,1)S(1)}, bf16[256,512]{1,0:T(8,128)(2,1)S(1)}, u32[]{:S(2)}, u32[]{:S(2)}) collective-permute-start(bf16[256,512]{1,0:T(8,128)(2,1)S(1)} %get-tuple-element.55), channel_id=1, source_target_pairs={{0,2},{1,3},{2,0},{3,1},{4,6},{5,7},{6,4},{7,5},{8,10},{9,11},{10,... | collective-permute-start | bytes 786440 | tf_op jit(solution)/shard_map/to_out_ahead/ppermute | solution.py:22
  76.0 1.6 %collective-permute-start.23 = (bf16[4,128,256]{2,1,0:T(8,128)(2,1)S(1)}, bf16[4,128,256]{2,1,0:T(8,128)(2,1)S(1)}, u32[]{:S(2)}, u32[]{:S(2)}) collective-permute-start(bf16[4,128,256]{2,1,0:T(8,128)(2,1)S(1)} %get-tuple-element.53), channel_id=1, source_target_pairs={{0,1},{1,0},{2,3},{3,2},{4,5},{5,4},{6,7},{7,6},{8,9},{9,8},{10,11... | collective-permute-start | bytes 786440 | tf_op jit(solution)/shard_map/to_normed/ppermute | solution.py:22
  76.1 1.9 %collective-permute-start.24 = (bf16[4,128,256]{2,1,0:T(8,128)(2,1)S(1)}, bf16[4,128,256]{2,1,0:T(8,128)(2,1)S(1)}, u32[]{:S(2)}, u32[]{:S(2)}) collective-permute-start(bf16[4,128,256]{2,1,0:T(8,128)(2,1)S(1)} %get-tuple-element.54), channel_id=1, source_target_pairs={{0,1},{1,0},{2,3},{3,2},{4,5},{5,4},{6,7},{7,6},{8,9},{9,8},{10,11... | collective-permute-start | bytes 786440 | tf_op jit(solution)/shard_map/to_normed/ppermute | solution.py:22
  76.8 1.1 %copy-start.6 = (s32[4]{0:T(128)S(1)}, s32[4]{0:T(128)}, u32[]{:S(2)}) copy-start(s32[4]{0:T(128)} %refs_0_.11) | copy-start | bytes 52

commit v3 on v2

--- a/solution.py
+++ b/solution.py
@@ -72,13 +72,14 @@
 
 
 def halves_kernel(count, chosen, *refs):
-    core = core_index()
+    core, odd = core_index(), lax.axis_index("leaf") % 2
     mine, other, outs, sem = refs[:count], refs[count : 2 * count], refs[2 * count : -1], refs[-1]
     copies = []
     for out, (parts, picks) in zip(outs, chosen):
         for slot, (i, p, own) in enumerate(picks):
             rows, width = mine[i].shape
             part = width // 2 // parts
+            p = {"even": odd, "odd": 1 - odd}.get(p, p)
             first = (core if own else 1 - core) * (width // 2) + p * part
             columns = pl.ds(pl.multiple_of(first, part), part)
             for source, place in ((mine[i], core), (other[i], 1 - core)):
@@ -120,10 +121,12 @@
     return [pair, *(swap(pair, "trunk", bit, name) for bit in bits)]
 
 
-def send_direct(pair, bits, name):
+def send_across(part, other, bits, name):
     steps = [0, bits[0], bits[1], bits[0] ^ bits[1]]
-    arrays = [pair, *(swap(pair, "trunk", step, name) for step in steps[1:])]
-    return arrays, [[(i, (slot,), steps[i] // 2) for i in range(4)] for slot in range(2)]
+    near = [swap(part, "trunk", step, name) for step in steps[1:]]
+    across = [swap(a, "leaf", 1, name + "_lane") for a in near]
+    arrays = [part, *near, other, *across]
+    return arrays, [[(4 * i + k, (0,), steps[k] // 2) for k in range(4)] for i in range(2)]
 
 
 def send_ahead(held, bits, name, through=(), **rest):
@@ -191,16 +194,39 @@
     )[0]
 
 
-def trunk_kernel(picks, mask, *refs):
-    xs, weights = refs[:2], refs[2:-6]
+def partial_kernel(picks, *refs):
+    xs, weights, outs = refs[:2], refs[2:-2], refs[-2:]
+    for side in range(2):
+        for tree in range(xs[0].shape[0]):
+            for part, out in zip(picks, outs):
+                out[side, tree] = project(xs[side], tree, part, weights)
+
+
+def trunk_partial(mine, other, weights, **rest):
+    trees, tok, _ = mine.shape
+    arrays, picks = weights
+    return call(
+        functools.partial(partial_kernel, picks),
+        "trunk_partial",
+        [shape_of((2, trees, tok, arrays[0].shape[-1]), F32)] * 2,
+        [mine, other, *arrays],
+        [VMEM] * (2 + len(arrays)),
+        **rest,
+    )
+
+
+def trunk_kernel(picks, mask, count, *refs):
+    xs, earlier, weights = refs[:2], refs[2 : 2 + count], refs[2 + count : -6]
     low_ref, high_ref, first_ref, keys_ref, values_ref, state_ref = refs[-6:]
     top = (lax.axis_index("trunk") & mask) == 0
     trees, heads = state_ref.shape[1:3]
     low = low_ref.shape[1]
     for side in range(2):
         for tree in range(trees):
-            keys = project(xs[side], tree, picks[0], weights).astype(BF16)
-            values = project(xs[side], tree, picks[1], weights).astype(BF16)
+            keys, values = (project(xs[side], tree, part, weights) for part in picks)
+            if earlier:
+                keys, values = keys + earlier[0][side, tree], values + earlier[1][side, tree]
+            keys, values = keys.astype(BF16), values.astype(BF16)
             keys_ref[side, tree] = keys
             values_ref[side, tree] = values
             for h in range(heads):
@@ -218,14 +244,14 @@
                         first_ref[tree, h - low] = jnp.where(top, total, jnp.zeros_like(total))
 
 
-def trunk_states(mine, other, weights, mask, **rest):
+def trunk_states(mine, other, weights, mask, earlier=(), **rest):
     trees, tok, width = mine.shape
     arrays, picks = weights
     cols = arrays[0].shape[-1]
     heads = cols // DH
     low = heads // 2
     return call(
-        functools.partial(trunk_kernel, picks, mask),
+        functools.partial(trunk_kernel, picks, mask, len(earlier)),
         "trunk_states",
         [
             shape_of((trees, low, DH, DH)),
@@ -235,8 +261,8 @@
             shape_of((2, trees, tok, cols)),
             shape_of((2, trees, heads, DH, DH), F32),
         ],
-        [mine, other, *arrays],
-        [VMEM] * (2 + len(arrays)),
+        [mine, other, *earlier, *arrays],
+        [VMEM] * (2 + len(earlier) + len(arrays)),
         **rest,
     )
 
@@ -340,7 +366,8 @@
     )
 
 
-def branch_kernel(query_picks, picks, count, blen, *refs):
+def branch_kernel(query_picks, by_lane, picks, count, blen, *refs):
+    odd = lax.axis_index("leaf") % 2
     xs, query_refs, weights = refs[:2], refs[2 : 2 + count], refs[2 + count : -2]
     q_out, intra_out = refs[-2:]
     rows = xs[0].shape[1]
@@ -349,11 +376,11 @@
     seen = (column <= row) & (column >= row - lax.rem(row, blen))
     for side in range(2):
         for slot in range(xs[0].shape[0]):
-            first = 0
-            for part in query_picks:
+            for i, part in enumerate(query_picks):
                 q = project(xs[side], slot, part, query_refs).astype(BF16)
-                q_out[side, slot, :, first : first + q.shape[1]] = q
-                first += q.shape[1]
+                place = (odd if i == 0 else 1 - odd) if by_lane else i
+                first = pl.multiple_of(place * q.shape[1], q.shape[1])
+                q_out[side, slot, :, pl.ds(first, q.shape[1])] = q
             k = project(xs[side], slot, picks[0], weights).astype(BF16)
             v = project(xs[side], slot, picks[1], weights).astype(BF16)
             for h in range(k.shape[1] // DH):
@@ -368,7 +395,7 @@
                 intra_out[side, slot, :, at] = dot(scores, v[:, at])
 
 
-def branch_parts(mine, other, queries, weights, **rest):
+def branch_parts(mine, other, queries, by_lane, weights, **rest):
     slots, blen, width = mine.shape
     join = 2 if slots % 2 == 0 else 1
     mine, other = (a.reshape(slots // join, join * blen, width) for a in (mine, other))
@@ -376,7 +403,9 @@
     cols = weights[0][0].shape[-1]
     lead = (2, slots // join, join * blen, cols)
     outs = call(
-        functools.partial(branch_kernel, queries[1], weights[1], len(queries[0]), blen),
+        functools.partial(
+            branch_kernel, queries[1], by_lane, weights[1], len(queries[0]), blen
+        ),
         "branch_parts",
         [shape_of(lead), shape_of(lead, F32)],
         [mine, other, *arrays],
@@ -523,14 +552,15 @@
 ):
     lanes, count = lax.axis_size("leaf"), lax.axis_size("trunk")
     bits = [1 << i for i in range(1, count.bit_length() - 1)]
-    paired = len(bits) == 2 and (2 * w_key.shape[0]) % DH == 0
+    paired = len(bits) == 2 and lanes % 2 == 0 and (2 * w_key.shape[0]) % DH == 0
     order = []
 
     if paired:
         kv, qo = [w_key, w_value], [w_query, w_out]
         kv_other = [swap(w, "trunk", 1, "core") for w in kv]
         touch(kv, order=order)
-        (pair,) = chip_halves(kv, kv_other, [(1, [(0, 0, True), (1, 0, True)])], order=order)
+        chosen = [(1, [(0, 0, True), (1, 0, True)])]
+        (pair,) = chip_halves(kv, kv_other, chosen, order=order, weight=40.0)
         held = send_pair(pair, bits, "kv")
         qo_other = [swap(w, "trunk", 1, "core") for w in qo]
     own_forks = pack_forks(fork_offset, fork_tree, order=order)
@@ -538,39 +568,52 @@
     trunk_other = swap(trunk_tokens, "trunk", 1, "tokens")
     branch_other = swap(branch_tokens, "trunk", 1, "tokens")
     if paired:
-        chosen = [(2, [(0, 0, True), (0, 1, True)]), (1, [(1, 0, True), (1, 0, False)])]
-        query_pair, out_pair = chip_halves(qo, qo_other, chosen, order=order)
+        chosen = [
+            (2, [(0, "even", True)]),
+            (2, [(0, "odd", True)]),
+            (1, [(1, 0, True), (1, 0, False)]),
+        ]
+        query, query_far, out_pair = chip_halves(
+            qo, qo_other, chosen, order=order, landed=[forks[1]]
+        )
         pair, _ = send_ahead(held, bits, "kv", order=order)
-        ready = [*pair[0][3:], branch_other, forks[1]]
-        _, query_pair = touch(ready, order=order, through=[query_pair])
-        queries = send_direct(query_pair, bits, "query")
+        arrays, picks = pair
+        near = arrays[:3], [part[:3] for part in picks]
+        *earlier, query = trunk_partial(
+            trunk_tokens, trunk_other, near, order=order, through=[query], landed=[branch_other]
+        )
+        queries = send_across(query, query_far, bits, "query")
+        last = arrays[3:], [[(n - 3, i, o) for n, i, o in part[3:]] for part in picks]
     else:
         pair = whole_pair([w_key, w_value], 1, [(0, 0), (1, 0)])
         queries = whole_pair([w_query], 2, [(0, 0), (0, 1)])
         out_full = lax.all_gather(w_out, "trunk", axis=0, tiled=True)
-
-    low, high, message, *kept = trunk_states(trunk_tokens, trunk_other, pair, bits[-1], order=order)
+        earlier, last = (), pair
+
+    low, high, message, *kept = trunk_states(
+        trunk_tokens, trunk_other, last, bits[-1], earlier, order=order
+    )
     low_terms, high_terms = [], []
     for step, (up, down) in enumerate(zip(bits, bits[::-1])):
         if step:
             low, message = scan_step(low, low_terms[-1][0], high, high_terms, down, order=order)
         low_terms.append((swap(low, "trunk", up, "scan"), up))
         high_terms.append(swap(message, "trunk", down, "scan"))
-        if not step:
-            (parts,) = fork_parts(forks, *kept, order=order)
-    passed = []
+    (parts,) = fork_parts(forks, *kept, order=order)
     if paired:
-        touch(queries[0][1:], order=order, weight=10.0)
-        passed = [out_pair]
+        touch(queries[0][5:], order=order, weight=2.0)
     sends = fork_states(
-        forks, parts, low_terms, high_terms, lanes, order=order, through=passed
+        forks, parts, low_terms, high_terms, lanes, order=order,
+        through=[out_pair] if paired else [],
     )
     far = sorted(range(1, lanes), key=lambda a: a == 1)
     moved = {a: swap(sends[a], "leaf", a, "lane") for a in far}
     received = [sends[0]] + [moved[a] for a in range(1, lanes)]
     if paired:
         held = send_pair(sends[lanes], bits, "out")
-    q, intra = branch_parts(branch_tokens, branch_other, queries, pair, order=order)
+    q, intra = branch_parts(
+        branch_tokens, branch_other, queries, paired, pair, order=order
+    )
     if paired:
         outs, _ = send_ahead(held, bits, "out", order=order)
     mine, *other = norm_parts(q, intra, received, order=order)

time: 80.8 us -> 73.9 us (0.915)
  waiting for transfers between devices: 38.6 us -> 29.6 us
  starting transfers between devices: 24.6 us -> 27.2 us
    ppermute x27 -> x30, waiting for transfers between devices: 38.6 us -> 29.6 us  [swap(): lax.ppermute(value, axis, [(i, i ^ bit) for i in range(lax.axis_size(axis...]
    ppermute x27 -> x30, starting transfers between devices: 24.6 us -> 27.2 us  [swap(): lax.ppermute(value, axis, [(i, i ^ bit) for i in range(lax.axis_size(axis...]
  transfers between devices with their start and end apart: 27 -> 30, of which waited for: 14 -> 14; matrix products, arithmetic and copies ran while one was open for 0% -> 0% of each run, Pallas kernels for 15% -> 16%
where the time goes in v3:
time: 73.9 us; the launch traced here: 73.7 us
  waiting for transfers between devices  29.6 us (40%)
  starting transfers between devices  27.2 us (37%)
  Pallas kernels  14.7 us (20%)
  local copies, waits for them, and re-layouts  1.94 us (3%)
    ppermute x30, waiting for transfers between devices, swap(): lax.ppermute(value, axis, [(i, i ^ bit) for i in range(lax.axis_size(axis...  29.6 us
    ppermute x30, starting transfers between devices, swap(): lax.ppermute(value, axis, [(i, i ^ bit) for i in range(lax.axis_size(axis...  27.2 us
    pallas_call x17, Pallas kernels, call(): pl.pallas_call(body, out_shape=[*outs, *(shape_of(a.shape, a.dtype) for a...  14.7 us
    unnamed x18, local copies, waits for them, and re-layouts  1.94 us
  transfers between devices with their start and end apart: 30, of which 14 were waited for; matrix products, arithmetic and copies ran while one was open for 0% of the time, Pallas kernels for 16%

profile of v3, /device:TPU:0, one launch (start us, length us, event | category | flops | bytes accessed | tf_op | source)
XLA Modules:
  0.0 73.7 jit_solution(14632996872029399884)
XLA Ops:
  0.0 0.5 collective-permute-start.2
  0.5 0.5 collective-permute-start.6
  1.0 0.5 collective-permute-start.1
  1.5 0.9 %copy-done.2 = bf16[128,1024]{1,0:T(8,128)(2,1)S(1)} copy-done((bf16[128,1024]{1,0:T(8,128)(2,1)S(1)}, bf16[128,1024]{1,0:T(8,128)(2,1)}, u32[]{:S(2)}) %copy-start.2) | copy-done | bytes 262168
  2.4 0.9 %copy-done.3 = bf16[128,1024]{1,0:T(8,128)(2,1)S(1)} copy-done((bf16[128,1024]{1,0:T(8,128)(2,1)S(1)}, bf16[128,1024]{1,0:T(8,128)(2,1)}, u32[]{:S(2)}) %copy-start.3) | copy-done | bytes 262168
  3.6 2.6 %collective-permute-start.5 = (bf16[2,256,512]{2,1,0:T(8,128)(2,1)S(1)}, bf16[2,256,512]{2,1,0:T(8,128)(2,1)S(1)}, u32[]{:S(2)}, u32[]{:S(2)}) collective-permute-start(bf16[2,256,512]{2,1,0:T(8,128)(2,1)S(1)} %chip_halves.2.refs_2_.refs_10_), channel_id=1, source_target_pairs={{0,4},{1,5},{2,6},{3,7},{4,0},{5,1},{6,2},{7,3},{8,12},{9,13},{10,... | collective-permute-start | bytes 1572872 | tf_op jit(solution)/shard_map/to_kv/ppermute | solution.py:22
  6.2 1.5 %collective-permute-start.4 = (bf16[2,256,512]{2,1,0:T(8,128)(2,1)S(1)}, bf16[2,256,512]{2,1,0:T(8,128)(2,1)S(1)}, u32[]{:S(2)}, u32[]{:S(2)}) collective-permute-start(bf16[2,256,512]{2,1,0:T(8,128)(2,1)S(1)} %chip_halves.2.refs_2_.refs_10_), channel_id=1, source_target_pairs={{0,2},{1,3},{2,0},{3,1},{4,6},{5,7},{6,4},{7,5},{8,10},{9,11},{10,... | collective-permute-start | bytes 1572872 | tf_op jit(solution)/shard_map/to_kv/ppermute | solution.py:22
  7.7 1.5 %collective-permute-done.7.refs_3_ = bf16[128,1024]{1,0:T(8,128)(2,1)S(1)} collective-permute-done((bf16[128,1024]{1,0:T(8,128)(2,1)S(1)}, bf16[128,1024]{1,0:T(8,128)(2,1)S(1)}, u32[]{:S(2)}, u32[]{:S(2)}) %collective-permute-start.7) | collective-permute-done | bytes 262176 | tf_op jit(solution)/shard_map/to_core/ppermute | solution.py:22
  9.3 1.0 %collective-permute-done.8.refs_5_.refs_1_ = s32[2,4]{1,0:T(2,128)S(1)} collective-permute-done((s32[2,4]{1,0:T(2,128)S(1)}, s32[2,4]{1,0:T(2,128)S(1)}, u32[]{:S(2)}, u32[]{:S(2)}) %collective-permute-start.8) | collective-permute-done | bytes 64 | tf_op jit(solution)/shard_map/to_forks/ppermute | solution.py:22
  10.5 8.2 %collective-permute-done.5.refs_1_.refs_4_.refs_12_ = bf16[2,256,512]{2,1,0:T(8,128)(2,1)S(1)} collective-permute-done((bf16[2,256,512]{2,1,0:T(8,128)(2,1)S(1)}, bf16[2,256,512]{2,1,0:T(8,128)(2,1)S(1)}, u32[]{:S(2)}, u32[]{:S(2)}) %collective-permute-start.5) | collective-permute-done | bytes 524320 | tf_op jit(solution)/shard_map/to_kv/ppermute | solution.py:22
  18.8 1.5 %collective-permute-done.4.refs_0_.refs_3_.refs_11_ = bf16[2,256,512]{2,1,0:T(8,128)(2,1)S(1)} collective-permute-done((bf16[2,256,512]{2,1,0:T(8,128)(2,1)S(1)}, bf16[2,256,512]{2,1,0:T(8,128)(2,1)S(1)}, u32[]{:S(2)}, u32[]{:S(2)}) %collective-permute-start.4) | collective-permute-done | bytes 524320 | tf_op jit(solution)/shard_map/to_kv/ppermute | solution.py:22
  20.3 1.6 %collective-permute-start.16 = (bf16[256,512]{1,0:T(8,128)(2,1)S(1)}, bf16[256,512]{1,0:T(8,128)(2,1)S(1)}, u32[]{:S(2)}, u32[]{:S(2)}) collective-permute-start(bf16[256,512]{1,0:T(8,128)(2,1)S(1)} %get-tuple-element.37), channel_id=1, source_target_pairs={{0,2},{1,3},{2,0},{3,1},{4,6},{5,7},{6,4},{7,5},{8,10},{9,11},{10,... | collective-permute-start | bytes 786440 | tf_op jit(solution)/shard_map/to_kv_ahead/ppermute | solution.py:22
  21.8 0.5 collective-permute-start.15
  22.4 1.8 %trunk_partial.1 = (f32[2,2,256,512]{3,2,1,0:T(8,128)S(1)}, f32[2,2,256,512]{3,2,1,0:T(8,128)S(1)}, bf16[1,256,256]{2,1,0:T(8,128)(2,1)S(1)}) custom-call(bf16[2,256,1024]{2,1,0:T(8,128)(2,1)S(1)} %copy-done, bf16[2,256,1024]{2,1,0:T(8,128)(2,1)S(1)} %collective-permute-done.1.refs_1_, ...), custom_call_target="tpu_custom_call", output_to_operand_aliasing={{2}: (5, {})} | custom-call | tf_op jit(solution)/shard_map/trunk_partial/pallas_call | solution.py:40
  24.2 1.6 %collective-permute-start.11 = (bf16[1,256,256]{2,1,0:T(8,128)(2,1)S(1)}, bf16[1,256,256]{2,1,0:T(8,128)(2,1)S(1)}, u32[]{:S(2)}, u32[]{:S(2)}) collective-permute-start(bf16[1,256,256]{2,1,0:T(8,128)(2,1)S(1)} %get-tuple-element.35.refs_2_), channel_id=1, source_target_pairs={{0,6},{1,7},{2,4},{3,5},{4,2},{5,3},{6,0},{7,1},{8,14},{9,15},{10,... | collective-permute-start | bytes 393224 | tf_op jit(solution)/shard_map/to_query/ppermute | solution.py:22
  25.8 0.4 collective-permute-start.10
  26.1 1.6 %collective-permute-start.9 = (bf16[1,256,256]{2,1,0:T(8,128)(2,1)S(1)}, bf16[1,256,256]{2,1,0:T(8,128)(2,1)S(1)}, u32[]{:S(2)}, u32[]{:S(2)}) collective-permute-start(bf16[1,256,256]{2,1,0:T(8,128)(2,1)S(1)} %get-tuple-element.35.refs_2_), channel_id=1, source_target_pairs={{0,2},{1,3},{2,0},{3,1},{4,6},{5,7},{6,4},{7,5},{8,10},{9,11},{10,... | collective-permute-start | bytes 393224 | tf_op jit(solution)/shard_map/to_query/ppermute | solution.py:22
  27.7 1.5 %collective-permute-done.16.refs_5_.refs_14_ = bf16[256,512]{1,0:T(8,128)(2,1)S(1)} collective-permute-done((bf16[256,512]{1,0:T(8,128)(2,1)S(1)}, bf16[256,512]{1,0:T(8,128)(2,1)S(1)}, u32[]{:S(2)}, u32[]{:S(2)}) %collective-permute-start.16) | collective-permute-done | bytes 262176 | tf_op jit(solution)/shard_map/to_kv_ahead/ppermute | solution.py:22
  29.2 4.7 %collective-permute-done.15.refs_4_.refs_13_ = bf16[256,512]{1,0:T(8,128)(2,1)S(1)} collective-permute-done((bf16[256,512]{1,0:T(8,128)(2,1)S(1)}, bf16[256,512]{1,0:T(8,128)(2,1)S(1)}, u32[]{:S(2)}, u32[]{:S(2)}) %collective-permute-start.15) | collective-permute-done | bytes 262176 | tf_op jit(solution)/shard_map/to_kv_ahead/ppermute | solution.py:22
  33.9 1.6 %trunk_states.1 = (bf16[2,2,128,128]{3,2,1,0:T(8,128)(2,1)S(1)}, bf16[2,2,128,128]{3,2,1,0:T(8,128)(2,1)S(1)}, bf16[2,2,128,128]{3,2,1,0:T(8,128)(2,1)S(1)}, bf1...) custom-call(bf16[2,256,1024]{2,1,0:T(8,128)(2,1)S(1)} %copy-done, ...), custom_call_target="tpu_custom_call" | custom-call | tf_op jit(solution)/shard_map/trunk_states/pallas_call | solution.py:40
  35.5 0.6 collective-permute-start.18
  36.0 1.6 %collective-permute-start.14 = (bf16[1,256,256]{2,1,0:T(8,128)(2,1)S(1)}, bf16[1,256,256]{2,1,0:T(8,128)(2,1)S(1)}, u32[]{:S(2)}, u32[]{:S(2)}) collective-permute-start(bf16[1,256,256]{2,1,0:T(8,128)(2,1)S(1)} %collective-permute-done.11.refs_5_), channel_id=1, source_target_pairs={{0,8},{8,0},{16,24},{24,16},{1,9},{9,1},{17,25},{25,17},{2,10},{10... | collective-permute-start | bytes 393224 | tf_op jit(solution)/shard_map/to_query_lane/ppermute | solution.py:22
  37.6 0.4 collective-permute-start.13
  38.1 1.6 %collective-permute-start.12 = (bf16[1,256,256]{2,1,0:T(8,128)(2,1)S(1)}, bf16[1,256,256]{2,1,0:T(8,128)(2,1)S(1)}, u32[]{:S(2)}, u32[]{:S(2)}) collective-permute-start(bf16[1,256,256]{2,1,0:T(8,128)(2,1)S(1)} %collective-permute-done.9.refs_3_), channel_id=1, source_target_pairs={{0,8},{8,0},{16,24},{24,16},{1,9},{9,1},{17,25},{25,17},{2,10},{10... | collective-permute-start | bytes 393224 | tf_op jit(solution)/shard_map/to_query_lane/ppermute | solution.py:22
  39.7 2.1 %collective-permute-done.18.refs_3_.refs_5_ = bf16[2,2,128,128]{3,2,1,0:T(8,128)(2,1)S(1)} collective-permute-done((bf16[2,2,128,128]{3,2,1,0:T(8,128)(2,1)S(1)}, bf16[2,2,128,128]{3,2,1,0:T(8,128)(2,1)S(1)}, u32[]{:S(2)}, u32[]{:S(2)}) %collective-permute-start.18) | collective-permute-done | bytes 131104 | tf_op jit(solution)/shard_map/to_scan/ppermute | solution.py:22
  41.8 0.6 collective-permute-start.20
  42.5 0.9 %collective-permute-start.19 = (bf16[2,2,128,128]{3,2,1,0:T(8,128)(2,1)S(1)}, bf16[2,2,128,128]{3,2,1,0:T(8,128)(2,1)S(1)}, u32[]{:S(2)}, u32[]{:S(2)}) collective-permute-start(bf16[2,2,128,128]{3,2,1,0:T(8,128)(2,1)S(1)} %get-tuple-element.46.refs_5_), channel_id=1, source_target_pairs={{0,4},{1,5},{2,6},{3,7},{4,0},{5,1},{6,2},{7,3},{8,12},{9,13},{10,... | collective-permute-start | bytes 393224 | tf_op jit(solution)/shard_map/to_scan/ppermute | solution.py:22
  43.3 1.4 %fork_parts.1.refs_3_.refs_2_ = f32[2,4,4,128,128]{4,3,2,1,0:T(8,128)S(1)} custom-call(s32[2,4]{1,0:T(2,128)S(1)} %pack_forks.1.refs_4_.refs_0_, s32[2,4]{1,0:T(2,128)S(1)} %collective-permute-done.8.refs_5_.refs_1_, bf16[2,2,256,512]{3,2,1,0:T(8,128)(2,1)S(1)} %get-tuple-element.40.refs_2_, bf16[2,2,256,512]{3,2,1,0:T(8,128)(2,1)S(1)} %get-tuple-element.41.refs_3_, ...), custom_call_target="tpu_custom_call" | custom-call | tf_op jit(solution)/shard_map/fork_parts/pallas_call | solution.py:40
  44.8 3.2 %collective-permute-done.20.refs_6_ = bf16[2,2,128,128]{3,2,1,0:T(8,128)(2,1)S(1)} collective-permute-done((bf16[2,2,128,128]{3,2,1,0:T(8,128)(2,1)S(1)}, bf16[2,2,128,128]{3,2,1,0:T(8,128)(2,1)S(1)}, u32[]{:S(2)}, u32[]{:S(2)}) %collective-permute-start.20) | collective-permute-done | bytes 131104 | tf_op jit(solution)/shard_map/to_scan/ppermute | solution.py:22
  48.0 0.7 %collective-permute-done.19.refs_4_ = bf16[2,2,128,128]{3,2,1,0:T(8,128)(2,1)S(1)} collective-permute-done((bf16[2,2,128,128]{3,2,1,0:T(8,128)(2,1)S(1)}, bf16[2,2,128,128]{3,2,1,0:T(8,128)(2,1)S(1)}, u32[]{:S(2)}, u32[]{:S(2)}) %collective-permute-start.19) | collective-permute-done | bytes 131104 | tf_op jit(solution)/shard_map/to_scan/ppermute | solution.py:22
  48.7 0.9 %fork_states.1 = (bf16[2,1,4,128,128]{4,3,2,1,0:T(8,128)(2,1)S(1)}, bf16[2,1,4,128,128]{4,3,2,1,0:T(8,128)(2,1)S(1)}, bf16[2,1,4,128,128]{4,3,2,1,0:T(8,128)(2,1...) custom-call(s32[2,4]{1,0:T(2,128)S(1)} %pack_forks.1.refs_4_.refs_0_, ...), custom_call_target="tpu_custom_call", output_to_operand_aliasing={{4}: (7, {})} | custom-call | tf_op jit(solution)/shard_map/fork_states/pallas_call | solution.py:40
  49.7 1.0 %collective-permute-start.25 = (bf16[2,256,512]{2,1,0:T(8,128)(2,1)S(1)}, bf16[2,256,512]{2,1,0:T(8,128)(2,1)S(1)}, u32[]{:S(2)}, u32[]{:S(2)}) collective-permute-start(bf16[2,256,512]{2,1,0:T(8,128)(2,1)S(1)} %get-tuple-element.55.refs_0_), channel_id=1, source_target_pairs={{0,4},{1,5},{2,6},{3,7},{4,0},{5,1},{6,2},{7,3},{8,12},{9,13},{10,... | collective-permute-start | bytes 1572872 | tf_op jit(solution)/shard_map/to_out/ppermute | solution.py:22
  50.7 1.4 %collective-permute-start.24 = (bf16[2,256,512]{2,1,0:T(8,128)(2,1)S(1)}, bf16[2,256,512]{2,1,0:T(8,128)(2,1)S(1)}, u32[]{:S(2)}, u32[]{:S(2)}) collective-permute-start(bf16[2,256,512]{2,1,0:T(8,128)(2,1)S(1)} %get-tuple-element.55.refs_0_), channel_id=1, source_target_pairs={{0,2},{1,3},{2,0},{3,1},{4,6},{5,7},{6,4},{7,5},{8,10},{9,11},{10,... | collective-permute-start | bytes 1572872 | tf_op jit(solution)/shard_map/to_out/ppermute | solution.py:22
  52.1 1.6 %collective-permute-start.21 = (bf16[2,1,4,128,128]{4,3,2,1,0:T(8,128)(2,1)S(1)}, bf16[2,1,4,128,128]{4,3,2,1,0:T(8,128)(2,1)S(1)}, u32[]{:S(2)}, u32[]{:S(2)}) collective-permute-start(bf16[2,1,4,128,128]{4,3,2,1,0:T(8,128)(2,1)S(1)} %get-tuple-element.52), channel_id=1, source_target_pairs={{0,8},{8,0},{16,24},{24,16},{1,9},{9,1},{17,25},{25,17},{2,10},{10... | collective-permute-start | bytes 786440 | tf_op jit(solution)/shard_map/to_lane/ppermute | solution.py:22
  53.7 2.6 %collective-permute-start.22 = (bf16[2,1,4,128,128]{4,3,2,1,0:T(8,128)(2,1)S(1)}, bf16[2,1,4,128,128]{4,3,2,1,0:T(8,128)(2,1)S(1)}, u32[]{:S(2)}, u32[]{:S(2)}) collective-permute-start(bf16[2,1,4,128,128]{4,3,2,1,0:T(8,128)(2,1)S(1)} %get-tuple-element.53), channel_id=1, source_target_pairs={{0,16},{8,24},{16,0},{24,8},{1,17},{9,25},{17,1},{25,9},{2,18},{10... | collective-permute-start | bytes 786440 | tf_op jit(solution)/shard_map/to_lane/ppermute | solution.py:22
  56.3 0.2 collective-permute-start.23
  56.5 4.7 %branch_parts.1 = (bf16[2,2,256,512]{3,2,1,0:T(8,128)(2,1)S(1)}, f32[2,2,256,512]{3,2,1,0:T(8,128)S(1)}) custom-call(bf16[2,256,1024]{2,1,0:T(8,128)(2,1)S(1)} %bitcast.7, bf16[2,256,1024]{2,1,0:T(8,128)(2,1)S(1)} %bitcast.5, bf16[1,256,256]{2,1,0:T(8,128)(2,1)S(1)} %get-tuple-element.35.refs_2_, bf16[1,256,256]{2,1,0:T(8,128)(2,1)S(1)} %collective-permute-done.9.refs_3_, ...), custom_call_target="tpu_custom_call" | custom-call | tf_op jit(solution)/shard_map/branch_parts/pallas_call | solution.py:40
  61.2 0.5 collective-permute-done.25.refs_1_.refs_2_
  61.7 0.9 %collective-permute-done.24.refs_0_.refs_1_ = bf16[2,256,512]{2,1,0:T(8,128)(2,1)S(1)} collective-permute-done((bf16[2,256,512]{2,1,0:T(8,128)(2,1)S(1)}, bf16[2,256,512]{2,1,0:T(8,128)(2,1)S(1)}, u32[]{:S(2)}, u32[]{:S(2)}) %collective-permute-start.24) | collective-permute-done | bytes 524320 | tf_op jit(solution)/shard_map/to_out/ppermute | solution.py:22
  62.7 1.5 %collective-permute-start.29 = (bf16[256,512]{1,0:T(8,128)(2,1)S(1)}, bf16[256,512]{1,0:T(8,128)(2,1)S(1)}, u32[]{:S(2)}, u32[]{:S(2)}) collective-permute-start(bf16[256,512]{1,0:T(8,128)(2,1)S(1)} %get-tuple-element.59), channel_id=1, source_target_pairs={{0,2},{1,3},{2,0},{3,1},{4,6},{5,7},{6,4},{7,5},{8,10},{9,11},{10,... | collective-permute-start | bytes 786440 | tf_op jit(solution)/shard_map/to_out_ahead/ppermute | solution.py:22
  64.2 1.3 %collective-permute-start.28 = (bf16[256,512]{1,0:T(8,128)(2,1)S(1)}, bf16[256,512]{1,0:T(8,128)(2,1)S(1)}, u32[]{:S(2)}, u32[]{:S(2)}) collective-permute-start(bf16[256,512]{1,0:T(8,128)(2,1)S(1)} %get-tuple-element.56.refs_6_), channel_id=1, source_target_pairs={{0,4},{1,5},{2,6},{3,7},{4,0},{5,1},{6,2},{7,3},{8,12},{9,13},{10,... | collective-permute-start | bytes 786440 | tf_op jit(solution)/shard_map/to_out_ahead/ppermute | solution.py:22
  65.5 2.2 %collective-permute-done.22.refs_4_ = bf16[2,1,4,128,128]{4,3,2,1,0:T(8,128)(2,1)S(1)} collective-permute-done((bf16[2,1,4,128,128]{4,3,2,1,0:T(8,128)(2,1)S(1)}, bf16[2,1,4,128,128]{4,3,2,1,0:T(8,128)(2,1)S(1)}, u32[]{:S(2)}, u32[]{:S(2)}) %collective-permute-start.22) | collective-permute-done | bytes 262176 | tf_op jit(solution)/shard_map/to_lane/ppermute | solution.py:22
  67.8 0.8 %norm_parts.1 = (bf16[4,128,512]{2,1,0:T(8,128)(2,1)S(1)}, bf16[4,128,256]{2,1,0:T(8,128)(2,1)S(1)}, bf16[4,128,256]{2,1,0:T(8,128)(2,1)S(1)}) custom-call(bf16[2,4,128,512]{3,2,1,0:T(8,128)(2,1)S(1)} %bitcast.4, f32[2,4,128,512]{3,2,1,0:T(8,128)S(1)} %bitcast.6, bf16[2,1,4,128,128]{4,3,2,1,0:T(8,128)(2,1)S(1)} %get-tuple-element.49.refs_15_.refs_2_, ...), custom_call_target="tpu_custom_call" | custom-call | tf_op jit(solution)/shard_map/norm_parts/pallas_call | solution.py:40
  68.6 0.5 collective-permute-start.27
  69.2 1.4 %collective-permute-done.28.refs_3_ = bf16[256,512]{1,0:T(8,128)(2,1)S(1)} collective-permute-done((bf16[256,512]{1,0:T(8,128)(2,1)S(1)}, bf16[256,512]{1,0:T(8,128)(2,1)S(1)}, u32[]{:S(2)}, u32[]{:S(2)}) %collective-permute-start.28) | collective-permute-done | bytes 262176 | tf_op jit(solution)/shard_map/to_out_ahead/ppermute | solution.py:22
  70.6 0.3 place_rows.1.refs_1_.refs_2_.refs_3_
  70.9 0.7 %out_sum.1.refs_4_.refs_5_ = f32[4,128,1024]{2,1,0:T(8,128)S(1)} custom-call(bf16[4,128,512]{2,1,0:T(8,128)(2,1)S(1)} %get-tuple-element.60.refs_5_.refs_0_, bf16[1024,1024]{1,0:T(8,128)(2,1)S(1)} %place_rows.1.refs_1_.refs_2_.refs_3_, bf16[1024,1024]{1,0:T(8,128)(2,1)S(1)} %place_rows.1.refs_1_.refs_2_.refs_3_), custom_call_target="tpu_custom_call" | custom-call | flops 4000000000 | tf_op jit(solution)/shard_map/out_sum/pallas_call | solution.py:40
  71.7 2.0 %out_last.1 = bf16[4,128,1024]{2,1,0:T(8,128)(2,1)} custom-call(s32[4]{0:T(128)S(1)} %copy-done.6, bf16[4,128,256]{2,1,0:T(8,128)(2,1)S(1)} %collective-permute-done.26.refs_1_, bf16[4,128,256]{2,1,0:T(8,128)(2,1)S(1)} %collective-permute-done.27.refs_2_, bf16[1024,1024]{1,0:T(8,128)(2,1)S(1)} %place_rows.1.refs_1_.refs_2_.refs_3_, ...), custom_call_target="tpu_custom_call" | custom-call | tf_op jit(solution)/shard_map/out_last/pallas_call | solution.py:40
  (47 shorter events, 1.0 us)
Async XLA Ops:
  0.0 3.4 %collective-permute-start.2 = (bf16[128,1024]{1,0:T(8,128)(2,1)}, bf16[128,1024]{1,0:T(8,128)(2,1)S(1)}, u32[]{:S(2)}, u32[]{:S(2)}) collective-permute-start(bf16[128,1024]{1,0:T(8,128)(2,1)} %refs_0_.8), channel_id=1, source_target_pairs={{0,1},{1,0},{2,3},{3,2},{4,5},{5,4},{6,7},{7,6},{8,9},{9,8},{10,11... | collective-permute-start | bytes 786440 | tf_op jit(solution)/shard_map/to_core/ppermute | solution.py:22
  0.5 3.0 %collective-permute-start.3 = (bf16[128,1024]{1,0:T(8,128)(2,1)}, bf16[128,1024]{1,0:T(8,128)(2,1)S(1)}, u32[]{:S(2)}, u32[]{:S(2)}) collective-permute-start(bf16[128,1024]{1,0:T(8,128)(2,1)} %refs_1_.5), channel_id=1, source_target_pairs={{0,1},{1,0},{2,3},{3,2},{4,5},{5,4},{6,7},{7,6},{8,9},{9,8},{10,11... | collective-permute-start | bytes 786440 | tf_op jit(solution)/shard_map/to_core/ppermute | solution.py:22
  0.5 7.1 %collective-permute-start.6 = (bf16[128,1024]{1,0:T(8,128)(2,1)}, bf16[128,1024]{1,0:T(8,128)(2,1)S(1)}, u32[]{:S(2)}, u32[]{:S(2)}) collective-permute-start(bf16[128,1024]{1,0:T(8,128)(2,1)} %refs_0_.10), channel_id=1, source_target_pairs={{0,1},{1,0},{2,3},{3,2},{4,5},{5,4},{6,7},{7,6},{8,9},{9,8},{10,11... | collective-permute-start | bytes 786440 | tf_op jit(solution)/shard_map/to_core/ppermute | solution.py:22
  1.0 21.4 %collective-permute-start = (bf16[4,128,1024]{2,1,0:T(8,128)(2,1)}, bf16[4,128,1024]{2,1,0:T(8,128)(2,1)S(1)}, u32[]{:S(2)}, u32[]{:S(2)}) collective-permute-start(bf16[4,128,1024]{2,1,0:T(8,128)(2,1)} %param.10), channel_id=1, source_target_pairs={{0,1},{1,0},{2,3},{3,2},{4,5},{5,4},{6,7},{7,6},{8,9},{9,8},{10,11... | collective-permute-start | bytes 3145736 | tf_op jit(solution)/shard_map/to_tokens/ppermute | solution.py:22
  1.0 21.3 %collective-permute-start.1 = (bf16[2,256,1024]{2,1,0:T(8,128)(2,1)}, bf16[2,256,1024]{2,1,0:T(8,128)(2,1)S(1)}, u32[]{:S(2)}, u32[]{:S(2)}) collective-permute-start(bf16[2,256,1024]{2,1,0:T(8,128)(2,1)} %refs_0_.12), channel_id=1, source_target_pairs={{0,1},{1,0},{2,3},{3,2},{4,5},{5,4},{6,7},{7,6},{8,9},{9,8},{10,11... | collective-permute-start | bytes 3145736 | tf_op jit(solution)/shard_map/to_tokens/ppermute | solution.py:22
  1.5 0.9 %copy-start.2 = (bf16[128,1024]{1,0:T(8,128)(2,1)S(1)}, bf16[128,1024]{1,0:T(8,128)(2,1)}, u32[]{:S(2)}) copy-start(bf16[128,1024]{1,0:T(8,128)(2,1)} %refs_0_.8) | copy-start | bytes 786436
  2.4 0.9 %copy-start.3 = (bf16[128,1024]{1,0:T(8,128)(2,1)S(1)}, bf16[128,1024]{1,0:T(8,128)(2,1)}, u32[]{:S(2)}) copy-start(bf16[128,1024]{1,0:T(8,128)(2,1)} %refs_1_.5) | copy-start | bytes 786436
  3.4 4.3 %copy-start.5 = (bf16[128,1024]{1,0:T(8,128)(2,1)S(1)}, bf16[128,1024]{1,0:T(8,128)(2,1)}, u32[]{:S(2)}) copy-start(bf16[128,1024]{1,0:T(8,128)(2,1)} %refs_1_.7) | copy-start | bytes 786436
  3.4 4.3 %copy-start.7 = (s32[1,1,4]{2,1,0:T(1,128)S(1)}, s32[1,1,4]{2,1,0:T(1,128)}, u32[]{:S(2)}) copy-start(s32[1,1,4]{2,1,0:T(1,128)} %refs_0_.9) | copy-start | bytes 52
  3.4 4.3 %copy-start.8 = (s32[1,1,4]{2,1,0:T(1,128)S(1)}, s32[1,1,4]{2,1,0:T(1,128)}, u32[]{:S(2)}) copy-start(s32[1,1,4]{2,1,0:T(1,128)} %refs_1_.6) | copy-start | bytes 52
  3.4 6.9 %copy-start.4 = (bf16[128,1024]{1,0:T(8,128)(2,1)S(1)}, bf16[128,1024]{1,0:T(8,128)(2,1)}, u32[]{:S(2)}) copy-start(bf16[128,1024]{1,0:T(8,128)(2,1)} %refs_0_.10) | copy-start | bytes 786436
  3.6 18.8 %copy-start = (bf16[2,256,1024]{2,1,0:T(8,128)(2,1)S(1)}, bf16[2,256,1024]{2,1,0:T(8,128)(2,1)}, u32[]{:S(2)}) copy-start(bf16[2,256,1024]{2,1,0:T(8,128)(2,1)} %refs_0_.12) | copy-start | bytes 3145732
  3.6 15.2 %collective-permute-start.5 = (bf16[2,256,512]{2,1,0:T(8,128)(2,1)S(1)}, bf16[2,256,512]{2,1,0:T(8,128)(2,1)S(1)}, u32[]{:S(2)}, u32[]{:S(2)}) collective-permute-start(bf16[2,256,512]{2,1,0:T(8,128)(2,1)S(1)} %chip_halves.2.refs_2_.refs_10_), channel_id=1, source_target_pairs={{0,4},{1,5},{2,6},{3,7},{4,0},{5,1},{6,2},{7,3},{8,12},{9,13},{10,... | collective-permute-start | bytes 1572872 | tf_op jit(solution)/shard_map/to_kv/ppermute | solution.py:22
  6.2 14.1 %collective-permute-start.4 = (bf16[2,256,512]{2,1,0:T(8,128)(2,1)S(1)}, bf16[2,256,512]{2,1,0:T(8,128)(2,1)S(1)}, u32[]{:S(2)}, u32[]{:S(2)}) collective-permute-start(bf16[2,256,512]{2,1,0:T(8,128)(2,1)S(1)} %chip_halves.2.refs_2_.refs_10_), channel_id=1, source_target_pairs={{0,2},{1,3},{2,0},{3,1},{4,6},{5,7},{6,4},{7,5},{8,10},{9,11},{10,... | collective-permute-start | bytes 1572872 | tf_op jit(solution)/shard_map/to_kv/ppermute | solution.py:22
  7.7 1.5 %collective-permute-start.7 = (bf16[128,1024]{1,0:T(8,128)(2,1)S(1)}, bf16[128,1024]{1,0:T(8,128)(2,1)S(1)}, u32[]{:S(2)}, u32[]{:S(2)}) collective-permute-start(bf16[128,1024]{1,0:T(8,128)(2,1)S(1)} %copy-done.5), channel_id=1, source_target_pairs={{0,1},{1,0},{2,3},{3,2},{4,5},{5,4},{6,7},{7,6},{8,9},{9,8},{10,11... | collective-permute-start | bytes 786440 | tf_op jit(solution)/shard_map/to_core/ppermute | solution.py:22
  9.2 1.1 %collective-permute-start.8 = (s32[2,4]{1,0:T(2,128)S(1)}, s32[2,4]{1,0:T(2,128)S(1)}, u32[]{:S(2)}, u32[]{:S(2)}) collective-permute-start(s32[2,4]{1,0:T(2,128)S(1)} %pack_forks.1.refs_4_.refs_0_), channel_id=1, source_target_pairs={{0,1},{1,0},{2,3},{3,2},{4,5},{5,4},{6,7},{7,6},{8,9},{9,8},{10,11... | collective-permute-start | bytes 104 | tf_op jit(solution)/shard_map/to_forks/ppermute | solution.py:22
  20.3 9.0 %collective-permute-start.16 = (bf16[256,512]{1,0:T(8,128)(2,1)S(1)}, bf16[256,512]{1,0:T(8,128)(2,1)S(1)}, u32[]{:S(2)}, u32[]{:S(2)}) collective-permute-start(bf16[256,512]{1,0:T(8,128)(2,1)S(1)} %get-tuple-element.37), channel_id=1, source_target_pairs={{0,2},{1,3},{2,0},{3,1},{4,6},{5,7},{6,4},{7,5},{8,10},{9,11},{10,... | collective-permute-start | bytes 786440 | tf_op jit(solution)/shard_map/to_kv_ahead/ppermute | solution.py:22
  21.8 12.1 %collective-permute-start.15 = (bf16[256,512]{1,0:T(8,128)(2,1)S(1)}, bf16[256,512]{1,0:T(8,128)(2,1)S(1)}, u32[]{:S(2)}, u32[]{:S(2)}) collective-permute-start(bf16[256,512]{1,0:T(8,128)(2,1)S(1)} %get-tuple-element.34.refs_6_), channel_id=1, source_target_pairs={{0,4},{1,5},{2,6},{3,7},{4,0},{5,1},{6,2},{7,3},{8,12},{9,13},{10,... | collective-permute-start | bytes 786440 | tf_op jit(solution)/shard_map/to_kv_ahead/ppermute | solution.py:22
  24.2 11.9 %collective-permute-start.11 = (bf16[1,256,256]{2,1,0:T(8,128)(2,1)S(1)}, bf16[1,256,256]{2,1,0:T(8,128)(2,1)S(1)}, u32[]{:S(2)}, u32[]{:S(2)}) collective-permute-start(bf16[1,256,256]{2,1,0:T(8,128)(2,1)S(1)} %get-tuple-element.35.refs_2_), channel_id=1, source_target_pairs={{0,6},{1,7},{2,4},{3,5},{4,2},{5,3},{6,0},{7,1},{8,14},{9,15},{10,... | collective-permute-start | bytes 393224 | tf_op jit(solution)/shard_map/to_query/ppermute | solution.py:22
  25.8 11.9 %collective-permute-start.10 = (bf16[1,256,256]{2,1,0:T(8,128)(2,1)S(1)}, bf16[1,256,256]{2,1,0:T(8,128)(2,1)S(1)}, u32[]{:S(2)}, u32[]{:S(2)}) collective-permute-start(bf16[1,256,256]{2,1,0:T(8,128)(2,1)S(1)} %get-tuple-element.35.refs_2_), channel_id=1, source_target_pairs={{0,4},{1,5},{2,6},{3,7},{4,0},{5,1},{6,2},{7,3},{8,12},{9,13},{10,... | collective-permute-start | bytes 393224 | tf_op jit(solution)/shard_map/to_query/ppermute | solution.py:22
  26.1 12.0 %collective-permute-start.9 = (bf16[1,256,256]{2,1,0:T(8,128)(2,1)S(1)}, bf16[1,256,256]{2,1,0:T(8,128)(2,1)S(1)}, u32[]{:S(2)}, u32[]{:S(2)}) collective-permute-start(bf16[1,256,256]{2,1,0:T(8,128)(2,1)S(1)} %get-tuple-element.35.refs_2_), channel_id=1, source_target_pairs={{0,2},{1,3},{2,0},{3,1},{4,6},{5,7},{6,4},{7,5},{8,10},{9,11},{10,... | collective-permute-start | bytes 393224 | tf_op jit(solution)/shard_map/to_query/ppermute | solution.py:22
  35.5 6.3 %collective-permute-start.18 = (bf16[2,2,128,128]{3,2,1,0:T(8,128)(2,1)S(1)}, bf16[2,2,128,128]{3,2,1,0:T(8,128)(2,1)S(1)}, u32[]{:S(2)}, u32[]{:S(2)}) collective-permute-start(bf16[2,2,128,128]{3,2,1,0:T(8,128)(2,1)S(1)} %get-tuple-element.45), channel_id=1, source_target_pairs={{0,4},{1,5},{2,6},{3,7},{4,0},{5,1},{6,2},{7,3},{8,12},{9,13},{10,... | collective-permute-start | bytes 393224 | tf_op jit(solution)/shard_map/to_scan/ppermute | solution.py:22
  36.0 5.7 %collective-permute-start.17 = (bf16[2,2,128,128]{3,2,1,0:T(8,128)(2,1)S(1)}, bf16[2,2,128,128]{3,2,1,0:T(8,128)(2,1)S(1)}, u32[]{:S(2)}, u32[]{:S(2)}) collective-permute-start(bf16[2,2,128,128]{3,2,1,0:T(8,128)(2,1)S(1)} %get-tuple-element.43.refs_0_.refs_4_), channel_id=1, source_target_pairs={{0,2},{1,3},{2,0},{3,1},{4,6},{5,7},{6,4},{7,5},{8,10},{9,11},{10,... | collective-permute-start | bytes 393224 | tf_op jit(solution)/shard_map/to_scan/ppermute | solution.py:22
  36.0 8.7 %collective-permute-start.14 = (bf16[1,256,256]{2,1,0:T(8,128)(2,1)S(1)}, bf16[1,256,256]{2,1,0:T(8,128)(2,1)S(1)}, u32[]{:S(2)}, u32[]{:S(2)}) collective-permute-start(bf16[1,256,256]{2,1,0:T(8,128)(2,1)S(1)} %collective-permute-done.11.refs_5_), channel_id=1, source_target_pairs={{0,8},{8,0},{16,24},{24,16},{1,9},{9,1},{17,25},{25,17},{2,10},{10... | collective-permute-start | bytes 393224 | tf_op jit(solution)/shard_map/to_query_lane/ppermute | solution.py:22
  37.6 7.2 %collective-permute-start.13 = (bf16[1,256,256]{2,1,0:T(8,128)(2,1)S(1)}, bf16[1,256,256]{2,1,0:T(8,128)(2,1)S(1)}, u32[]{:S(2)}, u32[]{:S(2)}) collective-permute-start(bf16[1,256,256]{2,1,0:T(8,128)(2,1)S(1)} %collective-permute-done.10.refs_4_), channel_id=1, source_target_pairs={{0,8},{8,0},{16,24},{24,16},{1,9},{9,1},{17,25},{25,17},{2,10},{10... | collective-permute-start | bytes 393224 | tf_op jit(solution)/shard_map/to_query_lane/ppermute | solution.py:22
  38.1 6.7 %collective-permute-start.12 = (bf16[1,256,256]{2,1,0:T(8,128)(2,1)S(1)}, bf16[1,256,256]{2,1,0:T(8,128)(2,1)S(1)}, u32[]{:S(2)}, u32[]{:S(2)}) collective-permute-start(bf16[1,256,256]{2,1,0:T(8,128)(2,1)S(1)} %collective-permute-done.9.refs_3_), channel_id=1, source_target_pairs={{0,8},{8,0},{16,24},{24,16},{1,9},{9,1},{17,25},{25,17},{2,10},{10... | collective-permute-start | bytes 393224 | tf_op jit(solution)/shard_map/to_query_lane/ppermute | solution.py:22
  41.8 6.2 %collective-permute-start.20 = (bf16[2,2,128,128]{3,2,1,0:T(8,128)(2,1)S(1)}, bf16[2,2,128,128]{3,2,1,0:T(8,128)(2,1)S(1)}, u32[]{:S(2)}, u32[]{:S(2)}) collective-permute-start(bf16[2,2,128,128]{3,2,1,0:T(8,128)(2,1)S(1)} %get-tuple-element.47), channel_id=1, source_target_pairs={{0,2},{1,3},{2,0},{3,1},{4,6},{5,7},{6,4},{7,5},{8,10},{9,11},{10,... | collective-permute-start | bytes 393224 | tf_op jit(solution)/shard_map/to_scan/ppermute | solution.py:22
  42.5 6.3 %collective-permute-start.19 = (bf16[2,2,128,128]{3,2,1,0:T(8,128)(2,1)S(1)}, bf16[2,2,128,128]{3,2,1,0:T(8,128)(2,1)S(1)}, u32[]{:S(2)}, u32[]{:S(2)}) collective-permute-start(bf16[2,2,128,128]{3,2,1,0:T(8,128)(2,1)S(1)} %get-tuple-element.46.refs_5_), channel_id=1, source_target_pairs={{0,4},{1,5},{2,6},{3,7},{4,0},{5,1},{6,2},{7,3},{8,12},{9,13},{10,... | collective-permute-start | bytes 393224 | tf_op jit(solution)/shard_map/to_scan/ppermute | solution.py:22
  44.8 11.7 %copy-start.1 = (bf16[4,128,1024]{2,1,0:T(8,128)(2,1)S(1)}, bf16[4,128,1024]{2,1,0:T(8,128)(2,1)}, u32[]{:S(2)}) copy-start(bf16[4,128,1024]{2,1,0:T(8,128)(2,1)} %param.10) | copy-start | bytes 3145732
  49.7 12.1 %collective-permute-start.25 = (bf16[2,256,512]{2,1,0:T(8,128)(2,1)S(1)}, bf16[2,256,512]{2,1,0:T(8,128)(2,1)S(1)}, u32[]{:S(2)}, u32[]{:S(2)}) collective-permute-start(bf16[2,256,512]{2,1,0:T(8,128)(2,1)S(1)} %get-tuple-element.55.refs_0_), channel_id=1, source_target_pairs={{0,4},{1,5},{2,6},{3,7},{4,0},{5,1},{6,2},{7,3},{8,12},{9,13},{10,... | collective-permute-start | bytes 1572872 | tf_op jit(solution)/shard_map/to_out/ppermute | solution.py:22
  50.7 12.0 %collective-permute-start.24 = (bf16[2,256,512]{2,1,0:T(8,128)(2,1)S(1)}, bf16[2,256,512]{2,1,0:T(8,128)(2,1)S(1)}, u32[]{:S(2)}, u32[]{:S(2)}) collective-permute-start(bf16[2,256,512]{2,1,0:T(8,128)(2,1)S(1)} %get-tuple-element.55.refs_0_), channel_id=1, source_target_pairs={{0,2},{1,3},{2,0},{3,1},{4,6},{5,7},{6,4},{7,5},{8,10},{9,11},{10,... | collective-permute-start | bytes 1572872 | tf_op jit(solution)/shard_map/to_out/ppermute | solution.py:22
  52.1 13.4 %collective-permute-start.21 = (bf16[2,1,4,128,128]{4,3,2,1,0:T(8,128)(2,1)S(1)}, bf16[2,1,4,128,128]{4,3,2,1,0:T(8,128)(2,1)S(1)}, u32[]{:S(2)}, u32[]{:S(2)}) collective-permute-start(bf16[2,1,4,128,128]{4,3,2,1,0:T(8,128)(2,1)S(1)} %get-tuple-element.52), channel_id=1, source_target_pairs={{0,8},{8,0},{16,24},{24,16},{1,9},{9,1},{17,25},{25,17},{2,10},{10... | collective-permute-start | bytes 786440 | tf_op jit(solution)/shard_map/to_lane/ppermute | solution.py:22
  53.7 14.0 %collective-permute-start.22 = (bf16[2,1,4,128,128]{4,3,2,1,0:T(8,128)(2,1)S(1)}, bf16[2,1,4,128,128]{4,3,2,1,0:T(8,128)(2,1)S(1)}, u32[]{:S(2)}, u32[]{:S(2)}) collective-permute-start(bf16[2,1,4,128,128]{4,3,2,1,0:T(8,128)(2,1)S(1)} %get-tuple-element.53), channel_id=1, source_target_pairs={{0,16},{8,24},{16,0},{24,8},{1,17},{9,25},{17,1},{25,9},{2,18},{10... | collective-permute-start | bytes 786440 | tf_op jit(solution)/shard_map/to_lane/ppermute | solution.py:22
  56.3 11.5 %collective-permute-start.23 = (bf16[2,1,4,128,128]{4,3,2,1,0:T(8,128)(2,1)S(1)}, bf16[2,1,4,128,128]{4,3,2,1,0:T(8,128)(2,1)S(1)}, u32[]{:S(2)}, u32[]{:S(2)}) collective-permute-start(bf16[2,1,4,128,128]{4,3,2,1,0:T(8,128)(2,1)S(1)} %get-tuple-element.54), channel_id=1, source_target_pairs={{0,24},{8,16},{16,8},{24,0},{1,25},{9,17},{17,9},{25,1},{2,26},{10... | collective-permute-start | bytes 786440 | tf_op jit(solution)/shard_map/to_lane/ppermute | solution.py:22
  62.7 6.4 %collective-permute-start.29 = (bf16[256,512]{1,0:T(8,128)(2,1)S(1)}, bf16[256,512]{1,0:T(8,128)(2,1)S(1)}, u32[]{:S(2)}, u32[]{:S(2)}) collective-permute-start(bf16[256,512]{1,0:T(8,128)(2,1)S(1)} %get-tuple-element.59), channel_id=1, source_target_pairs={{0,2},{1,3},{2,0},{3,1},{4,6},{5,7},{6,4},{7,5},{8,10},{9,11},{10,... | collective-permute-start | bytes 786440 | tf_op jit(solution)/shard_map/to_out_ahead/ppermute | solution.py:22
  64.2 6.4 %collective-permute-start.28 = (bf16[256,512]{1,0:T(8,128)(2,1)S(1)}, bf16[256,512]{1,0:T(8,128)(2,1)S(1)}, u32[]{:S(2)}, u32[]{:S(2)}) collective-permute-start(bf16[256,512]{1,0:T(8,128)(2,1)S(1)} %get-tuple-element.56.refs_6_), channel_id=1, source_target_pairs={{0,4},{1,5},{2,6},{3,7},{4,0},{5,1},{6,2},{7,3},{8,12},{9,13},{10,... | collective-permute-start | bytes 786440 | tf_op jit(solution)/shard_map/to_out_ahead/ppermute | solution.py:22
  68.5 3.1 %collective-permute-start.26 = (bf16[4,128,256]{2,1,0:T(8,128)(2,1)S(1)}, bf16[4,128,256]{2,1,0:T(8,128)(2,1)S(1)}, u32[]{:S(2)}, u32[]{:S(2)}) collective-permute-start(bf16[4,128,256]{2,1,0:T(8,128)(2,1)S(1)} %get-tuple-element.57), channel_id=1, source_target_pairs={{0,1},{1,0},{2,3},{3,2},{4,5},{5,4},{6,7},{7,6},{8,9},{9,8},{10,11... | collective-permute-start | bytes 786440 | tf_op jit(solution)/shard_map/to_normed/ppermute | solution.py:22
  68.6 3.0 %collective-permute-start.27 = (bf16[4,128,256]{2,1,0:T(8,128)(2,1)S(1)}, bf16[4,128,256]{2,1,0:T(8,128)(2,1)S(1)}, u32[]{:S(2)}, u32[]{:S(2)}) collective-permute-start(bf16[4,128,256]{2,1,0:T(8,128)(2,1)S(1)} %get-tuple-element.58), channel_id=1, source_target_pairs={{0,1},{1,0},{2,3},{3,2},{4,5},{5,4},{6,7},{7,6},{8,9},{9,8},{10,11... | collective-permute-start | bytes 786440 | tf_op jit(solution)/shard_map/to_normed/ppermute | solution.py:22
  70.9 0.8 %copy-start.6 = (s32[4]{0:T(128)S(1)}, s32[4]{0:T(128)}, u32[]{:S(2)}) copy-start(s32[4]{0:T(128)} %refs_0_.13) | copy-start | bytes 52

commit v4 on v3

v4 whole, which is shorter than its diff:
```python
import functools

import jax
import jax.numpy as jnp
from jax import lax
from jax.experimental import pallas as pl
from jax.experimental.pallas import tpu as pltpu
from jax.sharding import PartitionSpec as P

H = 8
DH = 128
F32 = jnp.float32
BF16 = jnp.bfloat16
VMEM_BYTES = 16 * 1024 * 1024
ANY = pl.BlockSpec(memory_space=pl.ANY)
VMEM = pl.BlockSpec(memory_space=pltpu.VMEM)
SMEM = pl.BlockSpec(memory_space=pltpu.SMEM)


def swap(value, axis, bit, name="rows"):
    with jax.named_scope("to_" + name):
        return lax.ppermute(value, axis, [(i, i ^ bit) for i in range(lax.axis_size(axis))])


def turn(value, step, bits, name):
    bit = lambda i: bits[0] if (i % 2 == 1) == (step == 1) else bits[1]
    with jax.named_scope("to_" + name):
        count = lax.axis_size("trunk")
        return lax.ppermute(value, "trunk", [(i, i ^ bit(i)) for i in range(count)])


def dot(left, right):
    return jnp.dot(left, right, preferred_element_type=F32)


def shape_of(shape, dtype=BF16):
    return jax.ShapeDtypeStruct(tuple(shape), dtype)


def call(kernel, name, outs, inputs, specs, out_specs=None, scratch=(), order=None, through=(), landed=(), weight=0.0):
    after = (*(order or ()), *landed)
    n, t, w, m = len(inputs), len(through), len(after), len(outs)

    def body(*refs):
        kernel(*refs[:n], *refs[n + t + w : n + t + w + m], *refs[n + 2 * t + w + m :])

    results = pl.pallas_call(
        body,
        out_shape=[*outs, *(shape_of(a.shape, a.dtype) for a in through)],
        in_specs=[*specs, *[ANY] * (t + w)],
        out_specs=[*(out_specs or [VMEM] * m), *[ANY] * t],
        scratch_shapes=list(scratch),
        input_output_aliases={n + i: m + i for i in range(t)},
        compiler_params=pltpu.CompilerParams(vmem_limit_bytes=VMEM_BYTES),
        cost_estimate=pl.CostEstimate(
            flops=int(weight * 1e9), bytes_accessed=0, transcendentals=0
        ),
        name=name,
    )(*inputs, *through, *after)
    if order is not None:
        order[:] = [results[0]]
    return results


def core_index():
    return lax.axis_index("trunk") % 2


def chip_index():
    return lax.axis_index("trunk") // 2


def touch_kernel(*refs):
    refs[-1][...] = jnp.zeros_like(refs[-1])


def touch(arrays, **rest):
    return call(touch_kernel, "touch", [shape_of((8, DH), F32)], arrays, [ANY] * len(arrays), **rest)


def halves_kernel(count, chosen, *refs):
    core, odd = core_index(), lax.axis_index("leaf") % 2
    mine, other, outs, sem = refs[:count], refs[count : 2 * count], refs[2 * count : -1], refs[-1]
    copies = []
    for out, (parts, picks) in zip(outs, chosen):
        for slot, (i, p, own) in enumerate(picks):
            rows, width = other[i].shape
            part = width // 2 // parts
            p = {"even": odd, "odd": 1 - odd}.get(p, p)
            first = (core if own else 1 - core) * (width // 2) + p * part
            columns = pl.ds(pl.multiple_of(first, part), part)
            for source, place in ((mine[i], core), (other[i], 1 - core)):
                target = out.at[slot, pl.ds(pl.multiple_of(place * rows, rows), rows)]
                part_of = source if source.shape[1] == part else source.at[:, columns]
                copies.append(pltpu.make_async_copy(part_of, target, sem.at[len(copies)]))
    for copy in copies:
        copy.start()
    for copy in copies:
        copy.wait()


def chip_halves(mine, other, chosen, **rest):
    rows, width = other[0].shape
    return call(
        functools.partial(halves_kernel, len(mine), chosen),
        "chip_halves",
        [shape_of((len(picks), 2 * rows, width // 2 // parts)) for parts, picks in chosen],
        [*mine, *other],
        [ANY] * (2 * len(mine)),
        scratch=[pltpu.SemaphoreType.DMA((sum(2 * len(picks) for _, picks in chosen),))],
        **rest,
    )


def send_near(pair, bits, name):
    return [pair, *(turn(pair, step, bits, name) for step in (1, 2))]


def send_far(near, held, bits, name):
    arrays = [*near, turn(held, 2, bits, name + "_far")]
    return arrays, [[(i, (slot,), i) for i in range(4)] for slot in range(near[0].shape[0])]


def lane_pieces(near, far, other, across):
    arrays = [*near, far, other, *across]
    return arrays, [[(4 * i + k, (0,), k) for k in range(4)] for i in range(2)]


def whole_pair(weights, parts, chosen):
    arrays = []
    for i, p in chosen:
        full = lax.all_gather(weights[i], "trunk", axis=0, tiled=True)
        part = full.shape[1] // 2 // parts
        start = core_index() * (full.shape[1] // 2) + p * part
        arrays.append(lax.dynamic_slice_in_dim(full, start, part, axis=1))
    return arrays, [[(i, (), None)] for i in range(len(arrays))]


def chip_after(steps):
    first = jnp.where(core_index() == 1, 1, 2)
    return chip_index() ^ (0, first, 3 - first, 3)[steps]


def project(x_ref, lead, picks, refs):
    total = None
    for number, index, steps in picks:
        weight = refs[number][index] if index else refs[number][...]
        depth = weight.shape[0]
        if steps is None:
            left = x_ref[lead]
        else:
            left = x_ref[lead, :, pl.ds(pl.multiple_of(chip_after(steps) * depth, depth), depth)]
        term = dot(left, weight)
        total = term if total is None else total + term
    return total


def pack_kernel(offset_ref, tree_ref, out_ref):
    out_ref[0:1] = offset_ref[0]
    out_ref[1:2] = tree_ref[0]


def pack_forks(offset, tree, **rest):
    return call(
        pack_kernel,
        "pack_forks",
        [shape_of((2, offset.shape[2]), jnp.int32)],
        [offset, tree],
        [VMEM] * 2,
        **rest,
    )[0]


def partial_kernel(picks, *refs):
    xs, weights, outs = refs[:2], refs[2:-2], refs[-2:]
    for side in range(2):
        for tree in range(xs[0].shape[0]):
            for part, out in zip(picks, outs):
                out[side, tree] = project(xs[side], tree, part, weights)


def trunk_partial(mine, other, weights, **rest):
    trees, tok, _ = mine.shape
    arrays, picks = weights
    return call(
        functools.partial(partial_kernel, picks),
        "trunk_partial",
        [shape_of((2, trees, tok, arrays[0].shape[-1]), F32)] * 2,
        [mine, other, *arrays],
        [VMEM] * (2 + len(arrays)),
        **rest,
    )


def trunk_kernel(picks, mask, count, parts, *refs):
    xs, earlier, weights = refs[:2], refs[2 : 2 + count], refs[2 + count : -3 - 2 * parts]
    totals, firsts = refs[-3 - 2 * parts : -3 - parts], refs[-3 - parts : -3]
    keys_ref, values_ref, state_ref = refs[-3:]
    sent = (core_index() == 1) | ((lax.axis_index("trunk") & mask) == 0)
    trees, heads = state_ref.shape[1:3]
    for side in range(2):
        for tree in range(trees):
            keys, values = (project(xs[side], tree, part, weights) for part in picks)
            if earlier:
                keys, values = keys + earlier[0][side, tree], values + earlier[1][side, tree]
            keys, values = keys.astype(BF16), values.astype(BF16)
            keys_ref[side, tree] = keys
            values_ref[side, tree] = values
            for h in range(heads):
                at = slice(h * DH, (h + 1) * DH)
                state = lax.dot_general(
                    keys[:, at], values[:, at], (((0,), (0,)), ((), ())), preferred_element_type=F32
                )
                state_ref[side, tree, h] = state
                if side:
                    total = (state_ref[0, tree, h] + state).astype(BF16)
                    part, place = divmod(h, heads // parts)
                    totals[part][tree, place] = total
                    firsts[part][tree, place] = jnp.where(sent, total, jnp.zeros_like(total))


def trunk_states(mine, other, weights, mask, parts, earlier=(), **rest):
    trees, tok, width = mine.shape
    arrays, picks = weights
    cols = arrays[0].shape[-1]
    heads = cols // DH
    parts = parts if heads % parts == 0 else 1
    out = call(
        functools.partial(trunk_kernel, picks, mask, len(earlier), parts),
        "trunk_states",
        [
            *[shape_of((trees, heads // parts, DH, DH))] * (2 * parts),
            shape_of((2, trees, tok, cols)),
            shape_of((2, trees, tok, cols)),
            shape_of((2, trees, heads, DH, DH), F32),
        ],
        [mine, other, *earlier, *arrays],
        [VMEM] * (2 + len(earlier) + len(arrays)),
        **rest,
    )
    return out[:parts], out[parts : 2 * parts], out[2 * parts :]


def part_kernel(mine_ref, other_ref, keys_ref, values_ref, state_ref, fork_ref):
    core = core_index()
    tok = keys_ref.shape[2]
    entries, heads = fork_ref.shape[1:3]
    place = lax.broadcasted_iota(jnp.int32, (tok, DH), 0)
    for side in range(2):
        ints = other_ref if side else mine_ref
        for e in range(entries):
            tree = ints[1, e]
            inside = place < ints[0, e]
            odd = core != side
            for h in range(heads):
                at = slice(h * DH, (h + 1) * DH)
                keys = keys_ref[side, tree, :, at]
                part = lax.dot_general(
                    jnp.where(inside, keys, jnp.zeros_like(keys)),
                    values_ref[side, tree, :, at],
                    (((0,), (0,)), ((), ())),
                    preferred_element_type=F32,
                )
                lower = state_ref[1 - side, tree, h]
                fork_ref[side, e, h] = part + jnp.where(odd, lower, jnp.zeros_like(lower))


def fork_parts(forks, keys, values, states, **rest):
    _, _, tok, cols = keys.shape
    entries, heads = forks[0].shape[1], cols // DH
    return call(
        part_kernel,
        "fork_parts",
        [shape_of((2, entries, heads, DH, DH), F32)],
        [*forks, keys, values, states],
        [SMEM] * 2 + [VMEM] * 3,
        **rest,
    )


def scan_kernel(mask, count, *refs):
    adds = (core_index() == 1) | ((lax.axis_index("trunk") & mask) == 0)
    for held_ref, in_ref, out_ref in zip(refs[:count], refs[count : 2 * count], refs[2 * count :]):
        held = held_ref[...].astype(F32)
        if mask:
            held = jnp.where(adds, held, jnp.zeros_like(held))
        out_ref[...] = (held + in_ref[...].astype(F32)).astype(BF16)


def scan_step(held, received, mask, **rest):
    return call(
        functools.partial(scan_kernel, mask, len(held)),
        "scan_step",
        [shape_of(h.shape) for h in held],
        [*held, *received],
        [VMEM] * (2 * len(held)),
        **rest,
    )


def fork_kernel(masks, both, lanes, parts, *refs):
    count = len(masks) * parts
    ints, fork_ref, terms = refs[:2], refs[2], refs[3 : 3 + count]
    outs, carried_ref = refs[-1 - lanes : -1], refs[-1]
    index, lane = lax.axis_index("trunk"), lax.axis_index("leaf")
    cap = outs[0].shape[1]
    heads = terms[0].shape[1]
    for part in range(parts):
        carried = None
        for mask, ref in zip(masks, terms[part::parts]):
            term = ref[...].astype(F32)
            counts = (index & mask) != 0
            if both:
                counts = counts | (core_index() == 0)
            term = jnp.where(counts, term, jnp.zeros_like(term))
            carried = term if carried is None else carried + term
        carried_ref[:, part * heads : (part + 1) * heads] = carried
    for apart in range(lanes):
        for side in range(2):
            for c in range(cap):
                entry = (lane ^ apart) * cap + c
                state = fork_ref[side, entry] + carried_ref[ints[side][1, entry]]
                outs[apart][side, c] = state.astype(BF16)


def fork_states(forks, parts, terms, masks, both, lanes, **rest):
    _, entries, heads = parts.shape[:3]
    shape = (2, entries // lanes, heads, DH, DH)
    return call(
        functools.partial(fork_kernel, masks, both, lanes, len(terms[0])),
        "fork_states",
        [shape_of(shape)] * lanes,
        [*forks, parts, *(t for term in terms for t in term)],
        [SMEM] * 2 + [VMEM] * (1 + len(terms) * len(terms[0])),
        scratch=[pltpu.VMEM((terms[0][0].shape[0], heads, DH, DH), F32)],
        **rest,
    )


def branch_kernel(counts, picks, by_lane, blen, *refs):
    odd = lax.axis_index("leaf") % 2
    xs, q_out, intra_out = refs[:2], *refs[-2:]
    query_refs, weights = refs[2 : 2 + counts[0]], refs[2 + counts[0] : -2]
    rows = xs[0].shape[1]
    row = lax.broadcasted_iota(jnp.int32, (rows, rows), 0)
    column = lax.broadcasted_iota(jnp.int32, (rows, rows), 1)
    seen = (column <= row) & (column >= row - lax.rem(row, blen))
    for side in range(2):
        for slot in range(xs[0].shape[0]):
            for i, part in enumerate(picks[0]):
                q = project(xs[side], slot, part, query_refs).astype(BF16)
                place = (odd if i == 0 else 1 - odd) if by_lane else i
                first = pl.multiple_of(place * q.shape[1], q.shape[1])
                q_out[side, slot, :, pl.ds(first, q.shape[1])] = q
            k, v = (project(xs[side], slot, part, weights).astype(BF16) for part in picks[1])
            for h in range(k.shape[1] // DH):
                at = slice(h * DH, (h + 1) * DH)
                scores = lax.dot_general(
                    q_out[side, slot, :, at],
                    k[:, at],
                    (((1,), (1,)), ((), ())),
                    preferred_element_type=F32,
                )
                scores = jnp.where(seen, scores, 0.0).astype(BF16)
                intra_out[side, slot, :, at] = dot(scores, v[:, at])


def branch_parts(mine, other, queries, pair, by_lane, **rest):
    slots, blen, width = mine.shape
    join = 2 if slots % 2 == 0 else 1
    mine, other = (a.reshape(slots // join, join * blen, width) for a in (mine, other))
    weights = [queries, pair]
    arrays = [a for held, _ in weights for a in held]
    cols = pair[0][0].shape[-1]
    lead = (2, slots // join, join * blen, cols)
    outs = call(
        functools.partial(
            branch_kernel, [len(held) for held, _ in weights], [p for _, p in weights], by_lane, blen
        ),
        "branch_parts",
        [shape_of(lead), shape_of(lead, F32)],
        [mine, other, *arrays],
        [VMEM] * (2 + len(arrays)),
        **rest,
    )
    return [o.reshape(2, slots, blen, cols) for o in outs]


def norm_kernel(aparts, q_ref, intra_ref, *refs):
    states, outs = refs[: len(aparts)], refs[len(aparts) :]
    lane = lax.axis_index("leaf")
    cap, heads = states[0].shape[1:3]
    for number, apart in enumerate(aparts):
        for side in range(2):
            for c in range(cap):
                slot = (lane ^ apart) * cap + c
                for h in range(heads):
                    at = slice(h * DH, (h + 1) * DH)
                    total = intra_ref[side, slot, :, at] + dot(
                        q_ref[side, slot, :, at], states[number][side, c, h]
                    )
                    meansq = jnp.mean(total * total, axis=-1, keepdims=True)
                    normed = (total * lax.rsqrt(meansq + 1e-06)).astype(BF16)
                    outs[side][number * cap + c, :, at] = normed


def norm_parts(queries, intra, states, aparts, **rest):
    _, _, blen, cols = queries.shape
    count = len(aparts) * states[0].shape[1]
    return call(
        functools.partial(norm_kernel, aparts),
        "norm_parts",
        [shape_of((count, blen, cols))] * 2,
        [queries, intra, *(states[a] for a in aparts)],
        [VMEM] * (2 + len(aparts)),
        **rest,
    )


def place_kernel(picks, *refs):
    core = core_index()
    sources, out_ref, sem = refs[:-2], refs[-2], refs[-1]
    copies = []
    for slot, number, index, steps in picks:
        source = sources[number].at[index] if index else sources[number]
        rows, half = source.shape
        first = (core if slot == 0 else 1 - core) * half
        target = out_ref.at[
            pl.ds(pl.multiple_of(chip_after(steps) * rows, rows), rows),
            pl.ds(pl.multiple_of(first, half), half),
        ]
        copies.append(pltpu.make_async_copy(source, target, sem.at[len(copies)]))
    for copy in copies:
        copy.start()
    for copy in copies:
        copy.wait()


def place_rows(weights, shape, **rest):
    arrays, picks = weights
    chosen = [(slot, *pick) for slot, part in enumerate(picks) for pick in part]
    return call(
        functools.partial(place_kernel, chosen),
        "place_rows",
        [shape_of(shape)],
        arrays,
        [ANY] * len(arrays),
        scratch=[pltpu.SemaphoreType.DMA((len(chosen),))],
        **rest,
    )[0]


def rows_of(w_ref, first, core, count):
    half = w_ref.shape[0] // 2
    return w_ref[pl.ds(pl.multiple_of(core * half + first, count), count), :]


def out_sum_kernel(*refs):
    inputs, w_ref, out_ref = refs[:-2], refs[-2], refs[-1]
    weight = rows_of(w_ref, 0, core_index(), inputs[0].shape[2])
    first = 0
    for ref in inputs:
        slots, blen, cols = ref.shape
        out_ref[first : first + slots * blen] = dot(ref[...].reshape(slots * blen, cols), weight)
        first += slots * blen


def out_sum(normed, weights, **rest):
    rows = sum(n.shape[0] * n.shape[1] for n in normed)
    return call(
        out_sum_kernel,
        "out_sum",
        [shape_of((rows, weights.shape[1]), F32)],
        [*normed, weights],
        [VMEM] * (len(normed) + 1),
        **rest,
    )[0]


def out_last_kernel(aparts, cap, len_ref, *refs):
    inputs, (w_ref, total_ref, out_ref, held_ref, sem) = refs[:-5], refs[-5:]
    weight = rows_of(w_ref, 0, 1 - core_index(), inputs[0].shape[2])
    lane = lax.axis_index("leaf")
    blen = inputs[0].shape[1]
    row = lax.broadcasted_iota(jnp.int32, (blen, w_ref.shape[1]), 0)
    copies, place = [], 0
    for ref in inputs:
        count = ref.shape[0]
        rows = slice(place * blen, (place + count) * blen)
        total = total_ref[rows] + dot(ref[...].reshape(count * blen, ref.shape[2]), weight)
        for i in range(count):
            slot = (lane ^ aparts[place // cap]) * cap + place % cap
            part = total[i * blen : (i + 1) * blen]
            held_ref[place] = jnp.where(row < len_ref[slot], part, 0.0).astype(BF16)
            copies.append(pltpu.make_async_copy(held_ref.at[place], out_ref.at[slot], sem.at[place]))
            copies[-1].start()
            place += 1
    for copy in copies:
        copy.wait()


def out_last(lengths, normed, aparts, weights, total, **rest):
    slots, blen = lengths.shape[0], normed[0].shape[1]
    shape = (slots, blen, weights.shape[1])
    return call(
        functools.partial(out_last_kernel, aparts, slots // len(aparts)),
        "out_last",
        [shape_of(shape)],
        [lengths, *normed, weights, total],
        [SMEM] + [VMEM] * (2 + len(normed)),
        [ANY],
        scratch=[pltpu.VMEM(shape, BF16), pltpu.SemaphoreType.DMA((slots,))],
        **rest,
    )[0]


def shards(
    trunk_tokens, branch_tokens, fork_offset, fork_tree, branch_len, w_query, w_key, w_value, w_out
):
    lanes, count = lax.axis_size("leaf"), lax.axis_size("trunk")
    bits = [1 << i for i in range(1, count.bit_length() - 1)]
    paired = len(bits) == 2 and lanes % 2 == 0 and (2 * w_key.shape[0]) % DH == 0
    order = []
    chain = functools.partial(touch, order=order)

    if paired:
        kv, qo = [w_key, w_value], [w_query, w_out]
        kv_other = [swap(w, "trunk", 1, "core") for w in kv]
        half = w_key.shape[1] // 2
        kv = [lax.dynamic_slice_in_dim(w, core_index() * half, half, axis=1) for w in kv]
        chain(kv)
        chosen = [(1, [(0, 0, True), (1, 0, True)])]
        (own_kv,) = chip_halves(kv, kv_other, chosen, order=order, weight=40.0)
        near = send_near(own_kv, bits, "kv")
        qo_other = [swap(w, "trunk", 1, "core") for w in qo]
    own_forks = pack_forks(fork_offset, fork_tree, order=order)
    forks = (own_forks, swap(own_forks, "trunk", 1, "forks"))
    trunk_other = swap(trunk_tokens, "trunk", 1, "tokens")
    branch_other = swap(branch_tokens, "trunk", 1, "tokens")
    trunk = trunk_tokens, trunk_other
    if paired:
        chosen = [
            (2, [(0, "even", True)]),
            (2, [(0, "odd", True)]),
            (1, [(1, 0, True), (1, 0, False)]),
            (1, [(1, 0, True), (1, 0, False)]),
        ]
        own_q, other_q, own_o, again_o = chip_halves(qo, qo_other, chosen, order=order, landed=[forks[1]])
        _, near[1] = chain([], through=[near[1]])
        arrays, picks = pair = send_far(near, near[1], bits, "kv")
        at_hand = arrays[:3], [part[:3] for part in picks]
        earlier = trunk_partial(*trunk, at_hand, order=order, landed=[branch_other])
        _, own_q = chain(arrays[3:], through=[own_q])
        near_q = send_near(own_q, bits, "query")
        last = arrays[3:], [[(0, i, steps) for _, i, steps in part[3:]] for part in picks]
    else:
        pair = whole_pair([w_key, w_value], 1, [(0, 0), (1, 0)])
        queries = whole_pair([w_query], 2, [(0, 0), (0, 1)])
        out_full = lax.all_gather(w_out, "trunk", axis=0, tiled=True)
        earlier, last = (), pair

    def scan_round(held, number):
        if paired:
            return [turn(h, 1 + number, bits, "scan") for h in held]
        return [swap(h, "trunk", bits[number]) for h in held]

    mask = bits[1] if paired else 0
    held, first, kept = trunk_states(*trunk, last, mask, 1, earlier, order=order)
    terms = [scan_round(first, 0)]
    if paired:
        _, near_q[1] = chain(near_q[2:], through=[near_q[1]], weight=5.0)
        far_q = turn(near_q[1], 2, bits, "query_far")
        across = [swap(a, "leaf", 1, "query_lane") for a in near_q[1:]]
    for number in range(1, len(bits)):
        held = scan_step(held, terms[-1], bits[0] if paired else 0, order=order)
        terms.append(scan_round(held, number))
    if paired:
        _, far_q = chain([], through=[far_q])
        last_q = swap(far_q, "leaf", 1, "query_lane")
        queries = lane_pieces(near_q, far_q, other_q, [*across, last_q])
    (parts,) = fork_parts(forks, *kept, order=order)
    if paired:
        chain(across, weight=6.0)
    sends = fork_states(
        forks, parts, terms, bits, paired, lanes, order=order, through=[own_o] if paired else []
    )
    far = sorted(range(1, lanes), key=lambda a: a == 1)
    moved = {a: swap(sends[a], "leaf", a, "lane") for a in far}
    received = [sends[0]] + [moved[a] for a in range(1, lanes)]
    if paired:
        held_o = turn(sends[lanes], 1, bits, "out")
        _, again_o = chain([last_q], through=[again_o])
        near_o = [again_o, held_o, turn(again_o, 2, bits, "out")]
    q, intra = branch_parts(
        branch_tokens, branch_other, queries, pair, paired, order=order, weight=20.0
    )
    if paired:
        _, near_o[1] = chain([], through=[held_o])
        outs = send_far(near_o, near_o[1], bits, "out")
    aparts = list(range(lanes))
    split = [aparts[:-1], aparts[-1:]] if lanes > 1 else [aparts]
    mine, other = [], []
    for part in split:
        if mine and paired:
            chain(near_o[2:3], weight=1.0)
        own, theirs = norm_parts(q, intra, received, part, order=order, weight=4.0 if mine else 0.5)
        mine.append(own)
        other.append(swap(theirs, "trunk", 1, "normed"))
    if paired:
        chain(other[:1])
        out_full = place_rows(
            outs, (w_out.shape[0] * count, w_out.shape[1]), order=order, weight=8.0
        )
    total = out_sum(mine, out_full, order=order)
    return out_last(branch_len, other, aparts, out_full, total, order=order)


def solution(mesh):
    in_specs = (
        P("leaf", "trunk", None),
        P(("leaf", "trunk"), None, None),
        P("leaf", "trunk", None),
        P("leaf", "trunk", None),
        P(("leaf", "trunk")),
        P("trunk", None),
        P("trunk", None),
        P("trunk", None),
        P("trunk", None),
    )
    out_specs = P(("leaf", "trunk"), None, None)
    return jax.shard_map(shards, mesh=mesh, in_specs=in_specs, out_specs=out_specs, check_vma=False)
```

time: 73.9 us -> 73.3 us (level)
  starting transfers between devices: 27.2 us -> 25.6 us
  waiting for transfers between devices: 29.6 us -> 30.7 us
  local copies, waits for them, and re-layouts: 1.94 us -> 1.03 us
  Pallas kernels: 14.7 us -> 15.5 us
    ppermute x0 -> x11, waiting for transfers between devices: none -> 21.7 us  [turn(): return lax.ppermute(value, 'trunk', [(i, i ^ bit(i)) for i in range(count)])]
    ppermute x30 -> x15, waiting for transfers between devices: 29.6 us -> 9.07 us  [swap(): lax.ppermute(value, axis, [(i, i ^ bit) for i in range(lax.axis_size(axis...]
    ppermute x30 -> x15, starting transfers between devices: 27.2 us -> 10.3 us  [swap(): lax.ppermute(value, axis, [(i, i ^ bit) for i in range(lax.axis_size(axis...]
    ppermute x0 -> x11, starting transfers between devices: none -> 15.3 us  [turn(): return lax.ppermute(value, 'trunk', [(i, i ^ bit(i)) for i in range(count)])]
    unnamed x18 -> x14, local copies, waits for them, and re-layouts: 1.94 us -> 0.04 us
    dynamic_slice x0 -> x1, local copies, waits for them, and re-layouts: none -> 0.98 us  [shards(): lax.dynamic_slice_in_dim(w, core_index() * half, half, axis=1)]
    pallas_call x17 -> x24, Pallas kernels: 14.7 us -> 15.5 us  [call(): pl.pallas_call(body, out_shape=[*outs, *(shape_of(a.shape, a.dtype) for a...]
  transfers between devices with their start and end apart: 30 -> 26, of which waited for: 14 -> 15; matrix products, arithmetic and copies ran while one was open for 0% -> 1% of each run, Pallas kernels for 16% -> 18%
where the time goes in v4:
time: 73.3 us; the launch traced here: 73.1 us
  waiting for transfers between devices  30.7 us (42%)
  starting transfers between devices  25.6 us (35%)
  Pallas kernels  15.5 us (21%)
  local copies, waits for them, and re-layouts  1.03 us (1%)
    ppermute x11, waiting for transfers between devices, turn(): return lax.ppermute(value, 'trunk', [(i, i ^ bit(i)) for i in range(count)])  21.7 us
    pallas_call x24, Pallas kernels, call(): pl.pallas_call(body, out_shape=[*outs, *(shape_of(a.shape, a.dtype) for a...  15.5 us
    ppermute x11, starting transfers between devices, turn(): return lax.ppermute(value, 'trunk', [(i, i ^ bit(i)) for i in range(count)])  15.3 us
    ppermute x15, starting transfers between devices, swap(): lax.ppermute(value, axis, [(i, i ^ bit) for i in range(lax.axis_size(axis...  10.3 us
    ppermute x15, waiting for transfers between devices, swap(): lax.ppermute(value, axis, [(i, i ^ bit) for i in range(lax.axis_size(axis...  9.07 us
  transfers between devices with their start and end apart: 26, of which 15 were waited for; matrix products, arithmetic and copies ran while one was open for 1% of the time, Pallas kernels for 18%

profile of v4, /device:TPU:0, one launch (start us, length us, event | category | flops | bytes accessed | tf_op | source)
XLA Modules:
  0.0 73.1 jit_solution(5691653749849039225)
XLA Ops:
  0.0 0.5 collective-permute-start.1
  0.5 0.5 collective-permute-start
  1.0 1.0 %constant_dynamic-slice_fusion = (bf16[128,512]{1,0:T(8,128)(2,1)S(1)}, bf16[128,512]{1,0:T(8,128)(2,1)S(1)}) fusion(bf16[128,1024]{1,0:T(8,128)(2,1)} %param.16, s32[]{:T(128)S(6)} %select_n.14, bf16[128,1024]{1,0:T(8,128)(2,1)} %param.15), kind=kLoop, calls=%fused_computation | loop fusion | bytes 524292 | tf_op jit(solution)/shard_map/dynamic_slice | solution.py:530
  2.0 0.2 collective-permute-done.2.refs_3_
  2.2 0.4 chip_halves.2.refs_2_.refs_10_
  2.6 3.0 %collective-permute-start.3 = (bf16[2,256,512]{2,1,0:T(8,128)(2,1)S(1)}, bf16[2,256,512]{2,1,0:T(8,128)(2,1)S(1)}, u32[]{:S(2)}, u32[]{:S(2)}) collective-permute-start(bf16[2,256,512]{2,1,0:T(8,128)(2,1)S(1)} %chip_halves.2.refs_2_.refs_10_), channel_id=1, source_target_pairs={{0,4},{1,3},{2,6},{3,1},{4,0},{5,7},{6,2},{7,5},{8,12},{9,11},{10,... | collective-permute-start | bytes 1572872 | tf_op jit(solution)/shard_map/to_kv/ppermute | solution.py:29
  5.6 0.5 collective-permute-start.4
  6.2 2.4 %collective-permute-done.4.refs_2_ = bf16[128,1024]{1,0:T(8,128)(2,1)S(1)} collective-permute-done((bf16[128,1024]{1,0:T(8,128)(2,1)S(1)}, bf16[128,1024]{1,0:T(8,128)(2,1)S(1)}, u32[]{:S(2)}, u32[]{:S(2)}) %collective-permute-start.4) | collective-permute-done | bytes 262176 | tf_op jit(solution)/shard_map/to_core/ppermute | solution.py:22
  8.6 1.5 %collective-permute-start.9 = (bf16[2,256,512]{2,1,0:T(8,128)(2,1)S(1)}, bf16[2,256,512]{2,1,0:T(8,128)(2,1)S(1)}, u32[]{:S(2)}, u32[]{:S(2)}) collective-permute-start(bf16[2,256,512]{2,1,0:T(8,128)(2,1)S(1)} %chip_halves.2.refs_2_.refs_10_), channel_id=1, source_target_pairs={{0,2},{1,5},{2,0},{3,7},{4,6},{5,1},{6,4},{7,3},{8,10},{9,13},{10,... | collective-permute-start | bytes 1572872 | tf_op jit(solution)/shard_map/to_kv/ppermute | solution.py:29
  10.1 1.1 %collective-permute-done.6.refs_5_.refs_1_ = s32[2,4]{1,0:T(2,128)S(1)} collective-permute-done((s32[2,4]{1,0:T(2,128)S(1)}, s32[2,4]{1,0:T(2,128)S(1)}, u32[]{:S(2)}, u32[]{:S(2)}) %collective-permute-start.6) | collective-permute-done | bytes 64 | tf_op jit(solution)/shard_map/to_forks/ppermute | solution.py:22
  11.2 0.3 chip_halves.3
  11.6 2.8 %collective-permute-done.3.refs_0_ = bf16[2,256,512]{2,1,0:T(8,128)(2,1)S(1)} collective-permute-done((bf16[2,256,512]{2,1,0:T(8,128)(2,1)S(1)}, bf16[2,256,512]{2,1,0:T(8,128)(2,1)S(1)}, u32[]{:S(2)}, u32[]{:S(2)}) %collective-permute-start.3) | collective-permute-done | bytes 524320 | tf_op jit(solution)/shard_map/to_kv/ppermute | solution.py:29
  14.4 2.2 %collective-permute-start.7 = (bf16[2,256,512]{2,1,0:T(8,128)(2,1)S(1)}, bf16[2,256,512]{2,1,0:T(8,128)(2,1)S(1)}, u32[]{:S(2)}, u32[]{:S(2)}) collective-permute-start(bf16[2,256,512]{2,1,0:T(8,128)(2,1)S(1)} %get-tuple-element.40.refs_3_.refs_11_), channel_id=1, source_target_pairs={{0,2},{1,5},{2,0},{3,7},{4,6},{5,1},{6,4},{7,3},{8,10},{9,13},{10,... | collective-permute-start | bytes 1572872 | tf_op jit(solution)/shard_map/to_kv_far/ppermute | solution.py:29
  16.6 1.2 %collective-permute-done.9.refs_4_.refs_12_ = bf16[2,256,512]{2,1,0:T(8,128)(2,1)S(1)} collective-permute-done((bf16[2,256,512]{2,1,0:T(8,128)(2,1)S(1)}, bf16[2,256,512]{2,1,0:T(8,128)(2,1)S(1)}, u32[]{:S(2)}, u32[]{:S(2)}) %collective-permute-start.9) | collective-permute-done | bytes 524320 | tf_op jit(solution)/shard_map/to_kv/ppermute | solution.py:29
  17.8 1.8 %trunk_partial.1 = (f32[2,2,256,512]{3,2,1,0:T(8,128)S(1)}, f32[2,2,256,512]{3,2,1,0:T(8,128)S(1)}) custom-call(bf16[2,256,1024]{2,1,0:T(8,128)(2,1)S(1)} %copy-done, bf16[2,256,1024]{2,1,0:T(8,128)(2,1)S(1)} %collective-permute-done.8.refs_1_, bf16[2,256,512]{2,1,0:T(8,128)(2,1)S(1)} %chip_halves.2.refs_2_.refs_10_, ...), custom_call_target="tpu_custom_call" | custom-call | tf_op jit(solution)/shard_map/trunk_partial/pallas_call | solution.py:47
  19.6 4.1 %collective-permute-done.7.refs_0_.refs_4_.refs_13_ = bf16[2,256,512]{2,1,0:T(8,128)(2,1)S(1)} collective-permute-done((bf16[2,256,512]{2,1,0:T(8,128)(2,1)S(1)}, bf16[2,256,512]{2,1,0:T(8,128)(2,1)S(1)}, u32[]{:S(2)}, u32[]{:S(2)}) %collective-permute-start.7) | collective-permute-done | bytes 524320 | tf_op jit(solution)/shard_map/to_kv_far/ppermute | solution.py:29
  23.7 2.5 %collective-permute-start.11 = (bf16[1,256,256]{2,1,0:T(8,128)(2,1)S(1)}, bf16[1,256,256]{2,1,0:T(8,128)(2,1)S(1)}, u32[]{:S(2)}, u32[]{:S(2)}) collective-permute-start(bf16[1,256,256]{2,1,0:T(8,128)(2,1)S(1)} %get-tuple-element.43.refs_2_), channel_id=1, source_target_pairs={{0,4},{1,3},{2,6},{3,1},{4,0},{5,7},{6,2},{7,5},{8,12},{9,11},{10,... | collective-permute-start | bytes 393224 | tf_op jit(solution)/shard_map/to_query/ppermute | solution.py:29
  26.2 2.0 %collective-permute-start.10 = (bf16[1,256,256]{2,1,0:T(8,128)(2,1)S(1)}, bf16[1,256,256]{2,1,0:T(8,128)(2,1)S(1)}, u32[]{:S(2)}, u32[]{:S(2)}) collective-permute-start(bf16[1,256,256]{2,1,0:T(8,128)(2,1)S(1)} %get-tuple-element.43.refs_2_), channel_id=1, source_target_pairs={{0,2},{1,5},{2,0},{3,7},{4,6},{5,1},{6,4},{7,3},{8,10},{9,13},{10,... | collective-permute-start | bytes 393224 | tf_op jit(solution)/shard_map/to_query/ppermute | solution.py:29
  28.2 1.6 %trunk_states.1 = (bf16[2,4,128,128]{3,2,1,0:T(8,128)(2,1)S(1)}, bf16[2,4,128,128]{3,2,1,0:T(8,128)(2,1)S(1)}, bf16[2,2,256,512]{3,2,1,0:T(8,128)(2,1)S(1)}, bf1...) custom-call(bf16[2,256,1024]{2,1,0:T(8,128)(2,1)S(1)} %copy-done, ...), custom_call_target="tpu_custom_call" | custom-call | tf_op jit(solution)/shard_map/trunk_states/pallas_call | solution.py:47
  29.9 0.3 collective-permute-done.11.refs_1_
  30.2 1.9 %collective-permute-done.10.refs_0_.refs_4_ = bf16[1,256,256]{2,1,0:T(8,128)(2,1)S(1)} collective-permute-done((bf16[1,256,256]{2,1,0:T(8,128)(2,1)S(1)}, bf16[1,256,256]{2,1,0:T(8,128)(2,1)S(1)}, u32[]{:S(2)}, u32[]{:S(2)}) %collective-permute-start.10) | collective-permute-done | bytes 131104 | tf_op jit(solution)/shard_map/to_query/ppermute | solution.py:29
  32.1 2.5 %collective-permute-start.12 = (bf16[1,256,256]{2,1,0:T(8,128)(2,1)S(1)}, bf16[1,256,256]{2,1,0:T(8,128)(2,1)S(1)}, u32[]{:S(2)}, u32[]{:S(2)}) collective-permute-start(bf16[1,256,256]{2,1,0:T(8,128)(2,1)S(1)} %get-tuple-element.47.refs_3_), channel_id=1, source_target_pairs={{0,2},{1,5},{2,0},{3,7},{4,6},{5,1},{6,4},{7,3},{8,10},{9,13},{10,... | collective-permute-start | bytes 393224 | tf_op jit(solution)/shard_map/to_query_far/ppermute | solution.py:29
  34.6 1.6 %collective-permute-start.14 = (bf16[1,256,256]{2,1,0:T(8,128)(2,1)S(1)}, bf16[1,256,256]{2,1,0:T(8,128)(2,1)S(1)}, u32[]{:S(2)}, u32[]{:S(2)}) collective-permute-start(bf16[1,256,256]{2,1,0:T(8,128)(2,1)S(1)} %get-tuple-element.47.refs_3_), channel_id=1, source_target_pairs={{0,8},{8,0},{16,24},{24,16},{1,9},{9,1},{17,25},{25,17},{2,10},{10... | collective-permute-start | bytes 393224 | tf_op jit(solution)/shard_map/to_query_lane/ppermute | solution.py:22
  36.2 0.4 collective-permute-start.15
  36.6 1.6 %collective-permute-done.13.refs_1_.refs_3_ = bf16[2,4,128,128]{3,2,1,0:T(8,128)(2,1)S(1)} collective-permute-done((bf16[2,4,128,128]{3,2,1,0:T(8,128)(2,1)S(1)}, bf16[2,4,128,128]{3,2,1,0:T(8,128)(2,1)S(1)}, u32[]{:S(2)}, u32[]{:S(2)}) %collective-permute-start.13) | collective-permute-done | bytes 262176 | tf_op jit(solution)/shard_map/to_scan/ppermute | solution.py:29
  38.3 0.1 scan_step.1.refs_1_
  38.4 0.1 collective-permute-start.17
  38.5 1.6 %collective-permute-start.16 = (bf16[1,256,256]{2,1,0:T(8,128)(2,1)S(1)}, bf16[1,256,256]{2,1,0:T(8,128)(2,1)S(1)}, u32[]{:S(2)}, u32[]{:S(2)}) collective-permute-start(bf16[1,256,256]{2,1,0:T(8,128)(2,1)S(1)} %get-tuple-element.50.refs_5_), channel_id=1, source_target_pairs={{0,8},{8,0},{16,24},{24,16},{1,9},{9,1},{17,25},{25,17},{2,10},{10... | collective-permute-start | bytes 393224 | tf_op jit(solution)/shard_map/to_query_lane/ppermute | solution.py:22
  40.1 1.4 %fork_parts.1.refs_2_ = f32[2,4,4,128,128]{4,3,2,1,0:T(8,128)S(1)} custom-call(s32[2,4]{1,0:T(2,128)S(1)} %pack_forks.1.refs_4_.refs_0_, s32[2,4]{1,0:T(2,128)S(1)} %collective-permute-done.6.refs_5_.refs_1_, bf16[2,2,256,512]{3,2,1,0:T(8,128)(2,1)S(1)} %get-tuple-element.53.refs_2_, bf16[2,2,256,512]{3,2,1,0:T(8,128)(2,1)S(1)} %get-tuple-element.54.refs_3_, ...), custom_call_target="tpu_custom_call" | custom-call | tf_op jit(solution)/shard_map/fork_parts/pallas_call | solution.py:47
  41.6 0.8 %collective-permute-done.15.refs_1_.refs_8_ = bf16[1,256,256]{2,1,0:T(8,128)(2,1)S(1)} collective-permute-done((bf16[1,256,256]{2,1,0:T(8,128)(2,1)S(1)}, bf16[1,256,256]{2,1,0:T(8,128)(2,1)S(1)}, u32[]{:S(2)}, u32[]{:S(2)}) %collective-permute-start.15) | collective-permute-done | bytes 131104 | tf_op jit(solution)/shard_map/to_query_lane/ppermute | solution.py:22
  42.4 2.4 %collective-permute-done.17.refs_4_ = bf16[2,4,128,128]{3,2,1,0:T(8,128)(2,1)S(1)} collective-permute-done((bf16[2,4,128,128]{3,2,1,0:T(8,128)(2,1)S(1)}, bf16[2,4,128,128]{3,2,1,0:T(8,128)(2,1)S(1)}, u32[]{:S(2)}, u32[]{:S(2)}) %collective-permute-start.17) | collective-permute-done | bytes 262176 | tf_op jit(solution)/shard_map/to_scan/ppermute | solution.py:29
  44.8 1.0 %fork_states.1 = (bf16[2,1,4,128,128]{4,3,2,1,0:T(8,128)(2,1)S(1)}, bf16[2,1,4,128,128]{4,3,2,1,0:T(8,128)(2,1)S(1)}, bf16[2,1,4,128,128]{4,3,2,1,0:T(8,128)(2,1...) custom-call(s32[2,4]{1,0:T(2,128)S(1)} %pack_forks.1.refs_4_.refs_0_, ...), custom_call_target="tpu_custom_call", output_to_operand_aliasing={{4}: (5, {})} | custom-call | tf_op jit(solution)/shard_map/fork_states/pallas_call | solution.py:47
  45.8 1.6 %collective-permute-start.18 = (bf16[2,1,4,128,128]{4,3,2,1,0:T(8,128)(2,1)S(1)}, bf16[2,1,4,128,128]{4,3,2,1,0:T(8,128)(2,1)S(1)}, u32[]{:S(2)}, u32[]{:S(2)}) collective-permute-start(bf16[2,1,4,128,128]{4,3,2,1,0:T(8,128)(2,1)S(1)} %get-tuple-element.62), channel_id=1, source_target_pairs={{0,8},{8,0},{16,24},{24,16},{1,9},{9,1},{17,25},{25,17},{2,10},{10... | collective-permute-start | bytes 786440 | tf_op jit(solution)/shard_map/to_lane/ppermute | solution.py:22
  47.4 2.6 %collective-permute-start.19 = (bf16[2,1,4,128,128]{4,3,2,1,0:T(8,128)(2,1)S(1)}, bf16[2,1,4,128,128]{4,3,2,1,0:T(8,128)(2,1)S(1)}, u32[]{:S(2)}, u32[]{:S(2)}) collective-permute-start(bf16[2,1,4,128,128]{4,3,2,1,0:T(8,128)(2,1)S(1)} %get-tuple-element.63), channel_id=1, source_target_pairs={{0,16},{8,24},{16,0},{24,8},{1,17},{9,25},{17,1},{25,9},{2,18},{10... | collective-permute-start | bytes 786440 | tf_op jit(solution)/shard_map/to_lane/ppermute | solution.py:22
  50.0 0.2 collective-permute-start.22
  50.3 4.8 %branch_parts.1 = (bf16[2,2,256,512]{3,2,1,0:T(8,128)(2,1)S(1)}, f32[2,2,256,512]{3,2,1,0:T(8,128)S(1)}) custom-call(bf16[2,256,1024]{2,1,0:T(8,128)(2,1)S(1)} %bitcast.9, bf16[2,256,1024]{2,1,0:T(8,128)(2,1)S(1)} %bitcast.8, bf16[1,256,256]{2,1,0:T(8,128)(2,1)S(1)} %get-tuple-element.43.refs_2_, bf16[1,256,256]{2,1,0:T(8,128)(2,1)S(1)} %get-tuple-element.47.refs_3_, ...), custom_call_target="tpu_custom_call" | custom-call | flops 20000000000 | tf_op jit(solution)/shard_map/branch_parts/pallas_call | solution.py:47
  55.1 5.8 %collective-permute-done.20.refs_0_ = bf16[2,256,512]{2,1,0:T(8,128)(2,1)S(1)} collective-permute-done((bf16[2,256,512]{2,1,0:T(8,128)(2,1)S(1)}, bf16[2,256,512]{2,1,0:T(8,128)(2,1)S(1)}, u32[]{:S(2)}, u32[]{:S(2)}) %collective-permute-start.20) | collective-permute-done | bytes 524320 | tf_op jit(solution)/shard_map/to_out/ppermute | solution.py:29
  60.9 1.5 %collective-permute-start.25 = (bf16[2,256,512]{2,1,0:T(8,128)(2,1)S(1)}, bf16[2,256,512]{2,1,0:T(8,128)(2,1)S(1)}, u32[]{:S(2)}, u32[]{:S(2)}) collective-permute-start(bf16[2,256,512]{2,1,0:T(8,128)(2,1)S(1)} %get-tuple-element.71.refs_1_), channel_id=1, source_target_pairs={{0,2},{1,5},{2,0},{3,7},{4,6},{5,1},{6,4},{7,3},{8,10},{9,13},{10,... | collective-permute-start | bytes 1572872 | tf_op jit(solution)/shard_map/to_out_far/ppermute | solution.py:29
  62.3 3.7 %collective-permute-done.19.refs_4_ = bf16[2,1,4,128,128]{4,3,2,1,0:T(8,128)(2,1)S(1)} collective-permute-done((bf16[2,1,4,128,128]{4,3,2,1,0:T(8,128)(2,1)S(1)}, bf16[2,1,4,128,128]{4,3,2,1,0:T(8,128)(2,1)S(1)}, u32[]{:S(2)}, u32[]{:S(2)}) %collective-permute-start.19) | collective-permute-done | bytes 262176 | tf_op jit(solution)/shard_map/to_lane/ppermute | solution.py:22
  66.1 0.7 norm_parts.2
  66.8 0.1 collective-permute-start.21
  66.9 0.4 norm_parts.3
  67.3 0.5 collective-permute-start.24
  67.8 0.8 %collective-permute-done.21.refs_0_.refs_1_ = bf16[3,128,512]{2,1,0:T(8,128)(2,1)S(1)} collective-permute-done((bf16[3,128,512]{2,1,0:T(8,128)(2,1)S(1)}, bf16[3,128,512]{2,1,0:T(8,128)(2,1)S(1)}, u32[]{:S(2)}, u32[]{:S(2)}) %collective-permute-start.21) | collective-permute-done | bytes 393248 | tf_op jit(solution)/shard_map/to_normed/ppermute | solution.py:22
  68.6 1.5 %collective-permute-done.25.refs_3_ = bf16[2,256,512]{2,1,0:T(8,128)(2,1)S(1)} collective-permute-done((bf16[2,256,512]{2,1,0:T(8,128)(2,1)S(1)}, bf16[2,256,512]{2,1,0:T(8,128)(2,1)S(1)}, u32[]{:S(2)}, u32[]{:S(2)}) %collective-permute-start.25) | collective-permute-done | bytes 524320 | tf_op jit(solution)/shard_map/to_out_far/ppermute | solution.py:29
  70.0 0.3 place_rows.1.refs_2_.refs_3_
  70.3 0.7 out_sum.1.refs_4_.refs_5_
  71.1 2.1 %out_last.1 = bf16[4,128,1024]{2,1,0:T(8,128)(2,1)} custom-call(s32[4]{0:T(128)S(1)} %copy-done.3, bf16[3,128,512]{2,1,0:T(8,128)(2,1)S(1)} %collective-permute-done.21.refs_0_.refs_1_, bf16[1,128,512]{2,1,0:T(8,128)(2,1)S(1)} %collective-permute-done.24.refs_2_, bf16[1024,1024]{1,0:T(8,128)(2,1)S(1)} %place_rows.1.refs_2_.refs_3_, ...), custom_call_target="tpu_custom_call" | custom-call | tf_op jit(solution)/shard_map/out_last/pallas_call | solution.py:47
  (43 shorter events, 0.4 us)
Async XLA Ops:
  0.0 2.0 %collective-permute-start.1 = (bf16[128,1024]{1,0:T(8,128)(2,1)}, bf16[128,1024]{1,0:T(8,128)(2,1)S(1)}, u32[]{:S(2)}, u32[]{:S(2)}) collective-permute-start(bf16[128,1024]{1,0:T(8,128)(2,1)} %param.15), channel_id=1, source_target_pairs={{0,1},{1,0},{2,3},{3,2},{4,5},{5,4},{6,7},{7,6},{8,9},{9,8},{10,11... | collective-permute-start | bytes 786440 | tf_op jit(solution)/shard_map/to_core/ppermute | solution.py:22
  0.5 1.7 %collective-permute-start.2 = (bf16[128,1024]{1,0:T(8,128)(2,1)}, bf16[128,1024]{1,0:T(8,128)(2,1)S(1)}, u32[]{:S(2)}, u32[]{:S(2)}) collective-permute-start(bf16[128,1024]{1,0:T(8,128)(2,1)} %param.16), channel_id=1, source_target_pairs={{0,1},{1,0},{2,3},{3,2},{4,5},{5,4},{6,7},{7,6},{8,9},{9,8},{10,11... | collective-permute-start | bytes 786440 | tf_op jit(solution)/shard_map/to_core/ppermute | solution.py:22
  0.5 17.3 %collective-permute-start = (bf16[4,128,1024]{2,1,0:T(8,128)(2,1)}, bf16[4,128,1024]{2,1,0:T(8,128)(2,1)S(1)}, u32[]{:S(2)}, u32[]{:S(2)}) collective-permute-start(bf16[4,128,1024]{2,1,0:T(8,128)(2,1)} %param.10), channel_id=1, source_target_pairs={{0,1},{1,0},{2,3},{3,2},{4,5},{5,4},{6,7},{7,6},{8,9},{9,8},{10,11... | collective-permute-start | bytes 3145736 | tf_op jit(solution)/shard_map/to_tokens/ppermute | solution.py:22
  2.0 3.6 %copy-start = (bf16[2,256,1024]{2,1,0:T(8,128)(2,1)S(1)}, bf16[2,256,1024]{2,1,0:T(8,128)(2,1)}, u32[]{:S(2)}) copy-start(bf16[2,256,1024]{2,1,0:T(8,128)(2,1)} %refs_0_.8) | copy-start | bytes 3145732
  2.0 3.6 %copy-start.1 = (bf16[128,1024]{1,0:T(8,128)(2,1)S(1)}, bf16[128,1024]{1,0:T(8,128)(2,1)}, u32[]{:S(2)}) copy-start(bf16[128,1024]{1,0:T(8,128)(2,1)} %refs_0_.6) | copy-start | bytes 786436
  2.0 4.1 %copy-start.2 = (bf16[128,1024]{1,0:T(8,128)(2,1)S(1)}, bf16[128,1024]{1,0:T(8,128)(2,1)}, u32[]{:S(2)}) copy-start(bf16[128,1024]{1,0:T(8,128)(2,1)} %refs_1_.3) | copy-start | bytes 786436
  2.0 4.1 %copy-start.4 = (s32[1,1,4]{2,1,0:T(1,128)S(1)}, s32[1,1,4]{2,1,0:T(1,128)}, u32[]{:S(2)}) copy-start(s32[1,1,4]{2,1,0:T(1,128)} %refs_0_.5) | copy-start | bytes 52
  2.0 4.1 %copy-start.5 = (s32[1,1,4]{2,1,0:T(1,128)S(1)}, s32[1,1,4]{2,1,0:T(1,128)}, u32[]{:S(2)}) copy-start(s32[1,1,4]{2,1,0:T(1,128)} %refs_1_.2) | copy-start | bytes 52
  2.6 11.8 %collective-permute-start.3 = (bf16[2,256,512]{2,1,0:T(8,128)(2,1)S(1)}, bf16[2,256,512]{2,1,0:T(8,128)(2,1)S(1)}, u32[]{:S(2)}, u32[]{:S(2)}) collective-permute-start(bf16[2,256,512]{2,1,0:T(8,128)(2,1)S(1)} %chip_halves.2.refs_2_.refs_10_), channel_id=1, source_target_pairs={{0,4},{1,3},{2,6},{3,1},{4,0},{5,7},{6,2},{7,5},{8,12},{9,11},{10,... | collective-permute-start | bytes 1572872 | tf_op jit(solution)/shard_map/to_kv/ppermute | solution.py:29
  5.6 12.2 %collective-permute-start.8 = (bf16[2,256,1024]{2,1,0:T(8,128)(2,1)S(1)}, bf16[2,256,1024]{2,1,0:T(8,128)(2,1)S(1)}, u32[]{:S(2)}, u32[]{:S(2)}) collective-permute-start(bf16[2,256,1024]{2,1,0:T(8,128)(2,1)S(1)} %copy-done), channel_id=1, source_target_pairs={{0,1},{1,0},{2,3},{3,2},{4,5},{5,4},{6,7},{7,6},{8,9},{9,8},{10,11... | collective-permute-start | bytes 3145736 | tf_op jit(solution)/shard_map/to_tokens/ppermute | solution.py:22
  5.6 3.0 %collective-permute-start.4 = (bf16[128,1024]{1,0:T(8,128)(2,1)S(1)}, bf16[128,1024]{1,0:T(8,128)(2,1)S(1)}, u32[]{:S(2)}, u32[]{:S(2)}) collective-permute-start(bf16[128,1024]{1,0:T(8,128)(2,1)S(1)} %copy-done.1), channel_id=1, source_target_pairs={{0,1},{1,0},{2,3},{3,2},{4,5},{5,4},{6,7},{7,6},{8,9},{9,8},{10,11... | collective-permute-start | bytes 786440 | tf_op jit(solution)/shard_map/to_core/ppermute | solution.py:22
  6.1 4.0 %collective-permute-start.5 = (bf16[128,1024]{1,0:T(8,128)(2,1)S(1)}, bf16[128,1024]{1,0:T(8,128)(2,1)S(1)}, u32[]{:S(2)}, u32[]{:S(2)}) collective-permute-start(bf16[128,1024]{1,0:T(8,128)(2,1)S(1)} %copy-done.2), channel_id=1, source_target_pairs={{0,1},{1,0},{2,3},{3,2},{4,5},{5,4},{6,7},{7,6},{8,9},{9,8},{10,11... | collective-permute-start | bytes 786440 | tf_op jit(solution)/shard_map/to_core/ppermute | solution.py:22
  8.6 9.2 %collective-permute-start.9 = (bf16[2,256,512]{2,1,0:T(8,128)(2,1)S(1)}, bf16[2,256,512]{2,1,0:T(8,128)(2,1)S(1)}, u32[]{:S(2)}, u32[]{:S(2)}) collective-permute-start(bf16[2,256,512]{2,1,0:T(8,128)(2,1)S(1)} %chip_halves.2.refs_2_.refs_10_), channel_id=1, source_target_pairs={{0,2},{1,5},{2,0},{3,7},{4,6},{5,1},{6,4},{7,3},{8,10},{9,13},{10,... | collective-permute-start | bytes 1572872 | tf_op jit(solution)/shard_map/to_kv/ppermute | solution.py:29
  10.1 1.1 %collective-permute-start.6 = (s32[2,4]{1,0:T(2,128)S(1)}, s32[2,4]{1,0:T(2,128)S(1)}, u32[]{:S(2)}, u32[]{:S(2)}) collective-permute-start(s32[2,4]{1,0:T(2,128)S(1)} %pack_forks.1.refs_4_.refs_0_), channel_id=1, source_target_pairs={{0,1},{1,0},{2,3},{3,2},{4,5},{5,4},{6,7},{7,6},{8,9},{9,8},{10,11... | collective-permute-start | bytes 104 | tf_op jit(solution)/shard_map/to_forks/ppermute | solution.py:22
  14.4 9.3 %collective-permute-start.7 = (bf16[2,256,512]{2,1,0:T(8,128)(2,1)S(1)}, bf16[2,256,512]{2,1,0:T(8,128)(2,1)S(1)}, u32[]{:S(2)}, u32[]{:S(2)}) collective-permute-start(bf16[2,256,512]{2,1,0:T(8,128)(2,1)S(1)} %get-tuple-element.40.refs_3_.refs_11_), channel_id=1, source_target_pairs={{0,2},{1,5},{2,0},{3,7},{4,6},{5,1},{6,4},{7,3},{8,10},{9,13},{10,... | collective-permute-start | bytes 1572872 | tf_op jit(solution)/shard_map/to_kv_far/ppermute | solution.py:29
  23.7 6.5 %collective-permute-start.11 = (bf16[1,256,256]{2,1,0:T(8,128)(2,1)S(1)}, bf16[1,256,256]{2,1,0:T(8,128)(2,1)S(1)}, u32[]{:S(2)}, u32[]{:S(2)}) collective-permute-start(bf16[1,256,256]{2,1,0:T(8,128)(2,1)S(1)} %get-tuple-element.43.refs_2_), channel_id=1, source_target_pairs={{0,4},{1,3},{2,6},{3,1},{4,0},{5,7},{6,2},{7,5},{8,12},{9,11},{10,... | collective-permute-start | bytes 393224 | tf_op jit(solution)/shard_map/to_query/ppermute | solution.py:29
  26.2 5.9 %collective-permute-start.10 = (bf16[1,256,256]{2,1,0:T(8,128)(2,1)S(1)}, bf16[1,256,256]{2,1,0:T(8,128)(2,1)S(1)}, u32[]{:S(2)}, u32[]{:S(2)}) collective-permute-start(bf16[1,256,256]{2,1,0:T(8,128)(2,1)S(1)} %get-tuple-element.43.refs_2_), channel_id=1, source_target_pairs={{0,2},{1,5},{2,0},{3,7},{4,6},{5,1},{6,4},{7,3},{8,10},{9,13},{10,... | collective-permute-start | bytes 393224 | tf_op jit(solution)/shard_map/to_query/ppermute | solution.py:29
  29.8 8.4 %collective-permute-start.13 = (bf16[2,4,128,128]{3,2,1,0:T(8,128)(2,1)S(1)}, bf16[2,4,128,128]{3,2,1,0:T(8,128)(2,1)S(1)}, u32[]{:S(2)}, u32[]{:S(2)}) collective-permute-start(bf16[2,4,128,128]{3,2,1,0:T(8,128)(2,1)S(1)} %get-tuple-element.48), channel_id=1, source_target_pairs={{0,4},{1,3},{2,6},{3,1},{4,0},{5,7},{6,2},{7,5},{8,12},{9,11},{10,... | collective-permute-start | bytes 786440 | tf_op jit(solution)/shard_map/to_scan/ppermute | solution.py:29
  32.1 6.3 %collective-permute-start.12 = (bf16[1,256,256]{2,1,0:T(8,128)(2,1)S(1)}, bf16[1,256,256]{2,1,0:T(8,128)(2,1)S(1)}, u32[]{:S(2)}, u32[]{:S(2)}) collective-permute-start(bf16[1,256,256]{2,1,0:T(8,128)(2,1)S(1)} %get-tuple-element.47.refs_3_), channel_id=1, source_target_pairs={{0,2},{1,5},{2,0},{3,7},{4,6},{5,1},{6,4},{7,3},{8,10},{9,13},{10,... | collective-permute-start | bytes 393224 | tf_op jit(solution)/shard_map/to_query_far/ppermute | solution.py:29
  34.6 7.0 %collective-permute-start.14 = (bf16[1,256,256]{2,1,0:T(8,128)(2,1)S(1)}, bf16[1,256,256]{2,1,0:T(8,128)(2,1)S(1)}, u32[]{:S(2)}, u32[]{:S(2)}) collective-permute-start(bf16[1,256,256]{2,1,0:T(8,128)(2,1)S(1)} %get-tuple-element.47.refs_3_), channel_id=1, source_target_pairs={{0,8},{8,0},{16,24},{24,16},{1,9},{9,1},{17,25},{25,17},{2,10},{10... | collective-permute-start | bytes 393224 | tf_op jit(solution)/shard_map/to_query_lane/ppermute | solution.py:22
  36.2 6.2 %collective-permute-start.15 = (bf16[1,256,256]{2,1,0:T(8,128)(2,1)S(1)}, bf16[1,256,256]{2,1,0:T(8,128)(2,1)S(1)}, u32[]{:S(2)}, u32[]{:S(2)}) collective-permute-start(bf16[1,256,256]{2,1,0:T(8,128)(2,1)S(1)} %collective-permute-done.10.refs_0_.refs_4_), channel_id=1, source_target_pairs={{0,8},{8,0},{16,24},{24,16},{1,9},{9,1},{17,25},{25,17},{2,10},{10... | collective-permute-start | bytes 393224 | tf_op jit(solution)/shard_map/to_query_lane/ppermute | solution.py:22
  38.4 6.4 %collective-permute-start.17 = (bf16[2,4,128,128]{3,2,1,0:T(8,128)(2,1)S(1)}, bf16[2,4,128,128]{3,2,1,0:T(8,128)(2,1)S(1)}, u32[]{:S(2)}, u32[]{:S(2)}) collective-permute-start(bf16[2,4,128,128]{3,2,1,0:T(8,128)(2,1)S(1)} %scan_step.1.refs_1_), channel_id=1, source_target_pairs={{0,2},{1,5},{2,0},{3,7},{4,6},{5,1},{6,4},{7,3},{8,10},{9,13},{10,... | collective-permute-start | bytes 786440 | tf_op jit(solution)/shard_map/to_scan/ppermute | solution.py:29
  38.5 11.8 %collective-permute-start.16 = (bf16[1,256,256]{2,1,0:T(8,128)(2,1)S(1)}, bf16[1,256,256]{2,1,0:T(8,128)(2,1)S(1)}, u32[]{:S(2)}, u32[]{:S(2)}) collective-permute-start(bf16[1,256,256]{2,1,0:T(8,128)(2,1)S(1)} %get-tuple-element.50.refs_5_), channel_id=1, source_target_pairs={{0,8},{8,0},{16,24},{24,16},{1,9},{9,1},{17,25},{25,17},{2,10},{10... | collective-permute-start | bytes 393224 | tf_op jit(solution)/shard_map/to_query_lane/ppermute | solution.py:22
  42.4 7.9 %copy-start.6 = (bf16[4,128,1024]{2,1,0:T(8,128)(2,1)S(1)}, bf16[4,128,1024]{2,1,0:T(8,128)(2,1)}, u32[]{:S(2)}) copy-start(bf16[4,128,1024]{2,1,0:T(8,128)(2,1)} %param.10) | copy-start | bytes 3145732
  45.8 16.6 %collective-permute-start.18 = (bf16[2,1,4,128,128]{4,3,2,1,0:T(8,128)(2,1)S(1)}, bf16[2,1,4,128,128]{4,3,2,1,0:T(8,128)(2,1)S(1)}, u32[]{:S(2)}, u32[]{:S(2)}) collective-permute-start(bf16[2,1,4,128,128]{4,3,2,1,0:T(8,128)(2,1)S(1)} %get-tuple-element.62), channel_id=1, source_target_pairs={{0,8},{8,0},{16,24},{24,16},{1,9},{9,1},{17,25},{25,17},{2,10},{10... | collective-permute-start | bytes 786440 | tf_op jit(solution)/shard_map/to_lane/ppermute | solution.py:22
  47.4 18.7 %collective-permute-start.19 = (bf16[2,1,4,128,128]{4,3,2,1,0:T(8,128)(2,1)S(1)}, bf16[2,1,4,128,128]{4,3,2,1,0:T(8,128)(2,1)S(1)}, u32[]{:S(2)}, u32[]{:S(2)}) collective-permute-start(bf16[2,1,4,128,128]{4,3,2,1,0:T(8,128)(2,1)S(1)} %get-tuple-element.63), channel_id=1, source_target_pairs={{0,16},{8,24},{16,0},{24,8},{1,17},{9,25},{17,1},{25,9},{2,18},{10... | collective-permute-start | bytes 786440 | tf_op jit(solution)/shard_map/to_lane/ppermute | solution.py:22
  50.0 16.9 %collective-permute-start.22 = (bf16[2,1,4,128,128]{4,3,2,1,0:T(8,128)(2,1)S(1)}, bf16[2,1,4,128,128]{4,3,2,1,0:T(8,128)(2,1)S(1)}, u32[]{:S(2)}, u32[]{:S(2)}) collective-permute-start(bf16[2,1,4,128,128]{4,3,2,1,0:T(8,128)(2,1)S(1)} %get-tuple-element.67), channel_id=1, source_target_pairs={{0,24},{8,16},{16,8},{24,0},{1,25},{9,17},{17,9},{25,1},{2,26},{10... | collective-permute-start | bytes 786440 | tf_op jit(solution)/shard_map/to_lane/ppermute | solution.py:22
  50.2 16.6 %collective-permute-start.23 = (bf16[2,256,512]{2,1,0:T(8,128)(2,1)S(1)}, bf16[2,256,512]{2,1,0:T(8,128)(2,1)S(1)}, u32[]{:S(2)}, u32[]{:S(2)}) collective-permute-start(bf16[2,256,512]{2,1,0:T(8,128)(2,1)S(1)} %get-tuple-element.68.refs_0_), channel_id=1, source_target_pairs={{0,2},{1,5},{2,0},{3,7},{4,6},{5,1},{6,4},{7,3},{8,10},{9,13},{10,... | collective-permute-start | bytes 1572872 | tf_op jit(solution)/shard_map/to_out/ppermute | solution.py:29
  50.2 10.6 %collective-permute-start.20 = (bf16[2,256,512]{2,1,0:T(8,128)(2,1)S(1)}, bf16[2,256,512]{2,1,0:T(8,128)(2,1)S(1)}, u32[]{:S(2)}, u32[]{:S(2)}) collective-permute-start(bf16[2,256,512]{2,1,0:T(8,128)(2,1)S(1)} %get-tuple-element.64), channel_id=1, source_target_pairs={{0,4},{1,3},{2,6},{3,1},{4,0},{5,7},{6,2},{7,5},{8,12},{9,11},{10,... | collective-permute-start | bytes 1572872 | tf_op jit(solution)/shard_map/to_out/ppermute | solution.py:29
  60.9 9.2 %collective-permute-start.25 = (bf16[2,256,512]{2,1,0:T(8,128)(2,1)S(1)}, bf16[2,256,512]{2,1,0:T(8,128)(2,1)S(1)}, u32[]{:S(2)}, u32[]{:S(2)}) collective-permute-start(bf16[2,256,512]{2,1,0:T(8,128)(2,1)S(1)} %get-tuple-element.71.refs_1_), channel_id=1, source_target_pairs={{0,2},{1,5},{2,0},{3,7},{4,6},{5,1},{6,4},{7,3},{8,10},{9,13},{10,... | collective-permute-start | bytes 1572872 | tf_op jit(solution)/shard_map/to_out_far/ppermute | solution.py:29
  66.8 1.8 %collective-permute-start.21 = (bf16[3,128,512]{2,1,0:T(8,128)(2,1)S(1)}, bf16[3,128,512]{2,1,0:T(8,128)(2,1)S(1)}, u32[]{:S(2)}, u32[]{:S(2)}) collective-permute-start(bf16[3,128,512]{2,1,0:T(8,128)(2,1)S(1)} %get-tuple-element.66), channel_id=1, source_target_pairs={{0,1},{1,0},{2,3},{3,2},{4,5},{5,4},{6,7},{7,6},{8,9},{9,8},{10,11... | collective-permute-start | bytes 1179656 | tf_op jit(solution)/shard_map/to_normed/ppermute | solution.py:22
  67.3 3.8 %collective-permute-start.24 = (bf16[1,128,512]{2,1,0:T(8,128)(2,1)S(1)}, bf16[1,128,512]{2,1,0:T(8,128)(2,1)S(1)}, u32[]{:S(2)}, u32[]{:S(2)}) collective-permute-start(bf16[1,128,512]{2,1,0:T(8,128)(2,1)S(1)} %get-tuple-element.70), channel_id=1, source_target_pairs={{0,1},{1,0},{2,3},{3,2},{4,5},{5,4},{6,7},{7,6},{8,9},{9,8},{10,11... | collective-permute-start | bytes 393224 | tf_op jit(solution)/shard_map/to_normed/ppermute | solution.py:22
  70.3 0.8 %copy-start.3 = (s32[4]{0:T(128)S(1)}, s32[4]{0:T(128)}, u32[]{:S(2)}) copy-start(s32[4]{0:T(128)} %refs_0_.9) | copy-start | bytes 52

commit v5 on v4

--- a/solution.py
+++ b/solution.py
@@ -597,7 +597,7 @@
     if paired:
         _, near_o[1] = chain([], through=[held_o])
         outs = send_far(near_o, near_o[1], bits, "out")
-    aparts = list(range(lanes))
+    aparts = sorted(range(lanes), key=lambda a: a == 2)
     split = [aparts[:-1], aparts[-1:]] if lanes > 1 else [aparts]
     mine, other = [], []
     for part in split:

time: 73.3 us -> 72.8 us (level)
    ppermute x15, waiting for transfers between devices: 9.07 us -> 10.9 us  [swap(): lax.ppermute(value, axis, [(i, i ^ bit) for i in range(lax.axis_size(axis...]
    ppermute x11, waiting for transfers between devices: 21.7 us -> 20.1 us  [turn(): return lax.ppermute(value, 'trunk', [(i, i ^ bit(i)) for i in range(count)])]
where the time goes in v5:
time: 72.8 us; the launch traced here: 72.7 us
  waiting for transfers between devices  31 us (43%)
  starting transfers between devices  24.9 us (34%)
  Pallas kernels  15.5 us (21%)
  local copies, waits for them, and re-layouts  1.03 us (1%)
    ppermute x11, waiting for transfers between devices, turn(): return lax.ppermute(value, 'trunk', [(i, i ^ bit(i)) for i in range(count)])  20.1 us
    pallas_call x24, Pallas kernels, call(): pl.pallas_call(body, out_shape=[*outs, *(shape_of(a.shape, a.dtype) for a...  15.5 us
    ppermute x11, starting transfers between devices, turn(): return lax.ppermute(value, 'trunk', [(i, i ^ bit(i)) for i in range(count)])  15.3 us
    ppermute x15, waiting for transfers between devices, swap(): lax.ppermute(value, axis, [(i, i ^ bit) for i in range(lax.axis_size(axis...  10.9 us
    ppermute x15, starting transfers between devices, swap(): lax.ppermute(value, axis, [(i, i ^ bit) for i in range(lax.axis_size(axis...  9.58 us
  transfers between devices with their start and end apart: 26, of which 15 were waited for; matrix products, arithmetic and copies ran while one was open for 1% of the time, Pallas kernels for 18%

profile of v5, /device:TPU:0, one launch (start us, length us, event | category | flops | bytes accessed | tf_op | source)
XLA Modules:
  0.0 72.7 jit_solution(11433494717223032415)
XLA Ops:
  0.0 0.5 collective-permute-start.1
  0.5 0.5 collective-permute-start
  1.0 1.0 %constant_dynamic-slice_fusion = (bf16[128,512]{1,0:T(8,128)(2,1)S(1)}, bf16[128,512]{1,0:T(8,128)(2,1)S(1)}) fusion(bf16[128,1024]{1,0:T(8,128)(2,1)} %param.16, s32[]{:T(128)S(6)} %select_n.14, bf16[128,1024]{1,0:T(8,128)(2,1)} %param.15), kind=kLoop, calls=%fused_computation | loop fusion | bytes 524292 | tf_op jit(solution)/shard_map/dynamic_slice | solution.py:530
  2.0 0.2 collective-permute-done.2.refs_3_
  2.2 0.4 chip_halves.2.refs_2_.refs_10_
  2.6 3.0 %collective-permute-start.3 = (bf16[2,256,512]{2,1,0:T(8,128)(2,1)S(1)}, bf16[2,256,512]{2,1,0:T(8,128)(2,1)S(1)}, u32[]{:S(2)}, u32[]{:S(2)}) collective-permute-start(bf16[2,256,512]{2,1,0:T(8,128)(2,1)S(1)} %chip_halves.2.refs_2_.refs_10_), channel_id=1, source_target_pairs={{0,4},{1,3},{2,6},{3,1},{4,0},{5,7},{6,2},{7,5},{8,12},{9,11},{10,... | collective-permute-start | bytes 1572872 | tf_op jit(solution)/shard_map/to_kv/ppermute | solution.py:29
  5.6 0.5 collective-permute-start.4
  6.2 2.4 %collective-permute-done.4.refs_2_ = bf16[128,1024]{1,0:T(8,128)(2,1)S(1)} collective-permute-done((bf16[128,1024]{1,0:T(8,128)(2,1)S(1)}, bf16[128,1024]{1,0:T(8,128)(2,1)S(1)}, u32[]{:S(2)}, u32[]{:S(2)}) %collective-permute-start.4) | collective-permute-done | bytes 262176 | tf_op jit(solution)/shard_map/to_core/ppermute | solution.py:22
  8.6 1.5 %collective-permute-start.9 = (bf16[2,256,512]{2,1,0:T(8,128)(2,1)S(1)}, bf16[2,256,512]{2,1,0:T(8,128)(2,1)S(1)}, u32[]{:S(2)}, u32[]{:S(2)}) collective-permute-start(bf16[2,256,512]{2,1,0:T(8,128)(2,1)S(1)} %chip_halves.2.refs_2_.refs_10_), channel_id=1, source_target_pairs={{0,2},{1,5},{2,0},{3,7},{4,6},{5,1},{6,4},{7,3},{8,10},{9,13},{10,... | collective-permute-start | bytes 1572872 | tf_op jit(solution)/shard_map/to_kv/ppermute | solution.py:29
  10.1 1.1 %collective-permute-done.6.refs_5_.refs_1_ = s32[2,4]{1,0:T(2,128)S(1)} collective-permute-done((s32[2,4]{1,0:T(2,128)S(1)}, s32[2,4]{1,0:T(2,128)S(1)}, u32[]{:S(2)}, u32[]{:S(2)}) %collective-permute-start.6) | collective-permute-done | bytes 64 | tf_op jit(solution)/shard_map/to_forks/ppermute | solution.py:22
  11.2 0.3 chip_halves.3
  11.6 2.8 %collective-permute-done.3.refs_0_ = bf16[2,256,512]{2,1,0:T(8,128)(2,1)S(1)} collective-permute-done((bf16[2,256,512]{2,1,0:T(8,128)(2,1)S(1)}, bf16[2,256,512]{2,1,0:T(8,128)(2,1)S(1)}, u32[]{:S(2)}, u32[]{:S(2)}) %collective-permute-start.3) | collective-permute-done | bytes 524320 | tf_op jit(solution)/shard_map/to_kv/ppermute | solution.py:29
  14.4 2.2 %collective-permute-start.7 = (bf16[2,256,512]{2,1,0:T(8,128)(2,1)S(1)}, bf16[2,256,512]{2,1,0:T(8,128)(2,1)S(1)}, u32[]{:S(2)}, u32[]{:S(2)}) collective-permute-start(bf16[2,256,512]{2,1,0:T(8,128)(2,1)S(1)} %get-tuple-element.40.refs_3_.refs_11_), channel_id=1, source_target_pairs={{0,2},{1,5},{2,0},{3,7},{4,6},{5,1},{6,4},{7,3},{8,10},{9,13},{10,... | collective-permute-start | bytes 1572872 | tf_op jit(solution)/shard_map/to_kv_far/ppermute | solution.py:29
  16.6 1.2 %collective-permute-done.9.refs_4_.refs_12_ = bf16[2,256,512]{2,1,0:T(8,128)(2,1)S(1)} collective-permute-done((bf16[2,256,512]{2,1,0:T(8,128)(2,1)S(1)}, bf16[2,256,512]{2,1,0:T(8,128)(2,1)S(1)}, u32[]{:S(2)}, u32[]{:S(2)}) %collective-permute-start.9) | collective-permute-done | bytes 524320 | tf_op jit(solution)/shard_map/to_kv/ppermute | solution.py:29
  17.8 1.8 %trunk_partial.1 = (f32[2,2,256,512]{3,2,1,0:T(8,128)S(1)}, f32[2,2,256,512]{3,2,1,0:T(8,128)S(1)}) custom-call(bf16[2,256,1024]{2,1,0:T(8,128)(2,1)S(1)} %copy-done, bf16[2,256,1024]{2,1,0:T(8,128)(2,1)S(1)} %collective-permute-done.8.refs_1_, bf16[2,256,512]{2,1,0:T(8,128)(2,1)S(1)} %chip_halves.2.refs_2_.refs_10_, ...), custom_call_target="tpu_custom_call" | custom-call | tf_op jit(solution)/shard_map/trunk_partial/pallas_call | solution.py:47
  19.6 4.1 %collective-permute-done.7.refs_0_.refs_4_.refs_13_ = bf16[2,256,512]{2,1,0:T(8,128)(2,1)S(1)} collective-permute-done((bf16[2,256,512]{2,1,0:T(8,128)(2,1)S(1)}, bf16[2,256,512]{2,1,0:T(8,128)(2,1)S(1)}, u32[]{:S(2)}, u32[]{:S(2)}) %collective-permute-start.7) | collective-permute-done | bytes 524320 | tf_op jit(solution)/shard_map/to_kv_far/ppermute | solution.py:29
  23.7 2.5 %collective-permute-start.11 = (bf16[1,256,256]{2,1,0:T(8,128)(2,1)S(1)}, bf16[1,256,256]{2,1,0:T(8,128)(2,1)S(1)}, u32[]{:S(2)}, u32[]{:S(2)}) collective-permute-start(bf16[1,256,256]{2,1,0:T(8,128)(2,1)S(1)} %get-tuple-element.43.refs_2_), channel_id=1, source_target_pairs={{0,4},{1,3},{2,6},{3,1},{4,0},{5,7},{6,2},{7,5},{8,12},{9,11},{10,... | collective-permute-start | bytes 393224 | tf_op jit(solution)/shard_map/to_query/ppermute | solution.py:29
  26.2 2.0 %collective-permute-start.10 = (bf16[1,256,256]{2,1,0:T(8,128)(2,1)S(1)}, bf16[1,256,256]{2,1,0:T(8,128)(2,1)S(1)}, u32[]{:S(2)}, u32[]{:S(2)}) collective-permute-start(bf16[1,256,256]{2,1,0:T(8,128)(2,1)S(1)} %get-tuple-element.43.refs_2_), channel_id=1, source_target_pairs={{0,2},{1,5},{2,0},{3,7},{4,6},{5,1},{6,4},{7,3},{8,10},{9,13},{10,... | collective-permute-start | bytes 393224 | tf_op jit(solution)/shard_map/to_query/ppermute | solution.py:29
  28.2 1.6 %trunk_states.1 = (bf16[2,4,128,128]{3,2,1,0:T(8,128)(2,1)S(1)}, bf16[2,4,128,128]{3,2,1,0:T(8,128)(2,1)S(1)}, bf16[2,2,256,512]{3,2,1,0:T(8,128)(2,1)S(1)}, bf1...) custom-call(bf16[2,256,1024]{2,1,0:T(8,128)(2,1)S(1)} %copy-done, ...), custom_call_target="tpu_custom_call" | custom-call | tf_op jit(solution)/shard_map/trunk_states/pallas_call | solution.py:47
  29.8 0.1 collective-permute-start.13
  29.9 0.3 collective-permute-done.11.refs_1_
  30.2 1.9 %collective-permute-done.10.refs_0_.refs_4_ = bf16[1,256,256]{2,1,0:T(8,128)(2,1)S(1)} collective-permute-done((bf16[1,256,256]{2,1,0:T(8,128)(2,1)S(1)}, bf16[1,256,256]{2,1,0:T(8,128)(2,1)S(1)}, u32[]{:S(2)}, u32[]{:S(2)}) %collective-permute-start.10) | collective-permute-done | bytes 131104 | tf_op jit(solution)/shard_map/to_query/ppermute | solution.py:29
  32.1 2.5 %collective-permute-start.12 = (bf16[1,256,256]{2,1,0:T(8,128)(2,1)S(1)}, bf16[1,256,256]{2,1,0:T(8,128)(2,1)S(1)}, u32[]{:S(2)}, u32[]{:S(2)}) collective-permute-start(bf16[1,256,256]{2,1,0:T(8,128)(2,1)S(1)} %get-tuple-element.47.refs_3_), channel_id=1, source_target_pairs={{0,2},{1,5},{2,0},{3,7},{4,6},{5,1},{6,4},{7,3},{8,10},{9,13},{10,... | collective-permute-start | bytes 393224 | tf_op jit(solution)/shard_map/to_query_far/ppermute | solution.py:29
  34.6 1.6 %collective-permute-start.14 = (bf16[1,256,256]{2,1,0:T(8,128)(2,1)S(1)}, bf16[1,256,256]{2,1,0:T(8,128)(2,1)S(1)}, u32[]{:S(2)}, u32[]{:S(2)}) collective-permute-start(bf16[1,256,256]{2,1,0:T(8,128)(2,1)S(1)} %get-tuple-element.47.refs_3_), channel_id=1, source_target_pairs={{0,8},{8,0},{16,24},{24,16},{1,9},{9,1},{17,25},{25,17},{2,10},{10... | collective-permute-start | bytes 393224 | tf_op jit(solution)/shard_map/to_query_lane/ppermute | solution.py:22
  36.2 0.4 collective-permute-start.15
  36.6 1.6 %collective-permute-done.13.refs_1_.refs_3_ = bf16[2,4,128,128]{3,2,1,0:T(8,128)(2,1)S(1)} collective-permute-done((bf16[2,4,128,128]{3,2,1,0:T(8,128)(2,1)S(1)}, bf16[2,4,128,128]{3,2,1,0:T(8,128)(2,1)S(1)}, u32[]{:S(2)}, u32[]{:S(2)}) %collective-permute-start.13) | collective-permute-done | bytes 262176 | tf_op jit(solution)/shard_map/to_scan/ppermute | solution.py:29
  38.3 0.1 scan_step.1.refs_1_
  38.4 0.1 collective-permute-start.17
  38.5 1.6 %collective-permute-start.16 = (bf16[1,256,256]{2,1,0:T(8,128)(2,1)S(1)}, bf16[1,256,256]{2,1,0:T(8,128)(2,1)S(1)}, u32[]{:S(2)}, u32[]{:S(2)}) collective-permute-start(bf16[1,256,256]{2,1,0:T(8,128)(2,1)S(1)} %get-tuple-element.50.refs_5_), channel_id=1, source_target_pairs={{0,8},{8,0},{16,24},{24,16},{1,9},{9,1},{17,25},{25,17},{2,10},{10... | collective-permute-start | bytes 393224 | tf_op jit(solution)/shard_map/to_query_lane/ppermute | solution.py:22
  40.1 1.4 %fork_parts.1.refs_2_ = f32[2,4,4,128,128]{4,3,2,1,0:T(8,128)S(1)} custom-call(s32[2,4]{1,0:T(2,128)S(1)} %pack_forks.1.refs_4_.refs_0_, s32[2,4]{1,0:T(2,128)S(1)} %collective-permute-done.6.refs_5_.refs_1_, bf16[2,2,256,512]{3,2,1,0:T(8,128)(2,1)S(1)} %get-tuple-element.53.refs_2_, bf16[2,2,256,512]{3,2,1,0:T(8,128)(2,1)S(1)} %get-tuple-element.54.refs_3_, ...), custom_call_target="tpu_custom_call" | custom-call | tf_op jit(solution)/shard_map/fork_parts/pallas_call | solution.py:47
  41.6 0.8 %collective-permute-done.15.refs_1_.refs_8_ = bf16[1,256,256]{2,1,0:T(8,128)(2,1)S(1)} collective-permute-done((bf16[1,256,256]{2,1,0:T(8,128)(2,1)S(1)}, bf16[1,256,256]{2,1,0:T(8,128)(2,1)S(1)}, u32[]{:S(2)}, u32[]{:S(2)}) %collective-permute-start.15) | collective-permute-done | bytes 131104 | tf_op jit(solution)/shard_map/to_query_lane/ppermute | solution.py:22
  42.4 2.4 %collective-permute-done.17.refs_4_ = bf16[2,4,128,128]{3,2,1,0:T(8,128)(2,1)S(1)} collective-permute-done((bf16[2,4,128,128]{3,2,1,0:T(8,128)(2,1)S(1)}, bf16[2,4,128,128]{3,2,1,0:T(8,128)(2,1)S(1)}, u32[]{:S(2)}, u32[]{:S(2)}) %collective-permute-start.17) | collective-permute-done | bytes 262176 | tf_op jit(solution)/shard_map/to_scan/ppermute | solution.py:29
  44.8 1.0 %fork_states.1 = (bf16[2,1,4,128,128]{4,3,2,1,0:T(8,128)(2,1)S(1)}, bf16[2,1,4,128,128]{4,3,2,1,0:T(8,128)(2,1)S(1)}, bf16[2,1,4,128,128]{4,3,2,1,0:T(8,128)(2,1...) custom-call(s32[2,4]{1,0:T(2,128)S(1)} %pack_forks.1.refs_4_.refs_0_, ...), custom_call_target="tpu_custom_call", output_to_operand_aliasing={{4}: (5, {})} | custom-call | tf_op jit(solution)/shard_map/fork_states/pallas_call | solution.py:47
  45.8 1.6 %collective-permute-start.18 = (bf16[2,1,4,128,128]{4,3,2,1,0:T(8,128)(2,1)S(1)}, bf16[2,1,4,128,128]{4,3,2,1,0:T(8,128)(2,1)S(1)}, u32[]{:S(2)}, u32[]{:S(2)}) collective-permute-start(bf16[2,1,4,128,128]{4,3,2,1,0:T(8,128)(2,1)S(1)} %get-tuple-element.62), channel_id=1, source_target_pairs={{0,8},{8,0},{16,24},{24,16},{1,9},{9,1},{17,25},{25,17},{2,10},{10... | collective-permute-start | bytes 786440 | tf_op jit(solution)/shard_map/to_lane/ppermute | solution.py:22
  47.4 2.5 %collective-permute-start.19 = (bf16[2,1,4,128,128]{4,3,2,1,0:T(8,128)(2,1)S(1)}, bf16[2,1,4,128,128]{4,3,2,1,0:T(8,128)(2,1)S(1)}, u32[]{:S(2)}, u32[]{:S(2)}) collective-permute-start(bf16[2,1,4,128,128]{4,3,2,1,0:T(8,128)(2,1)S(1)} %get-tuple-element.63), channel_id=1, source_target_pairs={{0,24},{8,16},{16,8},{24,0},{1,25},{9,17},{17,9},{25,1},{2,26},{10... | collective-permute-start | bytes 786440 | tf_op jit(solution)/shard_map/to_lane/ppermute | solution.py:22
  49.9 0.1 collective-permute-start.22
  50.1 4.7 %branch_parts.1 = (bf16[2,2,256,512]{3,2,1,0:T(8,128)(2,1)S(1)}, f32[2,2,256,512]{3,2,1,0:T(8,128)S(1)}) custom-call(bf16[2,256,1024]{2,1,0:T(8,128)(2,1)S(1)} %bitcast.9, bf16[2,256,1024]{2,1,0:T(8,128)(2,1)S(1)} %bitcast.8, bf16[1,256,256]{2,1,0:T(8,128)(2,1)S(1)} %get-tuple-element.43.refs_2_, bf16[1,256,256]{2,1,0:T(8,128)(2,1)S(1)} %get-tuple-element.47.refs_3_, ...), custom_call_target="tpu_custom_call" | custom-call | flops 20000000000 | tf_op jit(solution)/shard_map/branch_parts/pallas_call | solution.py:47
  54.8 5.5 %collective-permute-done.20.refs_0_ = bf16[2,256,512]{2,1,0:T(8,128)(2,1)S(1)} collective-permute-done((bf16[2,256,512]{2,1,0:T(8,128)(2,1)S(1)}, bf16[2,256,512]{2,1,0:T(8,128)(2,1)S(1)}, u32[]{:S(2)}, u32[]{:S(2)}) %collective-permute-start.20) | collective-permute-done | bytes 524320 | tf_op jit(solution)/shard_map/to_out/ppermute | solution.py:29
  60.3 1.5 %collective-permute-start.25 = (bf16[2,256,512]{2,1,0:T(8,128)(2,1)S(1)}, bf16[2,256,512]{2,1,0:T(8,128)(2,1)S(1)}, u32[]{:S(2)}, u32[]{:S(2)}) collective-permute-start(bf16[2,256,512]{2,1,0:T(8,128)(2,1)S(1)} %get-tuple-element.71.refs_1_), channel_id=1, source_target_pairs={{0,2},{1,5},{2,0},{3,7},{4,6},{5,1},{6,4},{7,3},{8,10},{9,13},{10,... | collective-permute-start | bytes 1572872 | tf_op jit(solution)/shard_map/to_out_far/ppermute | solution.py:29
  61.8 0.7 norm_parts.2
  62.6 6.2 %collective-permute-done.22.refs_2_ = bf16[2,1,4,128,128]{4,3,2,1,0:T(8,128)(2,1)S(1)} collective-permute-done((bf16[2,1,4,128,128]{4,3,2,1,0:T(8,128)(2,1)S(1)}, bf16[2,1,4,128,128]{4,3,2,1,0:T(8,128)(2,1)S(1)}, u32[]{:S(2)}, u32[]{:S(2)}) %collective-permute-start.22) | collective-permute-done | bytes 262176 | tf_op jit(solution)/shard_map/to_lane/ppermute | solution.py:22
  68.8 0.4 norm_parts.3
  69.2 0.1 collective-permute-start.24
  69.3 0.2 collective-permute-done.25.refs_3_
  69.5 0.3 place_rows.1.refs_2_.refs_3_
  69.8 0.7 out_sum.1.refs_4_.refs_5_
  70.5 0.1 collective-permute-done.24.refs_2_
  70.6 2.1 %out_last.1 = bf16[4,128,1024]{2,1,0:T(8,128)(2,1)} custom-call(s32[4]{0:T(128)S(1)} %copy-done.3, bf16[3,128,512]{2,1,0:T(8,128)(2,1)S(1)} %collective-permute-done.21.refs_0_.refs_1_, bf16[1,128,512]{2,1,0:T(8,128)(2,1)S(1)} %collective-permute-done.24.refs_2_, bf16[1024,1024]{1,0:T(8,128)(2,1)S(1)} %place_rows.1.refs_2_.refs_3_, ...), custom_call_target="tpu_custom_call" | custom-call | tf_op jit(solution)/shard_map/out_last/pallas_call | solution.py:47
  (43 shorter events, 0.4 us)
Async XLA Ops:
  0.0 2.0 %collective-permute-start.1 = (bf16[128,1024]{1,0:T(8,128)(2,1)}, bf16[128,1024]{1,0:T(8,128)(2,1)S(1)}, u32[]{:S(2)}, u32[]{:S(2)}) collective-permute-start(bf16[128,1024]{1,0:T(8,128)(2,1)} %param.15), channel_id=1, source_target_pairs={{0,1},{1,0},{2,3},{3,2},{4,5},{5,4},{6,7},{7,6},{8,9},{9,8},{10,11... | collective-permute-start | bytes 786440 | tf_op jit(solution)/shard_map/to_core/ppermute | solution.py:22
  0.5 1.7 %collective-permute-start.2 = (bf16[128,1024]{1,0:T(8,128)(2,1)}, bf16[128,1024]{1,0:T(8,128)(2,1)S(1)}, u32[]{:S(2)}, u32[]{:S(2)}) collective-permute-start(bf16[128,1024]{1,0:T(8,128)(2,1)} %param.16), channel_id=1, source_target_pairs={{0,1},{1,0},{2,3},{3,2},{4,5},{5,4},{6,7},{7,6},{8,9},{9,8},{10,11... | collective-permute-start | bytes 786440 | tf_op jit(solution)/shard_map/to_core/ppermute | solution.py:22
  0.5 17.3 %collective-permute-start = (bf16[4,128,1024]{2,1,0:T(8,128)(2,1)}, bf16[4,128,1024]{2,1,0:T(8,128)(2,1)S(1)}, u32[]{:S(2)}, u32[]{:S(2)}) collective-permute-start(bf16[4,128,1024]{2,1,0:T(8,128)(2,1)} %param.10), channel_id=1, source_target_pairs={{0,1},{1,0},{2,3},{3,2},{4,5},{5,4},{6,7},{7,6},{8,9},{9,8},{10,11... | collective-permute-start | bytes 3145736 | tf_op jit(solution)/shard_map/to_tokens/ppermute | solution.py:22
  2.0 3.6 %copy-start = (bf16[2,256,1024]{2,1,0:T(8,128)(2,1)S(1)}, bf16[2,256,1024]{2,1,0:T(8,128)(2,1)}, u32[]{:S(2)}) copy-start(bf16[2,256,1024]{2,1,0:T(8,128)(2,1)} %refs_0_.8) | copy-start | bytes 3145732
  2.0 3.6 %copy-start.1 = (bf16[128,1024]{1,0:T(8,128)(2,1)S(1)}, bf16[128,1024]{1,0:T(8,128)(2,1)}, u32[]{:S(2)}) copy-start(bf16[128,1024]{1,0:T(8,128)(2,1)} %refs_0_.6) | copy-start | bytes 786436
  2.0 4.1 %copy-start.2 = (bf16[128,1024]{1,0:T(8,128)(2,1)S(1)}, bf16[128,1024]{1,0:T(8,128)(2,1)}, u32[]{:S(2)}) copy-start(bf16[128,1024]{1,0:T(8,128)(2,1)} %refs_1_.3) | copy-start | bytes 786436
  2.0 4.1 %copy-start.4 = (s32[1,1,4]{2,1,0:T(1,128)S(1)}, s32[1,1,4]{2,1,0:T(1,128)}, u32[]{:S(2)}) copy-start(s32[1,1,4]{2,1,0:T(1,128)} %refs_0_.5) | copy-start | bytes 52
  2.0 4.1 %copy-start.5 = (s32[1,1,4]{2,1,0:T(1,128)S(1)}, s32[1,1,4]{2,1,0:T(1,128)}, u32[]{:S(2)}) copy-start(s32[1,1,4]{2,1,0:T(1,128)} %refs_1_.2) | copy-start | bytes 52
  2.6 11.8 %collective-permute-start.3 = (bf16[2,256,512]{2,1,0:T(8,128)(2,1)S(1)}, bf16[2,256,512]{2,1,0:T(8,128)(2,1)S(1)}, u32[]{:S(2)}, u32[]{:S(2)}) collective-permute-start(bf16[2,256,512]{2,1,0:T(8,128)(2,1)S(1)} %chip_halves.2.refs_2_.refs_10_), channel_id=1, source_target_pairs={{0,4},{1,3},{2,6},{3,1},{4,0},{5,7},{6,2},{7,5},{8,12},{9,11},{10,... | collective-permute-start | bytes 1572872 | tf_op jit(solution)/shard_map/to_kv/ppermute | solution.py:29
  5.6 12.2 %collective-permute-start.8 = (bf16[2,256,1024]{2,1,0:T(8,128)(2,1)S(1)}, bf16[2,256,1024]{2,1,0:T(8,128)(2,1)S(1)}, u32[]{:S(2)}, u32[]{:S(2)}) collective-permute-start(bf16[2,256,1024]{2,1,0:T(8,128)(2,1)S(1)} %copy-done), channel_id=1, source_target_pairs={{0,1},{1,0},{2,3},{3,2},{4,5},{5,4},{6,7},{7,6},{8,9},{9,8},{10,11... | collective-permute-start | bytes 3145736 | tf_op jit(solution)/shard_map/to_tokens/ppermute | solution.py:22
  5.6 3.0 %collective-permute-start.4 = (bf16[128,1024]{1,0:T(8,128)(2,1)S(1)}, bf16[128,1024]{1,0:T(8,128)(2,1)S(1)}, u32[]{:S(2)}, u32[]{:S(2)}) collective-permute-start(bf16[128,1024]{1,0:T(8,128)(2,1)S(1)} %copy-done.1), channel_id=1, source_target_pairs={{0,1},{1,0},{2,3},{3,2},{4,5},{5,4},{6,7},{7,6},{8,9},{9,8},{10,11... | collective-permute-start | bytes 786440 | tf_op jit(solution)/shard_map/to_core/ppermute | solution.py:22
  6.1 4.0 %collective-permute-start.5 = (bf16[128,1024]{1,0:T(8,128)(2,1)S(1)}, bf16[128,1024]{1,0:T(8,128)(2,1)S(1)}, u32[]{:S(2)}, u32[]{:S(2)}) collective-permute-start(bf16[128,1024]{1,0:T(8,128)(2,1)S(1)} %copy-done.2), channel_id=1, source_target_pairs={{0,1},{1,0},{2,3},{3,2},{4,5},{5,4},{6,7},{7,6},{8,9},{9,8},{10,11... | collective-permute-start | bytes 786440 | tf_op jit(solution)/shard_map/to_core/ppermute | solution.py:22
  8.6 9.2 %collective-permute-start.9 = (bf16[2,256,512]{2,1,0:T(8,128)(2,1)S(1)}, bf16[2,256,512]{2,1,0:T(8,128)(2,1)S(1)}, u32[]{:S(2)}, u32[]{:S(2)}) collective-permute-start(bf16[2,256,512]{2,1,0:T(8,128)(2,1)S(1)} %chip_halves.2.refs_2_.refs_10_), channel_id=1, source_target_pairs={{0,2},{1,5},{2,0},{3,7},{4,6},{5,1},{6,4},{7,3},{8,10},{9,13},{10,... | collective-permute-start | bytes 1572872 | tf_op jit(solution)/shard_map/to_kv/ppermute | solution.py:29
  10.1 1.1 %collective-permute-start.6 = (s32[2,4]{1,0:T(2,128)S(1)}, s32[2,4]{1,0:T(2,128)S(1)}, u32[]{:S(2)}, u32[]{:S(2)}) collective-permute-start(s32[2,4]{1,0:T(2,128)S(1)} %pack_forks.1.refs_4_.refs_0_), channel_id=1, source_target_pairs={{0,1},{1,0},{2,3},{3,2},{4,5},{5,4},{6,7},{7,6},{8,9},{9,8},{10,11... | collective-permute-start | bytes 104 | tf_op jit(solution)/shard_map/to_forks/ppermute | solution.py:22
  14.4 9.3 %collective-permute-start.7 = (bf16[2,256,512]{2,1,0:T(8,128)(2,1)S(1)}, bf16[2,256,512]{2,1,0:T(8,128)(2,1)S(1)}, u32[]{:S(2)}, u32[]{:S(2)}) collective-permute-start(bf16[2,256,512]{2,1,0:T(8,128)(2,1)S(1)} %get-tuple-element.40.refs_3_.refs_11_), channel_id=1, source_target_pairs={{0,2},{1,5},{2,0},{3,7},{4,6},{5,1},{6,4},{7,3},{8,10},{9,13},{10,... | collective-permute-start | bytes 1572872 | tf_op jit(solution)/shard_map/to_kv_far/ppermute | solution.py:29
  23.7 6.5 %collective-permute-start.11 = (bf16[1,256,256]{2,1,0:T(8,128)(2,1)S(1)}, bf16[1,256,256]{2,1,0:T(8,128)(2,1)S(1)}, u32[]{:S(2)}, u32[]{:S(2)}) collective-permute-start(bf16[1,256,256]{2,1,0:T(8,128)(2,1)S(1)} %get-tuple-element.43.refs_2_), channel_id=1, source_target_pairs={{0,4},{1,3},{2,6},{3,1},{4,0},{5,7},{6,2},{7,5},{8,12},{9,11},{10,... | collective-permute-start | bytes 393224 | tf_op jit(solution)/shard_map/to_query/ppermute | solution.py:29
  26.2 5.9 %collective-permute-start.10 = (bf16[1,256,256]{2,1,0:T(8,128)(2,1)S(1)}, bf16[1,256,256]{2,1,0:T(8,128)(2,1)S(1)}, u32[]{:S(2)}, u32[]{:S(2)}) collective-permute-start(bf16[1,256,256]{2,1,0:T(8,128)(2,1)S(1)} %get-tuple-element.43.refs_2_), channel_id=1, source_target_pairs={{0,2},{1,5},{2,0},{3,7},{4,6},{5,1},{6,4},{7,3},{8,10},{9,13},{10,... | collective-permute-start | bytes 393224 | tf_op jit(solution)/shard_map/to_query/ppermute | solution.py:29
  29.8 8.4 %collective-permute-start.13 = (bf16[2,4,128,128]{3,2,1,0:T(8,128)(2,1)S(1)}, bf16[2,4,128,128]{3,2,1,0:T(8,128)(2,1)S(1)}, u32[]{:S(2)}, u32[]{:S(2)}) collective-permute-start(bf16[2,4,128,128]{3,2,1,0:T(8,128)(2,1)S(1)} %get-tuple-element.48), channel_id=1, source_target_pairs={{0,4},{1,3},{2,6},{3,1},{4,0},{5,7},{6,2},{7,5},{8,12},{9,11},{10,... | collective-permute-start | bytes 786440 | tf_op jit(solution)/shard_map/to_scan/ppermute | solution.py:29
  32.1 6.3 %collective-permute-start.12 = (bf16[1,256,256]{2,1,0:T(8,128)(2,1)S(1)}, bf16[1,256,256]{2,1,0:T(8,128)(2,1)S(1)}, u32[]{:S(2)}, u32[]{:S(2)}) collective-permute-start(bf16[1,256,256]{2,1,0:T(8,128)(2,1)S(1)} %get-tuple-element.47.refs_3_), channel_id=1, source_target_pairs={{0,2},{1,5},{2,0},{3,7},{4,6},{5,1},{6,4},{7,3},{8,10},{9,13},{10,... | collective-permute-start | bytes 393224 | tf_op jit(solution)/shard_map/to_query_far/ppermute | solution.py:29
  34.6 7.0 %collective-permute-start.14 = (bf16[1,256,256]{2,1,0:T(8,128)(2,1)S(1)}, bf16[1,256,256]{2,1,0:T(8,128)(2,1)S(1)}, u32[]{:S(2)}, u32[]{:S(2)}) collective-permute-start(bf16[1,256,256]{2,1,0:T(8,128)(2,1)S(1)} %get-tuple-element.47.refs_3_), channel_id=1, source_target_pairs={{0,8},{8,0},{16,24},{24,16},{1,9},{9,1},{17,25},{25,17},{2,10},{10... | collective-permute-start | bytes 393224 | tf_op jit(solution)/shard_map/to_query_lane/ppermute | solution.py:22
  36.2 6.2 %collective-permute-start.15 = (bf16[1,256,256]{2,1,0:T(8,128)(2,1)S(1)}, bf16[1,256,256]{2,1,0:T(8,128)(2,1)S(1)}, u32[]{:S(2)}, u32[]{:S(2)}) collective-permute-start(bf16[1,256,256]{2,1,0:T(8,128)(2,1)S(1)} %collective-permute-done.10.refs_0_.refs_4_), channel_id=1, source_target_pairs={{0,8},{8,0},{16,24},{24,16},{1,9},{9,1},{17,25},{25,17},{2,10},{10... | collective-permute-start | bytes 393224 | tf_op jit(solution)/shard_map/to_query_lane/ppermute | solution.py:22
  38.4 6.4 %collective-permute-start.17 = (bf16[2,4,128,128]{3,2,1,0:T(8,128)(2,1)S(1)}, bf16[2,4,128,128]{3,2,1,0:T(8,128)(2,1)S(1)}, u32[]{:S(2)}, u32[]{:S(2)}) collective-permute-start(bf16[2,4,128,128]{3,2,1,0:T(8,128)(2,1)S(1)} %scan_step.1.refs_1_), channel_id=1, source_target_pairs={{0,2},{1,5},{2,0},{3,7},{4,6},{5,1},{6,4},{7,3},{8,10},{9,13},{10,... | collective-permute-start | bytes 786440 | tf_op jit(solution)/shard_map/to_scan/ppermute | solution.py:29
  38.5 11.5 %collective-permute-start.16 = (bf16[1,256,256]{2,1,0:T(8,128)(2,1)S(1)}, bf16[1,256,256]{2,1,0:T(8,128)(2,1)S(1)}, u32[]{:S(2)}, u32[]{:S(2)}) collective-permute-start(bf16[1,256,256]{2,1,0:T(8,128)(2,1)S(1)} %get-tuple-element.50.refs_5_), channel_id=1, source_target_pairs={{0,8},{8,0},{16,24},{24,16},{1,9},{9,1},{17,25},{25,17},{2,10},{10... | collective-permute-start | bytes 393224 | tf_op jit(solution)/shard_map/to_query_lane/ppermute | solution.py:22
  42.4 7.7 %copy-start.6 = (bf16[4,128,1024]{2,1,0:T(8,128)(2,1)S(1)}, bf16[4,128,1024]{2,1,0:T(8,128)(2,1)}, u32[]{:S(2)}) copy-start(bf16[4,128,1024]{2,1,0:T(8,128)(2,1)} %param.10) | copy-start | bytes 3145732
  45.8 16.1 %collective-permute-start.18 = (bf16[2,1,4,128,128]{4,3,2,1,0:T(8,128)(2,1)S(1)}, bf16[2,1,4,128,128]{4,3,2,1,0:T(8,128)(2,1)S(1)}, u32[]{:S(2)}, u32[]{:S(2)}) collective-permute-start(bf16[2,1,4,128,128]{4,3,2,1,0:T(8,128)(2,1)S(1)} %get-tuple-element.62), channel_id=1, source_target_pairs={{0,8},{8,0},{16,24},{24,16},{1,9},{9,1},{17,25},{25,17},{2,10},{10... | collective-permute-start | bytes 786440 | tf_op jit(solution)/shard_map/to_lane/ppermute | solution.py:22
  47.4 14.4 %collective-permute-start.19 = (bf16[2,1,4,128,128]{4,3,2,1,0:T(8,128)(2,1)S(1)}, bf16[2,1,4,128,128]{4,3,2,1,0:T(8,128)(2,1)S(1)}, u32[]{:S(2)}, u32[]{:S(2)}) collective-permute-start(bf16[2,1,4,128,128]{4,3,2,1,0:T(8,128)(2,1)S(1)} %get-tuple-element.63), channel_id=1, source_target_pairs={{0,24},{8,16},{16,8},{24,0},{1,25},{9,17},{17,9},{25,1},{2,26},{10... | collective-permute-start | bytes 786440 | tf_op jit(solution)/shard_map/to_lane/ppermute | solution.py:22
  49.9 18.9 %collective-permute-start.22 = (bf16[2,1,4,128,128]{4,3,2,1,0:T(8,128)(2,1)S(1)}, bf16[2,1,4,128,128]{4,3,2,1,0:T(8,128)(2,1)S(1)}, u32[]{:S(2)}, u32[]{:S(2)}) collective-permute-start(bf16[2,1,4,128,128]{4,3,2,1,0:T(8,128)(2,1)S(1)} %get-tuple-element.67), channel_id=1, source_target_pairs={{0,16},{8,24},{16,0},{24,8},{1,17},{9,25},{17,1},{25,9},{2,18},{10... | collective-permute-start | bytes 786440 | tf_op jit(solution)/shard_map/to_lane/ppermute | solution.py:22
  50.0 12.6 %collective-permute-start.23 = (bf16[2,256,512]{2,1,0:T(8,128)(2,1)S(1)}, bf16[2,256,512]{2,1,0:T(8,128)(2,1)S(1)}, u32[]{:S(2)}, u32[]{:S(2)}) collective-permute-start(bf16[2,256,512]{2,1,0:T(8,128)(2,1)S(1)} %get-tuple-element.68.refs_0_), channel_id=1, source_target_pairs={{0,2},{1,5},{2,0},{3,7},{4,6},{5,1},{6,4},{7,3},{8,10},{9,13},{10,... | collective-permute-start | bytes 1572872 | tf_op jit(solution)/shard_map/to_out/ppermute | solution.py:29
  50.0 10.3 %collective-permute-start.20 = (bf16[2,256,512]{2,1,0:T(8,128)(2,1)S(1)}, bf16[2,256,512]{2,1,0:T(8,128)(2,1)S(1)}, u32[]{:S(2)}, u32[]{:S(2)}) collective-permute-start(bf16[2,256,512]{2,1,0:T(8,128)(2,1)S(1)} %get-tuple-element.64), channel_id=1, source_target_pairs={{0,4},{1,3},{2,6},{3,1},{4,0},{5,7},{6,2},{7,5},{8,12},{9,11},{10,... | collective-permute-start | bytes 1572872 | tf_op jit(solution)/shard_map/to_out/ppermute | solution.py:29
  60.3 9.2 %collective-permute-start.25 = (bf16[2,256,512]{2,1,0:T(8,128)(2,1)S(1)}, bf16[2,256,512]{2,1,0:T(8,128)(2,1)S(1)}, u32[]{:S(2)}, u32[]{:S(2)}) collective-permute-start(bf16[2,256,512]{2,1,0:T(8,128)(2,1)S(1)} %get-tuple-element.71.refs_1_), channel_id=1, source_target_pairs={{0,2},{1,5},{2,0},{3,7},{4,6},{5,1},{6,4},{7,3},{8,10},{9,13},{10,... | collective-permute-start | bytes 1572872 | tf_op jit(solution)/shard_map/to_out_far/ppermute | solution.py:29
  62.5 6.8 %collective-permute-start.21 = (bf16[3,128,512]{2,1,0:T(8,128)(2,1)S(1)}, bf16[3,128,512]{2,1,0:T(8,128)(2,1)S(1)}, u32[]{:S(2)}, u32[]{:S(2)}) collective-permute-start(bf16[3,128,512]{2,1,0:T(8,128)(2,1)S(1)} %get-tuple-element.66), channel_id=1, source_target_pairs={{0,1},{1,0},{2,3},{3,2},{4,5},{5,4},{6,7},{7,6},{8,9},{9,8},{10,11... | collective-permute-start | bytes 1179656 | tf_op jit(solution)/shard_map/to_normed/ppermute | solution.py:22
  69.2 1.4 %collective-permute-start.24 = (bf16[1,128,512]{2,1,0:T(8,128)(2,1)S(1)}, bf16[1,128,512]{2,1,0:T(8,128)(2,1)S(1)}, u32[]{:S(2)}, u32[]{:S(2)}) collective-permute-start(bf16[1,128,512]{2,1,0:T(8,128)(2,1)S(1)} %get-tuple-element.70), channel_id=1, source_target_pairs={{0,1},{1,0},{2,3},{3,2},{4,5},{5,4},{6,7},{7,6},{8,9},{9,8},{10,11... | collective-permute-start | bytes 393224 | tf_op jit(solution)/shard_map/to_normed/ppermute | solution.py:22
  69.8 0.9 %copy-start.3 = (s32[4]{0:T(128)S(1)}, s32[4]{0:T(128)}, u32[]{:S(2)}) copy-start(s32[4]{0:T(128)} %refs_0_.9) | copy-start | bytes 52

commit v6 on v5

--- a/solution.py
+++ b/solution.py
@@ -23,7 +23,7 @@
 
 
 def turn(value, step, bits, name):
-    bit = lambda i: bits[0] if (i % 2 == 1) == (step == 1) else bits[1]
+    bit = lambda i: bits[0] if (i % 2 == 0) == (step == 1) else bits[1]
     with jax.named_scope("to_" + name):
         count = lax.axis_size("trunk")
         return lax.ppermute(value, "trunk", [(i, i ^ bit(i)) for i in range(count)])
@@ -137,7 +137,7 @@
 
 
 def chip_after(steps):
-    first = jnp.where(core_index() == 1, 1, 2)
+    first = jnp.where(core_index() == 0, 1, 2)
     return chip_index() ^ (0, first, 3 - first, 3)[steps]
 
 
@@ -196,7 +196,7 @@
     xs, earlier, weights = refs[:2], refs[2 : 2 + count], refs[2 + count : -3 - 2 * parts]
     totals, firsts = refs[-3 - 2 * parts : -3 - parts], refs[-3 - parts : -3]
     keys_ref, values_ref, state_ref = refs[-3:]
-    sent = (core_index() == 1) | ((lax.axis_index("trunk") & mask) == 0)
+    sent = (core_index() == 0) | ((lax.axis_index("trunk") & mask) == 0)
     trees, heads = state_ref.shape[1:3]
     for side in range(2):
         for tree in range(trees):
@@ -279,7 +279,7 @@
 
 
 def scan_kernel(mask, count, *refs):
-    adds = (core_index() == 1) | ((lax.axis_index("trunk") & mask) == 0)
+    adds = (core_index() == 0) | ((lax.axis_index("trunk") & mask) == 0)
     for held_ref, in_ref, out_ref in zip(refs[:count], refs[count : 2 * count], refs[2 * count :]):
         held = held_ref[...].astype(F32)
         if mask:
@@ -311,7 +311,7 @@
             term = ref[...].astype(F32)
             counts = (index & mask) != 0
             if both:
-                counts = counts | (core_index() == 0)
+                counts = counts | (core_index() == 1)
             term = jnp.where(counts, term, jnp.zeros_like(term))
             carried = term if carried is None else carried + term
         carried_ref[:, part * heads : (part + 1) * heads] = carried

time: 72.8 us -> 72.8 us (level)
  no operation moved by 1% of the time
where the time goes in v6:
time: 72.8 us; the launch traced here: 72.7 us
  waiting for transfers between devices  31 us (43%)
  starting transfers between devices  24.9 us (34%)
  Pallas kernels  15.5 us (21%)
  local copies, waits for them, and re-layouts  1.03 us (1%)
    ppermute x11, waiting for transfers between devices, turn(): return lax.ppermute(value, 'trunk', [(i, i ^ bit(i)) for i in range(count)])  19.9 us
    pallas_call x24, Pallas kernels, call(): pl.pallas_call(body, out_shape=[*outs, *(shape_of(a.shape, a.dtype) for a...  15.5 us
    ppermute x11, starting transfers between devices, turn(): return lax.ppermute(value, 'trunk', [(i, i ^ bit(i)) for i in range(count)])  15.3 us
    ppermute x15, waiting for transfers between devices, swap(): lax.ppermute(value, axis, [(i, i ^ bit) for i in range(lax.axis_size(axis...  11.1 us
    ppermute x15, starting transfers between devices, swap(): lax.ppermute(value, axis, [(i, i ^ bit) for i in range(lax.axis_size(axis...  9.57 us
  transfers between devices with their start and end apart: 26, of which 15 were waited for; matrix products, arithmetic and copies ran while one was open for 1% of the time, Pallas kernels for 18%

profile of v6, /device:TPU:0, one launch (start us, length us, event | category | flops | bytes accessed | tf_op | source)
XLA Modules:
  0.0 72.7 jit_solution(11056147901476530999)
XLA Ops:
  0.0 0.5 collective-permute-start.1
  0.5 0.5 collective-permute-start
  1.0 1.0 %constant_dynamic-slice_fusion = (bf16[128,512]{1,0:T(8,128)(2,1)S(1)}, bf16[128,512]{1,0:T(8,128)(2,1)S(1)}) fusion(bf16[128,1024]{1,0:T(8,128)(2,1)} %param.16, s32[]{:T(128)S(6)} %select_n.14, bf16[128,1024]{1,0:T(8,128)(2,1)} %param.15), kind=kLoop, calls=%fused_computation | loop fusion | bytes 524292 | tf_op jit(solution)/shard_map/dynamic_slice | solution.py:530
  2.0 0.2 collective-permute-done.2.refs_3_
  2.2 0.4 chip_halves.2.refs_2_.refs_10_
  2.6 2.9 %collective-permute-start.3 = (bf16[2,256,512]{2,1,0:T(8,128)(2,1)S(1)}, bf16[2,256,512]{2,1,0:T(8,128)(2,1)S(1)}, u32[]{:S(2)}, u32[]{:S(2)}) collective-permute-start(bf16[2,256,512]{2,1,0:T(8,128)(2,1)S(1)} %chip_halves.2.refs_2_.refs_10_), channel_id=1, source_target_pairs={{0,2},{1,5},{2,0},{3,7},{4,6},{5,1},{6,4},{7,3},{8,10},{9,13},{10,... | collective-permute-start | bytes 1572872 | tf_op jit(solution)/shard_map/to_kv/ppermute | solution.py:29
  5.5 0.5 collective-permute-start.4
  6.1 2.4 %collective-permute-done.4.refs_2_ = bf16[128,1024]{1,0:T(8,128)(2,1)S(1)} collective-permute-done((bf16[128,1024]{1,0:T(8,128)(2,1)S(1)}, bf16[128,1024]{1,0:T(8,128)(2,1)S(1)}, u32[]{:S(2)}, u32[]{:S(2)}) %collective-permute-start.4) | collective-permute-done | bytes 262176 | tf_op jit(solution)/shard_map/to_core/ppermute | solution.py:22
  8.6 1.5 %collective-permute-start.9 = (bf16[2,256,512]{2,1,0:T(8,128)(2,1)S(1)}, bf16[2,256,512]{2,1,0:T(8,128)(2,1)S(1)}, u32[]{:S(2)}, u32[]{:S(2)}) collective-permute-start(bf16[2,256,512]{2,1,0:T(8,128)(2,1)S(1)} %chip_halves.2.refs_2_.refs_10_), channel_id=1, source_target_pairs={{0,4},{1,3},{2,6},{3,1},{4,0},{5,7},{6,2},{7,5},{8,12},{9,11},{10,... | collective-permute-start | bytes 1572872 | tf_op jit(solution)/shard_map/to_kv/ppermute | solution.py:29
  10.1 1.1 %collective-permute-done.6.refs_5_.refs_1_ = s32[2,4]{1,0:T(2,128)S(1)} collective-permute-done((s32[2,4]{1,0:T(2,128)S(1)}, s32[2,4]{1,0:T(2,128)S(1)}, u32[]{:S(2)}, u32[]{:S(2)}) %collective-permute-start.6) | collective-permute-done | bytes 64 | tf_op jit(solution)/shard_map/to_forks/ppermute | solution.py:22
  11.2 0.3 chip_halves.3
  11.6 2.8 %collective-permute-done.3.refs_0_ = bf16[2,256,512]{2,1,0:T(8,128)(2,1)S(1)} collective-permute-done((bf16[2,256,512]{2,1,0:T(8,128)(2,1)S(1)}, bf16[2,256,512]{2,1,0:T(8,128)(2,1)S(1)}, u32[]{:S(2)}, u32[]{:S(2)}) %collective-permute-start.3) | collective-permute-done | bytes 524320 | tf_op jit(solution)/shard_map/to_kv/ppermute | solution.py:29
  14.3 2.3 %collective-permute-start.7 = (bf16[2,256,512]{2,1,0:T(8,128)(2,1)S(1)}, bf16[2,256,512]{2,1,0:T(8,128)(2,1)S(1)}, u32[]{:S(2)}, u32[]{:S(2)}) collective-permute-start(bf16[2,256,512]{2,1,0:T(8,128)(2,1)S(1)} %get-tuple-element.40.refs_3_.refs_11_), channel_id=1, source_target_pairs={{0,4},{1,3},{2,6},{3,1},{4,0},{5,7},{6,2},{7,5},{8,12},{9,11},{10,... | collective-permute-start | bytes 1572872 | tf_op jit(solution)/shard_map/to_kv_far/ppermute | solution.py:29
  16.6 1.2 %collective-permute-done.9.refs_4_.refs_12_ = bf16[2,256,512]{2,1,0:T(8,128)(2,1)S(1)} collective-permute-done((bf16[2,256,512]{2,1,0:T(8,128)(2,1)S(1)}, bf16[2,256,512]{2,1,0:T(8,128)(2,1)S(1)}, u32[]{:S(2)}, u32[]{:S(2)}) %collective-permute-start.9) | collective-permute-done | bytes 524320 | tf_op jit(solution)/shard_map/to_kv/ppermute | solution.py:29
  17.8 1.8 %trunk_partial.1 = (f32[2,2,256,512]{3,2,1,0:T(8,128)S(1)}, f32[2,2,256,512]{3,2,1,0:T(8,128)S(1)}) custom-call(bf16[2,256,1024]{2,1,0:T(8,128)(2,1)S(1)} %copy-done, bf16[2,256,1024]{2,1,0:T(8,128)(2,1)S(1)} %collective-permute-done.8.refs_1_, bf16[2,256,512]{2,1,0:T(8,128)(2,1)S(1)} %chip_halves.2.refs_2_.refs_10_, ...), custom_call_target="tpu_custom_call" | custom-call | tf_op jit(solution)/shard_map/trunk_partial/pallas_call | solution.py:47
  19.6 4.2 %collective-permute-done.7.refs_0_.refs_4_.refs_13_ = bf16[2,256,512]{2,1,0:T(8,128)(2,1)S(1)} collective-permute-done((bf16[2,256,512]{2,1,0:T(8,128)(2,1)S(1)}, bf16[2,256,512]{2,1,0:T(8,128)(2,1)S(1)}, u32[]{:S(2)}, u32[]{:S(2)}) %collective-permute-start.7) | collective-permute-done | bytes 524320 | tf_op jit(solution)/shard_map/to_kv_far/ppermute | solution.py:29
  23.8 2.4 %collective-permute-start.11 = (bf16[1,256,256]{2,1,0:T(8,128)(2,1)S(1)}, bf16[1,256,256]{2,1,0:T(8,128)(2,1)S(1)}, u32[]{:S(2)}, u32[]{:S(2)}) collective-permute-start(bf16[1,256,256]{2,1,0:T(8,128)(2,1)S(1)} %get-tuple-element.43.refs_2_), channel_id=1, source_target_pairs={{0,2},{1,5},{2,0},{3,7},{4,6},{5,1},{6,4},{7,3},{8,10},{9,13},{10,... | collective-permute-start | bytes 393224 | tf_op jit(solution)/shard_map/to_query/ppermute | solution.py:29
  26.2 2.0 %collective-permute-start.10 = (bf16[1,256,256]{2,1,0:T(8,128)(2,1)S(1)}, bf16[1,256,256]{2,1,0:T(8,128)(2,1)S(1)}, u32[]{:S(2)}, u32[]{:S(2)}) collective-permute-start(bf16[1,256,256]{2,1,0:T(8,128)(2,1)S(1)} %get-tuple-element.43.refs_2_), channel_id=1, source_target_pairs={{0,4},{1,3},{2,6},{3,1},{4,0},{5,7},{6,2},{7,5},{8,12},{9,11},{10,... | collective-permute-start | bytes 393224 | tf_op jit(solution)/shard_map/to_query/ppermute | solution.py:29
  28.2 1.6 %trunk_states.1 = (bf16[2,4,128,128]{3,2,1,0:T(8,128)(2,1)S(1)}, bf16[2,4,128,128]{3,2,1,0:T(8,128)(2,1)S(1)}, bf16[2,2,256,512]{3,2,1,0:T(8,128)(2,1)S(1)}, bf1...) custom-call(bf16[2,256,1024]{2,1,0:T(8,128)(2,1)S(1)} %copy-done, ...), custom_call_target="tpu_custom_call" | custom-call | tf_op jit(solution)/shard_map/trunk_states/pallas_call | solution.py:47
  29.8 0.1 collective-permute-start.13
  29.9 0.3 collective-permute-done.11.refs_1_
  30.2 1.9 %collective-permute-done.10.refs_0_.refs_4_ = bf16[1,256,256]{2,1,0:T(8,128)(2,1)S(1)} collective-permute-done((bf16[1,256,256]{2,1,0:T(8,128)(2,1)S(1)}, bf16[1,256,256]{2,1,0:T(8,128)(2,1)S(1)}, u32[]{:S(2)}, u32[]{:S(2)}) %collective-permute-start.10) | collective-permute-done | bytes 131104 | tf_op jit(solution)/shard_map/to_query/ppermute | solution.py:29
  32.1 2.5 %collective-permute-start.12 = (bf16[1,256,256]{2,1,0:T(8,128)(2,1)S(1)}, bf16[1,256,256]{2,1,0:T(8,128)(2,1)S(1)}, u32[]{:S(2)}, u32[]{:S(2)}) collective-permute-start(bf16[1,256,256]{2,1,0:T(8,128)(2,1)S(1)} %get-tuple-element.47.refs_3_), channel_id=1, source_target_pairs={{0,4},{1,3},{2,6},{3,1},{4,0},{5,7},{6,2},{7,5},{8,12},{9,11},{10,... | collective-permute-start | bytes 393224 | tf_op jit(solution)/shard_map/to_query_far/ppermute | solution.py:29
  34.6 1.6 %collective-permute-start.14 = (bf16[1,256,256]{2,1,0:T(8,128)(2,1)S(1)}, bf16[1,256,256]{2,1,0:T(8,128)(2,1)S(1)}, u32[]{:S(2)}, u32[]{:S(2)}) collective-permute-start(bf16[1,256,256]{2,1,0:T(8,128)(2,1)S(1)} %get-tuple-element.47.refs_3_), channel_id=1, source_target_pairs={{0,8},{8,0},{16,24},{24,16},{1,9},{9,1},{17,25},{25,17},{2,10},{10... | collective-permute-start | bytes 393224 | tf_op jit(solution)/shard_map/to_query_lane/ppermute | solution.py:22
  36.2 0.4 collective-permute-start.15
  36.6 1.6 %collective-permute-done.13.refs_1_.refs_3_ = bf16[2,4,128,128]{3,2,1,0:T(8,128)(2,1)S(1)} collective-permute-done((bf16[2,4,128,128]{3,2,1,0:T(8,128)(2,1)S(1)}, bf16[2,4,128,128]{3,2,1,0:T(8,128)(2,1)S(1)}, u32[]{:S(2)}, u32[]{:S(2)}) %collective-permute-start.13) | collective-permute-done | bytes 262176 | tf_op jit(solution)/shard_map/to_scan/ppermute | solution.py:29
  38.2 0.1 scan_step.1.refs_1_
  38.3 0.1 collective-permute-start.17
  38.4 1.6 %collective-permute-start.16 = (bf16[1,256,256]{2,1,0:T(8,128)(2,1)S(1)}, bf16[1,256,256]{2,1,0:T(8,128)(2,1)S(1)}, u32[]{:S(2)}, u32[]{:S(2)}) collective-permute-start(bf16[1,256,256]{2,1,0:T(8,128)(2,1)S(1)} %get-tuple-element.50.refs_5_), channel_id=1, source_target_pairs={{0,8},{8,0},{16,24},{24,16},{1,9},{9,1},{17,25},{25,17},{2,10},{10... | collective-permute-start | bytes 393224 | tf_op jit(solution)/shard_map/to_query_lane/ppermute | solution.py:22
  40.1 1.4 %fork_parts.1.refs_2_ = f32[2,4,4,128,128]{4,3,2,1,0:T(8,128)S(1)} custom-call(s32[2,4]{1,0:T(2,128)S(1)} %pack_forks.1.refs_4_.refs_0_, s32[2,4]{1,0:T(2,128)S(1)} %collective-permute-done.6.refs_5_.refs_1_, bf16[2,2,256,512]{3,2,1,0:T(8,128)(2,1)S(1)} %get-tuple-element.53.refs_2_, bf16[2,2,256,512]{3,2,1,0:T(8,128)(2,1)S(1)} %get-tuple-element.54.refs_3_, ...), custom_call_target="tpu_custom_call" | custom-call | tf_op jit(solution)/shard_map/fork_parts/pallas_call | solution.py:47
  41.5 0.9 %collective-permute-done.15.refs_1_.refs_8_ = bf16[1,256,256]{2,1,0:T(8,128)(2,1)S(1)} collective-permute-done((bf16[1,256,256]{2,1,0:T(8,128)(2,1)S(1)}, bf16[1,256,256]{2,1,0:T(8,128)(2,1)S(1)}, u32[]{:S(2)}, u32[]{:S(2)}) %collective-permute-start.15) | collective-permute-done | bytes 131104 | tf_op jit(solution)/shard_map/to_query_lane/ppermute | solution.py:22
  42.4 2.4 %collective-permute-done.17.refs_4_ = bf16[2,4,128,128]{3,2,1,0:T(8,128)(2,1)S(1)} collective-permute-done((bf16[2,4,128,128]{3,2,1,0:T(8,128)(2,1)S(1)}, bf16[2,4,128,128]{3,2,1,0:T(8,128)(2,1)S(1)}, u32[]{:S(2)}, u32[]{:S(2)}) %collective-permute-start.17) | collective-permute-done | bytes 262176 | tf_op jit(solution)/shard_map/to_scan/ppermute | solution.py:29
  44.8 1.0 %fork_states.1 = (bf16[2,1,4,128,128]{4,3,2,1,0:T(8,128)(2,1)S(1)}, bf16[2,1,4,128,128]{4,3,2,1,0:T(8,128)(2,1)S(1)}, bf16[2,1,4,128,128]{4,3,2,1,0:T(8,128)(2,1...) custom-call(s32[2,4]{1,0:T(2,128)S(1)} %pack_forks.1.refs_4_.refs_0_, ...), custom_call_target="tpu_custom_call", output_to_operand_aliasing={{4}: (5, {})} | custom-call | tf_op jit(solution)/shard_map/fork_states/pallas_call | solution.py:47
  45.7 1.6 %collective-permute-start.18 = (bf16[2,1,4,128,128]{4,3,2,1,0:T(8,128)(2,1)S(1)}, bf16[2,1,4,128,128]{4,3,2,1,0:T(8,128)(2,1)S(1)}, u32[]{:S(2)}, u32[]{:S(2)}) collective-permute-start(bf16[2,1,4,128,128]{4,3,2,1,0:T(8,128)(2,1)S(1)} %get-tuple-element.62), channel_id=1, source_target_pairs={{0,8},{8,0},{16,24},{24,16},{1,9},{9,1},{17,25},{25,17},{2,10},{10... | collective-permute-start | bytes 786440 | tf_op jit(solution)/shard_map/to_lane/ppermute | solution.py:22
  47.4 2.5 %collective-permute-start.19 = (bf16[2,1,4,128,128]{4,3,2,1,0:T(8,128)(2,1)S(1)}, bf16[2,1,4,128,128]{4,3,2,1,0:T(8,128)(2,1)S(1)}, u32[]{:S(2)}, u32[]{:S(2)}) collective-permute-start(bf16[2,1,4,128,128]{4,3,2,1,0:T(8,128)(2,1)S(1)} %get-tuple-element.63), channel_id=1, source_target_pairs={{0,24},{8,16},{16,8},{24,0},{1,25},{9,17},{17,9},{25,1},{2,26},{10... | collective-permute-start | bytes 786440 | tf_op jit(solution)/shard_map/to_lane/ppermute | solution.py:22
  49.8 0.1 collective-permute-start.22
  50.0 4.8 %branch_parts.1 = (bf16[2,2,256,512]{3,2,1,0:T(8,128)(2,1)S(1)}, f32[2,2,256,512]{3,2,1,0:T(8,128)S(1)}) custom-call(bf16[2,256,1024]{2,1,0:T(8,128)(2,1)S(1)} %bitcast.9, bf16[2,256,1024]{2,1,0:T(8,128)(2,1)S(1)} %bitcast.8, bf16[1,256,256]{2,1,0:T(8,128)(2,1)S(1)} %get-tuple-element.43.refs_2_, bf16[1,256,256]{2,1,0:T(8,128)(2,1)S(1)} %get-tuple-element.47.refs_3_, ...), custom_call_target="tpu_custom_call" | custom-call | flops 20000000000 | tf_op jit(solution)/shard_map/branch_parts/pallas_call | solution.py:47
  54.8 5.4 %collective-permute-done.20.refs_0_ = bf16[2,256,512]{2,1,0:T(8,128)(2,1)S(1)} collective-permute-done((bf16[2,256,512]{2,1,0:T(8,128)(2,1)S(1)}, bf16[2,256,512]{2,1,0:T(8,128)(2,1)S(1)}, u32[]{:S(2)}, u32[]{:S(2)}) %collective-permute-start.20) | collective-permute-done | bytes 524320 | tf_op jit(solution)/shard_map/to_out/ppermute | solution.py:29
  60.2 1.4 %collective-permute-start.25 = (bf16[2,256,512]{2,1,0:T(8,128)(2,1)S(1)}, bf16[2,256,512]{2,1,0:T(8,128)(2,1)S(1)}, u32[]{:S(2)}, u32[]{:S(2)}) collective-permute-start(bf16[2,256,512]{2,1,0:T(8,128)(2,1)S(1)} %get-tuple-element.71.refs_1_), channel_id=1, source_target_pairs={{0,4},{1,3},{2,6},{3,1},{4,0},{5,7},{6,2},{7,5},{8,12},{9,11},{10,... | collective-permute-start | bytes 1572872 | tf_op jit(solution)/shard_map/to_out_far/ppermute | solution.py:29
  61.7 0.7 norm_parts.2
  62.4 0.1 collective-permute-start.21
  62.5 6.3 %collective-permute-done.22.refs_2_ = bf16[2,1,4,128,128]{4,3,2,1,0:T(8,128)(2,1)S(1)} collective-permute-done((bf16[2,1,4,128,128]{4,3,2,1,0:T(8,128)(2,1)S(1)}, bf16[2,1,4,128,128]{4,3,2,1,0:T(8,128)(2,1)S(1)}, u32[]{:S(2)}, u32[]{:S(2)}) %collective-permute-start.22) | collective-permute-done | bytes 262176 | tf_op jit(solution)/shard_map/to_lane/ppermute | solution.py:22
  68.8 0.4 norm_parts.3
  69.3 0.1 collective-permute-done.25.refs_3_
  69.4 0.3 place_rows.1.refs_2_.refs_3_
  69.7 0.7 out_sum.1.refs_4_.refs_5_
  70.4 0.2 collective-permute-done.24.refs_2_
  70.6 2.1 %out_last.1 = bf16[4,128,1024]{2,1,0:T(8,128)(2,1)} custom-call(s32[4]{0:T(128)S(1)} %copy-done.3, bf16[3,128,512]{2,1,0:T(8,128)(2,1)S(1)} %collective-permute-done.21.refs_0_.refs_1_, bf16[1,128,512]{2,1,0:T(8,128)(2,1)S(1)} %collective-permute-done.24.refs_2_, bf16[1024,1024]{1,0:T(8,128)(2,1)S(1)} %place_rows.1.refs_2_.refs_3_, ...), custom_call_target="tpu_custom_call" | custom-call | tf_op jit(solution)/shard_map/out_last/pallas_call | solution.py:47
  (43 shorter events, 0.4 us)
Async XLA Ops:
  0.0 2.0 %collective-permute-start.1 = (bf16[128,1024]{1,0:T(8,128)(2,1)}, bf16[128,1024]{1,0:T(8,128)(2,1)S(1)}, u32[]{:S(2)}, u32[]{:S(2)}) collective-permute-start(bf16[128,1024]{1,0:T(8,128)(2,1)} %param.15), channel_id=1, source_target_pairs={{0,1},{1,0},{2,3},{3,2},{4,5},{5,4},{6,7},{7,6},{8,9},{9,8},{10,11... | collective-permute-start | bytes 786440 | tf_op jit(solution)/shard_map/to_core/ppermute | solution.py:22
  0.5 1.7 %collective-permute-start.2 = (bf16[128,1024]{1,0:T(8,128)(2,1)}, bf16[128,1024]{1,0:T(8,128)(2,1)S(1)}, u32[]{:S(2)}, u32[]{:S(2)}) collective-permute-start(bf16[128,1024]{1,0:T(8,128)(2,1)} %param.16), channel_id=1, source_target_pairs={{0,1},{1,0},{2,3},{3,2},{4,5},{5,4},{6,7},{7,6},{8,9},{9,8},{10,11... | collective-permute-start | bytes 786440 | tf_op jit(solution)/shard_map/to_core/ppermute | solution.py:22
  0.5 17.3 %collective-permute-start = (bf16[4,128,1024]{2,1,0:T(8,128)(2,1)}, bf16[4,128,1024]{2,1,0:T(8,128)(2,1)S(1)}, u32[]{:S(2)}, u32[]{:S(2)}) collective-permute-start(bf16[4,128,1024]{2,1,0:T(8,128)(2,1)} %param.10), channel_id=1, source_target_pairs={{0,1},{1,0},{2,3},{3,2},{4,5},{5,4},{6,7},{7,6},{8,9},{9,8},{10,11... | collective-permute-start | bytes 3145736 | tf_op jit(solution)/shard_map/to_tokens/ppermute | solution.py:22
  2.0 3.6 %copy-start = (bf16[2,256,1024]{2,1,0:T(8,128)(2,1)S(1)}, bf16[2,256,1024]{2,1,0:T(8,128)(2,1)}, u32[]{:S(2)}) copy-start(bf16[2,256,1024]{2,1,0:T(8,128)(2,1)} %refs_0_.8) | copy-start | bytes 3145732
  2.0 3.6 %copy-start.1 = (bf16[128,1024]{1,0:T(8,128)(2,1)S(1)}, bf16[128,1024]{1,0:T(8,128)(2,1)}, u32[]{:S(2)}) copy-start(bf16[128,1024]{1,0:T(8,128)(2,1)} %refs_0_.6) | copy-start | bytes 786436
  2.0 4.1 %copy-start.2 = (bf16[128,1024]{1,0:T(8,128)(2,1)S(1)}, bf16[128,1024]{1,0:T(8,128)(2,1)}, u32[]{:S(2)}) copy-start(bf16[128,1024]{1,0:T(8,128)(2,1)} %refs_1_.3) | copy-start | bytes 786436
  2.0 4.1 %copy-start.4 = (s32[1,1,4]{2,1,0:T(1,128)S(1)}, s32[1,1,4]{2,1,0:T(1,128)}, u32[]{:S(2)}) copy-start(s32[1,1,4]{2,1,0:T(1,128)} %refs_0_.5) | copy-start | bytes 52
  2.0 4.1 %copy-start.5 = (s32[1,1,4]{2,1,0:T(1,128)S(1)}, s32[1,1,4]{2,1,0:T(1,128)}, u32[]{:S(2)}) copy-start(s32[1,1,4]{2,1,0:T(1,128)} %refs_1_.2) | copy-start | bytes 52
  2.6 11.7 %collective-permute-start.3 = (bf16[2,256,512]{2,1,0:T(8,128)(2,1)S(1)}, bf16[2,256,512]{2,1,0:T(8,128)(2,1)S(1)}, u32[]{:S(2)}, u32[]{:S(2)}) collective-permute-start(bf16[2,256,512]{2,1,0:T(8,128)(2,1)S(1)} %chip_halves.2.refs_2_.refs_10_), channel_id=1, source_target_pairs={{0,2},{1,5},{2,0},{3,7},{4,6},{5,1},{6,4},{7,3},{8,10},{9,13},{10,... | collective-permute-start | bytes 1572872 | tf_op jit(solution)/shard_map/to_kv/ppermute | solution.py:29
  5.5 12.3 %collective-permute-start.8 = (bf16[2,256,1024]{2,1,0:T(8,128)(2,1)S(1)}, bf16[2,256,1024]{2,1,0:T(8,128)(2,1)S(1)}, u32[]{:S(2)}, u32[]{:S(2)}) collective-permute-start(bf16[2,256,1024]{2,1,0:T(8,128)(2,1)S(1)} %copy-done), channel_id=1, source_target_pairs={{0,1},{1,0},{2,3},{3,2},{4,5},{5,4},{6,7},{7,6},{8,9},{9,8},{10,11... | collective-permute-start | bytes 3145736 | tf_op jit(solution)/shard_map/to_tokens/ppermute | solution.py:22
  5.5 3.0 %collective-permute-start.4 = (bf16[128,1024]{1,0:T(8,128)(2,1)S(1)}, bf16[128,1024]{1,0:T(8,128)(2,1)S(1)}, u32[]{:S(2)}, u32[]{:S(2)}) collective-permute-start(bf16[128,1024]{1,0:T(8,128)(2,1)S(1)} %copy-done.1), channel_id=1, source_target_pairs={{0,1},{1,0},{2,3},{3,2},{4,5},{5,4},{6,7},{7,6},{8,9},{9,8},{10,11... | collective-permute-start | bytes 786440 | tf_op jit(solution)/shard_map/to_core/ppermute | solution.py:22
  6.0 4.0 %collective-permute-start.5 = (bf16[128,1024]{1,0:T(8,128)(2,1)S(1)}, bf16[128,1024]{1,0:T(8,128)(2,1)S(1)}, u32[]{:S(2)}, u32[]{:S(2)}) collective-permute-start(bf16[128,1024]{1,0:T(8,128)(2,1)S(1)} %copy-done.2), channel_id=1, source_target_pairs={{0,1},{1,0},{2,3},{3,2},{4,5},{5,4},{6,7},{7,6},{8,9},{9,8},{10,11... | collective-permute-start | bytes 786440 | tf_op jit(solution)/shard_map/to_core/ppermute | solution.py:22
  8.6 9.2 %collective-permute-start.9 = (bf16[2,256,512]{2,1,0:T(8,128)(2,1)S(1)}, bf16[2,256,512]{2,1,0:T(8,128)(2,1)S(1)}, u32[]{:S(2)}, u32[]{:S(2)}) collective-permute-start(bf16[2,256,512]{2,1,0:T(8,128)(2,1)S(1)} %chip_halves.2.refs_2_.refs_10_), channel_id=1, source_target_pairs={{0,4},{1,3},{2,6},{3,1},{4,0},{5,7},{6,2},{7,5},{8,12},{9,11},{10,... | collective-permute-start | bytes 1572872 | tf_op jit(solution)/shard_map/to_kv/ppermute | solution.py:29
  10.1 1.1 %collective-permute-start.6 = (s32[2,4]{1,0:T(2,128)S(1)}, s32[2,4]{1,0:T(2,128)S(1)}, u32[]{:S(2)}, u32[]{:S(2)}) collective-permute-start(s32[2,4]{1,0:T(2,128)S(1)} %pack_forks.1.refs_4_.refs_0_), channel_id=1, source_target_pairs={{0,1},{1,0},{2,3},{3,2},{4,5},{5,4},{6,7},{7,6},{8,9},{9,8},{10,11... | collective-permute-start | bytes 104 | tf_op jit(solution)/shard_map/to_forks/ppermute | solution.py:22
  14.3 9.4 %collective-permute-start.7 = (bf16[2,256,512]{2,1,0:T(8,128)(2,1)S(1)}, bf16[2,256,512]{2,1,0:T(8,128)(2,1)S(1)}, u32[]{:S(2)}, u32[]{:S(2)}) collective-permute-start(bf16[2,256,512]{2,1,0:T(8,128)(2,1)S(1)} %get-tuple-element.40.refs_3_.refs_11_), channel_id=1, source_target_pairs={{0,4},{1,3},{2,6},{3,1},{4,0},{5,7},{6,2},{7,5},{8,12},{9,11},{10,... | collective-permute-start | bytes 1572872 | tf_op jit(solution)/shard_map/to_kv_far/ppermute | solution.py:29
  23.8 6.4 %collective-permute-start.11 = (bf16[1,256,256]{2,1,0:T(8,128)(2,1)S(1)}, bf16[1,256,256]{2,1,0:T(8,128)(2,1)S(1)}, u32[]{:S(2)}, u32[]{:S(2)}) collective-permute-start(bf16[1,256,256]{2,1,0:T(8,128)(2,1)S(1)} %get-tuple-element.43.refs_2_), channel_id=1, source_target_pairs={{0,2},{1,5},{2,0},{3,7},{4,6},{5,1},{6,4},{7,3},{8,10},{9,13},{10,... | collective-permute-start | bytes 393224 | tf_op jit(solution)/shard_map/to_query/ppermute | solution.py:29
  26.2 5.9 %collective-permute-start.10 = (bf16[1,256,256]{2,1,0:T(8,128)(2,1)S(1)}, bf16[1,256,256]{2,1,0:T(8,128)(2,1)S(1)}, u32[]{:S(2)}, u32[]{:S(2)}) collective-permute-start(bf16[1,256,256]{2,1,0:T(8,128)(2,1)S(1)} %get-tuple-element.43.refs_2_), channel_id=1, source_target_pairs={{0,4},{1,3},{2,6},{3,1},{4,0},{5,7},{6,2},{7,5},{8,12},{9,11},{10,... | collective-permute-start | bytes 393224 | tf_op jit(solution)/shard_map/to_query/ppermute | solution.py:29
  29.8 8.4 %collective-permute-start.13 = (bf16[2,4,128,128]{3,2,1,0:T(8,128)(2,1)S(1)}, bf16[2,4,128,128]{3,2,1,0:T(8,128)(2,1)S(1)}, u32[]{:S(2)}, u32[]{:S(2)}) collective-permute-start(bf16[2,4,128,128]{3,2,1,0:T(8,128)(2,1)S(1)} %get-tuple-element.48), channel_id=1, source_target_pairs={{0,2},{1,5},{2,0},{3,7},{4,6},{5,1},{6,4},{7,3},{8,10},{9,13},{10,... | collective-permute-start | bytes 786440 | tf_op jit(solution)/shard_map/to_scan/ppermute | solution.py:29
  32.1 6.3 %collective-permute-start.12 = (bf16[1,256,256]{2,1,0:T(8,128)(2,1)S(1)}, bf16[1,256,256]{2,1,0:T(8,128)(2,1)S(1)}, u32[]{:S(2)}, u32[]{:S(2)}) collective-permute-start(bf16[1,256,256]{2,1,0:T(8,128)(2,1)S(1)} %get-tuple-element.47.refs_3_), channel_id=1, source_target_pairs={{0,4},{1,3},{2,6},{3,1},{4,0},{5,7},{6,2},{7,5},{8,12},{9,11},{10,... | collective-permute-start | bytes 393224 | tf_op jit(solution)/shard_map/to_query_far/ppermute | solution.py:29
  34.6 6.9 %collective-permute-start.14 = (bf16[1,256,256]{2,1,0:T(8,128)(2,1)S(1)}, bf16[1,256,256]{2,1,0:T(8,128)(2,1)S(1)}, u32[]{:S(2)}, u32[]{:S(2)}) collective-permute-start(bf16[1,256,256]{2,1,0:T(8,128)(2,1)S(1)} %get-tuple-element.47.refs_3_), channel_id=1, source_target_pairs={{0,8},{8,0},{16,24},{24,16},{1,9},{9,1},{17,25},{25,17},{2,10},{10... | collective-permute-start | bytes 393224 | tf_op jit(solution)/shard_map/to_query_lane/ppermute | solution.py:22
  36.2 6.2 %collective-permute-start.15 = (bf16[1,256,256]{2,1,0:T(8,128)(2,1)S(1)}, bf16[1,256,256]{2,1,0:T(8,128)(2,1)S(1)}, u32[]{:S(2)}, u32[]{:S(2)}) collective-permute-start(bf16[1,256,256]{2,1,0:T(8,128)(2,1)S(1)} %collective-permute-done.10.refs_0_.refs_4_), channel_id=1, source_target_pairs={{0,8},{8,0},{16,24},{24,16},{1,9},{9,1},{17,25},{25,17},{2,10},{10... | collective-permute-start | bytes 393224 | tf_op jit(solution)/shard_map/to_query_lane/ppermute | solution.py:22
  38.3 6.4 %collective-permute-start.17 = (bf16[2,4,128,128]{3,2,1,0:T(8,128)(2,1)S(1)}, bf16[2,4,128,128]{3,2,1,0:T(8,128)(2,1)S(1)}, u32[]{:S(2)}, u32[]{:S(2)}) collective-permute-start(bf16[2,4,128,128]{3,2,1,0:T(8,128)(2,1)S(1)} %scan_step.1.refs_1_), channel_id=1, source_target_pairs={{0,4},{1,3},{2,6},{3,1},{4,0},{5,7},{6,2},{7,5},{8,12},{9,11},{10,... | collective-permute-start | bytes 786440 | tf_op jit(solution)/shard_map/to_scan/ppermute | solution.py:29
  38.4 11.5 %collective-permute-start.16 = (bf16[1,256,256]{2,1,0:T(8,128)(2,1)S(1)}, bf16[1,256,256]{2,1,0:T(8,128)(2,1)S(1)}, u32[]{:S(2)}, u32[]{:S(2)}) collective-permute-start(bf16[1,256,256]{2,1,0:T(8,128)(2,1)S(1)} %get-tuple-element.50.refs_5_), channel_id=1, source_target_pairs={{0,8},{8,0},{16,24},{24,16},{1,9},{9,1},{17,25},{25,17},{2,10},{10... | collective-permute-start | bytes 393224 | tf_op jit(solution)/shard_map/to_query_lane/ppermute | solution.py:22
  42.4 7.7 %copy-start.6 = (bf16[4,128,1024]{2,1,0:T(8,128)(2,1)S(1)}, bf16[4,128,1024]{2,1,0:T(8,128)(2,1)}, u32[]{:S(2)}) copy-start(bf16[4,128,1024]{2,1,0:T(8,128)(2,1)} %param.10) | copy-start | bytes 3145732
  45.7 16.0 %collective-permute-start.18 = (bf16[2,1,4,128,128]{4,3,2,1,0:T(8,128)(2,1)S(1)}, bf16[2,1,4,128,128]{4,3,2,1,0:T(8,128)(2,1)S(1)}, u32[]{:S(2)}, u32[]{:S(2)}) collective-permute-start(bf16[2,1,4,128,128]{4,3,2,1,0:T(8,128)(2,1)S(1)} %get-tuple-element.62), channel_id=1, source_target_pairs={{0,8},{8,0},{16,24},{24,16},{1,9},{9,1},{17,25},{25,17},{2,10},{10... | collective-permute-start | bytes 786440 | tf_op jit(solution)/shard_map/to_lane/ppermute | solution.py:22
  47.4 14.3 %collective-permute-start.19 = (bf16[2,1,4,128,128]{4,3,2,1,0:T(8,128)(2,1)S(1)}, bf16[2,1,4,128,128]{4,3,2,1,0:T(8,128)(2,1)S(1)}, u32[]{:S(2)}, u32[]{:S(2)}) collective-permute-start(bf16[2,1,4,128,128]{4,3,2,1,0:T(8,128)(2,1)S(1)} %get-tuple-element.63), channel_id=1, source_target_pairs={{0,24},{8,16},{16,8},{24,0},{1,25},{9,17},{17,9},{25,1},{2,26},{10... | collective-permute-start | bytes 786440 | tf_op jit(solution)/shard_map/to_lane/ppermute | solution.py:22
  49.8 19.0 %collective-permute-start.22 = (bf16[2,1,4,128,128]{4,3,2,1,0:T(8,128)(2,1)S(1)}, bf16[2,1,4,128,128]{4,3,2,1,0:T(8,128)(2,1)S(1)}, u32[]{:S(2)}, u32[]{:S(2)}) collective-permute-start(bf16[2,1,4,128,128]{4,3,2,1,0:T(8,128)(2,1)S(1)} %get-tuple-element.67), channel_id=1, source_target_pairs={{0,16},{8,24},{16,0},{24,8},{1,17},{9,25},{17,1},{25,9},{2,18},{10... | collective-permute-start | bytes 786440 | tf_op jit(solution)/shard_map/to_lane/ppermute | solution.py:22
  50.0 12.5 %collective-permute-start.23 = (bf16[2,256,512]{2,1,0:T(8,128)(2,1)S(1)}, bf16[2,256,512]{2,1,0:T(8,128)(2,1)S(1)}, u32[]{:S(2)}, u32[]{:S(2)}) collective-permute-start(bf16[2,256,512]{2,1,0:T(8,128)(2,1)S(1)} %get-tuple-element.68.refs_0_), channel_id=1, source_target_pairs={{0,4},{1,3},{2,6},{3,1},{4,0},{5,7},{6,2},{7,5},{8,12},{9,11},{10,... | collective-permute-start | bytes 1572872 | tf_op jit(solution)/shard_map/to_out/ppermute | solution.py:29
  50.0 10.3 %collective-permute-start.20 = (bf16[2,256,512]{2,1,0:T(8,128)(2,1)S(1)}, bf16[2,256,512]{2,1,0:T(8,128)(2,1)S(1)}, u32[]{:S(2)}, u32[]{:S(2)}) collective-permute-start(bf16[2,256,512]{2,1,0:T(8,128)(2,1)S(1)} %get-tuple-element.64), channel_id=1, source_target_pairs={{0,2},{1,5},{2,0},{3,7},{4,6},{5,1},{6,4},{7,3},{8,10},{9,13},{10,... | collective-permute-start | bytes 1572872 | tf_op jit(solution)/shard_map/to_out/ppermute | solution.py:29
  60.2 9.2 %collective-permute-start.25 = (bf16[2,256,512]{2,1,0:T(8,128)(2,1)S(1)}, bf16[2,256,512]{2,1,0:T(8,128)(2,1)S(1)}, u32[]{:S(2)}, u32[]{:S(2)}) collective-permute-start(bf16[2,256,512]{2,1,0:T(8,128)(2,1)S(1)} %get-tuple-element.71.refs_1_), channel_id=1, source_target_pairs={{0,4},{1,3},{2,6},{3,1},{4,0},{5,7},{6,2},{7,5},{8,12},{9,11},{10,... | collective-permute-start | bytes 1572872 | tf_op jit(solution)/shard_map/to_out_far/ppermute | solution.py:29
  62.4 6.9 %collective-permute-start.21 = (bf16[3,128,512]{2,1,0:T(8,128)(2,1)S(1)}, bf16[3,128,512]{2,1,0:T(8,128)(2,1)S(1)}, u32[]{:S(2)}, u32[]{:S(2)}) collective-permute-start(bf16[3,128,512]{2,1,0:T(8,128)(2,1)S(1)} %get-tuple-element.66), channel_id=1, source_target_pairs={{0,1},{1,0},{2,3},{3,2},{4,5},{5,4},{6,7},{7,6},{8,9},{9,8},{10,11... | collective-permute-start | bytes 1179656 | tf_op jit(solution)/shard_map/to_normed/ppermute | solution.py:22
  69.2 1.4 %collective-permute-start.24 = (bf16[1,128,512]{2,1,0:T(8,128)(2,1)S(1)}, bf16[1,128,512]{2,1,0:T(8,128)(2,1)S(1)}, u32[]{:S(2)}, u32[]{:S(2)}) collective-permute-start(bf16[1,128,512]{2,1,0:T(8,128)(2,1)S(1)} %get-tuple-element.70), channel_id=1, source_target_pairs={{0,1},{1,0},{2,3},{3,2},{4,5},{5,4},{6,7},{7,6},{8,9},{9,8},{10,11... | collective-permute-start | bytes 393224 | tf_op jit(solution)/shard_map/to_normed/ppermute | solution.py:22
  69.7 0.9 %copy-start.3 = (s32[4]{0:T(128)S(1)}, s32[4]{0:T(128)}, u32[]{:S(2)}) copy-start(s32[4]{0:T(128)} %refs_0_.9) | copy-start | bytes 52

commit v7 on v6

--- a/solution.py
+++ b/solution.py
@@ -421,13 +421,13 @@
     core = core_index()
     sources, out_ref, sem = refs[:-2], refs[-2], refs[-1]
     copies = []
-    for slot, number, index, steps in picks:
+    for slot, number, index, steps, quarter in picks:
         source = sources[number].at[index] if index else sources[number]
-        rows, half = source.shape
-        first = (core if slot == 0 else 1 - core) * half
+        rows, part = source.shape
+        first = (core if slot == 0 else 1 - core) * (out_ref.shape[1] // 2) + quarter * part
         target = out_ref.at[
             pl.ds(pl.multiple_of(chip_after(steps) * rows, rows), rows),
-            pl.ds(pl.multiple_of(first, half), half),
+            pl.ds(pl.multiple_of(first, part), part),
         ]
         copies.append(pltpu.make_async_copy(source, target, sem.at[len(copies)]))
     for copy in copies:
@@ -543,7 +543,7 @@
             (2, [(0, "even", True)]),
             (2, [(0, "odd", True)]),
             (1, [(1, 0, True), (1, 0, False)]),
-            (1, [(1, 0, True), (1, 0, False)]),
+            (2, [(1, 0, True), (1, 1, True), (1, 0, False)]),
         ]
         own_q, other_q, own_o, again_o = chip_halves(qo, qo_other, chosen, order=order, landed=[forks[1]])
         _, near[1] = chain([], through=[near[1]])
@@ -590,19 +590,25 @@
     if paired:
         held_o = turn(sends[lanes], 1, bits, "out")
         _, again_o = chain([last_q], through=[again_o])
-        near_o = [again_o, held_o, turn(again_o, 2, bits, "out")]
+        near_o = [sends[lanes], held_o, turn(again_o, 2, bits, "out")]
     q, intra = branch_parts(
         branch_tokens, branch_other, queries, pair, paired, order=order, weight=20.0
     )
     if paired:
         _, near_o[1] = chain([], through=[held_o])
-        outs = send_far(near_o, near_o[1], bits, "out")
+        far_o = turn(near_o[1], 2, bits, "out_far")
+        crossed = swap(near_o[1], "trunk", 1, "out_core")
+        late = (0, slice(None), slice(near_o[1].shape[2] // 2, None))
+        outs = [*near_o, far_o, crossed], [
+            [(0, (0,), 0, 0), (1, (0,), 1, 0), (2, (0,), 2, 0), (2, (1,), 2, 1), (3, (0,), 3, 0)],
+            [(0, (1,), 0, 0), (1, (1,), 1, 0), (2, (2,), 2, 0), (4, late, 2, 1), (3, (1,), 3, 0)],
+        ]
     aparts = sorted(range(lanes), key=lambda a: a == 2)
     split = [aparts[:-1], aparts[-1:]] if lanes > 1 else [aparts]
     mine, other = [], []
+    if paired:
+        chain(near_o[2:3], weight=1.0)
     for part in split:
-        if mine and paired:
-            chain(near_o[2:3], weight=1.0)
         own, theirs = norm_parts(q, intra, received, part, order=order, weight=4.0 if mine else 0.5)
         mine.append(own)
         other.append(swap(theirs, "trunk", 1, "normed"))

time: 72.8 us -> 72.8 us (level)
    ppermute x11, waiting for transfers between devices: 19.9 us -> 18.7 us  [turn(): return lax.ppermute(value, 'trunk', [(i, i ^ bit(i)) for i in range(count)])]
    ppermute x15 -> x16, waiting for transfers between devices: 11.1 us -> 11.6 us  [swap(): lax.ppermute(value, axis, [(i, i ^ bit) for i in range(lax.axis_size(axis...]
    ppermute x15 -> x16, starting transfers between devices: 9.57 us -> 9.58 us  [swap(): lax.ppermute(value, axis, [(i, i ^ bit) for i in range(lax.axis_size(axis...]
  transfers between devices with their start and end apart: 26 -> 27, of which waited for: 15 -> 14; matrix products, arithmetic and copies ran while one was open for 1% -> 1% of each run, Pallas kernels for 18% -> 18%
where the time goes in v7:
time: 72.8 us; the launch traced here: 72.7 us
  waiting for transfers between devices  30.4 us (42%)
  starting transfers between devices  25.5 us (35%)
  Pallas kernels  15.5 us (21%)
  local copies, waits for them, and re-layouts  1.03 us (1%)
    ppermute x11, waiting for transfers between devices, turn(): return lax.ppermute(value, 'trunk', [(i, i ^ bit(i)) for i in range(count)])  18.7 us
    ppermute x11, starting transfers between devices, turn(): return lax.ppermute(value, 'trunk', [(i, i ^ bit(i)) for i in range(count)])  15.9 us
    pallas_call x24, Pallas kernels, call(): pl.pallas_call(body, out_shape=[*outs, *(shape_of(a.shape, a.dtype) for a...  15.5 us
    ppermute x16, waiting for transfers between devices, swap(): lax.ppermute(value, axis, [(i, i ^ bit) for i in range(lax.axis_size(axis...  11.6 us
    ppermute x16, starting transfers between devices, swap(): lax.ppermute(value, axis, [(i, i ^ bit) for i in range(lax.axis_size(axis...  9.58 us
  transfers between devices with their start and end apart: 27, of which 14 were waited for; matrix products, arithmetic and copies ran while one was open for 1% of the time, Pallas kernels for 18%

profile of v7, /device:TPU:0, one launch (start us, length us, event | category | flops | bytes accessed | tf_op | source)
XLA Modules:
  0.0 72.7 jit_solution(7592299772595282617)
XLA Ops:
  0.0 0.5 collective-permute-start.1
  0.5 0.5 collective-permute-start
  1.0 1.0 %constant_dynamic-slice_fusion = (bf16[128,512]{1,0:T(8,128)(2,1)S(1)}, bf16[128,512]{1,0:T(8,128)(2,1)S(1)}) fusion(bf16[128,1024]{1,0:T(8,128)(2,1)} %param.16, s32[]{:T(128)S(6)} %select_n.14, bf16[128,1024]{1,0:T(8,128)(2,1)} %param.15), kind=kLoop, calls=%fused_computation | loop fusion | bytes 524292 | tf_op jit(solution)/shard_map/dynamic_slice | solution.py:530
  2.0 0.2 collective-permute-done.2.refs_3_
  2.2 0.4 chip_halves.2.refs_2_.refs_10_
  2.6 2.9 %collective-permute-start.3 = (bf16[2,256,512]{2,1,0:T(8,128)(2,1)S(1)}, bf16[2,256,512]{2,1,0:T(8,128)(2,1)S(1)}, u32[]{:S(2)}, u32[]{:S(2)}) collective-permute-start(bf16[2,256,512]{2,1,0:T(8,128)(2,1)S(1)} %chip_halves.2.refs_2_.refs_10_), channel_id=1, source_target_pairs={{0,2},{1,5},{2,0},{3,7},{4,6},{5,1},{6,4},{7,3},{8,10},{9,13},{10,... | collective-permute-start | bytes 1572872 | tf_op jit(solution)/shard_map/to_kv/ppermute | solution.py:29
  5.5 0.5 collective-permute-start.4
  6.1 2.4 %collective-permute-done.4.refs_2_ = bf16[128,1024]{1,0:T(8,128)(2,1)S(1)} collective-permute-done((bf16[128,1024]{1,0:T(8,128)(2,1)S(1)}, bf16[128,1024]{1,0:T(8,128)(2,1)S(1)}, u32[]{:S(2)}, u32[]{:S(2)}) %collective-permute-start.4) | collective-permute-done | bytes 262176 | tf_op jit(solution)/shard_map/to_core/ppermute | solution.py:22
  8.6 1.5 %collective-permute-start.9 = (bf16[2,256,512]{2,1,0:T(8,128)(2,1)S(1)}, bf16[2,256,512]{2,1,0:T(8,128)(2,1)S(1)}, u32[]{:S(2)}, u32[]{:S(2)}) collective-permute-start(bf16[2,256,512]{2,1,0:T(8,128)(2,1)S(1)} %chip_halves.2.refs_2_.refs_10_), channel_id=1, source_target_pairs={{0,4},{1,3},{2,6},{3,1},{4,0},{5,7},{6,2},{7,5},{8,12},{9,11},{10,... | collective-permute-start | bytes 1572872 | tf_op jit(solution)/shard_map/to_kv/ppermute | solution.py:29
  10.1 1.1 %collective-permute-done.6.refs_5_.refs_1_ = s32[2,4]{1,0:T(2,128)S(1)} collective-permute-done((s32[2,4]{1,0:T(2,128)S(1)}, s32[2,4]{1,0:T(2,128)S(1)}, u32[]{:S(2)}, u32[]{:S(2)}) %collective-permute-start.6) | collective-permute-done | bytes 64 | tf_op jit(solution)/shard_map/to_forks/ppermute | solution.py:22
  11.2 0.3 chip_halves.3
  11.6 2.8 %collective-permute-done.3.refs_0_ = bf16[2,256,512]{2,1,0:T(8,128)(2,1)S(1)} collective-permute-done((bf16[2,256,512]{2,1,0:T(8,128)(2,1)S(1)}, bf16[2,256,512]{2,1,0:T(8,128)(2,1)S(1)}, u32[]{:S(2)}, u32[]{:S(2)}) %collective-permute-start.3) | collective-permute-done | bytes 524320 | tf_op jit(solution)/shard_map/to_kv/ppermute | solution.py:29
  14.3 2.3 %collective-permute-start.7 = (bf16[2,256,512]{2,1,0:T(8,128)(2,1)S(1)}, bf16[2,256,512]{2,1,0:T(8,128)(2,1)S(1)}, u32[]{:S(2)}, u32[]{:S(2)}) collective-permute-start(bf16[2,256,512]{2,1,0:T(8,128)(2,1)S(1)} %get-tuple-element.40.refs_3_.refs_11_), channel_id=1, source_target_pairs={{0,4},{1,3},{2,6},{3,1},{4,0},{5,7},{6,2},{7,5},{8,12},{9,11},{10,... | collective-permute-start | bytes 1572872 | tf_op jit(solution)/shard_map/to_kv_far/ppermute | solution.py:29
  16.6 1.2 %collective-permute-done.9.refs_4_.refs_12_ = bf16[2,256,512]{2,1,0:T(8,128)(2,1)S(1)} collective-permute-done((bf16[2,256,512]{2,1,0:T(8,128)(2,1)S(1)}, bf16[2,256,512]{2,1,0:T(8,128)(2,1)S(1)}, u32[]{:S(2)}, u32[]{:S(2)}) %collective-permute-start.9) | collective-permute-done | bytes 524320 | tf_op jit(solution)/shard_map/to_kv/ppermute | solution.py:29
  17.8 1.8 %trunk_partial.1 = (f32[2,2,256,512]{3,2,1,0:T(8,128)S(1)}, f32[2,2,256,512]{3,2,1,0:T(8,128)S(1)}) custom-call(bf16[2,256,1024]{2,1,0:T(8,128)(2,1)S(1)} %copy-done, bf16[2,256,1024]{2,1,0:T(8,128)(2,1)S(1)} %collective-permute-done.8.refs_1_, bf16[2,256,512]{2,1,0:T(8,128)(2,1)S(1)} %chip_halves.2.refs_2_.refs_10_, ...), custom_call_target="tpu_custom_call" | custom-call | tf_op jit(solution)/shard_map/trunk_partial/pallas_call | solution.py:47
  19.6 4.2 %collective-permute-done.7.refs_0_.refs_4_.refs_13_ = bf16[2,256,512]{2,1,0:T(8,128)(2,1)S(1)} collective-permute-done((bf16[2,256,512]{2,1,0:T(8,128)(2,1)S(1)}, bf16[2,256,512]{2,1,0:T(8,128)(2,1)S(1)}, u32[]{:S(2)}, u32[]{:S(2)}) %collective-permute-start.7) | collective-permute-done | bytes 524320 | tf_op jit(solution)/shard_map/to_kv_far/ppermute | solution.py:29
  23.8 2.4 %collective-permute-start.11 = (bf16[1,256,256]{2,1,0:T(8,128)(2,1)S(1)}, bf16[1,256,256]{2,1,0:T(8,128)(2,1)S(1)}, u32[]{:S(2)}, u32[]{:S(2)}) collective-permute-start(bf16[1,256,256]{2,1,0:T(8,128)(2,1)S(1)} %get-tuple-element.43.refs_2_), channel_id=1, source_target_pairs={{0,2},{1,5},{2,0},{3,7},{4,6},{5,1},{6,4},{7,3},{8,10},{9,13},{10,... | collective-permute-start | bytes 393224 | tf_op jit(solution)/shard_map/to_query/ppermute | solution.py:29
  26.2 2.0 %collective-permute-start.10 = (bf16[1,256,256]{2,1,0:T(8,128)(2,1)S(1)}, bf16[1,256,256]{2,1,0:T(8,128)(2,1)S(1)}, u32[]{:S(2)}, u32[]{:S(2)}) collective-permute-start(bf16[1,256,256]{2,1,0:T(8,128)(2,1)S(1)} %get-tuple-element.43.refs_2_), channel_id=1, source_target_pairs={{0,4},{1,3},{2,6},{3,1},{4,0},{5,7},{6,2},{7,5},{8,12},{9,11},{10,... | collective-permute-start | bytes 393224 | tf_op jit(solution)/shard_map/to_query/ppermute | solution.py:29
  28.2 1.6 %trunk_states.1 = (bf16[2,4,128,128]{3,2,1,0:T(8,128)(2,1)S(1)}, bf16[2,4,128,128]{3,2,1,0:T(8,128)(2,1)S(1)}, bf16[2,2,256,512]{3,2,1,0:T(8,128)(2,1)S(1)}, bf1...) custom-call(bf16[2,256,1024]{2,1,0:T(8,128)(2,1)S(1)} %copy-done, ...), custom_call_target="tpu_custom_call" | custom-call | tf_op jit(solution)/shard_map/trunk_states/pallas_call | solution.py:47
  29.8 0.1 collective-permute-start.13
  29.9 0.3 collective-permute-done.11.refs_1_
  30.2 1.9 %collective-permute-done.10.refs_0_.refs_4_ = bf16[1,256,256]{2,1,0:T(8,128)(2,1)S(1)} collective-permute-done((bf16[1,256,256]{2,1,0:T(8,128)(2,1)S(1)}, bf16[1,256,256]{2,1,0:T(8,128)(2,1)S(1)}, u32[]{:S(2)}, u32[]{:S(2)}) %collective-permute-start.10) | collective-permute-done | bytes 131104 | tf_op jit(solution)/shard_map/to_query/ppermute | solution.py:29
  32.1 2.5 %collective-permute-start.12 = (bf16[1,256,256]{2,1,0:T(8,128)(2,1)S(1)}, bf16[1,256,256]{2,1,0:T(8,128)(2,1)S(1)}, u32[]{:S(2)}, u32[]{:S(2)}) collective-permute-start(bf16[1,256,256]{2,1,0:T(8,128)(2,1)S(1)} %get-tuple-element.47.refs_3_), channel_id=1, source_target_pairs={{0,4},{1,3},{2,6},{3,1},{4,0},{5,7},{6,2},{7,5},{8,12},{9,11},{10,... | collective-permute-start | bytes 393224 | tf_op jit(solution)/shard_map/to_query_far/ppermute | solution.py:29
  34.6 1.6 %collective-permute-start.14 = (bf16[1,256,256]{2,1,0:T(8,128)(2,1)S(1)}, bf16[1,256,256]{2,1,0:T(8,128)(2,1)S(1)}, u32[]{:S(2)}, u32[]{:S(2)}) collective-permute-start(bf16[1,256,256]{2,1,0:T(8,128)(2,1)S(1)} %get-tuple-element.47.refs_3_), channel_id=1, source_target_pairs={{0,8},{8,0},{16,24},{24,16},{1,9},{9,1},{17,25},{25,17},{2,10},{10... | collective-permute-start | bytes 393224 | tf_op jit(solution)/shard_map/to_query_lane/ppermute | solution.py:22
  36.2 0.4 collective-permute-start.15
  36.6 1.6 %collective-permute-done.13.refs_1_.refs_3_ = bf16[2,4,128,128]{3,2,1,0:T(8,128)(2,1)S(1)} collective-permute-done((bf16[2,4,128,128]{3,2,1,0:T(8,128)(2,1)S(1)}, bf16[2,4,128,128]{3,2,1,0:T(8,128)(2,1)S(1)}, u32[]{:S(2)}, u32[]{:S(2)}) %collective-permute-start.13) | collective-permute-done | bytes 262176 | tf_op jit(solution)/shard_map/to_scan/ppermute | solution.py:29
  38.2 0.1 scan_step.1.refs_1_
  38.3 0.1 collective-permute-start.17
  38.4 1.6 %collective-permute-start.16 = (bf16[1,256,256]{2,1,0:T(8,128)(2,1)S(1)}, bf16[1,256,256]{2,1,0:T(8,128)(2,1)S(1)}, u32[]{:S(2)}, u32[]{:S(2)}) collective-permute-start(bf16[1,256,256]{2,1,0:T(8,128)(2,1)S(1)} %get-tuple-element.50.refs_5_), channel_id=1, source_target_pairs={{0,8},{8,0},{16,24},{24,16},{1,9},{9,1},{17,25},{25,17},{2,10},{10... | collective-permute-start | bytes 393224 | tf_op jit(solution)/shard_map/to_query_lane/ppermute | solution.py:22
  40.1 1.4 %fork_parts.1.refs_2_ = f32[2,4,4,128,128]{4,3,2,1,0:T(8,128)S(1)} custom-call(s32[2,4]{1,0:T(2,128)S(1)} %pack_forks.1.refs_4_.refs_0_, s32[2,4]{1,0:T(2,128)S(1)} %collective-permute-done.6.refs_5_.refs_1_, bf16[2,2,256,512]{3,2,1,0:T(8,128)(2,1)S(1)} %get-tuple-element.53.refs_2_, bf16[2,2,256,512]{3,2,1,0:T(8,128)(2,1)S(1)} %get-tuple-element.54.refs_3_, ...), custom_call_target="tpu_custom_call" | custom-call | tf_op jit(solution)/shard_map/fork_parts/pallas_call | solution.py:47
  41.5 0.9 %collective-permute-done.15.refs_1_.refs_8_ = bf16[1,256,256]{2,1,0:T(8,128)(2,1)S(1)} collective-permute-done((bf16[1,256,256]{2,1,0:T(8,128)(2,1)S(1)}, bf16[1,256,256]{2,1,0:T(8,128)(2,1)S(1)}, u32[]{:S(2)}, u32[]{:S(2)}) %collective-permute-start.15) | collective-permute-done | bytes 131104 | tf_op jit(solution)/shard_map/to_query_lane/ppermute | solution.py:22
  42.4 2.4 %collective-permute-done.17.refs_4_ = bf16[2,4,128,128]{3,2,1,0:T(8,128)(2,1)S(1)} collective-permute-done((bf16[2,4,128,128]{3,2,1,0:T(8,128)(2,1)S(1)}, bf16[2,4,128,128]{3,2,1,0:T(8,128)(2,1)S(1)}, u32[]{:S(2)}, u32[]{:S(2)}) %collective-permute-start.17) | collective-permute-done | bytes 262176 | tf_op jit(solution)/shard_map/to_scan/ppermute | solution.py:29
  44.8 1.0 %fork_states.1 = (bf16[2,1,4,128,128]{4,3,2,1,0:T(8,128)(2,1)S(1)}, bf16[2,1,4,128,128]{4,3,2,1,0:T(8,128)(2,1)S(1)}, bf16[2,1,4,128,128]{4,3,2,1,0:T(8,128)(2,1...) custom-call(s32[2,4]{1,0:T(2,128)S(1)} %pack_forks.1.refs_4_.refs_0_, ...), custom_call_target="tpu_custom_call", output_to_operand_aliasing={{4}: (5, {})} | custom-call | tf_op jit(solution)/shard_map/fork_states/pallas_call | solution.py:47
  45.7 1.6 %collective-permute-start.18 = (bf16[2,1,4,128,128]{4,3,2,1,0:T(8,128)(2,1)S(1)}, bf16[2,1,4,128,128]{4,3,2,1,0:T(8,128)(2,1)S(1)}, u32[]{:S(2)}, u32[]{:S(2)}) collective-permute-start(bf16[2,1,4,128,128]{4,3,2,1,0:T(8,128)(2,1)S(1)} %get-tuple-element.62), channel_id=1, source_target_pairs={{0,8},{8,0},{16,24},{24,16},{1,9},{9,1},{17,25},{25,17},{2,10},{10... | collective-permute-start | bytes 786440 | tf_op jit(solution)/shard_map/to_lane/ppermute | solution.py:22
  47.4 2.5 %collective-permute-start.19 = (bf16[2,1,4,128,128]{4,3,2,1,0:T(8,128)(2,1)S(1)}, bf16[2,1,4,128,128]{4,3,2,1,0:T(8,128)(2,1)S(1)}, u32[]{:S(2)}, u32[]{:S(2)}) collective-permute-start(bf16[2,1,4,128,128]{4,3,2,1,0:T(8,128)(2,1)S(1)} %get-tuple-element.63), channel_id=1, source_target_pairs={{0,24},{8,16},{16,8},{24,0},{1,25},{9,17},{17,9},{25,1},{2,26},{10... | collective-permute-start | bytes 786440 | tf_op jit(solution)/shard_map/to_lane/ppermute | solution.py:22
  49.8 0.1 collective-permute-start.23
  50.0 4.7 %branch_parts.1 = (bf16[2,2,256,512]{3,2,1,0:T(8,128)(2,1)S(1)}, f32[2,2,256,512]{3,2,1,0:T(8,128)S(1)}) custom-call(bf16[2,256,1024]{2,1,0:T(8,128)(2,1)S(1)} %bitcast.9, bf16[2,256,1024]{2,1,0:T(8,128)(2,1)S(1)} %bitcast.8, bf16[1,256,256]{2,1,0:T(8,128)(2,1)S(1)} %get-tuple-element.43.refs_2_, bf16[1,256,256]{2,1,0:T(8,128)(2,1)S(1)} %get-tuple-element.47.refs_3_, ...), custom_call_target="tpu_custom_call" | custom-call | flops 20000000000 | tf_op jit(solution)/shard_map/branch_parts/pallas_call | solution.py:47
  54.8 4.4 %collective-permute-done.21.refs_0_ = bf16[2,256,512]{2,1,0:T(8,128)(2,1)S(1)} collective-permute-done((bf16[2,256,512]{2,1,0:T(8,128)(2,1)S(1)}, bf16[2,256,512]{2,1,0:T(8,128)(2,1)S(1)}, u32[]{:S(2)}, u32[]{:S(2)}) %collective-permute-start.21) | collective-permute-done | bytes 524320 | tf_op jit(solution)/shard_map/to_out/ppermute | solution.py:29
  59.2 2.0 %collective-permute-start.25 = (bf16[2,256,512]{2,1,0:T(8,128)(2,1)S(1)}, bf16[2,256,512]{2,1,0:T(8,128)(2,1)S(1)}, u32[]{:S(2)}, u32[]{:S(2)}) collective-permute-start(bf16[2,256,512]{2,1,0:T(8,128)(2,1)S(1)} %get-tuple-element.71.refs_1_), channel_id=1, source_target_pairs={{0,4},{1,3},{2,6},{3,1},{4,0},{5,7},{6,2},{7,5},{8,12},{9,11},{10,... | collective-permute-start | bytes 1572872 | tf_op jit(solution)/shard_map/to_out_far/ppermute | solution.py:29
  61.2 0.7 norm_parts.2
  62.0 0.1 collective-permute-start.22
  62.0 6.8 %collective-permute-done.23.refs_2_ = bf16[2,1,4,128,128]{4,3,2,1,0:T(8,128)(2,1)S(1)} collective-permute-done((bf16[2,1,4,128,128]{4,3,2,1,0:T(8,128)(2,1)S(1)}, bf16[2,1,4,128,128]{4,3,2,1,0:T(8,128)(2,1)S(1)}, u32[]{:S(2)}, u32[]{:S(2)}) %collective-permute-start.23) | collective-permute-done | bytes 262176 | tf_op jit(solution)/shard_map/to_lane/ppermute | solution.py:22
  68.8 0.4 norm_parts.3
  69.2 0.1 collective-permute-start.24
  69.3 0.3 place_rows.1.refs_2_.refs_3_
  69.6 0.7 out_sum.1.refs_4_.refs_5_
  70.4 0.2 collective-permute-done.24.refs_2_
  70.6 2.1 %out_last.1 = bf16[4,128,1024]{2,1,0:T(8,128)(2,1)} custom-call(s32[4]{0:T(128)S(1)} %copy-done.3, bf16[3,128,512]{2,1,0:T(8,128)(2,1)S(1)} %collective-permute-done.22.refs_0_.refs_1_, bf16[1,128,512]{2,1,0:T(8,128)(2,1)S(1)} %collective-permute-done.24.refs_2_, bf16[1024,1024]{1,0:T(8,128)(2,1)S(1)} %place_rows.1.refs_2_.refs_3_, ...), custom_call_target="tpu_custom_call" | custom-call | tf_op jit(solution)/shard_map/out_last/pallas_call | solution.py:47
  (45 shorter events, 0.3 us)
Async XLA Ops:
  0.0 2.0 %collective-permute-start.1 = (bf16[128,1024]{1,0:T(8,128)(2,1)}, bf16[128,1024]{1,0:T(8,128)(2,1)S(1)}, u32[]{:S(2)}, u32[]{:S(2)}) collective-permute-start(bf16[128,1024]{1,0:T(8,128)(2,1)} %param.15), channel_id=1, source_target_pairs={{0,1},{1,0},{2,3},{3,2},{4,5},{5,4},{6,7},{7,6},{8,9},{9,8},{10,11... | collective-permute-start | bytes 786440 | tf_op jit(solution)/shard_map/to_core/ppermute | solution.py:22
  0.5 1.7 %collective-permute-start.2 = (bf16[128,1024]{1,0:T(8,128)(2,1)}, bf16[128,1024]{1,0:T(8,128)(2,1)S(1)}, u32[]{:S(2)}, u32[]{:S(2)}) collective-permute-start(bf16[128,1024]{1,0:T(8,128)(2,1)} %param.16), channel_id=1, source_target_pairs={{0,1},{1,0},{2,3},{3,2},{4,5},{5,4},{6,7},{7,6},{8,9},{9,8},{10,11... | collective-permute-start | bytes 786440 | tf_op jit(solution)/shard_map/to_core/ppermute | solution.py:22
  0.5 17.3 %collective-permute-start = (bf16[4,128,1024]{2,1,0:T(8,128)(2,1)}, bf16[4,128,1024]{2,1,0:T(8,128)(2,1)S(1)}, u32[]{:S(2)}, u32[]{:S(2)}) collective-permute-start(bf16[4,128,1024]{2,1,0:T(8,128)(2,1)} %param.10), channel_id=1, source_target_pairs={{0,1},{1,0},{2,3},{3,2},{4,5},{5,4},{6,7},{7,6},{8,9},{9,8},{10,11... | collective-permute-start | bytes 3145736 | tf_op jit(solution)/shard_map/to_tokens/ppermute | solution.py:22
  2.0 3.6 %copy-start = (bf16[2,256,1024]{2,1,0:T(8,128)(2,1)S(1)}, bf16[2,256,1024]{2,1,0:T(8,128)(2,1)}, u32[]{:S(2)}) copy-start(bf16[2,256,1024]{2,1,0:T(8,128)(2,1)} %refs_0_.8) | copy-start | bytes 3145732
  2.0 3.6 %copy-start.1 = (bf16[128,1024]{1,0:T(8,128)(2,1)S(1)}, bf16[128,1024]{1,0:T(8,128)(2,1)}, u32[]{:S(2)}) copy-start(bf16[128,1024]{1,0:T(8,128)(2,1)} %refs_0_.6) | copy-start | bytes 786436
  2.0 4.1 %copy-start.2 = (bf16[128,1024]{1,0:T(8,128)(2,1)S(1)}, bf16[128,1024]{1,0:T(8,128)(2,1)}, u32[]{:S(2)}) copy-start(bf16[128,1024]{1,0:T(8,128)(2,1)} %refs_1_.3) | copy-start | bytes 786436
  2.0 4.1 %copy-start.4 = (s32[1,1,4]{2,1,0:T(1,128)S(1)}, s32[1,1,4]{2,1,0:T(1,128)}, u32[]{:S(2)}) copy-start(s32[1,1,4]{2,1,0:T(1,128)} %refs_0_.5) | copy-start | bytes 52
  2.0 4.1 %copy-start.5 = (s32[1,1,4]{2,1,0:T(1,128)S(1)}, s32[1,1,4]{2,1,0:T(1,128)}, u32[]{:S(2)}) copy-start(s32[1,1,4]{2,1,0:T(1,128)} %refs_1_.2) | copy-start | bytes 52
  2.6 11.7 %collective-permute-start.3 = (bf16[2,256,512]{2,1,0:T(8,128)(2,1)S(1)}, bf16[2,256,512]{2,1,0:T(8,128)(2,1)S(1)}, u32[]{:S(2)}, u32[]{:S(2)}) collective-permute-start(bf16[2,256,512]{2,1,0:T(8,128)(2,1)S(1)} %chip_halves.2.refs_2_.refs_10_), channel_id=1, source_target_pairs={{0,2},{1,5},{2,0},{3,7},{4,6},{5,1},{6,4},{7,3},{8,10},{9,13},{10,... | collective-permute-start | bytes 1572872 | tf_op jit(solution)/shard_map/to_kv/ppermute | solution.py:29
  5.5 12.3 %collective-permute-start.8 = (bf16[2,256,1024]{2,1,0:T(8,128)(2,1)S(1)}, bf16[2,256,1024]{2,1,0:T(8,128)(2,1)S(1)}, u32[]{:S(2)}, u32[]{:S(2)}) collective-permute-start(bf16[2,256,1024]{2,1,0:T(8,128)(2,1)S(1)} %copy-done), channel_id=1, source_target_pairs={{0,1},{1,0},{2,3},{3,2},{4,5},{5,4},{6,7},{7,6},{8,9},{9,8},{10,11... | collective-permute-start | bytes 3145736 | tf_op jit(solution)/shard_map/to_tokens/ppermute | solution.py:22
  5.5 3.0 %collective-permute-start.4 = (bf16[128,1024]{1,0:T(8,128)(2,1)S(1)}, bf16[128,1024]{1,0:T(8,128)(2,1)S(1)}, u32[]{:S(2)}, u32[]{:S(2)}) collective-permute-start(bf16[128,1024]{1,0:T(8,128)(2,1)S(1)} %copy-done.1), channel_id=1, source_target_pairs={{0,1},{1,0},{2,3},{3,2},{4,5},{5,4},{6,7},{7,6},{8,9},{9,8},{10,11... | collective-permute-start | bytes 786440 | tf_op jit(solution)/shard_map/to_core/ppermute | solution.py:22
  6.0 4.0 %collective-permute-start.5 = (bf16[128,1024]{1,0:T(8,128)(2,1)S(1)}, bf16[128,1024]{1,0:T(8,128)(2,1)S(1)}, u32[]{:S(2)}, u32[]{:S(2)}) collective-permute-start(bf16[128,1024]{1,0:T(8,128)(2,1)S(1)} %copy-done.2), channel_id=1, source_target_pairs={{0,1},{1,0},{2,3},{3,2},{4,5},{5,4},{6,7},{7,6},{8,9},{9,8},{10,11... | collective-permute-start | bytes 786440 | tf_op jit(solution)/shard_map/to_core/ppermute | solution.py:22
  8.6 9.2 %collective-permute-start.9 = (bf16[2,256,512]{2,1,0:T(8,128)(2,1)S(1)}, bf16[2,256,512]{2,1,0:T(8,128)(2,1)S(1)}, u32[]{:S(2)}, u32[]{:S(2)}) collective-permute-start(bf16[2,256,512]{2,1,0:T(8,128)(2,1)S(1)} %chip_halves.2.refs_2_.refs_10_), channel_id=1, source_target_pairs={{0,4},{1,3},{2,6},{3,1},{4,0},{5,7},{6,2},{7,5},{8,12},{9,11},{10,... | collective-permute-start | bytes 1572872 | tf_op jit(solution)/shard_map/to_kv/ppermute | solution.py:29
  10.1 1.1 %collective-permute-start.6 = (s32[2,4]{1,0:T(2,128)S(1)}, s32[2,4]{1,0:T(2,128)S(1)}, u32[]{:S(2)}, u32[]{:S(2)}) collective-permute-start(s32[2,4]{1,0:T(2,128)S(1)} %pack_forks.1.refs_4_.refs_0_), channel_id=1, source_target_pairs={{0,1},{1,0},{2,3},{3,2},{4,5},{5,4},{6,7},{7,6},{8,9},{9,8},{10,11... | collective-permute-start | bytes 104 | tf_op jit(solution)/shard_map/to_forks/ppermute | solution.py:22
  14.3 9.4 %collective-permute-start.7 = (bf16[2,256,512]{2,1,0:T(8,128)(2,1)S(1)}, bf16[2,256,512]{2,1,0:T(8,128)(2,1)S(1)}, u32[]{:S(2)}, u32[]{:S(2)}) collective-permute-start(bf16[2,256,512]{2,1,0:T(8,128)(2,1)S(1)} %get-tuple-element.40.refs_3_.refs_11_), channel_id=1, source_target_pairs={{0,4},{1,3},{2,6},{3,1},{4,0},{5,7},{6,2},{7,5},{8,12},{9,11},{10,... | collective-permute-start | bytes 1572872 | tf_op jit(solution)/shard_map/to_kv_far/ppermute | solution.py:29
  23.8 6.4 %collective-permute-start.11 = (bf16[1,256,256]{2,1,0:T(8,128)(2,1)S(1)}, bf16[1,256,256]{2,1,0:T(8,128)(2,1)S(1)}, u32[]{:S(2)}, u32[]{:S(2)}) collective-permute-start(bf16[1,256,256]{2,1,0:T(8,128)(2,1)S(1)} %get-tuple-element.43.refs_2_), channel_id=1, source_target_pairs={{0,2},{1,5},{2,0},{3,7},{4,6},{5,1},{6,4},{7,3},{8,10},{9,13},{10,... | collective-permute-start | bytes 393224 | tf_op jit(solution)/shard_map/to_query/ppermute | solution.py:29
  26.2 5.9 %collective-permute-start.10 = (bf16[1,256,256]{2,1,0:T(8,128)(2,1)S(1)}, bf16[1,256,256]{2,1,0:T(8,128)(2,1)S(1)}, u32[]{:S(2)}, u32[]{:S(2)}) collective-permute-start(bf16[1,256,256]{2,1,0:T(8,128)(2,1)S(1)} %get-tuple-element.43.refs_2_), channel_id=1, source_target_pairs={{0,4},{1,3},{2,6},{3,1},{4,0},{5,7},{6,2},{7,5},{8,12},{9,11},{10,... | collective-permute-start | bytes 393224 | tf_op jit(solution)/shard_map/to_query/ppermute | solution.py:29
  29.8 8.4 %collective-permute-start.13 = (bf16[2,4,128,128]{3,2,1,0:T(8,128)(2,1)S(1)}, bf16[2,4,128,128]{3,2,1,0:T(8,128)(2,1)S(1)}, u32[]{:S(2)}, u32[]{:S(2)}) collective-permute-start(bf16[2,4,128,128]{3,2,1,0:T(8,128)(2,1)S(1)} %get-tuple-element.48), channel_id=1, source_target_pairs={{0,2},{1,5},{2,0},{3,7},{4,6},{5,1},{6,4},{7,3},{8,10},{9,13},{10,... | collective-permute-start | bytes 786440 | tf_op jit(solution)/shard_map/to_scan/ppermute | solution.py:29
  32.1 6.3 %collective-permute-start.12 = (bf16[1,256,256]{2,1,0:T(8,128)(2,1)S(1)}, bf16[1,256,256]{2,1,0:T(8,128)(2,1)S(1)}, u32[]{:S(2)}, u32[]{:S(2)}) collective-permute-start(bf16[1,256,256]{2,1,0:T(8,128)(2,1)S(1)} %get-tuple-element.47.refs_3_), channel_id=1, source_target_pairs={{0,4},{1,3},{2,6},{3,1},{4,0},{5,7},{6,2},{7,5},{8,12},{9,11},{10,... | collective-permute-start | bytes 393224 | tf_op jit(solution)/shard_map/to_query_far/ppermute | solution.py:29
  34.6 6.9 %collective-permute-start.14 = (bf16[1,256,256]{2,1,0:T(8,128)(2,1)S(1)}, bf16[1,256,256]{2,1,0:T(8,128)(2,1)S(1)}, u32[]{:S(2)}, u32[]{:S(2)}) collective-permute-start(bf16[1,256,256]{2,1,0:T(8,128)(2,1)S(1)} %get-tuple-element.47.refs_3_), channel_id=1, source_target_pairs={{0,8},{8,0},{16,24},{24,16},{1,9},{9,1},{17,25},{25,17},{2,10},{10... | collective-permute-start | bytes 393224 | tf_op jit(solution)/shard_map/to_query_lane/ppermute | solution.py:22
  36.2 6.2 %collective-permute-start.15 = (bf16[1,256,256]{2,1,0:T(8,128)(2,1)S(1)}, bf16[1,256,256]{2,1,0:T(8,128)(2,1)S(1)}, u32[]{:S(2)}, u32[]{:S(2)}) collective-permute-start(bf16[1,256,256]{2,1,0:T(8,128)(2,1)S(1)} %collective-permute-done.10.refs_0_.refs_4_), channel_id=1, source_target_pairs={{0,8},{8,0},{16,24},{24,16},{1,9},{9,1},{17,25},{25,17},{2,10},{10... | collective-permute-start | bytes 393224 | tf_op jit(solution)/shard_map/to_query_lane/ppermute | solution.py:22
  38.3 6.4 %collective-permute-start.17 = (bf16[2,4,128,128]{3,2,1,0:T(8,128)(2,1)S(1)}, bf16[2,4,128,128]{3,2,1,0:T(8,128)(2,1)S(1)}, u32[]{:S(2)}, u32[]{:S(2)}) collective-permute-start(bf16[2,4,128,128]{3,2,1,0:T(8,128)(2,1)S(1)} %scan_step.1.refs_1_), channel_id=1, source_target_pairs={{0,4},{1,3},{2,6},{3,1},{4,0},{5,7},{6,2},{7,5},{8,12},{9,11},{10,... | collective-permute-start | bytes 786440 | tf_op jit(solution)/shard_map/to_scan/ppermute | solution.py:29
  38.4 11.5 %collective-permute-start.16 = (bf16[1,256,256]{2,1,0:T(8,128)(2,1)S(1)}, bf16[1,256,256]{2,1,0:T(8,128)(2,1)S(1)}, u32[]{:S(2)}, u32[]{:S(2)}) collective-permute-start(bf16[1,256,256]{2,1,0:T(8,128)(2,1)S(1)} %get-tuple-element.50.refs_5_), channel_id=1, source_target_pairs={{0,8},{8,0},{16,24},{24,16},{1,9},{9,1},{17,25},{25,17},{2,10},{10... | collective-permute-start | bytes 393224 | tf_op jit(solution)/shard_map/to_query_lane/ppermute | solution.py:22
  42.4 7.7 %copy-start.6 = (bf16[4,128,1024]{2,1,0:T(8,128)(2,1)S(1)}, bf16[4,128,1024]{2,1,0:T(8,128)(2,1)}, u32[]{:S(2)}) copy-start(bf16[4,128,1024]{2,1,0:T(8,128)(2,1)} %param.10) | copy-start | bytes 3145732
  45.7 15.5 %collective-permute-start.18 = (bf16[2,1,4,128,128]{4,3,2,1,0:T(8,128)(2,1)S(1)}, bf16[2,1,4,128,128]{4,3,2,1,0:T(8,128)(2,1)S(1)}, u32[]{:S(2)}, u32[]{:S(2)}) collective-permute-start(bf16[2,1,4,128,128]{4,3,2,1,0:T(8,128)(2,1)S(1)} %get-tuple-element.62), channel_id=1, source_target_pairs={{0,8},{8,0},{16,24},{24,16},{1,9},{9,1},{17,25},{25,17},{2,10},{10... | collective-permute-start | bytes 786440 | tf_op jit(solution)/shard_map/to_lane/ppermute | solution.py:22
  47.4 13.9 %collective-permute-start.19 = (bf16[2,1,4,128,128]{4,3,2,1,0:T(8,128)(2,1)S(1)}, bf16[2,1,4,128,128]{4,3,2,1,0:T(8,128)(2,1)S(1)}, u32[]{:S(2)}, u32[]{:S(2)}) collective-permute-start(bf16[2,1,4,128,128]{4,3,2,1,0:T(8,128)(2,1)S(1)} %get-tuple-element.63), channel_id=1, source_target_pairs={{0,24},{8,16},{16,8},{24,0},{1,25},{9,17},{17,9},{25,1},{2,26},{10... | collective-permute-start | bytes 786440 | tf_op jit(solution)/shard_map/to_lane/ppermute | solution.py:22
  49.8 19.0 %collective-permute-start.23 = (bf16[2,1,4,128,128]{4,3,2,1,0:T(8,128)(2,1)S(1)}, bf16[2,1,4,128,128]{4,3,2,1,0:T(8,128)(2,1)S(1)}, u32[]{:S(2)}, u32[]{:S(2)}) collective-permute-start(bf16[2,1,4,128,128]{4,3,2,1,0:T(8,128)(2,1)S(1)} %get-tuple-element.68), channel_id=1, source_target_pairs={{0,16},{8,24},{16,0},{24,8},{1,17},{9,25},{17,1},{25,9},{2,18},{10... | collective-permute-start | bytes 786440 | tf_op jit(solution)/shard_map/to_lane/ppermute | solution.py:22
  50.0 9.3 %collective-permute-start.20 = (bf16[3,256,256]{2,1,0:T(8,128)(2,1)S(1)}, bf16[3,256,256]{2,1,0:T(8,128)(2,1)S(1)}, u32[]{:S(2)}, u32[]{:S(2)}) collective-permute-start(bf16[3,256,256]{2,1,0:T(8,128)(2,1)S(1)} %get-tuple-element.64), channel_id=1, source_target_pairs={{0,4},{1,3},{2,6},{3,1},{4,0},{5,7},{6,2},{7,5},{8,12},{9,11},{10,... | collective-permute-start | bytes 1179656 | tf_op jit(solution)/shard_map/to_out/ppermute | solution.py:29
  50.0 9.2 %collective-permute-start.21 = (bf16[2,256,512]{2,1,0:T(8,128)(2,1)S(1)}, bf16[2,256,512]{2,1,0:T(8,128)(2,1)S(1)}, u32[]{:S(2)}, u32[]{:S(2)}) collective-permute-start(bf16[2,256,512]{2,1,0:T(8,128)(2,1)S(1)} %get-tuple-element.65.refs_0_), channel_id=1, source_target_pairs={{0,2},{1,5},{2,0},{3,7},{4,6},{5,1},{6,4},{7,3},{8,10},{9,13},{10,... | collective-permute-start | bytes 1572872 | tf_op jit(solution)/shard_map/to_out/ppermute | solution.py:29
  59.2 10.1 %collective-permute-start.26 = (bf16[2,256,512]{2,1,0:T(8,128)(2,1)S(1)}, bf16[2,256,512]{2,1,0:T(8,128)(2,1)S(1)}, u32[]{:S(2)}, u32[]{:S(2)}) collective-permute-start(bf16[2,256,512]{2,1,0:T(8,128)(2,1)S(1)} %get-tuple-element.71.refs_1_), channel_id=1, source_target_pairs={{0,1},{1,0},{2,3},{3,2},{4,5},{5,4},{6,7},{7,6},{8,9},{9,8},{10,11... | collective-permute-start | bytes 1572872 | tf_op jit(solution)/shard_map/to_out_core/ppermute | solution.py:22
  59.2 10.1 %collective-permute-start.25 = (bf16[2,256,512]{2,1,0:T(8,128)(2,1)S(1)}, bf16[2,256,512]{2,1,0:T(8,128)(2,1)S(1)}, u32[]{:S(2)}, u32[]{:S(2)}) collective-permute-start(bf16[2,256,512]{2,1,0:T(8,128)(2,1)S(1)} %get-tuple-element.71.refs_1_), channel_id=1, source_target_pairs={{0,4},{1,3},{2,6},{3,1},{4,0},{5,7},{6,2},{7,5},{8,12},{9,11},{10,... | collective-permute-start | bytes 1572872 | tf_op jit(solution)/shard_map/to_out_far/ppermute | solution.py:29
  62.0 7.3 %collective-permute-start.22 = (bf16[3,128,512]{2,1,0:T(8,128)(2,1)S(1)}, bf16[3,128,512]{2,1,0:T(8,128)(2,1)S(1)}, u32[]{:S(2)}, u32[]{:S(2)}) collective-permute-start(bf16[3,128,512]{2,1,0:T(8,128)(2,1)S(1)} %get-tuple-element.67), channel_id=1, source_target_pairs={{0,1},{1,0},{2,3},{3,2},{4,5},{5,4},{6,7},{7,6},{8,9},{9,8},{10,11... | collective-permute-start | bytes 1179656 | tf_op jit(solution)/shard_map/to_normed/ppermute | solution.py:22
  69.2 1.4 %collective-permute-start.24 = (bf16[1,128,512]{2,1,0:T(8,128)(2,1)S(1)}, bf16[1,128,512]{2,1,0:T(8,128)(2,1)S(1)}, u32[]{:S(2)}, u32[]{:S(2)}) collective-permute-start(bf16[1,128,512]{2,1,0:T(8,128)(2,1)S(1)} %get-tuple-element.70), channel_id=1, source_target_pairs={{0,1},{1,0},{2,3},{3,2},{4,5},{5,4},{6,7},{7,6},{8,9},{9,8},{10,11... | collective-permute-start | bytes 393224 | tf_op jit(solution)/shard_map/to_normed/ppermute | solution.py:22
  69.6 1.0 %copy-start.3 = (s32[4]{0:T(128)S(1)}, s32[4]{0:T(128)}, u32[]{:S(2)}) copy-start(s32[4]{0:T(128)} %refs_0_.9) | copy-start | bytes 52
